TPU v7x, 32 devices: a whole 2x2x4 slice. The times are simulated.
32 devices in a mesh: seq: 8 (over y, x, core), wshard: 4 (over z).
Axes of the slice: x: 2, y: 2, z: 4, core: 2. Of those that a mesh axis runs over, the one named last changes fastest.
Arguments:
- tokens: bfloat16 [4, 4096, 1024], P('wshard', 'seq'), may hold values from -6 to 6
- slot_lengths: int32 [4, 3], P('wshard'), may hold values from 1 to 3584, as said below
- live_lengths: int32 [4, 3], P('wshard'), may hold values from 1 to 3584, as said below
- norm_gain: bfloat16 [1024], P('wshard'), may hold values from 0.099609375 to 1.8984375
- w_qkv: bfloat16 [1024, 3072], P('wshard'), may hold values from -0.1875 to 0.1875
- w_beta: bfloat16 [1024, 8], P('wshard'), may hold values from -0.1875 to 0.1875
- w_outgate: bfloat16 [1024, 1024], P('wshard'), may hold values from -0.1875 to 0.1875
- conv_weight: bfloat16 [4, 3072], P(None, 'wshard'), may hold values from -3 to 3
- ridge: bfloat16 [1024], P('wshard'), may hold values from 0.5 to 4
- head_gain: bfloat16 [1024], P('wshard'), may hold values from 0.099609375 to 1.8984375
- w_out: bfloat16 [1024, 1024], P('wshard'), may hold values from -0.1875 to 0.1875
- ffn_gain: bfloat16 [1024], P('wshard'), may hold values from 0.099609375 to 1.8984375
- w_gate: bfloat16 [1024, 2816], P('wshard'), may hold values from -0.1875 to 0.1875
- w_up: bfloat16 [1024, 2816], P('wshard'), may hold values from -0.1875 to 0.1875
- w_down: bfloat16 [2816, 1024], P('wshard'), may hold values from -0.109375 to 0.109375
- cotangent: bfloat16 [4, 4096, 1024], P('wshard', 'seq'), may hold values from -6 to 6
Outputs:
- output: bfloat16 [4, 4096, 1024], P('wshard', 'seq')
- grad_tokens: bfloat16 [4, 4096, 1024], P('wshard', 'seq')
- grad_norm_gain: float32 [1024], P('wshard')
- grad_w_qkv: float32 [1024, 3072], P('wshard')
- grad_w_beta: float32 [1024, 8], P('wshard')
- grad_w_outgate: float32 [1024, 1024], P('wshard')
- grad_conv_weight: float32 [4, 3072], P(None, 'wshard')
- grad_ridge: float32 [1024], P('wshard')
- grad_head_gain: float32 [1024], P('wshard')
- grad_w_out: float32 [1024, 1024], P('wshard')
- grad_ffn_gain: float32 [1024], P('wshard')
- grad_w_gate: float32 [1024, 2816], P('wshard')
- grad_w_up: float32 [1024, 2816], P('wshard')
- grad_w_down: float32 [2816, 1024], P('wshard')
Inputs may be any that keep to these rules, and one draw needn't show every extreme that they name: `slot_lengths`: each batch row has three slots that cover its 4096 positions in order: a head slot shorter than 512, a middle slot of exactly 3584 positions, and a tail slot; head and tail together hold 512 positions. `live_lengths`: A live length is at least 1 and at most its slot's length; the middle slot is live in full.
All inputs are finite; a program needn't handle non-finite values.
Results may differ from a plain program's by a relative error of at most 0.018.
The roundings to bfloat16 on the way count: a program that leaves them out, or rounds other values in their place, can miss the bound.
Values may be sent and summed in bfloat16 or wider, within the bound.
A program may use at most 256 MiB of HBM per device.

v0:
```python
import jax
import jax.numpy as jnp
from jax import lax
from jax.sharding import PartitionSpec as P

D = 1024
HEADS = 8
HEAD_DIM = 128
TAPS = 4
WINDOW = 1024
ITERS = 2


def passed_along(value, axis, steps):
    count = lax.axis_size(axis)
    initial, last = (max(0, -steps), min(count, count - steps))
    return lax.ppermute(value, axis, [(source, source + steps) for source in range(initial, last)])


def shortened(array):

    def short(part):
        return part.astype(jnp.bfloat16) if part.dtype == jnp.float32 else part

    return jax.tree.map(short, array)


def token_layout(slot_row, live_row, positions):
    starts = (jnp.cumsum(slot_row) - slot_row).astype(jnp.int32)
    after = positions[:, None] >= starts[None, :]
    segment = (jnp.sum(after.astype(jnp.int32), axis=1) - 1).astype(jnp.int32)
    chosen = segment[:, None] == jnp.arange(slot_row.shape[0], dtype=jnp.int32)[None, :]
    begin = jnp.sum(jnp.where(chosen, starts[None, :], 0), axis=1).astype(jnp.int32)
    limit = jnp.sum(jnp.where(chosen, live_row[None, :], 0), axis=1).astype(jnp.int32)
    valid = (segment >= 0) & (positions - begin < limit)
    return (segment, valid)


def conv_same(seg_conv, seg_own):
    row_count = seg_own.shape[0]
    stacked = jnp.stack(
        [
            seg_conv[TAPS - 1 - tap_index : TAPS - 1 - tap_index + row_count] == seg_own
            for tap_index in range(TAPS)
        ]
    )
    return stacked.astype(jnp.float32)[:, :, None]


def build_mask(query_pos, key_pos, seg_queries, seg_keys, valid_keys):
    spacing = query_pos[:, None] - key_pos[None, :]
    inside = (
        (spacing >= 0)
        & (spacing < WINDOW)
        & (seg_keys[None, :] == seg_queries[:, None])
        & valid_keys[None, :]
    )
    return inside.astype(jnp.float32)


def by_heads(array):
    return array.reshape(array.shape[0], HEADS, HEAD_DIM).transpose(1, 0, 2)


def from_heads(array):
    return array.transpose(1, 0, 2).reshape(array.shape[1], D)


def make_kit():

    @jax.custom_vjp
    def low(v):
        return lax.optimization_barrier(v.astype(jnp.bfloat16)).astype(jnp.float32)

    @jax.custom_vjp
    def low_back(v):
        return v

    def low_keep(v):
        return (low(v), None)

    def low_pass(kept, grad):
        return (grad,)

    def back_keep(v):
        return (v, None)

    def back_low(kept, grad):
        return (low(grad),)

    low.defvjp(low_keep, low_pass)
    low_back.defvjp(back_keep, back_low)

    @jax.custom_vjp
    def matmul(left, right):
        return jnp.dot(
            left.astype(jnp.bfloat16),
            right.astype(jnp.bfloat16),
            preferred_element_type=jnp.float32,
        )

    def matmul_keep(left, right):
        left_low = left.astype(jnp.bfloat16)
        right_low = right.astype(jnp.bfloat16)
        return (
            jnp.dot(left_low, right_low, preferred_element_type=jnp.float32),
            (left_low, right_low),
        )

    def matmul_grads(kept, grad):
        left_low, right_low = kept
        grad_low = grad.astype(jnp.bfloat16)
        grad_left = lax.dot_general(
            grad_low, right_low, (((1,), (1,)), ((), ())), preferred_element_type=jnp.float32
        )
        grad_right = lax.dot_general(
            left_low, grad_low, (((0,), (0,)), ((), ())), preferred_element_type=jnp.float32
        )
        return (grad_left, grad_right)

    matmul.defvjp(matmul_keep, matmul_grads)

    @jax.custom_vjp
    def matmul_t(left, right):
        return lax.dot_general(
            left.astype(jnp.bfloat16),
            right.astype(jnp.bfloat16),
            (((1,), (1,)), ((), ())),
            preferred_element_type=jnp.float32,
        )

    def matmul_t_keep(left, right):
        left_low = left.astype(jnp.bfloat16)
        right_low = right.astype(jnp.bfloat16)
        value = lax.dot_general(
            left_low, right_low, (((1,), (1,)), ((), ())), preferred_element_type=jnp.float32
        )
        return (value, (left_low, right_low))

    def matmul_t_grads(kept, grad):
        left_low, right_low = kept
        grad_low = grad.astype(jnp.bfloat16)
        grad_left = jnp.dot(grad_low, right_low, preferred_element_type=jnp.float32)
        grad_right = lax.dot_general(
            grad_low, left_low, (((0,), (0,)), ((), ())), preferred_element_type=jnp.float32
        )
        return (grad_left, grad_right)

    matmul_t.defvjp(matmul_t_keep, matmul_t_grads)

    def section_in(xrow, gain_in, mat_qkv, mat_beta, mat_og):
        hidden = low(
            xrow * lax.rsqrt(jnp.mean(xrow * xrow, axis=-1, keepdims=True) + 1e-06) * gain_in
        )
        qkv = low_back(low(matmul(hidden, mat_qkv)))
        beta = low(jax.nn.sigmoid(low_back(matmul(hidden, mat_beta))))
        gate_pre = low_back(matmul(hidden, mat_og))
        return (qkv, beta, gate_pre)

    def section_conv(qkv_ext, conv_taps, same):
        row_count = qkv_ext.shape[0] - (TAPS - 1)
        total = jnp.zeros((row_count, qkv_ext.shape[1]), jnp.float32)
        for tap_index in range(TAPS):
            source = qkv_ext[TAPS - 1 - tap_index : TAPS - 1 - tap_index + row_count]
            total = total + conv_taps[tap_index] * source * same[tap_index]
        active = jax.nn.silu(total)

        def unit_rows(block):
            shaped = block.reshape(row_count, HEADS, HEAD_DIM)
            shaped = shaped * lax.rsqrt(jnp.sum(shaped * shaped, axis=-1, keepdims=True) + 1e-06)
            return shaped.reshape(row_count, D)

        return (
            low(unit_rows(active[:, :D])),
            low(unit_rows(active[:, D : 2 * D])),
            low(active[:, 2 * D :]),
        )

    def head_mix(queries, key_rows, value_rows, weight, ridge_head, window_mask):
        scaling = window_mask * weight[None, :]
        solution = jnp.zeros_like(queries)
        residue = queries
        direction = queries
        energy = jnp.sum(residue * residue, axis=-1, keepdims=True)
        for sweep in range(ITERS):
            apply_scores = low_back(matmul_t(low(direction), key_rows))
            image_vec = (
                low_back(matmul(low(scaling * apply_scores), key_rows))
                + ridge_head[None, :] * direction
            )
            step_size = energy / jnp.sum(direction * image_vec, axis=-1, keepdims=True)
            solution = solution + step_size * direction
            residue = residue - step_size * image_vec
            energy_next = jnp.sum(residue * residue, axis=-1, keepdims=True)
            direction = residue + energy_next / energy * direction
            energy = energy_next
        scores = low_back(matmul_t(low(solution), key_rows))
        return low_back(matmul(low(scaling * scores), value_rows))

    def section_out(
        xrow, mixed, gate_pre, gain_head, mat_out, gain_ffn, mat_gate, mat_up, mat_down, valid
    ):
        row_count = xrow.shape[0]
        shaped = mixed.reshape(row_count, HEADS, HEAD_DIM)
        shaped = shaped * lax.rsqrt(jnp.mean(shaped * shaped, axis=-1, keepdims=True) + 1e-05)
        normed = shaped.reshape(row_count, D) * gain_head
        gated = low(normed * jax.nn.silu(gate_pre))
        middle = xrow + low_back(matmul(gated, mat_out))
        hidden = low(
            middle * lax.rsqrt(jnp.mean(middle * middle, axis=-1, keepdims=True) + 1e-06) * gain_ffn
        )
        inner = low(
            jax.nn.silu(low_back(matmul(hidden, mat_gate))) * low_back(matmul(hidden, mat_up))
        )
        return valid[:, None] * (middle + low_back(matmul(inner, mat_down)))

    return (section_in, section_conv, head_mix, section_out)


def on_device(
    tokens,
    slot_lengths,
    live_lengths,
    norm_gain,
    w_qkv,
    w_beta,
    w_outgate,
    conv_weight,
    ridge,
    head_gain,
    w_out,
    ffn_gain,
    w_gate,
    w_up,
    w_down,
    cotangent,
):
    section_in, section_conv, head_mix, section_out = make_kit()
    row_count = tokens.shape[1]
    depth = (WINDOW + row_count - 1) // row_count
    halo_rows = depth * row_count
    whole = (
        lax.all_gather(norm_gain, "wshard", axis=0, tiled=True),
        lax.all_gather(w_qkv, "wshard", axis=0, tiled=True),
        lax.all_gather(w_beta, "wshard", axis=0, tiled=True),
        lax.all_gather(w_outgate, "wshard", axis=0, tiled=True),
        lax.all_gather(conv_weight, "wshard", axis=1, tiled=True),
        lax.all_gather(ridge, "wshard", axis=0, tiled=True),
        lax.all_gather(head_gain, "wshard", axis=0, tiled=True),
        lax.all_gather(w_out, "wshard", axis=0, tiled=True),
        lax.all_gather(ffn_gain, "wshard", axis=0, tiled=True),
        lax.all_gather(w_gate, "wshard", axis=0, tiled=True),
        lax.all_gather(w_up, "wshard", axis=0, tiled=True),
        lax.all_gather(w_down, "wshard", axis=0, tiled=True),
    )
    params = tuple((member.astype(jnp.float32) for member in whole))
    rank = lax.axis_index("seq")
    positions = rank * row_count - halo_rows + jnp.arange(halo_rows + row_count, dtype=jnp.int32)
    segment, valid = token_layout(slot_lengths[0], live_lengths[0], positions)
    seg_own = segment[halo_rows:]
    valid_own = valid[halo_rows:].astype(jnp.float32)
    same = conv_same(segment[halo_rows - (TAPS - 1) :], seg_own)
    window_mask = build_mask(positions[halo_rows:], positions, seg_own, segment, valid)
    xrow = tokens[0].astype(jnp.float32)

    def back_half(xrow, mixed, gate_pre, gain_head, mat_out, gain_ffn, mat_gate, mat_up, mat_down):
        return section_out(
            xrow,
            mixed,
            gate_pre,
            gain_head,
            mat_out,
            gain_ffn,
            mat_gate,
            mat_up,
            mat_down,
            valid_own,
        )

    def conv_local(stacked, conv_taps):
        return section_conv(stacked, conv_taps, same)

    def head_local(queries, key_rows, value_rows, weight, ridge_head):
        return head_mix(queries, key_rows, value_rows, weight, ridge_head, window_mask)

    (qkv, beta, gate_pre), pull_front = jax.vjp(
        section_in, xrow, params[0], params[1], params[2], params[3]
    )
    tail_rows = qkv[row_count - (TAPS - 1) :].astype(jnp.bfloat16)
    before = passed_along(tail_rows, "seq", 1).astype(jnp.float32)
    (queries, key_rows, value_rows), pull_conv = jax.vjp(
        conv_local, jnp.concatenate([before, qkv]), params[4]
    )
    payload = (
        key_rows.astype(jnp.bfloat16),
        value_rows.astype(jnp.bfloat16),
        beta.astype(jnp.bfloat16),
    )
    arrivals = []
    moving = payload
    for hop_count in range(depth):
        moving = passed_along((moving[0], moving[1], moving[2]), "seq", 1)
        arrivals.append(moving)
    ordered = arrivals[::-1] + [payload]
    key_ext = jnp.concatenate([member[0] for member in ordered]).astype(jnp.float32)
    value_ext = jnp.concatenate([member[1] for member in ordered]).astype(jnp.float32)
    beta_ext = jnp.concatenate([member[2] for member in ordered]).astype(jnp.float32)
    head_inputs = (
        by_heads(queries),
        by_heads(key_ext),
        by_heads(value_ext),
        beta_ext.T,
        params[5].reshape(HEADS, HEAD_DIM),
    )
    mixed = from_heads(lax.map(lambda packed: head_local(*packed), head_inputs))
    output, pull_back = jax.vjp(
        back_half,
        xrow,
        mixed,
        gate_pre,
        params[6],
        params[7],
        params[8],
        params[9],
        params[10],
        params[11],
    )
    grad_out = cotangent[0].astype(jnp.float32)
    d_xout, d_mixed, d_gate, d_ghead, d_wout, d_gffn, d_wgate, d_wup, d_wdown = pull_back(grad_out)

    def head_grads(packed):
        head_values, pullback = jax.vjp(
            head_local, packed[0], packed[1], packed[2], packed[3], packed[4]
        )
        return pullback(packed[5])

    d_heads = lax.map(head_grads, head_inputs + (by_heads(d_mixed),))
    d_query = from_heads(d_heads[0])
    d_key_ext = from_heads(d_heads[1])
    d_value_ext = from_heads(d_heads[2])
    d_beta_ext = d_heads[3].T
    d_ridge = d_heads[4].reshape(D)

    def piece_at(hop_count):
        first_row = (depth - hop_count) * row_count
        return (
            d_key_ext[first_row : first_row + row_count],
            d_value_ext[first_row : first_row + row_count],
            d_beta_ext[first_row : first_row + row_count],
        )

    own_grads = piece_at(0)
    carried = jax.tree.map(jnp.zeros_like, own_grads)
    for hop_count in range(depth, 0, -1):
        carried = passed_along(
            shortened(jax.tree.map(jnp.add, carried, piece_at(hop_count))), "seq", -1
        )
    d_key, d_value, d_beta = jax.tree.map(jnp.add, own_grads, carried)
    d_ext, d_taps = pull_conv((d_query, d_key, d_value))
    returned = passed_along(shortened(d_ext[: TAPS - 1]), "seq", -1)
    padding_rows = jnp.zeros((row_count - (TAPS - 1), 3 * D), jnp.float32)
    d_qkv = d_ext[TAPS - 1 :] + jnp.concatenate([padding_rows, returned])
    d_xin, d_gin, d_wqkv, d_wbeta, d_wog = pull_front((d_qkv, d_beta, d_gate))
    shares = (
        lax.psum_scatter(
            d_gin.astype(jnp.bfloat16), "wshard", scatter_dimension=0, tiled=True
        ).astype(jnp.float32),
        lax.psum_scatter(
            d_wqkv.astype(jnp.bfloat16), "wshard", scatter_dimension=0, tiled=True
        ).astype(jnp.float32),
        lax.psum_scatter(
            d_wbeta.astype(jnp.bfloat16), "wshard", scatter_dimension=0, tiled=True
        ).astype(jnp.float32),
        lax.psum_scatter(
            d_wog.astype(jnp.bfloat16), "wshard", scatter_dimension=0, tiled=True
        ).astype(jnp.float32),
        lax.psum_scatter(
            d_taps.astype(jnp.bfloat16), "wshard", scatter_dimension=1, tiled=True
        ).astype(jnp.float32),
        lax.psum_scatter(
            d_ridge.astype(jnp.bfloat16), "wshard", scatter_dimension=0, tiled=True
        ).astype(jnp.float32),
        lax.psum_scatter(
            d_ghead.astype(jnp.bfloat16), "wshard", scatter_dimension=0, tiled=True
        ).astype(jnp.float32),
        lax.psum_scatter(
            d_wout.astype(jnp.bfloat16), "wshard", scatter_dimension=0, tiled=True
        ).astype(jnp.float32),
        lax.psum_scatter(
            d_gffn.astype(jnp.bfloat16), "wshard", scatter_dimension=0, tiled=True
        ).astype(jnp.float32),
        lax.psum_scatter(
            d_wgate.astype(jnp.bfloat16), "wshard", scatter_dimension=0, tiled=True
        ).astype(jnp.float32),
        lax.psum_scatter(
            d_wup.astype(jnp.bfloat16), "wshard", scatter_dimension=0, tiled=True
        ).astype(jnp.float32),
        lax.psum_scatter(
            d_wdown.astype(jnp.bfloat16), "wshard", scatter_dimension=0, tiled=True
        ).astype(jnp.float32),
    )
    totals = lax.psum(
        (
            shares[0],
            shares[1],
            shares[2],
            shares[3],
            shares[4],
            shares[5],
            shares[6],
            shares[7],
            shares[8],
            shares[9],
            shares[10],
            shares[11],
        ),
        "seq",
    )
    return (
        output.astype(jnp.bfloat16)[None],
        (d_xout + d_xin).astype(jnp.bfloat16)[None],
        totals[0],
        totals[1],
        totals[2],
        totals[3],
        totals[4],
        totals[5],
        totals[6],
        totals[7],
        totals[8],
        totals[9],
        totals[10],
        totals[11],
    )


def solution(mesh):
    return jax.shard_map(
        on_device,
        mesh=mesh,
        in_specs=(
            P("wshard", "seq", None),
            P("wshard", None),
            P("wshard", None),
            P("wshard"),
            P("wshard", None),
            P("wshard", None),
            P("wshard", None),
            P(None, "wshard"),
            P("wshard"),
            P("wshard"),
            P("wshard", None),
            P("wshard"),
            P("wshard", None),
            P("wshard", None),
            P("wshard", None),
            P("wshard", "seq", None),
        ),
        out_specs=(
            P("wshard", "seq", None),
            P("wshard", "seq", None),
            P("wshard"),
            P("wshard", None),
            P("wshard", None),
            P("wshard", None),
            P(None, "wshard"),
            P("wshard"),
            P("wshard"),
            P("wshard", None),
            P("wshard"),
            P("wshard", None),
            P("wshard", None),
            P("wshard", None),
        ),
        check_vma=False,
    )
```

profile of v0, /device:TPU:0, one launch (start us, length us, event | category | flops | bytes accessed | tf_op | source)
XLA Modules:
  0.0 1659.3 jit_solution(8864950850665586989)
XLA Ops:
  10.7 12.7 all-gather
  24.7 13.3 all_gather.37
  40.8 13.4 all_gather.38
  55.7 72.5 %all-gather.11.cloned.1.call-done = bf16[1024,3072]{1,0:T(8,128)(2,1)} async-done(((bf16[256,3072]{1,0:T(8,128)(2,1)}), bf16[1024,3072]{1,0:T(8,128)(2,1)}) %all-gather.11.cloned.1.call-update) | async-done | bytes 6291472 | tf_op jit(solution)/shard_map/all_gather | solution.py:244
  128.3 6.5 convolution_convert_fusion.4
  137.0 8.0 all-gather.2
  145.0 13.9 all-gather.1
  158.9 7.8 all-gather.3
  168.9 6.9 fusion.68
  193.3 4.6 fusion.85
  197.9 12.6 collective-permute-start.3
  210.6 24.3 %all-gather.21.cloned.1.call-done = bf16[2816,1024]{1,0:T(8,128)(2,1)} async-done(((bf16[704,1024]{1,0:T(8,128)(2,1)}), bf16[2816,1024]{1,0:T(8,128)(2,1)}) %all-gather.21.cloned.1.call-update) | async-done | bytes 5767184 | tf_op jit(solution)/shard_map/all_gather | solution.py:254
  234.9 8.6 fusion.135
  260.5 76.2 %while.30 = (s32[]{:T(128)}, f32[8,512,128]{2,1,0:T(8,128)}, f32[8,1536]{1,0:T(8,128)S(1)}, f32[8,512,128]{1,2,0:T(8,128)S(1)}, bf16[8,1536,128]{2,1,0:T(8,128)(...) while((s32[]{:T(128)}, f32[8,512,128]{2,1,0:T(8,128)}, ...), condition=%wide.region_12.13_spmd.clone, body=%wide.region_7.12_spmd.clone.sunk | while | flops 1233059328 | bytes 16508581 | solution.py:315
  339.2 4.8 multiply_convert_fusion.5
  349.2 84.6 %all-gather.19.cloned.1.call-done = bf16[1024,2816]{1,0:T(8,128)(2,1)} async-done(((bf16[256,2816]{1,0:T(8,128)(2,1)}), bf16[1024,2816]{1,0:T(8,128)(2,1)}) %all-gather.19.cloned.1.call-update) | async-done | bytes 5767184 | tf_op jit(solution)/shard_map/all_gather | solution.py:253
  433.8 7.5 fusion.134
  441.4 98.9 %all-gather.17.cloned.1.call-done = bf16[1024,2816]{1,0:T(8,128)(2,1)} async-done(((bf16[256,2816]{1,0:T(8,128)(2,1)}), bf16[1024,2816]{1,0:T(8,128)(2,1)}) %all-gather.17.cloned.1.call-update) | async-done | bytes 5767184 | tf_op jit(solution)/shard_map/all_gather | solution.py:252
  540.3 11.2 fusion.71
  556.9 4.0 multiply_reduce_fusion.9
  570.7 196.3 %while.31 = (s32[]{:T(128)}, f32[8,512,128]{1,2,0:T(8,128)}, f32[8,1536,128]{2,1,0:T(8,128)}, f32[8,1536,128]{2,1,0:T(8,128)}, f32[8,1536]{1,0:T(8,128)S(1)}, /*...) while((s32[]{:T(128)}, f32[8,512,128]{1,2,0:T(8,128)}, ...), condition=%wide.region_29.30_spmd.clone, body=%wide.region_17.29_spmd.clone.sunk | while | flops 3468761600 | bytes 96600080 | solution.py:337
  583.9 4.2 select_reduce_fusion.4
  608.4 4.3 select_reduce_fusion.4
  632.9 4.2 select_reduce_fusion.4
  657.4 4.3 select_reduce_fusion.4
  681.8 4.3 select_reduce_fusion.4
  706.3 4.3 select_reduce_fusion.4
  730.9 4.2 select_reduce_fusion.4
  755.4 4.3 select_reduce_fusion.4
  803.9 4.4 add_add_fusion.3
  812.1 8.8 multiply_reduce_fusion.8
  822.3 3.9 convolution_convert_fusion.6
  830.3 7.3 convolution_convert_fusion.2
  837.6 6.9 convolution_convert_fusion.1
  845.8 6.9 convolution_convert_fusion
  853.4 7.9 multiply_multiply_fusion.5
  861.3 6.2 pad_add_fusion
  868.8 16.4 collective-permute-done.13
  887.7 5.6 convolution_convert_fusion.3
  898.1 6.8 fusion.96
  906.8 10.4 fusion.76
  917.3 9.4 all-reduce.17
  931.2 18.7 %reduce-scatter.17.cloned.1.call-done = bf16[256,1024]{1,0:T(8,128)(2,1)} async-done(((bf16[1024,1024]{1,0:T(8,128)(2,1)}), bf16[256,1024]{1,0:T(8,128)(2,1)}) %reduce-scatter.17.cloned.1.call-update) | async-done | bytes 524304 | tf_op jit(solution)/shard_map/reduce_scatter | solution.py:386
  949.8 104.1 %reduce-scatter.19.cloned.1.call-done = bf16[256,2816]{1,0:T(8,128)(2,1)} async-done(((bf16[1024,2816]{1,0:T(8,128)(2,1)}), bf16[256,2816]{1,0:T(8,128)(2,1)}) %reduce-scatter.19.cloned.1.call-update) | async-done | bytes 1441808 | tf_op jit(solution)/shard_map/reduce_scatter | solution.py:392
  1053.9 105.1 %reduce-scatter.21.cloned.1.call-done = bf16[256,2816]{1,0:T(8,128)(2,1)} async-done(((bf16[1024,2816]{1,0:T(8,128)(2,1)}), bf16[256,2816]{1,0:T(8,128)(2,1)}) %reduce-scatter.21.cloned.1.call-update) | async-done | bytes 1441808 | tf_op jit(solution)/shard_map/reduce_scatter | solution.py:395
  1159.0 105.2 %reduce-scatter.23.cloned.1.call-done = bf16[704,1024]{1,0:T(8,128)(2,1)} async-done(((bf16[2816,1024]{1,0:T(8,128)(2,1)}), bf16[704,1024]{1,0:T(8,128)(2,1)}) %reduce-scatter.23.cloned.1.call-update) | async-done | bytes 1441808 | tf_op jit(solution)/shard_map/reduce_scatter | solution.py:398
  1264.2 113.5 %reduce-scatter.11.cloned.1.call-done = bf16[256,3072]{1,0:T(8,128)(2,1)} async-done(((bf16[1024,3072]{1,0:T(8,128)(2,1)}), bf16[256,3072]{1,0:T(8,128)(2,1)}) %reduce-scatter.11.cloned.1.call-update) | async-done | bytes 1572880 | tf_op jit(solution)/shard_map/reduce_scatter | solution.py:368
  1377.7 274.9 %all-reduce.19 = (f32[256]{0:T(256)}, f32[256,3072]{1,0:T(8,128)}, f32[256,8]{0,1:T(8,128)}, f32[256,1024]{1,0:T(8,128)}, f32[4,768]{1,0:T(4,128)}, /*index=5*/f...) all-reduce(f32[256]{0:T(256)S(1)} %dynamic-slice_convert_fusion.8, ...), channel_id=1, replica_groups=mesh['seq'=8,'wshard'=4] {'seq'}, use_global_device_ids=true, to_apply=%region_35.36 | all-reduce | flops 3479552 | bytes 20879360 | tf_op jit(solution)/shard_map/psum | solution.py:402
  (770 shorter events, 367.9 us)
Async XLA Ops:
  7.2 121.1 %all-gather.11.cloned.1.call-start = ((), (), s32[]{:S(2)}) async-start(), calls=%async_computation.8 | async-start | bytes 7864320 | tf_op jit(solution)/shard_map/all_gather | solution.py:244
  7.9 227.0 %all-gather.21.cloned.1.call-start = ((), (), s32[]{:S(2)}) async-start(), calls=%async_computation.13 | async-start | bytes 7208960 | tf_op jit(solution)/shard_map/all_gather | solution.py:254
  8.7 330.5 %all-gather.13.cloned.1.call-start = ((), (), s32[]{:S(2)}) async-start(), calls=%async_computation.9 | async-start | bytes 2621440 | tf_op jit(solution)/shard_map/all_gather | solution.py:246
  9.4 334.6 %all-gather.15.cloned.1.call-start = ((), (), s32[]{:S(2)}) async-start(), calls=%async_computation.10 | async-start | bytes 2621440 | tf_op jit(solution)/shard_map/all_gather | solution.py:250
  10.0 423.8 %all-gather.19.cloned.1.call-start = ((), (), s32[]{:S(2)}) async-start(), calls=%async_computation.12 | async-start | bytes 7208960 | tf_op jit(solution)/shard_map/all_gather | solution.py:253
  10.6 29.8 %copy-start.77 = (s32[1,3]{1,0:T(1,128)S(1)}, s32[1,3]{1,0:T(1,128)}, u32[]{:S(2)}) copy-start(s32[1,3]{1,0:T(1,128)} %param.21) | copy-start | bytes 40
  10.6 30.2 %copy-start.66 = (bf16[4,768]{1,0:T(4,128)(2,1)S(1)}, bf16[4,768]{1,0:T(4,128)(2,1)}, u32[]{:S(2)}) copy-start(bf16[4,768]{1,0:T(4,128)(2,1)} %param.27) | copy-start | bytes 18436
  10.6 43.6 %copy-start.71 = (s32[1,3]{1,0:T(1,128)S(1)}, s32[1,3]{1,0:T(1,128)}, u32[]{:S(2)}) copy-start(s32[1,3]{1,0:T(1,128)} %param.22) | copy-start | bytes 40
  10.6 43.8 %copy-start.23 = (bf16[1,512,1024]{2,1,0:T(8,128)(2,1)S(1)}, bf16[1,512,1024]{2,1,0:T(8,128)(2,1)}, u32[]{:S(2)}) copy-start(bf16[1,512,1024]{2,1,0:T(8,128)(2,1)} %param.35) | copy-start | bytes 3145732
  10.6 529.7 %all-gather.17.cloned.1.call-start = ((), (), s32[]{:S(2)}) async-start(), calls=%async_computation.11 | async-start | bytes 7208960 | tf_op jit(solution)/shard_map/all_gather | solution.py:252
  39.0 127.7 %collective-permute-start = (bf16[512,8]{0,1:T(8,128)(2,1)S(1)}, bf16[512,8]{0,1:T(8,128)(2,1)S(1)}, u32[]{:S(2)}, u32[]{:S(2)}) collective-permute-start(bf16[512,8]{0,1:T(8,128)(2,1)S(1)} %get-tuple-element.418), channel_id=1, source_target_pairs={{0,4},{4,8},{8,12},{12,16},{16,20},{20,24},{24,28},{1,5},{5,9},{9,... | collective-permute-start | bytes 24584 | tf_op jit(solution)/shard_map/ppermute | solution.py:17
  40.3 866.4 %reduce-scatter.13.cloned.1.call-start = ((), (), s32[]{:S(2)}) async-start(), calls=%async_computation.15 | async-start | bytes 20480 | tf_op jit(solution)/shard_map/reduce_scatter | solution.py:371
  54.2 114.7 %copy-start.41 = (f32[1,3072]{1,0:T(1,128)}, f32[1,3072]{1,0:T(1,128)S(1)}, u32[]{:S(2)}) copy-start(f32[1,3072]{1,0:T(1,128)S(1)} %get-tuple-element.407) | copy-start | bytes 36868
  54.2 114.7 %copy-start.43 = (f32[1,3072]{1,0:T(1,128)}, f32[1,3072]{1,0:T(1,128)S(1)}, u32[]{:S(2)}) copy-start(f32[1,3072]{1,0:T(1,128)S(1)} %get-tuple-element.408) | copy-start | bytes 36868
  54.2 114.7 %copy-start.45 = (f32[1,3072]{1,0:T(1,128)}, f32[1,3072]{1,0:T(1,128)S(1)}, u32[]{:S(2)}) copy-start(f32[1,3072]{1,0:T(1,128)S(1)} %get-tuple-element.409) | copy-start | bytes 36868
  54.2 114.7 %copy-start.47 = (f32[1,3072]{1,0:T(1,128)}, f32[1,3072]{1,0:T(1,128)S(1)}, u32[]{:S(2)}) copy-start(f32[1,3072]{1,0:T(1,128)S(1)} %get-tuple-element.410) | copy-start | bytes 36868
  54.4 506.5 %copy-start.64 = (f32[512]{0:T(512)}, f32[512]{0:T(512)S(1)}, u32[]{:S(2)}) copy-start(f32[512]{0:T(512)S(1)} %slice_convert_fusion.5) | copy-start | bytes 6148
  55.7 81.2 %copy-start.78 = (bf16[256]{0:T(256)(128)(2,1)S(1)}, bf16[256]{0:T(256)(128)(2,1)}, u32[]{:S(2)}) copy-start(bf16[256]{0:T(256)(128)(2,1)} %param.29) | copy-start | bytes 1540
  55.7 89.2 %copy-start.79 = (bf16[256]{0:T(256)(128)(2,1)S(1)}, bf16[256]{0:T(256)(128)(2,1)}, u32[]{:S(2)}) copy-start(bf16[256]{0:T(256)(128)(2,1)} %param.28) | copy-start | bytes 1540
  55.7 103.2 %copy-start.80 = (bf16[256]{0:T(256)(128)(2,1)S(1)}, bf16[256]{0:T(256)(128)(2,1)}, u32[]{:S(2)}) copy-start(bf16[256]{0:T(256)(128)(2,1)} %param.31) | copy-start | bytes 1540
  134.8 34.0 %copy-start.8 = (bf16[512,3072]{1,0:T(8,128)(2,1)}, bf16[512,3072]{1,0:T(8,128)(2,1)S(1)}, u32[]{:S(2)}) copy-start(bf16[512,3072]{1,0:T(8,128)(2,1)S(1)} %convolution_convert_fusion.4) | copy-start | bytes 9437188
  134.8 34.0 %collective-permute-start.2 = (bf16[3,3072]{1,0:T(4,128)(2,1)S(1)}, bf16[3,3072]{1,0:T(4,128)(2,1)S(1)}, u32[]{:S(2)}, u32[]{:S(2)}) collective-permute-start(bf16[3,3072]{1,0:T(4,128)(2,1)S(1)} %slice.170), channel_id=1, source_target_pairs={{0,4},{4,8},{8,12},{12,16},{16,20},{20,24},{24,28},{1,5},{5,9},{9,... | collective-permute-start | bytes 55304 | tf_op jit(solution)/shard_map/ppermute | solution.py:17
  136.8 32.1 %copy-start.52 = (f32[1,512]{1,0:T(1,128)}, f32[1,512]{1,0:T(1,128)S(1)}, u32[]{:S(2)}) copy-start(f32[1,512]{1,0:T(1,128)S(1)} %get-tuple-element.411) | copy-start | bytes 6148
  136.8 32.1 %copy-start.54 = (f32[1,512]{1,0:T(1,128)}, f32[1,512]{1,0:T(1,128)S(1)}, u32[]{:S(2)}) copy-start(f32[1,512]{1,0:T(1,128)S(1)} %get-tuple-element.412) | copy-start | bytes 6148
  136.9 32.1 %copy-start.56 = (f32[1,512]{1,0:T(1,128)}, f32[1,512]{1,0:T(1,128)S(1)}, u32[]{:S(2)}) copy-start(f32[1,512]{1,0:T(1,128)S(1)} %get-tuple-element.413) | copy-start | bytes 6148
  136.9 32.1 %copy-start.58 = (f32[1,512]{1,0:T(1,128)}, f32[1,512]{1,0:T(1,128)S(1)}, u32[]{:S(2)}) copy-start(f32[1,512]{1,0:T(1,128)S(1)} %get-tuple-element.414) | copy-start | bytes 6148
  166.7 43.8 %collective-permute-start.1 = (bf16[512,8]{0,1:T(8,128)(2,1)S(1)}, bf16[512,8]{0,1:T(8,128)(2,1)S(1)}, u32[]{:S(2)}, u32[]{:S(2)}) collective-permute-start(bf16[512,8]{0,1:T(8,128)(2,1)S(1)} %collective-permute-done), channel_id=1, source_target_pairs={{0,4},{4,8},{8,12},{12,16},{16,20},{20,24},{24,28},{1,5},{5,9},{9,... | collective-permute-start | bytes 24584 | tf_op jit(solution)/shard_map/ppermute | solution.py:17
  188.9 57.0 %collective-permute-start.5 = (bf16[512,1024]{1,0:T(8,128)(2,1)}, bf16[512,1024]{1,0:T(8,128)(2,1)}, u32[]{:S(2)}, u32[]{:S(2)}) collective-permute-start(bf16[512,1024]{1,0:T(8,128)(2,1)} %slice.254), channel_id=1, source_target_pairs={{0,4},{4,8},{8,12},{12,16},{16,20},{20,24},{24,28},{1,5},{5,9},{9,... | collective-permute-start | bytes 3145736 | tf_op jit(solution)/shard_map/ppermute | solution.py:17
  197.9 51.5 %collective-permute-start.3 = (bf16[512,1024]{1,0:T(8,128)(2,1)}, bf16[512,1024]{1,0:T(8,128)(2,1)}, u32[]{:S(2)}, u32[]{:S(2)}) collective-permute-start(bf16[512,1024]{1,0:T(8,128)(2,1)} %get-tuple-element.402), channel_id=1, source_target_pairs={{0,4},{4,8},{8,12},{12,16},{16,20},{20,24},{24,28},{1,5},{5,9},{9,... | collective-permute-start | bytes 3145736 | tf_op jit(solution)/shard_map/ppermute | solution.py:17
  245.9 11.2 collective-permute-start.6
  249.4 7.9 collective-permute-start.4
  260.5 78.7 %copy-start.11 = (bf16[512,1024]{1,0:T(8,128)(2,1)S(1)}, bf16[512,1024]{1,0:T(8,128)(2,1)}, u32[]{:S(2)}) copy-start(bf16[512,1024]{1,0:T(8,128)(2,1)} %copy-done.10) | copy-start | bytes 3145732
  349.2 191.1 %copy-start.27 = (bf16[512,1024]{1,0:T(8,128)(2,1)}, bf16[512,1024]{1,0:T(8,128)(2,1)S(1)}, u32[]{:S(2)}) copy-start(bf16[512,1024]{1,0:T(8,128)(2,1)S(1)} %multiply_convert_fusion.4) | copy-start | bytes 3145732
  772.2 10.5 collective-permute-start.11
  773.5 7.9 collective-permute-start.7
  780.1 11.9 collective-permute-start.9
  781.4 9.6 collective-permute-start.8
  784.1 12.4 collective-permute-start.12
  791.9 138.2 %reduce-scatter.25.cloned.1.call-start = ((), (), s32[]{:S(2)}) async-start(), calls=%async_computation.21 | async-start | bytes 983040
  795.1 13.2 collective-permute-start.10
  822.2 109.0 %reduce-scatter.15.cloned.1.call-start = ((), (), s32[]{:S(2)}) async-start(), calls=%async_computation.16 | async-start | bytes 2621440 | tf_op jit(solution)/shard_map/reduce_scatter | solution.py:374
  826.3 123.6 %reduce-scatter.17.cloned.1.call-start = ((), (), s32[]{:S(2)}) async-start(), calls=%async_computation.17 | async-start | bytes 2621440 | tf_op jit(solution)/shard_map/reduce_scatter | solution.py:386
  830.2 223.7 %reduce-scatter.19.cloned.1.call-start = ((), (), s32[]{:S(2)}) async-start(), calls=%async_computation.18 | async-start | bytes 7208960 | tf_op jit(solution)/shard_map/reduce_scatter | solution.py:392
  837.6 321.4 %reduce-scatter.21.cloned.1.call-start = ((), (), s32[]{:S(2)}) async-start(), calls=%async_computation.19 | async-start | bytes 7208960 | tf_op jit(solution)/shard_map/reduce_scatter | solution.py:395
  844.6 419.6 %reduce-scatter.23.cloned.1.call-start = ((), (), s32[]{:S(2)}) async-start(), calls=%async_computation.20 | async-start | bytes 7208960 | tf_op jit(solution)/shard_map/reduce_scatter | solution.py:398
  852.7 525.0 %reduce-scatter.11.cloned.1.call-start = ((), (), s32[]{:S(2)}) async-start(), calls=%async_computation.14 | async-start | bytes 7864320 | tf_op jit(solution)/shard_map/reduce_scatter | solution.py:368
  867.5 17.7 %collective-permute-start.13 = (bf16[3,3072]{1,0:T(4,128)(2,1)S(1)}, bf16[3,3072]{1,0:T(4,128)(2,1)S(1)}, u32[]{:S(2)}, u32[]{:S(2)}) collective-permute-start(bf16[3,3072]{1,0:T(4,128)(2,1)S(1)} %slice.255), channel_id=1, source_target_pairs={{4,0},{8,4},{12,8},{16,12},{20,16},{24,20},{28,24},{5,1},{9,5},{13... | collective-permute-start | bytes 55304 | tf_op jit(solution)/shard_map/ppermute | solution.py:17
  927.0 450.7 %copy-start.68 = (bf16[256,8]{0,1:T(8,128)(2,1)S(1)}, bf16[256,8]{0,1:T(8,128)(2,1)}, u32[]{:S(2)}) copy-start(bf16[256,8]{0,1:T(8,128)(2,1)} %reduce-scatter.13.cloned.1.call-done) | copy-start | bytes 12292
  (78 other events, 443.9 us)
Sparse Core Ops, SparseCore 0:
  9.6 118.6 all-gather.10
  129.8 105.0 all-gather.20
  236.5 44.3 all-gather.12
  282.3 44.6 all-gather.14
  328.4 105.3 all-gather.18
  435.3 104.9 all-gather.16
  792.1 26.2 reduce-scatter.12
  822.3 36.0 reduce-scatter.24
  860.8 43.1 reduce-scatter.14
  906.1 43.6 reduce-scatter.16
  952.3 101.6 reduce-scatter.18
  1056.2 102.7 reduce-scatter.20
  1161.4 102.7 reduce-scatter.22
  1266.4 111.2 reduce-scatter.10
where the time goes:
time: 1670 us; the launch traced here: 1660 us
  waiting for transfers between devices  747 us (45%)
  matrix products  364 us (22%)
  blocking collectives  353 us (21%)
  other arithmetic  79.6 us (5%)
  local copies, waits for them, and re-layouts  60.5 us (4%)
  starting transfers between devices  35.9 us (2%)
    psum x1, blocking collectives, on_device(): lax.psum((shares[0], shares[1], shares[2], shares[3], shares[4], shares[5...  275 us
    reduce_scatter x1, waiting for transfers between devices, on_device(): lax.psum_scatter(d_wqkv.astype(jnp.bfloat16), 'wshard', scatter_dimension...  114 us
    reduce_scatter x1, waiting for transfers between devices, on_device(): lax.psum_scatter(d_wdown.astype(jnp.bfloat16), 'wshard', scatter_dimensio...  105 us
    reduce_scatter x1, waiting for transfers between devices, on_device(): lax.psum_scatter(d_wup.astype(jnp.bfloat16), 'wshard', scatter_dimension=...  105 us
    reduce_scatter x1, waiting for transfers between devices, on_device(): lax.psum_scatter(d_wgate.astype(jnp.bfloat16), 'wshard', scatter_dimensio...  104 us
    all_gather x1, waiting for transfers between devices, on_device(): lax.all_gather(w_gate, 'wshard', axis=0, tiled=True)  98.9 us
    all_gather x1, waiting for transfers between devices, on_device(): lax.all_gather(w_up, 'wshard', axis=0, tiled=True)  84.6 us
    all_gather x1, waiting for transfers between devices, on_device(): lax.all_gather(w_qkv, 'wshard', axis=0, tiled=True)  72.5 us
  transfers between devices with their start and end apart: 28, of which 11 were waited for; matrix products, arithmetic and copies ran while one was open for 16% of the time, Pallas kernels for 0%

commit v1 on v0

v1 whole, which is shorter than its diff:
```python
import jax
import jax.numpy as jnp
from jax import lax
from jax.sharding import PartitionSpec as P

D = 1024
HEADS = 8
HEAD_DIM = 128
TAPS = 4
WINDOW = 1024
ITERS = 2


def passed_along(value, axis, steps):
    count = lax.axis_size(axis)
    initial, last = (max(0, -steps), min(count, count - steps))
    return lax.ppermute(value, axis, [(source, source + steps) for source in range(initial, last)])


def token_layout(slot_row, live_row, positions):
    starts = (jnp.cumsum(slot_row) - slot_row).astype(jnp.int32)
    after = positions[:, None] >= starts[None, :]
    segment = (jnp.sum(after.astype(jnp.int32), axis=1) - 1).astype(jnp.int32)
    chosen = segment[:, None] == jnp.arange(slot_row.shape[0], dtype=jnp.int32)[None, :]
    begin = jnp.sum(jnp.where(chosen, starts[None, :], 0), axis=1).astype(jnp.int32)
    limit = jnp.sum(jnp.where(chosen, live_row[None, :], 0), axis=1).astype(jnp.int32)
    valid = (segment >= 0) & (positions - begin < limit)
    return (segment, valid)


def conv_same(seg_conv, seg_own):
    row_count = seg_own.shape[0]
    stacked = jnp.stack(
        [
            seg_conv[TAPS - 1 - tap_index : TAPS - 1 - tap_index + row_count] == seg_own
            for tap_index in range(TAPS)
        ]
    )
    return stacked.astype(jnp.float32)[:, :, None]


def build_mask(query_pos, key_pos, seg_queries, seg_keys, valid_keys):
    spacing = query_pos[:, None] - key_pos[None, :]
    inside = (
        (spacing >= 0)
        & (spacing < WINDOW)
        & (seg_keys[None, :] == seg_queries[:, None])
        & valid_keys[None, :]
    )
    return inside.astype(jnp.float32)


def by_heads(array):
    return array.reshape(array.shape[0], HEADS, HEAD_DIM).transpose(1, 0, 2)


def from_heads(array):
    return array.transpose(1, 0, 2).reshape(array.shape[1], D)


def make_kit():

    @jax.custom_vjp
    def low(v):
        return lax.optimization_barrier(v.astype(jnp.bfloat16)).astype(jnp.float32)

    @jax.custom_vjp
    def low_back(v):
        return v

    def low_keep(v):
        return (low(v), None)

    def low_pass(kept, grad):
        return (grad,)

    def back_keep(v):
        return (v, None)

    def back_low(kept, grad):
        return (low(grad),)

    low.defvjp(low_keep, low_pass)
    low_back.defvjp(back_keep, back_low)

    @jax.custom_vjp
    def matmul(left, right):
        return jnp.dot(
            left.astype(jnp.bfloat16),
            right.astype(jnp.bfloat16),
            preferred_element_type=jnp.float32,
        )

    def matmul_keep(left, right):
        left_low = left.astype(jnp.bfloat16)
        right_low = right.astype(jnp.bfloat16)
        return (
            jnp.dot(left_low, right_low, preferred_element_type=jnp.float32),
            (left_low, right_low),
        )

    def matmul_grads(kept, grad):
        left_low, right_low = kept
        grad_low = grad.astype(jnp.bfloat16)
        grad_left = lax.dot_general(
            grad_low, right_low, (((1,), (1,)), ((), ())), preferred_element_type=jnp.float32
        )
        grad_right = lax.dot_general(
            left_low, grad_low, (((0,), (0,)), ((), ())), preferred_element_type=jnp.float32
        )
        return (grad_left, grad_right)

    matmul.defvjp(matmul_keep, matmul_grads)

    @jax.custom_vjp
    def matmul_t(left, right):
        return lax.dot_general(
            left.astype(jnp.bfloat16),
            right.astype(jnp.bfloat16),
            (((1,), (1,)), ((), ())),
            preferred_element_type=jnp.float32,
        )

    def matmul_t_keep(left, right):
        left_low = left.astype(jnp.bfloat16)
        right_low = right.astype(jnp.bfloat16)
        value = lax.dot_general(
            left_low, right_low, (((1,), (1,)), ((), ())), preferred_element_type=jnp.float32
        )
        return (value, (left_low, right_low))

    def matmul_t_grads(kept, grad):
        left_low, right_low = kept
        grad_low = grad.astype(jnp.bfloat16)
        grad_left = jnp.dot(grad_low, right_low, preferred_element_type=jnp.float32)
        grad_right = lax.dot_general(
            grad_low, left_low, (((0,), (0,)), ((), ())), preferred_element_type=jnp.float32
        )
        return (grad_left, grad_right)

    matmul_t.defvjp(matmul_t_keep, matmul_t_grads)

    def section_in(x_ext, gain_in, mat_qkv, mat_beta, mat_og, conv_taps, same, halo_rows):
        hidden = low(
            x_ext * lax.rsqrt(jnp.mean(x_ext * x_ext, axis=-1, keepdims=True) + 1e-06) * gain_in
        )
        skip = PRE - (TAPS - 1)
        q_in = low_back(low(matmul(hidden[halo_rows:], mat_qkv[:, :D])))
        kv_in = low_back(low(matmul(hidden, mat_qkv[:, D:])))
        beta = low(jax.nn.sigmoid(low_back(matmul(hidden[PRE:], mat_beta))))
        gate_pre = low_back(matmul(hidden[PRE + halo_rows :], mat_og))
        queries = section_conv(q_in[skip:], conv_taps[:, :D], same[:, halo_rows:], True)
        keys = section_conv(kv_in[skip:, :D], conv_taps[:, D : 2 * D], same, True)
        values = section_conv(kv_in[skip:, D:], conv_taps[:, 2 * D :], same, False)
        return (queries, keys, values, beta, gate_pre)

    def section_conv(rows_in, conv_taps, same, unit):
        row_count = rows_in.shape[0] - (TAPS - 1)
        total = jnp.zeros((row_count, rows_in.shape[1]), jnp.float32)
        for tap_index in range(TAPS):
            source = rows_in[TAPS - 1 - tap_index : TAPS - 1 - tap_index + row_count]
            total = total + conv_taps[tap_index] * source * same[tap_index]
        active = jax.nn.silu(total)
        if unit:
            shaped = active.reshape(row_count, HEADS, HEAD_DIM)
            shaped = shaped * lax.rsqrt(jnp.sum(shaped * shaped, axis=-1, keepdims=True) + 1e-06)
            active = shaped.reshape(row_count, D)
        return low(active)

    def head_mix(queries, key_rows, value_rows, weight, ridge_head, window_mask):
        scaling = window_mask * weight[None, :]
        solution = jnp.zeros_like(queries)
        residue = queries
        direction = queries
        energy = jnp.sum(residue * residue, axis=-1, keepdims=True)
        for sweep in range(ITERS):
            apply_scores = low_back(matmul_t(low(direction), key_rows))
            image_vec = (
                low_back(matmul(low(scaling * apply_scores), key_rows))
                + ridge_head[None, :] * direction
            )
            step_size = energy / jnp.sum(direction * image_vec, axis=-1, keepdims=True)
            solution = solution + step_size * direction
            residue = residue - step_size * image_vec
            energy_next = jnp.sum(residue * residue, axis=-1, keepdims=True)
            direction = residue + energy_next / energy * direction
            energy = energy_next
        scores = low_back(matmul_t(low(solution), key_rows))
        return low_back(matmul(low(scaling * scores), value_rows))

    def section_out(
        xrow, mixed, gate_pre, gain_head, mat_out, gain_ffn, mat_gate, mat_up, mat_down, valid
    ):
        row_count = xrow.shape[0]
        shaped = mixed.reshape(row_count, HEADS, HEAD_DIM)
        shaped = shaped * lax.rsqrt(jnp.mean(shaped * shaped, axis=-1, keepdims=True) + 1e-05)
        normed = shaped.reshape(row_count, D) * gain_head
        gated = low(normed * jax.nn.silu(gate_pre))
        middle = xrow + low_back(matmul(gated, mat_out))
        hidden = low(
            middle * lax.rsqrt(jnp.mean(middle * middle, axis=-1, keepdims=True) + 1e-06) * gain_ffn
        )
        inner = low(
            jax.nn.silu(low_back(matmul(hidden, mat_gate))) * low_back(matmul(hidden, mat_up))
        )
        return valid[:, None] * (middle + low_back(matmul(inner, mat_down)))

    return (section_in, section_conv, head_mix, section_out)


def bit_of(rank, bit):
    return lax.rem(lax.div(rank, 1 << bit), 2)


def swap_bit(value, bit):
    count = lax.axis_size("seq")
    return lax.ppermute(value, "seq", [(source, source ^ (1 << bit)) for source in range(count)])


def rotate(value, steps):
    count = lax.axis_size("wshard")
    return lax.ppermute(
        value, "wshard", [(source, (source + steps) % count) for source in range(count)]
    )


def seq_orders():
    bits = lax.axis_size("seq").bit_length() - 1
    far = list(range(1, bits))
    return far, far[::-1]


def gather_seq(value, order, lead):
    rank = lax.axis_index("seq")
    done = []
    for bit in order:
        other = swap_bit(value, bit)
        place = lead + sum(1 for earlier in done if earlier > bit)
        upper = bit_of(rank, bit) == 1
        low_half = jnp.where(upper, other, value)
        high_half = jnp.where(upper, value, other)
        value = jnp.stack([low_half, high_half], axis=place)
        done.append(bit)
    shape = value.shape
    return value.reshape(shape[:lead] + (1 << len(order),) + shape[lead + len(order) :])


def gather_seq_both(value, lead):
    half = value.shape[-1] // 2
    one, two = seq_orders()
    return jnp.concatenate(
        [
            gather_seq(value[..., :half], one + [0], lead),
            gather_seq(value[..., half:], two + [0], lead),
        ],
        axis=-1,
    )


def gather_weight(shard):
    rank = lax.axis_index("seq")
    place = lax.axis_index("wshard")
    parts = lax.axis_size("seq")
    shards = lax.axis_size("wshard")
    rows, columns = shard.shape
    piece = lax.dynamic_slice_in_dim(shard, rank * (rows // parts), rows // parts, 0)
    foreign = jnp.stack([rotate(piece, step) for step in range(1, shards)])
    foreign = gather_seq_both(foreign, 1).reshape(shards - 1, rows, columns)
    pieces = jnp.concatenate([shard[None], foreign])
    return jnp.concatenate(
        [
            lax.dynamic_index_in_dim(pieces, lax.rem(place - index + shards, shards), 0, False)
            for index in range(shards)
        ]
    )


def add_low(left, right):
    return (left.astype(jnp.float32) + right.astype(jnp.float32)).astype(jnp.bfloat16)


def halve_seq(value, order, remaining):
    rank = lax.axis_index("seq")
    remaining = list(remaining)
    for bit in order:
        axis = 1 + sum(1 for other in remaining if other > bit)
        mine = bit_of(rank, bit)
        keep = lax.dynamic_index_in_dim(value, mine, axis, False)
        send = lax.dynamic_index_in_dim(value, 1 - mine, axis, False)
        value = add_low(keep, swap_bit(send, bit))
        remaining.remove(bit)
    return value


def sum_weight(grad):
    place = lax.axis_index("wshard")
    parts = lax.axis_size("seq")
    shards = lax.axis_size("wshard")
    rows, columns = grad.shape
    bits = parts.bit_length() - 1
    everything = list(range(bits))
    piece_rows = rows // shards // parts
    value = grad.astype(jnp.bfloat16).reshape((shards,) + (2,) * bits + (piece_rows, columns))
    value = halve_seq(value, [0], everything)
    half = columns // 2
    one, two = seq_orders()
    value = jnp.concatenate(
        [
            halve_seq(value[..., :half], one, everything[1:]),
            halve_seq(value[..., half:], two, everything[1:]),
        ],
        axis=-1,
    )
    total = lax.dynamic_index_in_dim(value, place, 0, False).astype(jnp.float32)
    for step in range(1, shards):
        target = lax.rem(place + step, shards)
        arrived = rotate(lax.dynamic_index_in_dim(value, target, 0, False), step)
        total = total + arrived.astype(jnp.float32)
    whole = gather_seq_both(total.astype(jnp.bfloat16), 0)
    return whole.reshape(rows // shards, columns).astype(jnp.float32)


PRE = 16
SMALL = 128


def on_device(
    tokens,
    slot_lengths,
    live_lengths,
    norm_gain,
    w_qkv,
    w_beta,
    w_outgate,
    conv_weight,
    ridge,
    head_gain,
    w_out,
    ffn_gain,
    w_gate,
    w_up,
    w_down,
    cotangent,
):
    section_in, section_conv, head_mix, section_out = make_kit()
    row_count = tokens.shape[1]
    depth = (WINDOW + row_count - 1) // row_count
    halo_rows = depth * row_count
    shards = lax.axis_size("wshard")
    shard_rows = norm_gain.shape[0]
    tap_columns = TAPS * conv_weight.shape[1] // shard_rows

    own_tokens = tokens[0]
    pieces = [passed_along(own_tokens[row_count - PRE :], "seq", depth + 1)]
    for hop_count in range(depth, 0, -1):
        pieces.append(passed_along(own_tokens, "seq", hop_count))
    ext_tokens = jnp.concatenate(pieces + [own_tokens])

    small = jnp.concatenate(
        [
            w_beta,
            norm_gain[:, None],
            ridge[:, None],
            head_gain[:, None],
            ffn_gain[:, None],
            conv_weight.reshape(shard_rows, tap_columns),
        ],
        axis=1,
    )
    small = jnp.pad(small, ((0, 0), (0, SMALL - small.shape[1])))
    front = gather_weight(jnp.concatenate([w_qkv, small], axis=1))
    middle = gather_weight(jnp.concatenate([w_outgate, w_out, w_gate, w_up], axis=1))
    all_down = gather_weight(w_down)
    all_qkv = front[:, : 3 * D]
    small = front[:, 3 * D :].astype(jnp.float32)
    all_beta = small[:, :HEADS]
    gain_in, all_ridge, gain_head, gain_ffn = (small[:, HEADS + index] for index in range(4))
    taps = small[:, HEADS + 4 : HEADS + 4 + tap_columns]
    taps = taps.reshape(shards, TAPS, -1).transpose(1, 0, 2).reshape(TAPS, 3 * D)
    ffn = w_gate.shape[1]
    all_og = middle[:, :D].astype(jnp.float32)
    all_out = middle[:, D : 2 * D].astype(jnp.float32)
    all_gate = middle[:, 2 * D : 2 * D + ffn].astype(jnp.float32)
    all_up = middle[:, 2 * D + ffn :].astype(jnp.float32)
    all_down = all_down.astype(jnp.float32)
    all_qkv = all_qkv.astype(jnp.float32)

    rank = lax.axis_index("seq")
    first = rank * row_count - halo_rows - PRE
    positions = first + jnp.arange(PRE + halo_rows + row_count, dtype=jnp.int32)
    segment, valid = token_layout(slot_lengths[0], live_lengths[0], positions)
    seg_own = segment[PRE + halo_rows :]
    valid_own = valid[PRE + halo_rows :].astype(jnp.float32)
    same = conv_same(segment[PRE - (TAPS - 1) :], segment[PRE:])
    window_mask = build_mask(
        positions[PRE + halo_rows :], positions[PRE:], seg_own, segment[PRE:], valid[PRE:]
    )

    def back_half(xrow, mixed, gate_pre, gain_head, mat_out, gain_ffn, mat_gate, mat_up, mat_down):
        return section_out(
            xrow, mixed, gate_pre, gain_head, mat_out, gain_ffn, mat_gate, mat_up, mat_down, valid_own
        )

    def head_local(queries, key_rows, value_rows, weight, ridge_head):
        return head_mix(queries, key_rows, value_rows, weight, ridge_head, window_mask)

    def front_half(x_ext, gain_in, mat_qkv, mat_beta, mat_og, conv_taps):
        return section_in(
            x_ext, gain_in, mat_qkv, mat_beta, mat_og, conv_taps, same, halo_rows
        )

    x_ext = ext_tokens.astype(jnp.float32)
    xrow = x_ext[PRE + halo_rows :]
    (queries, key_ext, value_ext, beta_ext, gate_pre), pull_front = jax.vjp(
        front_half, x_ext, gain_in, all_qkv, all_beta, all_og, taps
    )
    head_inputs = (
        by_heads(queries),
        by_heads(key_ext),
        by_heads(value_ext),
        beta_ext.T,
        all_ridge.reshape(HEADS, HEAD_DIM),
    )
    mixed = from_heads(lax.map(lambda packed: head_local(*packed), head_inputs))
    output, pull_back = jax.vjp(
        back_half, xrow, mixed, gate_pre, gain_head, all_out, gain_ffn, all_gate, all_up, all_down
    )
    grad_out = cotangent[0].astype(jnp.float32)
    d_xout, d_mixed, d_gate, d_ghead, d_wout, d_gffn, d_wgate, d_wup, d_wdown = pull_back(grad_out)

    total_down = sum_weight(d_wdown)
    total_ffn = sum_weight(jnp.concatenate([d_wgate, d_wup], axis=1).astype(jnp.bfloat16))

    def head_grads(packed):
        head_values, pullback = jax.vjp(
            head_local, packed[0], packed[1], packed[2], packed[3], packed[4]
        )
        return pullback(packed[5])

    d_heads = lax.map(head_grads, head_inputs + (by_heads(d_mixed),))
    d_query = from_heads(d_heads[0])
    d_key_ext = from_heads(d_heads[1])
    d_value_ext = from_heads(d_heads[2])
    d_beta_ext = d_heads[3].T
    d_ridge = d_heads[4].reshape(D)
    d_xext, d_gin, d_wqkv, d_wbeta, d_wog, d_taps = pull_front(
        (d_query, d_key_ext, d_value_ext, d_beta_ext, d_gate)
    )
    d_tokens = d_xout + d_xext[PRE + halo_rows :]
    for hop_count in range(1, depth + 1):
        start = PRE + halo_rows - hop_count * row_count
        part = d_xext[start : start + row_count].astype(jnp.bfloat16)
        d_tokens = d_tokens + passed_along(part, "seq", -hop_count).astype(jnp.float32)
    part = passed_along(d_xext[:PRE].astype(jnp.bfloat16), "seq", -(depth + 1))
    part = jnp.pad(part.astype(jnp.float32), ((row_count - PRE, 0), (0, 0)))
    d_tokens = d_tokens + part

    d_small = jnp.concatenate(
        [
            d_wbeta,
            d_gin[:, None],
            d_ridge[:, None],
            d_ghead[:, None],
            d_gffn[:, None],
            d_taps.reshape(TAPS, shards, -1).transpose(1, 0, 2).reshape(D, tap_columns),
        ],
        axis=1,
    )
    d_small = jnp.pad(d_small, ((0, 0), (0, SMALL - d_small.shape[1])))
    total_middle = sum_weight(jnp.concatenate([d_wog, d_wout], axis=1).astype(jnp.bfloat16))
    total_front = sum_weight(jnp.concatenate([d_wqkv, d_small], axis=1).astype(jnp.bfloat16))
    t_small = total_front[:, 3 * D :]
    return (
        output.astype(jnp.bfloat16)[None],
        d_tokens.astype(jnp.bfloat16)[None],
        t_small[:, HEADS],
        total_front[:, : 3 * D],
        t_small[:, :HEADS],
        total_middle[:, :D],
        t_small[:, HEADS + 4 : HEADS + 4 + tap_columns].reshape(TAPS, -1),
        t_small[:, HEADS + 1],
        t_small[:, HEADS + 2],
        total_middle[:, D:],
        t_small[:, HEADS + 3],
        total_ffn[:, :ffn],
        total_ffn[:, ffn:],
        total_down,
    )


def solution(mesh):
    return jax.shard_map(
        on_device,
        mesh=mesh,
        in_specs=(
            P("wshard", "seq", None),
            P("wshard", None),
            P("wshard", None),
            P("wshard"),
            P("wshard", None),
            P("wshard", None),
            P("wshard", None),
            P(None, "wshard"),
            P("wshard"),
            P("wshard"),
            P("wshard", None),
            P("wshard"),
            P("wshard", None),
            P("wshard", None),
            P("wshard", None),
            P("wshard", "seq", None),
        ),
        out_specs=(
            P("wshard", "seq", None),
            P("wshard", "seq", None),
            P("wshard"),
            P("wshard", None),
            P("wshard", None),
            P("wshard", None),
            P(None, "wshard"),
            P("wshard"),
            P("wshard"),
            P("wshard", None),
            P("wshard"),
            P("wshard", None),
            P("wshard", None),
            P("wshard", None),
        ),
        check_vma=False,
    )
```

time: 1670 us -> 1200 us (0.72)
  waiting for transfers between devices: 747 us -> 279 us
  blocking collectives: 353 us -> 0 us
  other arithmetic: 79.6 us -> 252 us
  local copies, waits for them, and re-layouts: 60.5 us -> 143 us
  starting transfers between devices: 35.9 us -> 107 us
  matrix products: 364 us -> 403 us
    reduce_scatter x7 -> x0, waiting for transfers between devices: 447 us -> none  [the longest x1 114 us: on_device(): lax.psum_scatter(d_wqkv.astype(jnp.bfloat16), 'wshard', scatter_dimension...]
    all_gather x6 -> x0, waiting for transfers between devices: 280 us -> none  [the longest x1 98.9 us: on_device(): lax.all_gather(w_gate, 'wshard', axis=0, tiled=True)]
    ppermute x0 -> x83, waiting for transfers between devices: none -> 276 us  [the longest x62 178 us: swap_bit(): lax.ppermute(value, 'seq', [(source, source ^ 1 << bit) for source in ran...]
    psum x1 -> x0, blocking collectives: 275 us -> none  [on_device(): lax.psum((shares[0], shares[1], shares[2], shares[3], shares[4], shares[5...]
    ppermute x0 -> x83, starting transfers between devices: none -> 94.7 us  [the longest x62 55.7 us: swap_bit(): lax.ppermute(value, 'seq', [(source, source ^ 1 << bit) for source in ran...]
    all_gather x6 -> x0, blocking collectives: 69.1 us -> none  [the longest x1 13.9 us: on_device(): lax.all_gather(ridge, 'wshard', axis=0, tiled=True)]
    another operation x5 -> x88, other arithmetic: 0.18 us -> 40.2 us  [the longest x76 21.5 us: gather_seq(): value = jnp.stack([low_half, high_half], axis=place)]
    reduce_sum x1 -> x2, other arithmetic: 8.79 us -> 36.1 us  [section_conv(): total = total + conv_taps[tap_index] * source * same[tap_index]]
  transfers between devices with their start and end apart: 28 -> 89, of which waited for: 11 -> 38; matrix products, arithmetic and copies ran while one was open for 16% -> 26% of each run, Pallas kernels for 0% -> 0%
where the time goes in v1:
time: 1200 us; the launch traced here: 1190 us
  matrix products  403 us (34%)
  waiting for transfers between devices  279 us (23%)
  other arithmetic  252 us (21%)
  local copies, waits for them, and re-layouts  143 us (12%)
  starting transfers between devices  107 us (9%)
    ppermute x62, waiting for transfers between devices, swap_bit(): lax.ppermute(value, 'seq', [(source, source ^ 1 << bit) for source in ran...  178 us
    ppermute x21, waiting for transfers between devices, rotate(): lax.ppermute(value, 'wshard', [(source, (source + steps) % count) for sou...  97.7 us
    dot_general x32, matrix products, head_mix(): matmul(low(scaling * apply_scores), key_rows)  69.6 us
    dot_general x24, matrix products, matmul_keep(): jnp.dot(left_low, right_low, preferred_element_type=jnp.float32)  65 us
    ppermute x62, starting transfers between devices, swap_bit(): lax.ppermute(value, 'seq', [(source, source ^ 1 << bit) for source in ran...  55.7 us
    ppermute x21, starting transfers between devices, rotate(): lax.ppermute(value, 'wshard', [(source, (source + steps) % count) for sou...  39 us
    reduce_sum x2, other arithmetic, section_conv(): total = total + conv_taps[tap_index] * source * same[tap_index]  36.1 us
    dot_general x24, matrix products, matmul_t(): lax.dot_general(left.astype(jnp.bfloat16), right.astype(jnp.bfloat16), ((...  35.8 us
  transfers between devices with their start and end apart: 89, of which 38 were waited for; matrix products, arithmetic and copies ran while one was open for 26% of the time, Pallas kernels for 0%

profile of v1, /device:TPU:0, one launch (start us, length us, event | category | flops | bytes accessed | tf_op | source)
XLA Modules:
  0.0 1189.6 jit_solution(16605784455329296991)
XLA Ops:
  56.6 10.3 collective-permute-done.4
  68.7 5.8 collective-permute-done.24
  79.1 5.7 collective-permute-start.12
  86.4 24.5 %collective-permute-done.13 = bf16[32,7680]{1,0:T(8,128)(2,1)S(1)} collective-permute-done((bf16[32,7680]{1,0:T(8,128)(2,1)S(1)}, bf16[32,7680]{1,0:T(8,128)(2,1)S(1)}, u32[]{:S(2)}, u32[]{:S(2)}) %collective-permute-start.13) | collective-permute-done | bytes 491552 | tf_op jit(solution)/shard_map/ppermute | solution.py:222
  114.4 5.7 collective-permute-done.6
  123.7 9.4 collective-permute-done.28
  142.0 21.1 %collective-permute-done.10 = bf16[3,2,32,1600]{3,2,0,1:T(8,128)(2,1)S(1)} collective-permute-done((bf16[3,2,32,1600]{3,2,0,1:T(8,128)(2,1)S(1)}, bf16[3,2,32,1600]{3,2,0,1:T(8,128)(2,1)S(1)}, u32[]{:S(2)}, u32[]{:S(2)}) %collective-permute-start.10) | collective-permute-done | bytes 614432 | tf_op jit(solution)/shard_map/ppermute | solution.py:217
  174.9 10.3 fusion.142
  194.5 6.3 multiply_convert_fusion.1
  200.8 13.0 %convolution_convert_fusion = bf16[1552,2048]{1,0:T(8,128)(2,1)} fusion(bf16[1552,1024]{1,0:T(8,128)(2,1)S(1)} %multiply_convert_fusion.1, bf16[256,3200]{1,0:T(8,128)(2,1)S(1)} %get-tuple-element.593, bf16[256,3200]{1,0:T(8,128)(2,1)S(1)} %get-tuple-element.594, bf16[256,3200]{1,0:T(8,128)(2,1)S(1)} %get-tuple-element.595, ...), kind=kOutput, calls=%fused_computation.144 | convolution fusion | flops 6529515520 | bytes 16089088 | tf_op jit(solution)/shard_map/jvp()/dot_general | solution.py:98
  231.0 7.7 fusion.210
  252.2 6.7 fusion.71
  260.6 7.4 multiply_convert_fusion.2
  284.5 81.4 %while.30 = (s32[]{:T(128)}, f32[8,512,128]{2,1,0:T(8,128)}, f32[8,1536]{1,0:T(8,128)S(1)}, f32[8,512,128]{1,2,0:T(8,128)S(1)}, bf16[8,1536,128]{2,1,0:T(8,128)(...) while((s32[]{:T(128)}, f32[8,512,128]{2,1,0:T(8,128)}, ...), condition=%wide.region_12.13_spmd.clone, body=%wide.region_7.12_spmd.clone.sunk | while | flops 1233059328 | bytes 16508581 | solution.py:424
  382.8 7.4 maximum_maximum_fusion
  390.2 5.7 dynamic-slice_bitcast_fusion.3
  402.8 10.1 pad_maximum_fusion.3
  413.0 4.8 multiply_convert_fusion.7
  422.7 4.9 fusion.254
  427.6 18.9 %fusion.76 = (bf16[512,2816]{1,0:T(8,128)(2,1)}, bf16[512,2816]{1,0:T(8,128)(2,1)}, bf16[512,2816]{1,0:T(8,128)(2,1)}) fusion(f32[512,2816]{1,0:T(8,128)} %fusion.142, f32[512,2816]{1,0:T(8,128)} %fusion.254, bf16[512,1024]{1,0:T(8,128)(2,1)S(1)} %multiply_convert_fusion.6, bf16[256,7680]{1,0:T(8,128)(2,1)S(1)} %copy-done.6, ...), kind=kOutput, calls=%fused_computation.205 | convolution fusion | flops 2998927360 | bytes 36962304 | tf_op jit(solution)/shard_map/jvp()/dot_general | solution.py:98
  446.5 8.2 fusion.255
  454.7 8.4 multiply_reduce_fusion.21
  473.8 211.5 %while.31 = (s32[]{:T(128)}, f32[8,512,128]{1,2,0:T(8,128)}, f32[8,1536,128]{2,1,0:T(8,128)}, f32[8,1536,128]{2,1,0:T(8,128)}, f32[8,1536]{1,0:T(8,128)S(1)}, /*...) while((s32[]{:T(128)}, f32[8,512,128]{1,2,0:T(8,128)}, ...), condition=%wide.region_29.30_spmd.clone, body=%wide.region_17.29_spmd.clone.sunk | while | flops 3468761600 | bytes 96600080 | solution.py:440
  720.6 5.2 convolution_convert_fusion.3
  725.7 5.3 convolution_convert_fusion.2
  733.0 31.8 %multiply_reduce_fusion.11 = (f32[1024]{0:T(1024)S(1)}, f32[1024]{0:T(1024)S(1)}, f32[1024]{0:T(1024)S(1)}, f32[1024]{0:T(1024)S(1)}, f32[1024]{0:T(1024)S(1)}, ...) fusion(f32[1552,2048]{1,0:T(8,128)} %copy-done, ...), kind=kLoop, calls=%fused_computation.179 | loop fusion | flops 72343552 | bytes 94527488 | tf_op jit(solution)/shard_map/transpose(jvp())/reduce_sum | solution.py:162
  764.9 16.8 %multiply_multiply_fusion.5 = (f32[1536,1024]{1,0:T(8,128)}, f32[1536,1024]{1,0:T(8,128)}, f32[1536,1024]{1,0:T(8,128)}, f32[1536,1024]{1,0:T(8,128)}, f32[1536,...) fusion(f32[1536,1024]{1,0:T(8,128)} %get-tuple-element.544, ...), kind=kLoop, calls=%fused_computation.194 | loop fusion | flops 25165824 | bytes 62971904 | tf_op jit(solution)/shard_map/transpose(jvp())/mul | solution.py:162
  781.7 9.9 pad_add_fusion.1
  791.5 6.3 pad_add_fusion.2
  803.3 10.3 fusion.260
  813.7 25.3 %multiply_reduce_fusion.5 = (bf16[1024]{0:T(1024)(128)(2,1)S(1)}, f32[1552]{0:T(1024)S(1)}, f32[1552,1024]{1,0:T(8,128)}) fusion(f32[1552]{0:T(1024)S(1)} %copy-done.103, bf16[512,1024]{1,0:T(8,128)(2,1)} %bitcast.950, bf16[512,1024]{1,0:T(8,128)(2,1)} %copy-done.21, bf16[512,1024]{1,0:T(8,128)(2,1)} %copy-done.22, bf16[16,1024]{1,0:T(8,128)(2,1)S(1)} %copy-done.80, ...), kind=kOutput, calls=%fused_computation.149 | convolution fusion | flops 6553351680 | bytes 33015936 | tf_op jit(solution)/shard_map/transpose(jvp())/dot_general | solution.py:149
  839.1 7.1 fusion.220
  867.2 8.3 add_convert_fusion.1
  883.4 6.4 fusion.135
  898.9 9.1 collective-permute-done.48
  931.2 4.7 collective-permute-done.53
  943.2 14.9 %collective-permute-done.59 = bf16[2,32,1024]{2,1,0:T(8,128)(2,1)S(1)} collective-permute-done((bf16[2,32,1024]{2,1,0:T(8,128)(2,1)S(1)}, bf16[2,32,1024]{2,1,0:T(8,128)(2,1)S(1)}, u32[]{:S(2)}, u32[]{:S(2)}) %collective-permute-start.59) | collective-permute-done | bytes 131104 | tf_op jit(solution)/shard_map/ppermute | solution.py:217
  972.9 22.4 %collective-permute-done.77 = bf16[4,88,512]{2,1,0:T(8,128)(2,1)S(1)} collective-permute-done((bf16[4,88,512]{2,1,0:T(8,128)(2,1)S(1)}, bf16[4,88,512]{2,1,0:T(8,128)(2,1)S(1)}, u32[]{:S(2)}, u32[]{:S(2)}) %collective-permute-start.77) | collective-permute-done | bytes 360480 | tf_op jit(solution)/shard_map/ppermute | solution.py:217
  1003.7 10.5 collective-permute-done.81
  1023.3 4.6 collective-permute-done.87
  1028.2 4.6 collective-permute-done.37
  1039.5 14.4 %collective-permute-done.39 = bf16[32,3200]{1,0:T(8,128)(2,1)S(1)} collective-permute-done((bf16[32,3200]{1,0:T(8,128)(2,1)S(1)}, bf16[32,3200]{1,0:T(8,128)(2,1)S(1)}, u32[]{:S(2)}, u32[]{:S(2)}) %collective-permute-start.39) | collective-permute-done | bytes 204832 | tf_op jit(solution)/shard_map/ppermute | solution.py:222
  1065.9 8.5 fusion.63
  1081.2 31.1 %collective-permute-done.62 = bf16[4,2,32,2816]{3,2,0,1:T(8,128)(2,1)S(1)} collective-permute-done((bf16[4,2,32,2816]{3,2,0,1:T(8,128)(2,1)S(1)}, bf16[4,2,32,2816]{3,2,0,1:T(8,128)(2,1)S(1)}, u32[]{:S(2)}, u32[]{:S(2)}) %collective-permute-start.62) | collective-permute-done | bytes 1441824 | tf_op jit(solution)/shard_map/ppermute | solution.py:217
  1115.6 15.1 %collective-permute-done.63 = bf16[4,32,2816]{2,1,0:T(8,128)(2,1)S(1)} collective-permute-done((bf16[4,32,2816]{2,1,0:T(8,128)(2,1)S(1)}, bf16[4,32,2816]{2,1,0:T(8,128)(2,1)S(1)}, u32[]{:S(2)}, u32[]{:S(2)}) %collective-permute-start.63) | collective-permute-done | bytes 720928 | tf_op jit(solution)/shard_map/ppermute | solution.py:217
  1135.3 7.9 collective-permute-done.68
  1143.2 19.9 %collective-permute-done.67 = bf16[32,5632]{1,0:T(8,128)(2,1)S(1)} collective-permute-done((bf16[32,5632]{1,0:T(8,128)(2,1)S(1)}, bf16[32,5632]{1,0:T(8,128)(2,1)S(1)}, u32[]{:S(2)}, u32[]{:S(2)}) %collective-permute-start.67) | collective-permute-done | bytes 360480 | tf_op jit(solution)/shard_map/ppermute | solution.py:222
  1177.3 5.6 collective-permute-done.70
  (1239 shorter events, 674.5 us)
Async XLA Ops:
  0.6 136.8 %collective-permute-start.2 = (bf16[512,1024]{1,0:T(8,128)(2,1)}, bf16[512,1024]{1,0:T(8,128)(2,1)S(1)}, u32[]{:S(2)}, u32[]{:S(2)}) collective-permute-start(bf16[512,1024]{1,0:T(8,128)(2,1)} %bitcast.948), channel_id=1, source_target_pairs={{0,4},{4,8},{8,12},{12,16},{16,20},{20,24},{24,28},{1,5},{5,9},{9,... | collective-permute-start | bytes 3145736 | tf_op jit(solution)/shard_map/ppermute | solution.py:17
  3.1 134.7 %collective-permute-start.1 = (bf16[512,1024]{1,0:T(8,128)(2,1)}, bf16[512,1024]{1,0:T(8,128)(2,1)S(1)}, u32[]{:S(2)}, u32[]{:S(2)}) collective-permute-start(bf16[512,1024]{1,0:T(8,128)(2,1)} %bitcast.949), channel_id=1, source_target_pairs={{0,8},{4,12},{8,16},{12,20},{16,24},{20,28},{1,9},{5,13},{9,17},{1... | collective-permute-start | bytes 3145736 | tf_op jit(solution)/shard_map/ppermute | solution.py:17
  9.1 34.5 %collective-permute-start.23 = (bf16[88,1024]{1,0:T(8,128)(2,1)}, bf16[88,1024]{1,0:T(8,128)(2,1)}, u32[]{:S(2)}, u32[]{:S(2)}) collective-permute-start(bf16[88,1024]{1,0:T(8,128)(2,1)} %constant_dynamic-slice_fusion.8), channel_id=1, source_target_pairs={{0,3},{1,0},{2,1},{3,2},{4,7},{5,4},{6,5},{7,6},{8,11},{9,8},{10,9... | collective-permute-start | bytes 540680 | tf_op jit(solution)/shard_map/ppermute | solution.py:222
  12.7 33.8 %collective-permute-start.22 = (bf16[88,1024]{1,0:T(8,128)(2,1)}, bf16[88,1024]{1,0:T(8,128)(2,1)}, u32[]{:S(2)}, u32[]{:S(2)}) collective-permute-start(bf16[88,1024]{1,0:T(8,128)(2,1)} %constant_dynamic-slice_fusion.8), channel_id=1, source_target_pairs={{0,2},{1,3},{2,0},{3,1},{4,6},{5,7},{6,4},{7,5},{8,10},{9,11},{10,... | collective-permute-start | bytes 540680 | tf_op jit(solution)/shard_map/ppermute | solution.py:222
  12.7 34.9 %collective-permute-start.21 = (bf16[88,1024]{1,0:T(8,128)(2,1)}, bf16[88,1024]{1,0:T(8,128)(2,1)}, u32[]{:S(2)}, u32[]{:S(2)}) collective-permute-start(bf16[88,1024]{1,0:T(8,128)(2,1)} %constant_dynamic-slice_fusion.8), channel_id=1, source_target_pairs={{0,1},{1,2},{2,3},{3,0},{4,5},{5,6},{6,7},{7,4},{8,9},{9,10},{10,1... | collective-permute-start | bytes 540680 | tf_op jit(solution)/shard_map/ppermute | solution.py:222
  46.5 20.4 %collective-permute-start.4 = (bf16[32,3200]{1,0:T(8,128)(2,1)}, bf16[32,3200]{1,0:T(8,128)(2,1)S(1)}, u32[]{:S(2)}, u32[]{:S(2)}) collective-permute-start(bf16[32,3200]{1,0:T(8,128)(2,1)} %constant_dynamic-slice_fusion.10), channel_id=1, source_target_pairs={{0,2},{1,3},{2,0},{3,1},{4,6},{5,7},{6,4},{7,5},{8,10},{9,11},{10,... | collective-permute-start | bytes 614408 | tf_op jit(solution)/shard_map/ppermute | solution.py:222
  47.6 20.7 %collective-permute-start.3 = (bf16[32,3200]{1,0:T(8,128)(2,1)}, bf16[32,3200]{1,0:T(8,128)(2,1)S(1)}, u32[]{:S(2)}, u32[]{:S(2)}) collective-permute-start(bf16[32,3200]{1,0:T(8,128)(2,1)} %constant_dynamic-slice_fusion.10), channel_id=1, source_target_pairs={{0,1},{1,2},{2,3},{3,0},{4,5},{5,6},{6,7},{7,4},{8,9},{9,10},{10,1... | collective-permute-start | bytes 614408 | tf_op jit(solution)/shard_map/ppermute | solution.py:222
  52.4 32.6 %collective-permute-start.14 = (bf16[32,7680]{1,0:T(8,128)(2,1)S(1)}, bf16[32,7680]{1,0:T(8,128)(2,1)S(1)}, u32[]{:S(2)}, u32[]{:S(2)}) collective-permute-start(bf16[32,7680]{1,0:T(8,128)(2,1)S(1)} %constant_dynamic-slice_fusion.9), channel_id=1, source_target_pairs={{0,3},{1,0},{2,1},{3,2},{4,7},{5,4},{6,5},{7,6},{8,11},{9,8},{10,9... | collective-permute-start | bytes 1474568 | tf_op jit(solution)/shard_map/ppermute | solution.py:222
  74.6 36.4 %collective-permute-start.13 = (bf16[32,7680]{1,0:T(8,128)(2,1)S(1)}, bf16[32,7680]{1,0:T(8,128)(2,1)S(1)}, u32[]{:S(2)}, u32[]{:S(2)}) collective-permute-start(bf16[32,7680]{1,0:T(8,128)(2,1)S(1)} %constant_dynamic-slice_fusion.9), channel_id=1, source_target_pairs={{0,2},{1,3},{2,0},{3,1},{4,6},{5,7},{6,4},{7,5},{8,10},{9,11},{10,... | collective-permute-start | bytes 1474568 | tf_op jit(solution)/shard_map/ppermute | solution.py:222
  79.1 33.3 %collective-permute-start.12 = (bf16[32,7680]{1,0:T(8,128)(2,1)S(1)}, bf16[32,7680]{1,0:T(8,128)(2,1)S(1)}, u32[]{:S(2)}, u32[]{:S(2)}) collective-permute-start(bf16[32,7680]{1,0:T(8,128)(2,1)S(1)} %constant_dynamic-slice_fusion.9), channel_id=1, source_target_pairs={{0,1},{1,2},{2,3},{3,0},{4,5},{5,6},{6,7},{7,4},{8,9},{9,10},{10,1... | collective-permute-start | bytes 1474568 | tf_op jit(solution)/shard_map/ppermute | solution.py:222
  85.0 51.8 %collective-permute-start = (bf16[16,1024]{1,0:T(8,128)(2,1)S(1)}, bf16[16,1024]{1,0:T(8,128)(2,1)S(1)}, u32[]{:S(2)}, u32[]{:S(2)}) collective-permute-start(bf16[16,1024]{1,0:T(8,128)(2,1)S(1)} %copy-done.134), channel_id=1, source_target_pairs={{0,12},{4,16},{8,20},{12,24},{16,28},{1,13},{5,17},{9,21},{13,25},... | collective-permute-start | bytes 98312 | tf_op jit(solution)/shard_map/ppermute | solution.py:17
  133.1 31.9 %collective-permute-start.15 = (bf16[3,32,3840]{2,1,0:T(8,128)(2,1)S(1)}, bf16[3,32,3840]{2,1,0:T(8,128)(2,1)S(1)}, u32[]{:S(2)}, u32[]{:S(2)}) collective-permute-start(bf16[3,32,3840]{2,1,0:T(8,128)(2,1)S(1)} %get-tuple-element.655), channel_id=1, source_target_pairs={{0,8},{4,12},{8,0},{12,4},{16,24},{20,28},{24,16},{28,20},{1,9},{5... | collective-permute-start | bytes 2211848 | tf_op jit(solution)/shard_map/ppermute | solution.py:217
  134.9 30.7 %collective-permute-start.18 = (bf16[3,32,3840]{2,1,0:T(8,128)(2,1)S(1)}, bf16[3,32,3840]{2,1,0:T(8,128)(2,1)S(1)}, u32[]{:S(2)}, u32[]{:S(2)}) collective-permute-start(bf16[3,32,3840]{2,1,0:T(8,128)(2,1)S(1)} %get-tuple-element.656), channel_id=1, source_target_pairs={{0,16},{4,20},{8,24},{12,28},{16,0},{20,4},{24,8},{28,12},{1,17},{... | collective-permute-start | bytes 2211848 | tf_op jit(solution)/shard_map/ppermute | solution.py:217
  136.8 26.3 %collective-permute-start.10 = (bf16[3,2,32,1600]{3,2,0,1:T(8,128)(2,1)S(1)}, bf16[3,2,32,1600]{3,2,0,1:T(8,128)(2,1)S(1)}, u32[]{:S(2)}, u32[]{:S(2)}) collective-permute-start(bf16[3,2,32,1600]{3,2,0,1:T(8,128)(2,1)S(1)} %pad_maximum_fusion.39), channel_id=1, source_target_pairs={{0,8},{4,12},{8,0},{12,4},{16,24},{20,28},{24,16},{28,20},{1,9},{5... | collective-permute-start | bytes 1843208 | tf_op jit(solution)/shard_map/ppermute | solution.py:217
  137.5 27.2 %collective-permute-start.7 = (bf16[3,2,32,1600]{3,2,0,1:T(8,128)(2,1)S(1)}, bf16[3,2,32,1600]{3,2,0,1:T(8,128)(2,1)S(1)}, u32[]{:S(2)}, u32[]{:S(2)}) collective-permute-start(bf16[3,2,32,1600]{3,2,0,1:T(8,128)(2,1)S(1)} %pad_maximum_fusion.38), channel_id=1, source_target_pairs={{0,16},{4,20},{8,24},{12,28},{16,0},{20,4},{24,8},{28,12},{1,17},{... | collective-permute-start | bytes 1843208 | tf_op jit(solution)/shard_map/ppermute | solution.py:217
  137.8 31.2 %collective-permute-start.29 = (bf16[3,2,2,88,512]{4,3,0,1,2:T(8,128)(2,1)S(1)}, bf16[3,2,2,88,512]{4,3,0,1,2:T(8,128)(2,1)S(1)}, u32[]{:S(2)}, u32[]{:S(2)}) collective-permute-start(bf16[3,2,2,88,512]{4,3,0,1,2:T(8,128)(2,1)S(1)} %pad_maximum_fusion.29), channel_id=1, source_target_pairs={{0,4},{4,0},{8,12},{12,8},{16,20},{20,16},{24,28},{28,24},{1,5},{5... | collective-permute-start | bytes 3244040 | tf_op jit(solution)/shard_map/ppermute | solution.py:217
  164.7 20.6 %collective-permute-start.11 = (bf16[3,2,2,32,1600]{4,3,0,1,2:T(8,128)(2,1)S(1)}, bf16[3,2,2,32,1600]{4,3,0,1,2:T(8,128)(2,1)S(1)}, u32[]{:S(2)}, u32[]{:S(2)}) collective-permute-start(bf16[3,2,2,32,1600]{4,3,0,1,2:T(8,128)(2,1)S(1)} %pad_maximum_fusion.27), channel_id=1, source_target_pairs={{0,4},{4,0},{8,12},{12,8},{16,20},{20,16},{24,28},{28,24},{1,5},{5... | collective-permute-start | bytes 3686408 | tf_op jit(solution)/shard_map/ppermute | solution.py:217
  165.0 20.2 %collective-permute-start.8 = (bf16[3,2,2,32,1600]{4,3,0,1,2:T(8,128)(2,1)S(1)}, bf16[3,2,2,32,1600]{4,3,0,1,2:T(8,128)(2,1)S(1)}, u32[]{:S(2)}, u32[]{:S(2)}) collective-permute-start(bf16[3,2,2,32,1600]{4,3,0,1,2:T(8,128)(2,1)S(1)} %pad_maximum_fusion.26), channel_id=1, source_target_pairs={{0,4},{4,0},{8,12},{12,8},{16,20},{20,16},{24,28},{28,24},{1,5},{5... | collective-permute-start | bytes 3686408 | tf_op jit(solution)/shard_map/ppermute | solution.py:217
  167.2 108.8 %collective-permute-start.19 = (bf16[3,2,32,3840]{3,2,0,1:T(8,128)(2,1)}, bf16[3,2,32,3840]{3,2,0,1:T(8,128)(2,1)}, u32[]{:S(2)}, u32[]{:S(2)}) collective-permute-start(bf16[3,2,32,3840]{3,2,0,1:T(8,128)(2,1)} %pad_maximum_fusion.23), channel_id=1, source_target_pairs={{0,8},{4,12},{8,0},{12,4},{16,24},{20,28},{24,16},{28,20},{1,9},{5... | collective-permute-start | bytes 4423688 | tf_op jit(solution)/shard_map/ppermute | solution.py:217
  169.0 110.5 %collective-permute-start.16 = (bf16[3,2,32,3840]{3,2,0,1:T(8,128)(2,1)}, bf16[3,2,32,3840]{3,2,0,1:T(8,128)(2,1)}, u32[]{:S(2)}, u32[]{:S(2)}) collective-permute-start(bf16[3,2,32,3840]{3,2,0,1:T(8,128)(2,1)} %pad_maximum_fusion.22), channel_id=1, source_target_pairs={{0,16},{4,20},{8,24},{12,28},{16,0},{20,4},{24,8},{28,12},{1,17},{... | collective-permute-start | bytes 4423688 | tf_op jit(solution)/shard_map/ppermute | solution.py:217
  279.5 91.8 %collective-permute-start.20 = (bf16[3,2,2,32,3840]{4,3,0,1,2:T(8,128)(2,1)}, bf16[3,2,2,32,3840]{4,3,0,1,2:T(8,128)(2,1)}, u32[]{:S(2)}, u32[]{:S(2)}) collective-permute-start(bf16[3,2,2,32,3840]{4,3,0,1,2:T(8,128)(2,1)} %pad_maximum_fusion.13), channel_id=1, source_target_pairs={{0,4},{4,0},{8,12},{12,8},{16,20},{20,16},{24,28},{28,24},{1,5},{5... | collective-permute-start | bytes 8847368 | tf_op jit(solution)/shard_map/ppermute | solution.py:217
  284.4 92.8 %collective-permute-start.17 = (bf16[3,2,2,32,3840]{4,3,0,1,2:T(8,128)(2,1)}, bf16[3,2,2,32,3840]{4,3,0,1,2:T(8,128)(2,1)}, u32[]{:S(2)}, u32[]{:S(2)}) collective-permute-start(bf16[3,2,2,32,3840]{4,3,0,1,2:T(8,128)(2,1)} %pad_maximum_fusion.12), channel_id=1, source_target_pairs={{0,4},{4,0},{8,12},{12,8},{16,20},{20,16},{24,28},{28,24},{1,5},{5... | collective-permute-start | bytes 8847368 | tf_op jit(solution)/shard_map/ppermute | solution.py:217
  847.6 66.5 %collective-permute-start.31 = (bf16[512,1024]{1,0:T(8,128)(2,1)}, bf16[512,1024]{1,0:T(8,128)(2,1)}, u32[]{:S(2)}, u32[]{:S(2)}) collective-permute-start(bf16[512,1024]{1,0:T(8,128)(2,1)} %get-tuple-element.622), channel_id=1, source_target_pairs={{8,0},{12,4},{16,8},{20,12},{24,16},{28,20},{9,1},{13,5},{17,9},{2... | collective-permute-start | bytes 3145736 | tf_op jit(solution)/shard_map/ppermute | solution.py:17
  848.9 66.8 %collective-permute-start.30 = (bf16[512,1024]{1,0:T(8,128)(2,1)}, bf16[512,1024]{1,0:T(8,128)(2,1)}, u32[]{:S(2)}, u32[]{:S(2)}) collective-permute-start(bf16[512,1024]{1,0:T(8,128)(2,1)} %get-tuple-element.621), channel_id=1, source_target_pairs={{4,0},{8,4},{12,8},{16,12},{20,16},{24,20},{28,24},{5,1},{9,5},{13... | collective-permute-start | bytes 3145736 | tf_op jit(solution)/shard_map/ppermute | solution.py:17
  857.9 31.8 %collective-permute-start.47 = (bf16[4,2,2,32,2048]{4,3,2,1,0:T(8,128)(2,1)}, bf16[4,2,2,32,2048]{4,3,2,1,0:T(8,128)(2,1)}, u32[]{:S(2)}, u32[]{:S(2)}) collective-permute-start(bf16[4,2,2,32,2048]{4,3,2,1,0:T(8,128)(2,1)} %fusion.112), channel_id=1, source_target_pairs={{0,4},{4,0},{8,12},{12,8},{16,20},{20,16},{24,28},{28,24},{1,5},{5... | collective-permute-start | bytes 6291464 | tf_op jit(solution)/shard_map/ppermute | solution.py:217
  867.1 57.4 %collective-permute-start.75 = (bf16[4,2,2,88,1024]{4,3,2,1,0:T(8,128)(2,1)}, bf16[4,2,2,88,1024]{4,3,2,1,0:T(8,128)(2,1)}, u32[]{:S(2)}, u32[]{:S(2)}) collective-permute-start(bf16[4,2,2,88,1024]{4,3,2,1,0:T(8,128)(2,1)} %dynamic-slice_bitcast_fusion.4), channel_id=1, source_target_pairs={{0,4},{4,0},{8,12},{12,8},{16,20},{20,16},{24,28},{28,24},{1,5},{5... | collective-permute-start | bytes 8650760 | tf_op jit(solution)/shard_map/ppermute | solution.py:217
  910.1 53.2 %collective-permute-start.33 = (bf16[4,2,2,32,3200]{4,3,0,2,1:T(8,128)(2,1)S(1)}, bf16[4,2,2,32,3200]{4,3,0,2,1:T(8,128)(2,1)S(1)}, u32[]{:S(2)}, u32[]{:S(2)}) collective-permute-start(bf16[4,2,2,32,3200]{4,3,0,2,1:T(8,128)(2,1)S(1)} %bitcast.972), channel_id=1, source_target_pairs={{0,4},{4,0},{8,12},{12,8},{16,20},{20,16},{24,28},{28,24},{1,5},{5... | collective-permute-start | bytes 9830408 | tf_op jit(solution)/shard_map/ppermute | solution.py:217
  913.2 152.7 %collective-permute-start.61 = (bf16[4,2,2,32,5632]{4,3,2,1,0:T(8,128)(2,1)S(1)}, bf16[4,2,2,32,5632]{4,3,2,1,0:T(8,128)(2,1)}, u32[]{:S(2)}, u32[]{:S(2)}) collective-permute-start(bf16[4,2,2,32,5632]{4,3,2,1,0:T(8,128)(2,1)S(1)} %fusion.78), channel_id=1, source_target_pairs={{0,4},{4,0},{8,12},{12,8},{16,20},{20,16},{24,28},{28,24},{1,5},{5... | collective-permute-start | bytes 17301512 | tf_op jit(solution)/shard_map/ppermute | solution.py:217
  938.2 30.5 %collective-permute-start.76 = (bf16[4,2,88,512]{3,2,0,1:T(8,128)(2,1)S(1)}, bf16[4,2,88,512]{3,2,0,1:T(8,128)(2,1)S(1)}, u32[]{:S(2)}, u32[]{:S(2)}) collective-permute-start(bf16[4,2,88,512]{3,2,0,1:T(8,128)(2,1)S(1)} %bitcast.981), channel_id=1, source_target_pairs={{0,8},{4,12},{8,0},{12,4},{16,24},{20,28},{24,16},{28,20},{1,9},{5... | collective-permute-start | bytes 2162696 | tf_op jit(solution)/shard_map/ppermute | solution.py:217
  941.0 17.1 %collective-permute-start.59 = (bf16[2,32,1024]{2,1,0:T(8,128)(2,1)S(1)}, bf16[2,32,1024]{2,1,0:T(8,128)(2,1)S(1)}, u32[]{:S(2)}, u32[]{:S(2)}) collective-permute-start(bf16[2,32,1024]{2,1,0:T(8,128)(2,1)S(1)} %pad_maximum_fusion.60), channel_id=1, source_target_pairs={{0,8},{4,12},{8,0},{12,4},{16,24},{20,28},{24,16},{28,20},{1,9},{5... | collective-permute-start | bytes 393224 | tf_op jit(solution)/shard_map/ppermute | solution.py:217
  942.5 27.3 %collective-permute-start.78 = (bf16[4,2,88,512]{3,2,1,0:T(8,128)(2,1)S(1)}, bf16[4,2,88,512]{3,2,1,0:T(8,128)(2,1)S(1)}, u32[]{:S(2)}, u32[]{:S(2)}) collective-permute-start(bf16[4,2,88,512]{3,2,1,0:T(8,128)(2,1)S(1)} %dynamic-slice_bitcast_fusion.16), channel_id=1, source_target_pairs={{0,16},{4,20},{8,24},{12,28},{16,0},{20,4},{24,8},{28,12},{1,17},{... | collective-permute-start | bytes 2162696 | tf_op jit(solution)/shard_map/ppermute | solution.py:217
  966.0 33.1 %collective-permute-start.34 = (bf16[4,2,32,1600]{3,2,0,1:T(8,128)(2,1)S(1)}, bf16[4,2,32,1600]{3,2,0,1:T(8,128)(2,1)S(1)}, u32[]{:S(2)}, u32[]{:S(2)}) collective-permute-start(bf16[4,2,32,1600]{3,2,0,1:T(8,128)(2,1)S(1)} %dynamic-slice_bitcast_fusion.15), channel_id=1, source_target_pairs={{0,8},{4,12},{8,0},{12,4},{16,24},{20,28},{24,16},{28,20},{1,9},{5... | collective-permute-start | bytes 2457608 | tf_op jit(solution)/shard_map/ppermute | solution.py:217
  966.9 49.5 %collective-permute-start.36 = (bf16[4,2,32,1600]{3,2,0,1:T(8,128)(2,1)S(1)}, bf16[4,2,32,1600]{3,2,0,1:T(8,128)(2,1)S(1)}, u32[]{:S(2)}, u32[]{:S(2)}) collective-permute-start(bf16[4,2,32,1600]{3,2,0,1:T(8,128)(2,1)S(1)} %dynamic-slice_bitcast_fusion.14), channel_id=1, source_target_pairs={{0,16},{4,20},{8,24},{12,28},{16,0},{20,4},{24,8},{28,12},{1,17},{... | collective-permute-start | bytes 2457608 | tf_op jit(solution)/shard_map/ppermute | solution.py:217
  969.0 26.3 %collective-permute-start.77 = (bf16[4,88,512]{2,1,0:T(8,128)(2,1)S(1)}, bf16[4,88,512]{2,1,0:T(8,128)(2,1)S(1)}, u32[]{:S(2)}, u32[]{:S(2)}) collective-permute-start(bf16[4,88,512]{2,1,0:T(8,128)(2,1)S(1)} %dynamic-slice_bitcast_fusion.23), channel_id=1, source_target_pairs={{0,16},{4,20},{8,24},{12,28},{16,0},{20,4},{24,8},{28,12},{1,17},{... | collective-permute-start | bytes 1081352 | tf_op jit(solution)/shard_map/ppermute | solution.py:217
  970.0 25.4 %collective-permute-start.79 = (bf16[4,88,512]{2,1,0:T(8,128)(2,1)S(1)}, bf16[4,88,512]{2,1,0:T(8,128)(2,1)S(1)}, u32[]{:S(2)}, u32[]{:S(2)}) collective-permute-start(bf16[4,88,512]{2,1,0:T(8,128)(2,1)S(1)} %dynamic-slice_bitcast_fusion.22), channel_id=1, source_target_pairs={{0,8},{4,12},{8,0},{12,4},{16,24},{20,28},{24,16},{28,20},{1,9},{5... | collective-permute-start | bytes 1081352 | tf_op jit(solution)/shard_map/ppermute | solution.py:217
  997.2 17.0 %collective-permute-start.81 = (bf16[88,1024]{1,0:T(8,128)(2,1)S(1)}, bf16[88,1024]{1,0:T(8,128)(2,1)S(1)}, u32[]{:S(2)}, u32[]{:S(2)}) collective-permute-start(bf16[88,1024]{1,0:T(8,128)(2,1)S(1)} %get-tuple-element.696), channel_id=1, source_target_pairs={{0,2},{1,3},{2,0},{3,1},{4,6},{5,7},{6,4},{7,5},{8,10},{9,11},{10,... | collective-permute-start | bytes 540680 | tf_op jit(solution)/shard_map/ppermute | solution.py:222
  1002.3 25.8 %collective-permute-start.35 = (bf16[4,32,1600]{2,1,0:T(8,128)(2,1)S(1)}, bf16[4,32,1600]{2,1,0:T(8,128)(2,1)S(1)}, u32[]{:S(2)}, u32[]{:S(2)}) collective-permute-start(bf16[4,32,1600]{2,1,0:T(8,128)(2,1)S(1)} %dynamic-slice_bitcast_fusion.21), channel_id=1, source_target_pairs={{0,16},{4,20},{8,24},{12,28},{16,0},{20,4},{24,8},{28,12},{1,17},{... | collective-permute-start | bytes 1228808 | tf_op jit(solution)/shard_map/ppermute | solution.py:217
  1028.0 28.3 %collective-permute-start.88 = (bf16[2,2,88,512]{3,2,0,1:T(8,128)(2,1)S(1)}, bf16[2,2,88,512]{3,2,0,1:T(8,128)(2,1)S(1)}, u32[]{:S(2)}, u32[]{:S(2)}) collective-permute-start(bf16[2,2,88,512]{3,2,0,1:T(8,128)(2,1)S(1)} %pad_maximum_fusion.51), channel_id=1, source_target_pairs={{0,4},{4,0},{8,12},{12,8},{16,20},{20,16},{24,28},{28,24},{1,5},{5... | collective-permute-start | bytes 1081352 | tf_op jit(solution)/shard_map/ppermute | solution.py:217
  1033.2 20.7 %collective-permute-start.39 = (bf16[32,3200]{1,0:T(8,128)(2,1)S(1)}, bf16[32,3200]{1,0:T(8,128)(2,1)S(1)}, u32[]{:S(2)}, u32[]{:S(2)}) collective-permute-start(bf16[32,3200]{1,0:T(8,128)(2,1)S(1)} %get-tuple-element.685), channel_id=1, source_target_pairs={{0,2},{1,3},{2,0},{3,1},{4,6},{5,7},{6,4},{7,5},{8,10},{9,11},{10,... | collective-permute-start | bytes 614408 | tf_op jit(solution)/shard_map/ppermute | solution.py:222
  1039.4 17.1 %collective-permute-start.85 = (bf16[2,2,88,512]{3,2,0,1:T(8,128)(2,1)S(1)}, bf16[2,2,88,512]{3,2,0,1:T(8,128)(2,1)S(1)}, u32[]{:S(2)}, u32[]{:S(2)}) collective-permute-start(bf16[2,2,88,512]{3,2,0,1:T(8,128)(2,1)S(1)} %pad_maximum_fusion.50), channel_id=1, source_target_pairs={{0,4},{4,0},{8,12},{12,8},{16,20},{20,16},{24,28},{28,24},{1,5},{5... | collective-permute-start | bytes 1081352 | tf_op jit(solution)/shard_map/ppermute | solution.py:217
  1061.9 18.1 %collective-permute-start.42 = (bf16[2,32,1600]{2,1,0:T(8,128)(2,1)S(1)}, bf16[2,32,1600]{2,1,0:T(8,128)(2,1)S(1)}, u32[]{:S(2)}, u32[]{:S(2)}) collective-permute-start(bf16[2,32,1600]{2,1,0:T(8,128)(2,1)S(1)} %pad_maximum_fusion.55), channel_id=1, source_target_pairs={{0,16},{4,20},{8,24},{12,28},{16,0},{20,4},{24,8},{28,12},{1,17},{... | collective-permute-start | bytes 614408 | tf_op jit(solution)/shard_map/ppermute | solution.py:217
  1077.9 34.3 %collective-permute-start.62 = (bf16[4,2,32,2816]{3,2,0,1:T(8,128)(2,1)S(1)}, bf16[4,2,32,2816]{3,2,0,1:T(8,128)(2,1)S(1)}, u32[]{:S(2)}, u32[]{:S(2)}) collective-permute-start(bf16[4,2,32,2816]{3,2,0,1:T(8,128)(2,1)S(1)} %bitcast.978), channel_id=1, source_target_pairs={{0,8},{4,12},{8,0},{12,4},{16,24},{20,28},{24,16},{28,20},{1,9},{5... | collective-permute-start | bytes 4325384 | tf_op jit(solution)/shard_map/ppermute | solution.py:217
  1080.1 35.4 %collective-permute-start.43 = (bf16[2,2,32,1600]{3,2,1,0:T(8,128)(2,1)S(1)}, bf16[2,2,32,1600]{3,2,1,0:T(8,128)(2,1)S(1)}, u32[]{:S(2)}, u32[]{:S(2)}) collective-permute-start(bf16[2,2,32,1600]{3,2,1,0:T(8,128)(2,1)S(1)} %pad_maximum_fusion.46), channel_id=1, source_target_pairs={{0,4},{4,0},{8,12},{12,8},{16,20},{20,16},{24,28},{28,24},{1,5},{5... | collective-permute-start | bytes 1228808 | tf_op jit(solution)/shard_map/ppermute | solution.py:217
  1080.5 34.2 %collective-permute-start.64 = (bf16[4,2,32,2816]{3,2,1,0:T(8,128)(2,1)S(1)}, bf16[4,2,32,2816]{3,2,1,0:T(8,128)(2,1)S(1)}, u32[]{:S(2)}, u32[]{:S(2)}) collective-permute-start(bf16[4,2,32,2816]{3,2,1,0:T(8,128)(2,1)S(1)} %dynamic-slice_bitcast_fusion.9), channel_id=1, source_target_pairs={{0,16},{4,20},{8,24},{12,28},{16,0},{20,4},{24,8},{28,12},{1,17},{... | collective-permute-start | bytes 4325384 | tf_op jit(solution)/shard_map/ppermute | solution.py:217
  1112.7 18.0 %collective-permute-start.63 = (bf16[4,32,2816]{2,1,0:T(8,128)(2,1)S(1)}, bf16[4,32,2816]{2,1,0:T(8,128)(2,1)S(1)}, u32[]{:S(2)}, u32[]{:S(2)}) collective-permute-start(bf16[4,32,2816]{2,1,0:T(8,128)(2,1)S(1)} %dynamic-slice_bitcast_fusion.18), channel_id=1, source_target_pairs={{0,16},{4,20},{8,24},{12,28},{16,0},{20,4},{24,8},{28,12},{1,17},{... | collective-permute-start | bytes 2162696 | tf_op jit(solution)/shard_map/ppermute | solution.py:217
  1115.1 17.5 %collective-permute-start.65 = (bf16[4,32,2816]{2,1,0:T(8,128)(2,1)S(1)}, bf16[4,32,2816]{2,1,0:T(8,128)(2,1)S(1)}, u32[]{:S(2)}, u32[]{:S(2)}) collective-permute-start(bf16[4,32,2816]{2,1,0:T(8,128)(2,1)S(1)} %dynamic-slice_bitcast_fusion.17), channel_id=1, source_target_pairs={{0,8},{4,12},{8,0},{12,4},{16,24},{20,28},{24,16},{28,20},{1,9},{5... | collective-permute-start | bytes 2162696 | tf_op jit(solution)/shard_map/ppermute | solution.py:217
  1133.0 30.0 %collective-permute-start.67 = (bf16[32,5632]{1,0:T(8,128)(2,1)S(1)}, bf16[32,5632]{1,0:T(8,128)(2,1)S(1)}, u32[]{:S(2)}, u32[]{:S(2)}) collective-permute-start(bf16[32,5632]{1,0:T(8,128)(2,1)S(1)} %get-tuple-element.664), channel_id=1, source_target_pairs={{0,2},{1,3},{2,0},{3,1},{4,6},{5,7},{6,4},{7,5},{8,10},{9,11},{10,... | collective-permute-start | bytes 1081352 | tf_op jit(solution)/shard_map/ppermute | solution.py:222
  1133.1 30.0 %collective-permute-start.66 = (bf16[32,5632]{1,0:T(8,128)(2,1)S(1)}, bf16[32,5632]{1,0:T(8,128)(2,1)S(1)}, u32[]{:S(2)}, u32[]{:S(2)}) collective-permute-start(bf16[32,5632]{1,0:T(8,128)(2,1)S(1)} %get-tuple-element.663), channel_id=1, source_target_pairs={{0,1},{1,2},{2,3},{3,0},{4,5},{5,6},{6,7},{7,4},{8,9},{9,10},{10,1... | collective-permute-start | bytes 1081352 | tf_op jit(solution)/shard_map/ppermute | solution.py:222
  (225 other events, 3377.8 us)

commit v2 on v1

v2 whole, which is shorter than its diff:
```python
import functools
import jax
import jax.numpy as jnp
from jax import lax
from jax.experimental import pallas as pl
from jax.experimental.pallas import tpu as pltpu
from jax.sharding import PartitionSpec as P

D = 1024
HEADS = 8
HEAD_DIM = 128
TAPS = 4
WINDOW = 1024
PRE = 16
SMALL = 128
f32 = jnp.float32
bf16 = jnp.bfloat16
QB = 256
CH = 256
ROWS = 256


def mm(left, right):
    return jnp.dot(left, right, preferred_element_type=f32)


def mm_t(left, right):
    return lax.dot_general(left, right, (((1,), (1,)), ((), ())), preferred_element_type=f32)


def conv_total(ext_ref, slot, same, taps):
    total = taps[0:1] * ext_ref[slot, 8 : 8 + ROWS, :]
    for tap in range(1, TAPS):
        total = total + taps[tap : tap + 1] * ext_ref[slot, 8 - tap : 8 - tap + ROWS, :] * same[tap]
    return total


def unit_scale(active):
    return lax.rsqrt(jnp.sum(active * active, axis=-1, keepdims=True) + 1e-06)


def in_heads(work, *arrays):
    width = arrays[0].shape[1]
    return jnp.concatenate(
        [
            work(*(array[:, at : at + HEAD_DIM] for array in arrays))
            for at in range(0, width, HEAD_DIM)
        ],
        axis=1,
    )


def row_norm(x, gain):
    return (x * lax.rsqrt(jnp.mean(x * x, axis=-1, keepdims=True) + 1e-06) * gain).astype(bf16)


def front_kernel(
    first_own,
    x_ref,
    same_ref,
    gain_ref,
    w_ref,
    taps_ref,
    hid_ref,
    kvin_ref,
    qin_ref,
    qpre_ref,
    q_ref,
    k_ref,
    v_ref,
    beta_ref,
    ext_ref,
    tail_ref,
):
    step = pl.program_id(0)
    gain = gain_ref[...]
    kv_slots = 2 * D // CH

    @pl.when(step == 0)
    def before():
        hidden = row_norm(x_ref[0:PRE].astype(f32), gain)
        hid_ref[0:PRE] = hidden
        for slot in range(kv_slots):
            rows = mm(hidden, w_ref[:, D + CH * slot : D + CH * (slot + 1)]).astype(bf16)
            kvin_ref[0:PRE, CH * slot : CH * (slot + 1)] = rows
            ext_ref[slot, ROWS : ROWS + 8, :] = rows.astype(f32)[PRE - 8 :]

    def through(slot, hidden, same, column, in_ref, at):
        ext_ref[slot, 0:8, :] = ext_ref[slot, ROWS : ROWS + 8, :]
        rows = mm(hidden, w_ref[:, column : column + CH]).astype(bf16)
        in_ref[:, at : at + CH] = rows
        ext_ref[slot, 8 : 8 + ROWS, :] = rows.astype(f32)
        total = conv_total(ext_ref, slot, same, taps_ref[:, column : column + CH])
        return total * jax.nn.sigmoid(total)

    def unit(active):
        return in_heads(lambda part: part * unit_scale(part), active).astype(bf16)

    @pl.when(step > 0)
    def main():
        same = [same_ref[:, tap : tap + 1] for tap in range(TAPS)]
        hidden = row_norm(x_ref[...].astype(f32), gain)
        hid_ref[...] = hidden
        for slot in range(kv_slots):
            at = CH * slot
            active = through(slot, hidden, same, D + at, kvin_ref, at)
            if at < D:
                k_ref[:, at : at + CH] = unit(active)
            else:
                v_ref[:, at - D : at - D + CH] = active.astype(bf16)
        gates = jax.nn.sigmoid(mm(hidden, w_ref[:, 3 * D : 3 * D + SMALL])).astype(bf16)
        lane = lax.broadcasted_iota(jnp.int32, (ROWS, SMALL), 1)
        beta_ref[...] = jnp.where(lane < HEADS, gates.astype(f32), 0.0)

        @pl.when(step == first_own + 1)
        def own_history():
            rows = mm(tail_ref[...], w_ref[:, :D]).astype(bf16)
            qpre_ref[...] = rows
            for slot in range(D // CH):
                ext_ref[kv_slots + slot, ROWS : ROWS + 8, :] = rows.astype(f32)[
                    PRE - 8 :, CH * slot : CH * (slot + 1)
                ]

        @pl.when(step > first_own)
        def own():
            for slot in range(D // CH):
                at = CH * slot
                active = through(kv_slots + slot, hidden, same, at, qin_ref, at)
                q_ref[:, at : at + CH] = unit(active)

        tail_ref[...] = hidden[ROWS - PRE :]


def front(ext_tokens, same, gain, w_front, taps, own_rows):
    ext_rows = ext_tokens.shape[0]
    main_rows = ext_rows - PRE
    blocks = main_rows // ROWS
    first_own = (main_rows - own_rows) // ROWS

    def ext_block(step):
        return (jnp.where(step == 0, blocks, step - 1), 0)

    def main_block(step):
        return (jnp.maximum(step - 1, 0), 0)

    def own_block(step):
        return (jnp.maximum(step - 1 - first_own, 0), 0)

    def fixed(array):
        return pl.BlockSpec(array.shape, lambda step: (0, 0))

    shape = jax.ShapeDtypeStruct
    return pl.pallas_call(
        functools.partial(front_kernel, first_own),
        grid=(blocks + 1,),
        in_specs=[
            pl.BlockSpec((ROWS, D), ext_block),
            pl.BlockSpec((ROWS, TAPS), main_block),
            fixed(gain),
            fixed(w_front),
            fixed(taps),
        ],
        out_specs=[
            pl.BlockSpec((ROWS, D), ext_block),
            pl.BlockSpec((ROWS, 2 * D), ext_block),
            pl.BlockSpec((ROWS, D), own_block),
            pl.BlockSpec((PRE, D), lambda step: (0, 0)),
            pl.BlockSpec((ROWS, D), own_block),
            pl.BlockSpec((ROWS, D), main_block),
            pl.BlockSpec((ROWS, D), main_block),
            pl.BlockSpec((ROWS, SMALL), main_block),
        ],
        out_shape=[
            shape((ext_rows, D), bf16),
            shape((ext_rows, 2 * D), bf16),
            shape((own_rows, D), bf16),
            shape((PRE, D), bf16),
            shape((own_rows, D), bf16),
            shape((main_rows, D), bf16),
            shape((main_rows, D), bf16),
            shape((main_rows, SMALL), f32),
        ],
        scratch_shapes=[
            pltpu.VMEM((3 * D // CH, 8 + ROWS, CH), f32),
            pltpu.VMEM((PRE, D), bf16),
        ],
        compiler_params=pltpu.CompilerParams(
            dimension_semantics=("arbitrary",), vmem_limit_bytes=50 << 20
        ),
        cost_estimate=pl.CostEstimate(
            flops=4 * (main_rows * 2 + own_rows) * D * D, bytes_accessed=30 << 20, transcendentals=0
        ),
        name="front",
    )(ext_tokens, same, gain, w_front, taps)


def back_kernel(
    blocks,
    first_own,
    x_ref,
    kvin_ref,
    kvprev_ref,
    same_ref,
    qin_ref,
    qprev_ref,
    qpre_ref,
    dk_ref,
    dv_ref,
    dq_ref,
    beta_ref,
    dbeta_ref,
    dgate_ref,
    dres_ref,
    gain_ref,
    w_ref,
    wog_ref,
    taps_ref,
    dkvin_ref,
    dqin_ref,
    dqpre_ref,
    dbp_ref,
    dxhalo_ref,
    dxown_ref,
    dgain_ref,
    dtaps_ref,
    ext_ref,
    buf_ref,
    dh_ref,
):
    step = pl.program_id(0)
    block = blocks - 1 - step
    kv_slots = 2 * D // CH
    gain = gain_ref[...]

    @pl.when(step == 0)
    def clear():
        dgain_ref[...] = jnp.zeros_like(dgain_ref)
        dtaps_ref[...] = jnp.zeros_like(dtaps_ref)
        buf_ref[:, :, ROWS : ROWS + 8, :] = jnp.zeros_like(buf_ref[:, :, ROWS : ROWS + 8, :])

    def norm_back(x, dh):
        scale = lax.rsqrt(jnp.mean(x * x, axis=-1, keepdims=True) + 1e-06)
        normal = x * scale
        dgain_ref[...] += jnp.sum(dh * normal, axis=0, keepdims=True)
        scaled = dh * gain
        return scale * (scaled - normal * jnp.mean(scaled * normal, axis=-1, keepdims=True))

    def shifted(slot, start, count):
        total = buf_ref[slot, 1, start + 1 : start + 1 + count, :]
        for tap in range(2, TAPS):
            total = total + buf_ref[slot, tap, start + tap : start + tap + count, :]
        return total

    def through(slot, column, history, rows, grad, unit, same):
        ext_ref[slot, 0:8, :] = history
        ext_ref[slot, 8 : 8 + ROWS, :] = rows.astype(f32)
        taps = taps_ref[:, column : column + CH]
        total = conv_total(ext_ref, slot, same, taps)
        gate = jax.nn.sigmoid(total)
        active = total * gate
        if unit:

            def unit_back(part, part_grad):
                scale = unit_scale(part)
                normal = part * scale
                return scale * (
                    part_grad - normal * jnp.sum(part_grad * normal, axis=-1, keepdims=True)
                )

            grad = in_heads(unit_back, active, grad)
        grad = grad * (gate + active * (1.0 - gate))
        result = grad * taps[0:1]
        dtaps_ref[0:1, column : column + CH] += jnp.sum(
            grad * ext_ref[slot, 8 : 8 + ROWS, :], axis=0, keepdims=True
        )
        for tap in range(1, TAPS):
            held = grad * same[tap]
            dtaps_ref[tap : tap + 1, column : column + CH] += jnp.sum(
                held * ext_ref[slot, 8 - tap : 8 - tap + ROWS, :], axis=0, keepdims=True
            )
            buf_ref[slot, tap, 0:ROWS, :] = held * taps[tap : tap + 1]
        result = (result + shifted(slot, 0, ROWS)).astype(bf16)
        for tap in range(1, TAPS):
            buf_ref[slot, tap, ROWS : ROWS + 8, :] = buf_ref[slot, tap, 0:8, :]
        return result

    def before_rows(slot):
        for tap in range(1, TAPS):
            buf_ref[slot, tap, ROWS - PRE : ROWS, :] = jnp.zeros((PRE, CH), f32)
        return shifted(slot, ROWS - PRE, PRE).astype(bf16)

    @pl.when(step < blocks)
    def main():
        same = [same_ref[:, tap : tap + 1] for tap in range(TAPS)]
        beta = beta_ref[...]
        gates = (dbeta_ref[...] * beta * (1.0 - beta)).astype(bf16)
        dbp_ref[...] = gates
        dh = mm_t(gates, w_ref[:, 3 * D : 3 * D + SMALL])
        for slot in range(kv_slots):
            at = CH * slot
            grad = dk_ref[:, at : at + CH] if at < D else dv_ref[:, at - D : at - D + CH]
            history = kvprev_ref[PRE - 8 : PRE, at : at + CH].astype(f32)
            rows = kvin_ref[:, at : at + CH]
            rows = through(slot, D + at, history, rows, grad, at < D, same)
            dkvin_ref[:, at : at + CH] = rows
            dh = dh + mm_t(rows, w_ref[:, D + at : D + at + CH])
        dh_ref[...] = dh

        @pl.when(block >= first_own)
        def own():
            dh = mm_t(dgate_ref[...], wog_ref[...])
            for slot in range(D // CH):
                at = CH * slot
                history = jnp.where(
                    block == first_own,
                    qpre_ref[PRE - 8 :, at : at + CH].astype(f32),
                    qprev_ref[PRE - 8 :, at : at + CH].astype(f32),
                )
                rows = qin_ref[:, at : at + CH]
                rows = through(
                    kv_slots + slot, at, history, rows, dq_ref[:, at : at + CH], True, same
                )
                dqin_ref[:, at : at + CH] = rows
                dh = dh + mm_t(rows, w_ref[:, at : at + CH])
            dxown_ref[...] = dres_ref[...] + norm_back(x_ref[...].astype(f32), dh_ref[...] + dh)

        @pl.when(block == first_own - 1)
        def own_history():
            dh = jnp.zeros((PRE, D), f32)
            for slot in range(D // CH):
                at = CH * slot
                rows = before_rows(kv_slots + slot)
                dqpre_ref[:, at : at + CH] = rows
                dh = dh + mm_t(rows, w_ref[:, at : at + CH])
            dh_ref[ROWS - PRE : ROWS, :] += dh

        @pl.when(block < first_own)
        def halo():
            dxhalo_ref[...] = norm_back(x_ref[...].astype(f32), dh_ref[...]).astype(bf16)

    @pl.when(step == blocks)
    def before():
        dh = jnp.zeros((PRE, D), f32)
        for slot in range(kv_slots):
            at = CH * slot
            rows = before_rows(slot)
            dkvin_ref[0:PRE, at : at + CH] = rows
            dh = dh + mm_t(rows, w_ref[:, D + at : D + at + CH])
        dxhalo_ref[0:PRE, :] = norm_back(x_ref[0:PRE].astype(f32), dh).astype(bf16)


def back(
    ext_tokens, kvin, same, qin, qpre, dk, dv, dq, beta, dbeta, dgate, dres, gain, w_front, w_og, taps
):
    ext_rows = ext_tokens.shape[0]
    main_rows = ext_rows - PRE
    own_rows = dq.shape[0]
    blocks = main_rows // ROWS
    first_own = (main_rows - own_rows) // ROWS
    small_blocks = ROWS // PRE

    def ext_block(step):
        return (jnp.where(step == blocks, blocks, blocks - 1 - step), 0)

    def main_block(step):
        return (jnp.maximum(blocks - 1 - step, 0), 0)

    def prev_block(step):
        block = blocks - 1 - step
        return (jnp.where(block <= 0, blocks * small_blocks, small_blocks * block - 1), 0)

    def own_block(step):
        return (jnp.maximum(blocks - 1 - step - first_own, 0), 0)

    def own_prev_block(step):
        return (jnp.maximum(small_blocks * (blocks - 1 - step - first_own) - 1, 0), 0)

    def halo_block(step):
        block = jnp.minimum(blocks - 1 - step, first_own - 1)
        return (jnp.where(step == blocks, first_own, block), 0)

    def fixed(array):
        return pl.BlockSpec(array.shape, lambda step: (0, 0))

    shape = jax.ShapeDtypeStruct
    return pl.pallas_call(
        functools.partial(back_kernel, blocks, first_own),
        grid=(blocks + 1,),
        in_specs=[
            pl.BlockSpec((ROWS, D), ext_block),
            pl.BlockSpec((ROWS, 2 * D), ext_block),
            pl.BlockSpec((PRE, 2 * D), prev_block),
            pl.BlockSpec((ROWS, TAPS), main_block),
            pl.BlockSpec((ROWS, D), own_block),
            pl.BlockSpec((PRE, D), own_prev_block),
            fixed(qpre),
            pl.BlockSpec((ROWS, D), main_block),
            pl.BlockSpec((ROWS, D), main_block),
            pl.BlockSpec((ROWS, D), own_block),
            pl.BlockSpec((ROWS, SMALL), main_block),
            pl.BlockSpec((ROWS, SMALL), main_block),
            pl.BlockSpec((ROWS, D), own_block),
            pl.BlockSpec((ROWS, D), own_block),
            fixed(gain),
            fixed(w_front),
            fixed(w_og),
            fixed(taps),
        ],
        out_specs=[
            pl.BlockSpec((ROWS, 2 * D), ext_block),
            pl.BlockSpec((ROWS, D), own_block),
            pl.BlockSpec((PRE, D), lambda step: (0, 0)),
            pl.BlockSpec((ROWS, SMALL), main_block),
            pl.BlockSpec((ROWS, D), halo_block),
            pl.BlockSpec((ROWS, D), own_block),
            pl.BlockSpec((1, D), lambda step: (0, 0)),
            pl.BlockSpec((TAPS, 3 * D), lambda step: (0, 0)),
        ],
        out_shape=[
            shape((ext_rows, 2 * D), bf16),
            shape((own_rows, D), bf16),
            shape((PRE, D), bf16),
            shape((main_rows, SMALL), bf16),
            shape((main_rows - own_rows + PRE, D), bf16),
            shape((own_rows, D), f32),
            shape((1, D), f32),
            shape((TAPS, 3 * D), f32),
        ],
        scratch_shapes=[
            pltpu.VMEM((3 * D // CH, 8 + ROWS, CH), f32),
            pltpu.VMEM((3 * D // CH, TAPS, ROWS + 8, CH), f32),
            pltpu.VMEM((ROWS, D), f32),
        ],
        compiler_params=pltpu.CompilerParams(
            dimension_semantics=("arbitrary",), vmem_limit_bytes=56 << 20
        ),
        cost_estimate=pl.CostEstimate(
            flops=6 * (main_rows * 2 + own_rows) * D * D, bytes_accessed=40 << 20, transcendentals=0
        ),
        name="back",
    )(
        ext_tokens,
        kvin,
        kvin,
        same,
        qin,
        qin,
        qpre,
        dk,
        dv,
        dq,
        beta,
        dbeta,
        dgate,
        dres,
        gain,
        w_front,
        w_og,
        taps,
    )


def total(v):
    return jnp.sum(v,axis=0,keepdims=True)

def head_column(beta_ref, h):
    beta=beta_ref[...]
    lane=lax.broadcasted_iota(jnp.int32,beta.shape,1)
    return jnp.sum(jnp.where(lane==h,beta,0.0),axis=1,keepdims=True)

def attn_fwd_kernel(q_ref,k_ref,v_ref,beta_ref,mask_ref,ridge_ref,o_ref,a0_ref,a1_ref,kt_ref,vt_ref,w_ref):
    h=pl.program_id(0)
    rows=q_ref.shape[0]
    span=WINDOW+QB
    kt_ref[...]=k_ref[...].T
    vt_ref[...]=v_ref[...].T
    column=head_column(beta_ref,h)
    ridge=ridge_ref[...]
    blocks=range(rows//QB)
    chunks=range(span//CH)
    for b in blocks:
        for c in chunks:
            at=slice(QB*b+CH*c,QB*b+CH*(c+1))
            w_ref[b,CH*c:CH*(c+1),:]=mask_ref[at,QB*b:QB*(b+1)].astype(f32)*column[at]
    def apply(b,vector,right):
        low=vector.astype(bf16)
        out=jnp.zeros((HEAD_DIM,QB),f32)
        for c in chunks:
            at=slice(QB*b+CH*c,QB*b+CH*(c+1))
            s=mm(k_ref[at,:],low)
            s=(w_ref[b,CH*c:CH*(c+1),:]*s).astype(bf16)
            out=out+mm(right[:,at],s)
        return out
    q=[q_ref[QB*b:QB*(b+1),:].astype(f32).T for b in blocks]
    a0=[apply(b,q[b],kt_ref)+ridge*q[b] for b in blocks]
    for b in blocks: a0_ref[:,QB*b:QB*(b+1)]=a0[b]
    x1=[];p1=[];r1=[];e1=[]
    for b in blocks:
        e0=total(q[b]*q[b])
        s0=e0/total(q[b]*a0[b])
        x1.append(s0*q[b])
        r=q[b]-s0*a0[b]
        e=total(r*r)
        r1.append(r);e1.append(e)
        p1.append(r+e/e0*q[b])
    a1=[apply(b,p1[b],kt_ref)+ridge*p1[b] for b in blocks]
    for b in blocks: a1_ref[:,QB*b:QB*(b+1)]=a1[b]
    x2=[x1[b]+e1[b]/total(p1[b]*a1[b])*p1[b] for b in blocks]
    for b in blocks:
        o_ref[QB*b:QB*(b+1),:]=apply(b,x2[b],vt_ref).T

def attn_fwd(q,k,v,beta,mask_t,ridge):
    rows=q.shape[0]; keys=k.shape[0]
    head=lambda n: pl.BlockSpec((n,HEAD_DIM),lambda h:(0,h))
    heads_t=pl.BlockSpec((HEAD_DIM,rows),lambda h:(h,0))
    fixed=lambda a: pl.BlockSpec(a.shape,lambda h:(0,0))
    flops=6*2*rows*(WINDOW+QB)*D
    return pl.pallas_call(
        attn_fwd_kernel, grid=(HEADS,),
        in_specs=[head(rows),head(keys),head(keys),fixed(beta),fixed(mask_t),pl.BlockSpec((HEAD_DIM,1),lambda h:(h,0))],
        out_specs=[head(rows),heads_t,heads_t],
        out_shape=[jax.ShapeDtypeStruct((rows,D),f32)]+[jax.ShapeDtypeStruct((D,rows),f32)]*2,
        scratch_shapes=[pltpu.VMEM((HEAD_DIM,keys),bf16)]*2+[pltpu.VMEM((rows//QB,WINDOW+QB,QB),f32)],
        compiler_params=pltpu.CompilerParams(dimension_semantics=("arbitrary",),vmem_limit_bytes=48<<20),
        cost_estimate=pl.CostEstimate(flops=2*flops,bytes_accessed=20<<20,transcendentals=0),
        name="attn_fwd",
    )(q,k,v,beta,mask_t,ridge)

def attn_bwd_kernel(q_ref,k_ref,v_ref,beta_ref,mask_ref,ridge_ref,a0_ref,a1_ref,do_ref,dq_ref,dk_ref,dv_ref,dbeta_ref,dridge_ref,kt_ref,w_ref,acc_ref):
    h=pl.program_id(0)
    rows=q_ref.shape[0]
    span=WINDOW+QB
    kt_ref[...]=k_ref[...].T
    column=head_column(beta_ref,h)
    ridge=ridge_ref[...]
    blocks=range(rows//QB)
    chunks=range(span//CH)
    dk_ref[...]=jnp.zeros_like(dk_ref)
    dv_ref[...]=jnp.zeros_like(dv_ref)
    acc_ref[...]=jnp.zeros_like(acc_ref)
    for b in blocks:
        for c in chunks:
            at=slice(QB*b+CH*c,QB*b+CH*(c+1))
            w_ref[b,CH*c:CH*(c+1),:]=mask_ref[at,QB*b:QB*(b+1)].astype(f32)*column[at]
    def apply_back(b,vector,grad,grad_rows,right_ref,dright_ref):
        low=vector.astype(bf16)
        low_rows=vector.T.astype(bf16)
        out=jnp.zeros((HEAD_DIM,QB),f32)
        for c in chunks:
            at=slice(QB*b+CH*c,QB*b+CH*(c+1))
            w=w_ref[b,CH*c:CH*(c+1),:]
            s=mm(k_ref[at,:],low)
            dw=mm(right_ref[at,:],grad)
            masked=dw*mask_ref[at,QB*b:QB*(b+1)].astype(f32)
            for_beta=masked*s
            part=for_beta[:,:128]
            for lane in range(128,QB,128):
                part=part+for_beta[:,lane:lane+128]
            acc_ref[at,:]+=part
            ws=(w*s).astype(bf16)
            ds=(w*dw).astype(bf16)
            out=out+mm(kt_ref[:,at],ds)
            dright_ref[at,:]+=mm(ws,grad_rows)
            dk_ref[at,:]+=mm(ds,low_rows)
        return out
    st=[]
    for b in blocks:
        cols=slice(QB*b,QB*(b+1))
        q=q_ref[cols,:].astype(f32).T
        a0=a0_ref[:,cols]; a1=a1_ref[:,cols]
        e0=total(q*q); d0=total(q*a0); s0=e0/d0
        x1=s0*q; r1=q-s0*a0; e1=total(r1*r1); b0=e1/e0
        p1=r1+b0*q; d1=total(p1*a1); s1=e1/d1
        x2=x1+s1*p1
        st.append((q,a0,a1,e0,d0,s0,r1,e1,b0,p1,d1,s1,x2))
    dx2=[]
    for b in blocks:
        do=do_ref[QB*b:QB*(b+1),:]
        dx2.append(apply_back(b,st[b][12],do.astype(f32).T.astype(bf16),do,v_ref,dv_ref))
    da1=[];dp1=[];de1=[];dr=0
    for b in blocks:
        q,a0,a1,e0,d0,s0,r1,e1,b0,p1,d1,s1,x2=st[b]
        ds1=total(dx2[b]*p1)
        de1.append(ds1/d1)
        dd1=-ds1*s1/d1
        g=dd1*p1
        da1.append(g)
        dp1.append(s1*dx2[b]+dd1*a1+ridge*g)
        dr=dr+jnp.sum(g*p1,axis=1,keepdims=True)
    for b in blocks:
        g=da1[b]
        dp1[b]=dp1[b]+apply_back(b,st[b][9],g.astype(bf16),g.T.astype(bf16),k_ref,dk_ref)
    da0=[];dq=[]
    for b in blocks:
        q,a0,a1,e0,d0,s0,r1,e1,b0,p1,d1,s1,x2=st[b]
        db0=total(dp1[b]*q)
        dpq=b0*dp1[b]
        de=de1[b]+db0/e0
        de0=-db0*b0/e0
        dr1=dp1[b]+2.0*de*r1
        ds0=total(dx2[b]*q)-total(dr1*a0)
        dpq=dpq+s0*dx2[b]
        g=-s0*dr1
        de0=de0+ds0/d0
        dd0=-ds0*s0/d0
        dpq=dpq+dd0*a0
        g=g+dd0*q
        dpq=dpq+dr1+2.0*de0*q+ridge*g
        da0.append(g);dq.append(dpq)
        dr=dr+jnp.sum(g*q,axis=1,keepdims=True)
    for b in blocks:
        g=da0[b]
        t=dq[b]+apply_back(b,st[b][0],g.astype(bf16),g.T.astype(bf16),k_ref,dk_ref)
        dq_ref[QB*b:QB*(b+1),:]=t.T
    dridge_ref[...]=dr
    found=jnp.sum(acc_ref[...],axis=1,keepdims=True)
    lane=lax.broadcasted_iota(jnp.int32,dbeta_ref.shape,1)
    @pl.when(h==0)
    def _():
        dbeta_ref[...]=jnp.zeros_like(dbeta_ref)
    dbeta_ref[...]=jnp.where(lane==h,found,dbeta_ref[...])

def attn_bwd(q,k,v,beta,mask_t,ridge,a0,a1,do):
    rows=q.shape[0]; keys=k.shape[0]
    head=lambda n: pl.BlockSpec((n,HEAD_DIM),lambda h:(0,h))
    heads_t=pl.BlockSpec((HEAD_DIM,rows),lambda h:(h,0))
    fixed=lambda a: pl.BlockSpec(a.shape,lambda h:(0,0))
    rd=pl.BlockSpec((HEAD_DIM,1),lambda h:(h,0))
    flops=15*2*rows*(WINDOW+QB)*D
    return pl.pallas_call(
        attn_bwd_kernel, grid=(HEADS,),
        in_specs=[head(rows),head(keys),head(keys),fixed(beta),fixed(mask_t),rd,heads_t,heads_t,head(rows)],
        out_specs=[head(rows),head(keys),head(keys),fixed(beta),rd],
        out_shape=[jax.ShapeDtypeStruct((rows,D),f32),jax.ShapeDtypeStruct((keys,D),f32),jax.ShapeDtypeStruct((keys,D),f32),jax.ShapeDtypeStruct(beta.shape,f32),jax.ShapeDtypeStruct((D,1),f32)],
        scratch_shapes=[pltpu.VMEM((HEAD_DIM,keys),bf16),pltpu.VMEM((rows//QB,WINDOW+QB,QB),f32),pltpu.VMEM((keys,128),f32)],
        compiler_params=pltpu.CompilerParams(dimension_semantics=("arbitrary",),vmem_limit_bytes=48<<20),
        cost_estimate=pl.CostEstimate(flops=2*flops,bytes_accessed=30<<20,transcendentals=0),
        name="attn_bwd",
    )(q,k,v,beta,mask_t,ridge,a0,a1,do)


def passed_along(value, axis, steps):
    count = lax.axis_size(axis)
    initial, last = (max(0, -steps), min(count, count - steps))
    return lax.ppermute(value, axis, [(source, source + steps) for source in range(initial, last)])


def token_layout(slot_row, live_row, positions):
    starts = (jnp.cumsum(slot_row) - slot_row).astype(jnp.int32)
    after = positions[:, None] >= starts[None, :]
    segment = (jnp.sum(after.astype(jnp.int32), axis=1) - 1).astype(jnp.int32)
    chosen = segment[:, None] == jnp.arange(slot_row.shape[0], dtype=jnp.int32)[None, :]
    begin = jnp.sum(jnp.where(chosen, starts[None, :], 0), axis=1).astype(jnp.int32)
    limit = jnp.sum(jnp.where(chosen, live_row[None, :], 0), axis=1).astype(jnp.int32)
    valid = (segment >= 0) & (positions - begin < limit)
    return (segment, valid)


def make_kit():

    @jax.custom_vjp
    def low(v):
        return lax.optimization_barrier(v.astype(jnp.bfloat16)).astype(jnp.float32)

    @jax.custom_vjp
    def low_back(v):
        return v

    def low_keep(v):
        return (low(v), None)

    def low_pass(kept, grad):
        return (grad,)

    def back_keep(v):
        return (v, None)

    def back_low(kept, grad):
        return (low(grad),)

    low.defvjp(low_keep, low_pass)
    low_back.defvjp(back_keep, back_low)

    @jax.custom_vjp
    def matmul(left, right):
        return jnp.dot(
            left.astype(jnp.bfloat16),
            right.astype(jnp.bfloat16),
            preferred_element_type=jnp.float32,
        )

    def matmul_keep(left, right):
        left_low = left.astype(jnp.bfloat16)
        right_low = right.astype(jnp.bfloat16)
        return (
            jnp.dot(left_low, right_low, preferred_element_type=jnp.float32),
            (left_low, right_low),
        )

    def matmul_grads(kept, grad):
        left_low, right_low = kept
        grad_low = grad.astype(jnp.bfloat16)
        grad_left = lax.dot_general(
            grad_low, right_low, (((1,), (1,)), ((), ())), preferred_element_type=jnp.float32
        )
        grad_right = lax.dot_general(
            left_low, grad_low, (((0,), (0,)), ((), ())), preferred_element_type=jnp.float32
        )
        return (grad_left, grad_right)

    matmul.defvjp(matmul_keep, matmul_grads)

    def section_out(
        xrow, mixed, gate_pre, gain_head, mat_out, gain_ffn, mat_gate, mat_up, mat_down, valid
    ):
        row_count = xrow.shape[0]
        shaped = mixed.reshape(row_count, HEADS, HEAD_DIM)
        shaped = shaped * lax.rsqrt(jnp.mean(shaped * shaped, axis=-1, keepdims=True) + 1e-05)
        normed = shaped.reshape(row_count, D) * gain_head
        gated = low(normed * jax.nn.silu(gate_pre))
        middle = xrow + low_back(matmul(gated, mat_out))
        hidden = low(
            middle * lax.rsqrt(jnp.mean(middle * middle, axis=-1, keepdims=True) + 1e-06) * gain_ffn
        )
        inner = low(
            jax.nn.silu(low_back(matmul(hidden, mat_gate))) * low_back(matmul(hidden, mat_up))
        )
        return valid[:, None] * (middle + low_back(matmul(inner, mat_down)))

    return section_out


def bit_of(rank, bit):
    return lax.rem(lax.div(rank, 1 << bit), 2)


def swap_bit(value, bit):
    count = lax.axis_size("seq")
    return lax.ppermute(value, "seq", [(source, source ^ (1 << bit)) for source in range(count)])


def rotate(value, steps):
    count = lax.axis_size("wshard")
    return lax.ppermute(
        value, "wshard", [(source, (source + steps) % count) for source in range(count)]
    )


def seq_orders():
    bits = lax.axis_size("seq").bit_length() - 1
    far = list(range(1, bits))
    return far, far[::-1]


def gather_seq(value, order, lead):
    rank = lax.axis_index("seq")
    done = []
    for bit in order:
        other = swap_bit(value, bit)
        place = lead + sum(1 for earlier in done if earlier > bit)
        upper = bit_of(rank, bit) == 1
        low_half = jnp.where(upper, other, value)
        high_half = jnp.where(upper, value, other)
        value = jnp.stack([low_half, high_half], axis=place)
        done.append(bit)
    shape = value.shape
    return value.reshape(shape[:lead] + (1 << len(order),) + shape[lead + len(order) :])


def gather_seq_both(value, lead):
    half = value.shape[-1] // 2
    one, two = seq_orders()
    return jnp.concatenate(
        [
            gather_seq(value[..., :half], one + [0], lead),
            gather_seq(value[..., half:], two + [0], lead),
        ],
        axis=-1,
    )


def gather_weight(shard):
    rank = lax.axis_index("seq")
    place = lax.axis_index("wshard")
    parts = lax.axis_size("seq")
    shards = lax.axis_size("wshard")
    rows, columns = shard.shape
    piece = lax.dynamic_slice_in_dim(shard, rank * (rows // parts), rows // parts, 0)
    foreign = jnp.stack([rotate(piece, step) for step in range(1, shards)])
    foreign = gather_seq_both(foreign, 1).reshape(shards - 1, rows, columns)
    pieces = jnp.concatenate([shard[None], foreign])
    return jnp.concatenate(
        [
            lax.dynamic_index_in_dim(pieces, lax.rem(place - index + shards, shards), 0, False)
            for index in range(shards)
        ]
    )


def add_low(left, right):
    return (left.astype(jnp.float32) + right.astype(jnp.float32)).astype(jnp.bfloat16)


def halve_seq(value, order, remaining):
    rank = lax.axis_index("seq")
    remaining = list(remaining)
    for bit in order:
        axis = 1 + sum(1 for other in remaining if other > bit)
        mine = bit_of(rank, bit)
        keep = lax.dynamic_index_in_dim(value, mine, axis, False)
        send = lax.dynamic_index_in_dim(value, 1 - mine, axis, False)
        value = add_low(keep, swap_bit(send, bit))
        remaining.remove(bit)
    return value


def sum_weight(grad):
    place = lax.axis_index("wshard")
    parts = lax.axis_size("seq")
    shards = lax.axis_size("wshard")
    rows, columns = grad.shape
    bits = parts.bit_length() - 1
    everything = list(range(bits))
    piece_rows = rows // shards // parts
    value = grad.astype(jnp.bfloat16).reshape((shards,) + (2,) * bits + (piece_rows, columns))
    value = halve_seq(value, [0], everything)
    half = columns // 2
    one, two = seq_orders()
    value = jnp.concatenate(
        [
            halve_seq(value[..., :half], one, everything[1:]),
            halve_seq(value[..., half:], two, everything[1:]),
        ],
        axis=-1,
    )
    total = lax.dynamic_index_in_dim(value, place, 0, False).astype(jnp.float32)
    for step in range(1, shards):
        target = lax.rem(place + step, shards)
        arrived = rotate(lax.dynamic_index_in_dim(value, target, 0, False), step)
        total = total + arrived.astype(jnp.float32)
    whole = gather_seq_both(total.astype(jnp.bfloat16), 0)
    return whole.reshape(rows // shards, columns).astype(jnp.float32)


def on_device(
    tokens,
    slot_lengths,
    live_lengths,
    norm_gain,
    w_qkv,
    w_beta,
    w_outgate,
    conv_weight,
    ridge,
    head_gain,
    w_out,
    ffn_gain,
    w_gate,
    w_up,
    w_down,
    cotangent,
):
    section_out = make_kit()
    row_count = tokens.shape[1]
    depth = (WINDOW + row_count - 1) // row_count
    halo_rows = depth * row_count
    main_rows = halo_rows + row_count
    shards = lax.axis_size("wshard")
    shard_rows = norm_gain.shape[0]
    tap_columns = TAPS * conv_weight.shape[1] // shard_rows
    ffn = w_gate.shape[1]

    own_tokens = tokens[0]
    pieces = [passed_along(own_tokens, "seq", hop) for hop in range(depth, 0, -1)]
    pieces.append(own_tokens)
    pieces.append(passed_along(own_tokens[row_count - PRE :], "seq", depth + 1))
    ext_tokens = jnp.concatenate(pieces)

    small = jnp.concatenate(
        [
            w_beta,
            norm_gain[:, None],
            ridge[:, None],
            head_gain[:, None],
            ffn_gain[:, None],
            conv_weight.reshape(shard_rows, tap_columns),
        ],
        axis=1,
    )
    small = jnp.pad(small, ((0, 0), (0, SMALL - small.shape[1])))
    w_front = gather_weight(jnp.concatenate([w_qkv, small], axis=1))
    middle = gather_weight(jnp.concatenate([w_outgate, w_out, w_gate, w_up], axis=1))
    all_down = gather_weight(w_down)
    small = w_front[:, 3 * D :].astype(f32)
    gain_in, all_ridge, gain_head, gain_ffn = (small[:, HEADS + index] for index in range(4))
    taps = small[:, HEADS + 4 : HEADS + 4 + tap_columns]
    taps = taps.reshape(shards, TAPS, -1).transpose(1, 0, 2).reshape(TAPS, 3 * D)
    all_og = middle[:, :D]
    all_out = middle[:, D : 2 * D].astype(f32)
    all_gate = middle[:, 2 * D : 2 * D + ffn].astype(f32)
    all_up = middle[:, 2 * D + ffn :].astype(f32)
    all_down = all_down.astype(f32)

    rank = lax.axis_index("seq")
    first = rank * row_count - halo_rows - PRE
    positions = first + jnp.arange(PRE + main_rows, dtype=jnp.int32)
    segment, valid = token_layout(slot_lengths[0], live_lengths[0], positions)
    main_seg = segment[PRE:]
    own_seg = main_seg[halo_rows:]
    valid_own = valid[PRE + halo_rows :].astype(f32)
    same = jnp.stack(
        [segment[PRE - tap : PRE - tap + main_rows] == main_seg for tap in range(TAPS)], axis=1
    ).astype(f32)
    spacing = positions[None, PRE + halo_rows :] - positions[PRE:, None]
    mask = (
        (spacing >= 0)
        & (spacing < WINDOW)
        & (main_seg[:, None] == own_seg[None, :])
        & valid[PRE:, None]
    ).astype(bf16)
    gain_row = gain_in[None, :]
    ridge_column = all_ridge[:, None]
    x_own = own_tokens.astype(f32)

    hidden, kv_in, q_in, q_pre, queries, keys, values, beta = front(
        ext_tokens, same, gain_row, w_front, taps, row_count
    )
    hidden_own = hidden[halo_rows:main_rows]
    gate_pre = jnp.dot(hidden_own, all_og, preferred_element_type=f32)
    mixed, image0, image1 = attn_fwd(queries, keys, values, beta, mask, ridge_column)

    def back_half(xrow, mixed, gate_pre, gain_head, mat_out, gain_ffn, mat_gate, mat_up, mat_down):
        return section_out(
            xrow, mixed, gate_pre, gain_head, mat_out, gain_ffn, mat_gate, mat_up, mat_down, valid_own
        )

    output, pull_back = jax.vjp(
        back_half, x_own, mixed, gate_pre, gain_head, all_out, gain_ffn, all_gate, all_up, all_down
    )
    grad_out = cotangent[0].astype(f32)
    d_xout, d_mixed, d_gate, d_ghead, d_wout, d_gffn, d_wgate, d_wup, d_wdown = pull_back(grad_out)
    d_gate = d_gate.astype(bf16)

    total_down = sum_weight(d_wdown)
    total_ffn = sum_weight(jnp.concatenate([d_wgate, d_wup], axis=1).astype(bf16))

    d_query, d_key, d_value, d_beta, d_ridge = attn_bwd(
        queries, keys, values, beta, mask, ridge_column, image0, image1, d_mixed.astype(bf16)
    )
    d_kv_in, d_q_in, d_q_pre, d_beta_pre, d_halo, d_own, d_gain, d_taps = back(
        ext_tokens,
        kv_in,
        same,
        q_in,
        q_pre,
        d_key,
        d_value,
        d_query,
        beta,
        d_beta,
        d_gate,
        d_xout,
        gain_row,
        w_front,
        all_og,
        taps,
    )

    def weight_grad(left, right):
        return lax.dot_general(
            left, right, (((0,), (0,)), ((), ())), preferred_element_type=f32
        ).astype(bf16)

    d_wog = weight_grad(hidden_own, d_gate)
    d_wq = weight_grad(
        hidden[halo_rows - PRE : main_rows], jnp.concatenate([d_q_pre, d_q_in])
    )
    d_wkv = weight_grad(hidden, d_kv_in)
    d_wbeta = weight_grad(hidden[:main_rows], d_beta_pre)[:, :HEADS]

    d_tokens = d_own
    for hop in range(1, depth + 1):
        start = halo_rows - hop * row_count
        part = passed_along(d_halo[start : start + row_count], "seq", -hop)
        d_tokens = d_tokens + part.astype(f32)
    part = passed_along(d_halo[halo_rows:], "seq", -(depth + 1)).astype(f32)
    d_tokens = d_tokens + jnp.pad(part, ((row_count - PRE, 0), (0, 0)))

    d_small = jnp.concatenate(
        [
            d_wbeta.astype(f32),
            d_gain.reshape(D, 1),
            d_ridge,
            d_ghead[:, None],
            d_gffn[:, None],
            d_taps.reshape(TAPS, shards, -1).transpose(1, 0, 2).reshape(D, tap_columns),
        ],
        axis=1,
    ).astype(bf16)
    d_small = jnp.pad(d_small, ((0, 0), (0, SMALL - d_small.shape[1])))
    total_middle = sum_weight(jnp.concatenate([d_wog, d_wout.astype(bf16)], axis=1))
    total_front = sum_weight(jnp.concatenate([d_wq, d_wkv, d_small], axis=1))
    t_small = total_front[:, 3 * D :]
    return (
        output.astype(bf16)[None],
        d_tokens.astype(bf16)[None],
        t_small[:, HEADS],
        total_front[:, : 3 * D],
        t_small[:, :HEADS],
        total_middle[:, :D],
        t_small[:, HEADS + 4 : HEADS + 4 + tap_columns].reshape(TAPS, -1),
        t_small[:, HEADS + 1],
        t_small[:, HEADS + 2],
        total_middle[:, D:],
        t_small[:, HEADS + 3],
        total_ffn[:, :ffn],
        total_ffn[:, ffn:],
        total_down,
    )


def solution(mesh):
    return jax.shard_map(
        on_device,
        mesh=mesh,
        in_specs=(
            P("wshard", "seq", None),
            P("wshard", None),
            P("wshard", None),
            P("wshard"),
            P("wshard", None),
            P("wshard", None),
            P("wshard", None),
            P(None, "wshard"),
            P("wshard"),
            P("wshard"),
            P("wshard", None),
            P("wshard"),
            P("wshard", None),
            P("wshard", None),
            P("wshard", None),
            P("wshard", "seq", None),
        ),
        out_specs=(
            P("wshard", "seq", None),
            P("wshard", "seq", None),
            P("wshard"),
            P("wshard", None),
            P("wshard", None),
            P("wshard", None),
            P(None, "wshard"),
            P("wshard"),
            P("wshard"),
            P("wshard", None),
            P("wshard"),
            P("wshard", None),
            P("wshard", None),
            P("wshard", None),
        ),
        check_vma=False,
    )
```

time: 1200 us -> 906 us (0.76)
  matrix products: 403 us -> 100 us
  Pallas kernels: 0 us -> 173 us
  other arithmetic: 252 us -> 123 us
  local copies, waits for them, and re-layouts: 143 us -> 92.5 us
  waiting for transfers between devices: 279 us -> 296 us
    dot_general x176 -> x5, matrix products: 293 us -> 28.2 us  [the longest x4 23.2 us: weight_grad(): lax.dot_general(left, right, (((0,), (0,)), ((), ())), preferred_element_...]
    pallas_call x0 -> x4, Pallas kernels: none -> 173 us  [the longest x1 66.2 us: attn_bwd(): pl.pallas_call(attn_bwd_kernel, grid=(HEADS,), in_specs=[head(rows), head...]
    reduce_sum x48 -> x0, other arithmetic: 53.6 us -> none  [the longest x2 36.1 us: section_conv(): total = total + conv_taps[tap_index] * source * same[tap_index]]
    dot_general x24 -> x4, matrix products: 65 us -> 29.1 us  [matmul_keep(): jnp.dot(left_low, right_low, preferred_element_type=jnp.float32)]
    ppermute x62, waiting for transfers between devices: 178 us -> 213 us  [swap_bit(): lax.ppermute(value, 'seq', [(source, source ^ 1 << bit) for source in ran...]
    convert_element_type x31 -> x1, other arithmetic: 28 us -> 0.24 us  [low(): return lax.optimization_barrier(v.astype(jnp.bfloat16)).astype(jnp.float32)]
    add_any x30 -> x0, other arithmetic: 18.3 us -> none  [the longest x2 16.1 us: section_conv(): source = rows_in[TAPS - 1 - tap_index:TAPS - 1 - tap_index + row_count]]
    mul x4 -> x0, other arithmetic: 17.6 us -> none  [the longest x2 17.6 us: section_conv(): total = total + conv_taps[tap_index] * source * same[tap_index]]
  transfers between devices with their start and end apart: 89 -> 89, of which waited for: 38 -> 40; matrix products, arithmetic and copies ran while one was open for 26% -> 20% of each run, Pallas kernels for 0% -> 6%
where the time goes in v2:
time: 906 us; the launch traced here: 898 us
  waiting for transfers between devices  296 us (33%)
  Pallas kernels  173 us (19%)
  other arithmetic  123 us (14%)
  starting transfers between devices  109 us (12%)
  matrix products  100 us (11%)
  local copies, waits for them, and re-layouts  92.5 us (10%)
    ppermute x62, waiting for transfers between devices, swap_bit(): lax.ppermute(value, 'seq', [(source, source ^ 1 << bit) for source in ran...  213 us
    ppermute x21, waiting for transfers between devices, rotate(): lax.ppermute(value, 'wshard', [(source, (source + steps) % count) for sou...  80.9 us
    pallas_call x1, Pallas kernels, attn_bwd(): pl.pallas_call(attn_bwd_kernel, grid=(HEADS,), in_specs=[head(rows), head...  66.2 us
    ppermute x62, starting transfers between devices, swap_bit(): lax.ppermute(value, 'seq', [(source, source ^ 1 << bit) for source in ran...  57.4 us
    pallas_call x1, Pallas kernels, back(): pl.pallas_call(functools.partial(back_kernel, blocks, first_own), grid=(b...  51.1 us
    ppermute x21, starting transfers between devices, rotate(): lax.ppermute(value, 'wshard', [(source, (source + steps) % count) for sou...  39.5 us
    pallas_call x1, Pallas kernels, attn_fwd(): pl.pallas_call(attn_fwd_kernel, grid=(HEADS,), in_specs=[head(rows), head...  30.6 us
    dot_general x4, matrix products, matmul_keep(): jnp.dot(left_low, right_low, preferred_element_type=jnp.float32)  29.1 us
  transfers between devices with their start and end apart: 89, of which 40 were waited for; matrix products, arithmetic and copies ran while one was open for 20% of the time, Pallas kernels for 6%

profile of v2, /device:TPU:0, one launch (start us, length us, event | category | flops | bytes accessed | tf_op | source)
XLA Modules:
  0.0 897.7 jit_solution(2952075942159128539)
XLA Ops:
  10.1 5.0 collective-permute-start.5
  32.8 13.3 %collective-permute-start.3 = (bf16[32,3200]{1,0:T(8,128)(2,1)}, bf16[32,3200]{1,0:T(8,128)(2,1)S(1)}, u32[]{:S(2)}, u32[]{:S(2)}) collective-permute-start(bf16[32,3200]{1,0:T(8,128)(2,1)} %constant_dynamic-slice_fusion.10), channel_id=1, source_target_pairs={{0,1},{1,2},{2,3},{3,0},{4,5},{5,6},{6,7},{7,4},{8,9},{9,10},{10,1... | collective-permute-start | bytes 614408 | tf_op jit(solution)/shard_map/ppermute | solution.py:744
  49.6 4.0 collective-permute-start
  57.9 27.1 %collective-permute-done.24 = bf16[3,88,512]{2,1,0:T(8,128)(2,1)S(1)} collective-permute-done((bf16[3,88,512]{2,1,0:T(8,128)(2,1)S(1)}, bf16[3,88,512]{2,1,0:T(8,128)(2,1)S(1)}, u32[]{:S(2)}, u32[]{:S(2)}) %collective-permute-start.24) | collective-permute-done | bytes 270368 | tf_op jit(solution)/shard_map/ppermute | solution.py:739
  85.0 7.6 collective-permute-done.27
  96.0 19.6 %collective-permute-done.13 = bf16[32,7680]{1,0:T(8,128)(2,1)S(1)} collective-permute-done((bf16[32,7680]{1,0:T(8,128)(2,1)S(1)}, bf16[32,7680]{1,0:T(8,128)(2,1)S(1)}, u32[]{:S(2)}, u32[]{:S(2)}) %collective-permute-start.13) | collective-permute-done | bytes 491552 | tf_op jit(solution)/shard_map/ppermute | solution.py:744
  120.5 6.2 collective-permute-done.6
  130.2 11.2 %collective-permute-done.28 = bf16[3,2,88,512]{3,2,0,1:T(8,128)(2,1)S(1)} collective-permute-done((bf16[3,2,88,512]{3,2,0,1:T(8,128)(2,1)S(1)}, bf16[3,2,88,512]{3,2,0,1:T(8,128)(2,1)S(1)}, u32[]{:S(2)}, u32[]{:S(2)}) %collective-permute-start.28) | collective-permute-done | bytes 540704 | tf_op jit(solution)/shard_map/ppermute | solution.py:739
  148.5 24.8 %collective-permute-done.10 = bf16[3,2,32,1600]{3,2,0,1:T(8,128)(2,1)S(1)} collective-permute-done((bf16[3,2,32,1600]{3,2,0,1:T(8,128)(2,1)S(1)}, bf16[3,2,32,1600]{3,2,0,1:T(8,128)(2,1)S(1)}, u32[]{:S(2)}, u32[]{:S(2)}) %collective-permute-start.10) | collective-permute-done | bytes 614432 | tf_op jit(solution)/shard_map/ppermute | solution.py:739
  184.0 10.5 %fusion.46 = f32[512,2816]{1,0:T(8,128)} fusion(bf16[512,1024]{1,0:T(8,128)(2,1)S(1)} %copy-done.59, bf16[704,1024]{1,0:T(8,128)(2,1)S(1)} %get-tuple-element.200, bf16[704,1024]{1,0:T(8,128)(2,1)S(1)} %get-tuple-element.201, bf16[704,1024]{1,0:T(8,128)(2,1)S(1)} %get-tuple-element.202, bf16[704,1024]{1,0:T(8,128)(2,1)S(1)} %get-tuple-element.199), kind=kOutput, calls=%fused_computation.192 | convolution fusion | flops 2975858688 | bytes 12582912 | tf_op jit(solution)/shard_map/transpose(jvp())/dot_general | solution.py:728
  199.7 13.1 %pad_maximum_fusion.1.w_ref = bf16[1024,3200]{1,0:T(8,128)(2,1)S(1)} fusion(bf16[256,3200]{1,0:T(8,128)(2,1)S(1)} %get-tuple-element.188, bf16[256,3200]{1,0:T(8,128)(2,1)S(1)} %get-tuple-element.189, bf16[256,3200]{1,0:T(8,128)(2,1)S(1)} %get-tuple-element.190, bf16[256,3200]{1,0:T(8,128)(2,1)S(1)} %get-tuple-element.187), kind=kLoop, calls=%fused_computation.13 | loop fusion | flops 26214400 | bytes 13107200 | tf_op jit(solution)/shard_map/concatenate | solution.py:792
  216.0 24.7 %front.1 = (bf16[1552,1024]{1,0:T(8,128)(2,1)}, bf16[1552,2048]{1,0:T(8,128)(2,1)}, bf16[512,1024]{1,0:T(8,128)(2,1)S(1)}, bf16[16,1024]{1,0:T(8,128)(2,1)S(1)},...) custom-call(bf16[1552,1024]{1,0:T(8,128)(2,1)} %pad_maximum_fusion.1, ...), custom_call_target="tpu_custom_call" | custom-call | flops 15032385536 | bytes 31457280 | tf_op jit(solution)/shard_map/front/pallas_call | solution.py:153
  250.7 30.6 %attn_fwd.1 = (f32[512,1024]{1,0:T(8,128)S(1)}, f32[1024,512]{1,0:T(8,128)}, f32[1024,512]{1,0:T(8,128)}) custom-call(bf16[512,1024]{1,0:T(8,128)(2,1)S(1)} %get-tuple-element.38.q_ref, bf16[1536,1024]{1,0:T(8,128)(2,1)} %get-tuple-element.39.k_ref, bf16[1536,1024]{1,0:T(8,128)(2,1)} %get-tuple-element.40.v_ref, f32[1536,128]{1,0:T(8,128)S(1)} %get-tuple-element.41.beta_ref, ...), custom_call_target="tpu_custom_call" | custom-call | flops 16106127360 | bytes 20971520 | tf_op jit(solution)/shard_map/attn_fwd/pallas_call | solution.py:518
  300.1 7.4 maximum_maximum_fusion
  307.5 5.6 dynamic-slice_bitcast_fusion.3
  313.2 3.8 pad_maximum_fusion.17
  320.0 10.3 %pad_maximum_fusion.4 = bf16[1024,2816]{1,0:T(8,128)(2,1)S(1)} fusion(bf16[256,7680]{1,0:T(8,128)(2,1)S(1)} %copy-done.11, bf16[256,7680]{1,0:T(8,128)(2,1)S(1)} %copy-done.12, bf16[256,7680]{1,0:T(8,128)(2,1)S(1)} %copy-done.14, bf16[256,7680]{1,0:T(8,128)(2,1)S(1)} %copy-done.10), kind=kLoop, calls=%fused_computation.25 | loop fusion | flops 23068672 | bytes 21495808 | tf_op jit(solution)/shard_map/concatenate | solution.py:792
  330.9 5.0 multiply_convert_fusion.4
  337.6 4.9 fusion.124
  342.5 18.5 %fusion.7 = (bf16[512,2816]{1,0:T(8,128)(2,1)}, bf16[512,2816]{1,0:T(8,128)(2,1)}, bf16[512,2816]{1,0:T(8,128)(2,1)}) fusion(f32[512,2816]{1,0:T(8,128)} %fusion.46, f32[512,2816]{1,0:T(8,128)} %fusion.124, bf16[512,1024]{1,0:T(8,128)(2,1)S(1)} %multiply_convert_fusion.3, bf16[256,7680]{1,0:T(8,128)(2,1)S(1)} %copy-done.11, ...), kind=kOutput, calls=%fused_computation.20 | convolution fusion | flops 2998927360 | bytes 36962304 | tf_op jit(solution)/shard_map/jvp()/dot_general | solution.py:696
  361.0 8.2 fusion.125
  369.2 6.4 multiply_reduce_fusion
  382.7 5.1 convolution_convert_fusion.2
  387.8 5.2 convolution_convert_fusion.1
  408.5 66.2 %attn_bwd.1 = (f32[512,1024]{1,0:T(8,128)}, f32[1536,1024]{1,0:T(8,128)}, f32[1536,1024]{1,0:T(8,128)}, f32[1536,128]{1,0:T(8,128)S(1)}, f32[1024,1]{1,0:T(8,128)S(1)}) custom-call(bf16[512,1024]{1,0:T(8,128)(2,1)S(1)} %copy-done.8, bf16[1536,1024]{1,0:T(8,128)(2,1)} %get-tuple-element.39.k_ref, bf16[1536,1024]{1,0:T(8,128)(2,1)} %get-tuple-element.40.v_ref, ...), custom_call_target="tpu_custom_call" | custom-call | flops 40265318400 | bytes 31457280 | tf_op jit(solution)/shard_map/attn_bwd/pallas_call | solution.py:630
  475.6 51.1 %back.1 = (bf16[1552,2048]{1,0:T(8,128)(2,1)}, bf16[512,1024]{1,0:T(8,128)(2,1)}, bf16[16,1024]{1,0:T(8,128)(2,1)}, bf16[1536,128]{1,0:T(8,128)(2,1)}, bf16[1040...) custom-call(bf16[1552,1024]{1,0:T(8,128)(2,1)} %pad_maximum_fusion.10.x_ref, ...), custom_call_target="tpu_custom_call" | custom-call | flops 22548578304 | bytes 41943040 | tf_op jit(solution)/shard_map/back/pallas_call | solution.py:386
  536.4 12.5 %convolution_convert_fusion.3 = bf16[1024,2048]{1,0:T(8,128)(2,1)} fusion(bf16[1552,1024]{1,0:T(8,128)(2,1)} %get-tuple-element.43, bf16[1552,2048]{1,0:T(8,128)(2,1)} %get-tuple-element.57), kind=kOutput, calls=%fused_computation.49 | convolution fusion | flops 6511656960 | bytes 13729792 | tf_op jit(solution)/shard_map/dot_general | solution.py:970
  548.9 4.4 convolution_convert_fusion.6
  556.2 4.6 pad_maximum_fusion.9
  560.8 6.6 copy.304
  587.8 4.1 fusion.2
  593.3 4.4 fusion.38
  607.6 8.1 collective-permute-done.48
  626.9 4.0 collective-permute-done.49
  639.3 4.6 collective-permute-done.53
  651.3 14.0 %collective-permute-done.59 = bf16[2,32,1024]{2,1,0:T(8,128)(2,1)S(1)} collective-permute-done((bf16[2,32,1024]{2,1,0:T(8,128)(2,1)S(1)}, bf16[2,32,1024]{2,1,0:T(8,128)(2,1)S(1)}, u32[]{:S(2)}, u32[]{:S(2)}) %collective-permute-start.59) | collective-permute-done | bytes 131104 | tf_op jit(solution)/shard_map/ppermute | solution.py:739
  679.9 23.4 %collective-permute-done.77 = bf16[4,88,512]{2,1,0:T(8,128)(2,1)S(1)} collective-permute-done((bf16[4,88,512]{2,1,0:T(8,128)(2,1)S(1)}, bf16[4,88,512]{2,1,0:T(8,128)(2,1)S(1)}, u32[]{:S(2)}, u32[]{:S(2)}) %collective-permute-start.77) | collective-permute-done | bytes 360480 | tf_op jit(solution)/shard_map/ppermute | solution.py:739
  711.5 10.7 %collective-permute-done.81 = bf16[88,1024]{1,0:T(8,128)(2,1)S(1)} collective-permute-done((bf16[88,1024]{1,0:T(8,128)(2,1)S(1)}, bf16[88,1024]{1,0:T(8,128)(2,1)S(1)}, u32[]{:S(2)}, u32[]{:S(2)}) %collective-permute-start.81) | collective-permute-done | bytes 180256 | tf_op jit(solution)/shard_map/ppermute | solution.py:744
  731.2 4.6 collective-permute-done.87
  736.1 4.6 collective-permute-done.37
  741.1 4.0 collective-permute-start.39
  747.4 14.4 %collective-permute-done.39 = bf16[32,3200]{1,0:T(8,128)(2,1)S(1)} collective-permute-done((bf16[32,3200]{1,0:T(8,128)(2,1)S(1)}, bf16[32,3200]{1,0:T(8,128)(2,1)S(1)}, u32[]{:S(2)}, u32[]{:S(2)}) %collective-permute-start.39) | collective-permute-done | bytes 204832 | tf_op jit(solution)/shard_map/ppermute | solution.py:744
  773.7 8.5 fusion.1
  789.1 30.9 %collective-permute-done.62 = bf16[4,2,32,2816]{3,2,0,1:T(8,128)(2,1)S(1)} collective-permute-done((bf16[4,2,32,2816]{3,2,0,1:T(8,128)(2,1)S(1)}, bf16[4,2,32,2816]{3,2,0,1:T(8,128)(2,1)S(1)}, u32[]{:S(2)}, u32[]{:S(2)}) %collective-permute-start.62) | collective-permute-done | bytes 1441824 | tf_op jit(solution)/shard_map/ppermute | solution.py:739
  823.5 15.1 %collective-permute-done.63 = bf16[4,32,2816]{2,1,0:T(8,128)(2,1)S(1)} collective-permute-done((bf16[4,32,2816]{2,1,0:T(8,128)(2,1)S(1)}, bf16[4,32,2816]{2,1,0:T(8,128)(2,1)S(1)}, u32[]{:S(2)}, u32[]{:S(2)}) %collective-permute-start.63) | collective-permute-done | bytes 720928 | tf_op jit(solution)/shard_map/ppermute | solution.py:739
  843.5 7.6 collective-permute-done.68
  851.1 19.9 %collective-permute-done.67 = bf16[32,5632]{1,0:T(8,128)(2,1)S(1)} collective-permute-done((bf16[32,5632]{1,0:T(8,128)(2,1)S(1)}, bf16[32,5632]{1,0:T(8,128)(2,1)S(1)}, u32[]{:S(2)}, u32[]{:S(2)}) %collective-permute-start.67) | collective-permute-done | bytes 360480 | tf_op jit(solution)/shard_map/ppermute | solution.py:744
  885.2 5.6 collective-permute-done.70
  (588 shorter events, 282.1 us)
Async XLA Ops:
  10.1 44.8 %collective-permute-start.5 = (bf16[32,3200]{1,0:T(8,128)(2,1)}, bf16[32,3200]{1,0:T(8,128)(2,1)}, u32[]{:S(2)}, u32[]{:S(2)}) collective-permute-start(bf16[32,3200]{1,0:T(8,128)(2,1)} %constant_dynamic-slice_fusion.10), channel_id=1, source_target_pairs={{0,3},{1,0},{2,1},{3,2},{4,7},{5,4},{6,5},{7,6},{8,11},{9,8},{10,9... | collective-permute-start | bytes 614408 | tf_op jit(solution)/shard_map/ppermute | solution.py:744
  15.1 39.9 %collective-permute-start.4 = (bf16[32,3200]{1,0:T(8,128)(2,1)}, bf16[32,3200]{1,0:T(8,128)(2,1)}, u32[]{:S(2)}, u32[]{:S(2)}) collective-permute-start(bf16[32,3200]{1,0:T(8,128)(2,1)} %constant_dynamic-slice_fusion.10), channel_id=1, source_target_pairs={{0,2},{1,3},{2,0},{3,1},{4,6},{5,7},{6,4},{7,5},{8,10},{9,11},{10,... | collective-permute-start | bytes 614408 | tf_op jit(solution)/shard_map/ppermute | solution.py:744
  17.2 31.1 %collective-permute-start.22 = (bf16[88,1024]{1,0:T(8,128)(2,1)}, bf16[88,1024]{1,0:T(8,128)(2,1)}, u32[]{:S(2)}, u32[]{:S(2)}) collective-permute-start(bf16[88,1024]{1,0:T(8,128)(2,1)} %constant_dynamic-slice_fusion.8), channel_id=1, source_target_pairs={{0,2},{1,3},{2,0},{3,1},{4,6},{5,7},{6,4},{7,5},{8,10},{9,11},{10,... | collective-permute-start | bytes 540680 | tf_op jit(solution)/shard_map/ppermute | solution.py:744
  19.6 30.0 %collective-permute-start.21 = (bf16[88,1024]{1,0:T(8,128)(2,1)}, bf16[88,1024]{1,0:T(8,128)(2,1)}, u32[]{:S(2)}, u32[]{:S(2)}) collective-permute-start(bf16[88,1024]{1,0:T(8,128)(2,1)} %constant_dynamic-slice_fusion.8), channel_id=1, source_target_pairs={{0,1},{1,2},{2,3},{3,0},{4,5},{5,6},{6,7},{7,4},{8,9},{9,10},{10,1... | collective-permute-start | bytes 540680 | tf_op jit(solution)/shard_map/ppermute | solution.py:744
  32.8 23.7 %collective-permute-start.3 = (bf16[32,3200]{1,0:T(8,128)(2,1)}, bf16[32,3200]{1,0:T(8,128)(2,1)S(1)}, u32[]{:S(2)}, u32[]{:S(2)}) collective-permute-start(bf16[32,3200]{1,0:T(8,128)(2,1)} %constant_dynamic-slice_fusion.10), channel_id=1, source_target_pairs={{0,1},{1,2},{2,3},{3,0},{4,5},{5,6},{6,7},{7,4},{8,9},{9,10},{10,1... | collective-permute-start | bytes 614408 | tf_op jit(solution)/shard_map/ppermute | solution.py:744
  48.3 96.2 %collective-permute-start.1 = (bf16[512,1024]{1,0:T(8,128)(2,1)S(1)}, bf16[512,1024]{1,0:T(8,128)(2,1)S(1)}, u32[]{:S(2)}, u32[]{:S(2)}) collective-permute-start(bf16[512,1024]{1,0:T(8,128)(2,1)S(1)} %bitcast.527), channel_id=1, source_target_pairs={{0,4},{4,8},{8,12},{12,16},{16,20},{20,24},{24,28},{1,5},{5,9},{9,... | collective-permute-start | bytes 3145736 | tf_op jit(solution)/shard_map/ppermute | solution.py:645
  49.6 96.4 %collective-permute-start = (bf16[512,1024]{1,0:T(8,128)(2,1)S(1)}, bf16[512,1024]{1,0:T(8,128)(2,1)S(1)}, u32[]{:S(2)}, u32[]{:S(2)}) collective-permute-start(bf16[512,1024]{1,0:T(8,128)(2,1)S(1)} %bitcast.528), channel_id=1, source_target_pairs={{0,8},{4,12},{8,16},{12,20},{16,24},{20,28},{1,9},{5,13},{9,17},{1... | collective-permute-start | bytes 3145736 | tf_op jit(solution)/shard_map/ppermute | solution.py:645
  54.9 37.9 %collective-permute-start.14 = (bf16[32,7680]{1,0:T(8,128)(2,1)S(1)}, bf16[32,7680]{1,0:T(8,128)(2,1)S(1)}, u32[]{:S(2)}, u32[]{:S(2)}) collective-permute-start(bf16[32,7680]{1,0:T(8,128)(2,1)S(1)} %copy-done.65), channel_id=1, source_target_pairs={{0,3},{1,0},{2,1},{3,2},{4,7},{5,4},{6,5},{7,6},{8,11},{9,8},{10,9... | collective-permute-start | bytes 1474568 | tf_op jit(solution)/shard_map/ppermute | solution.py:744
  55.0 30.0 %collective-permute-start.24 = (bf16[3,88,512]{2,1,0:T(8,128)(2,1)S(1)}, bf16[3,88,512]{2,1,0:T(8,128)(2,1)S(1)}, u32[]{:S(2)}, u32[]{:S(2)}) collective-permute-start(bf16[3,88,512]{2,1,0:T(8,128)(2,1)S(1)} %get-tuple-element.292), channel_id=1, source_target_pairs={{0,8},{4,12},{8,0},{12,4},{16,24},{20,28},{24,16},{28,20},{1,9},{5... | collective-permute-start | bytes 811016 | tf_op jit(solution)/shard_map/ppermute | solution.py:739
  56.5 36.1 %collective-permute-start.27 = (bf16[3,88,512]{2,1,0:T(8,128)(2,1)S(1)}, bf16[3,88,512]{2,1,0:T(8,128)(2,1)S(1)}, u32[]{:S(2)}, u32[]{:S(2)}) collective-permute-start(bf16[3,88,512]{2,1,0:T(8,128)(2,1)S(1)} %get-tuple-element.293), channel_id=1, source_target_pairs={{0,16},{4,20},{8,24},{12,28},{16,0},{20,4},{24,8},{28,12},{1,17},{... | collective-permute-start | bytes 811016 | tf_op jit(solution)/shard_map/ppermute | solution.py:739
  85.0 30.6 %collective-permute-start.13 = (bf16[32,7680]{1,0:T(8,128)(2,1)S(1)}, bf16[32,7680]{1,0:T(8,128)(2,1)S(1)}, u32[]{:S(2)}, u32[]{:S(2)}) collective-permute-start(bf16[32,7680]{1,0:T(8,128)(2,1)S(1)} %copy-done.65), channel_id=1, source_target_pairs={{0,2},{1,3},{2,0},{3,1},{4,6},{5,7},{6,4},{7,5},{8,10},{9,11},{10,... | collective-permute-start | bytes 1474568 | tf_op jit(solution)/shard_map/ppermute | solution.py:744
  92.6 26.2 %collective-permute-start.12 = (bf16[32,7680]{1,0:T(8,128)(2,1)S(1)}, bf16[32,7680]{1,0:T(8,128)(2,1)S(1)}, u32[]{:S(2)}, u32[]{:S(2)}) collective-permute-start(bf16[32,7680]{1,0:T(8,128)(2,1)S(1)} %copy-done.65), channel_id=1, source_target_pairs={{0,1},{1,2},{2,3},{3,0},{4,5},{5,6},{6,7},{7,4},{8,9},{9,10},{10,1... | collective-permute-start | bytes 1474568 | tf_op jit(solution)/shard_map/ppermute | solution.py:744
  92.8 51.2 %collective-permute-start.2 = (bf16[16,1024]{1,0:T(8,128)(2,1)S(1)}, bf16[16,1024]{1,0:T(8,128)(2,1)S(1)}, u32[]{:S(2)}, u32[]{:S(2)}) collective-permute-start(bf16[16,1024]{1,0:T(8,128)(2,1)S(1)} %slice_bitcast_fusion), channel_id=1, source_target_pairs={{0,12},{4,16},{8,20},{12,24},{16,28},{1,13},{5,17},{9,21},{13,25},... | collective-permute-start | bytes 98312 | tf_op jit(solution)/shard_map/ppermute | solution.py:645
  141.4 34.2 %collective-permute-start.15 = (bf16[3,32,3840]{2,1,0:T(8,128)(2,1)S(1)}, bf16[3,32,3840]{2,1,0:T(8,128)(2,1)S(1)}, u32[]{:S(2)}, u32[]{:S(2)}) collective-permute-start(bf16[3,32,3840]{2,1,0:T(8,128)(2,1)S(1)} %get-tuple-element.235), channel_id=1, source_target_pairs={{0,8},{4,12},{8,0},{12,4},{16,24},{20,28},{24,16},{28,20},{1,9},{5... | collective-permute-start | bytes 2211848 | tf_op jit(solution)/shard_map/ppermute | solution.py:739
  141.8 31.4 %collective-permute-start.10 = (bf16[3,2,32,1600]{3,2,0,1:T(8,128)(2,1)S(1)}, bf16[3,2,32,1600]{3,2,0,1:T(8,128)(2,1)S(1)}, u32[]{:S(2)}, u32[]{:S(2)}) collective-permute-start(bf16[3,2,32,1600]{3,2,0,1:T(8,128)(2,1)S(1)} %pad_maximum_fusion.37), channel_id=1, source_target_pairs={{0,8},{4,12},{8,0},{12,4},{16,24},{20,28},{24,16},{28,20},{1,9},{5... | collective-permute-start | bytes 1843208 | tf_op jit(solution)/shard_map/ppermute | solution.py:739
  143.9 32.2 %collective-permute-start.18 = (bf16[3,32,3840]{2,1,0:T(8,128)(2,1)S(1)}, bf16[3,32,3840]{2,1,0:T(8,128)(2,1)S(1)}, u32[]{:S(2)}, u32[]{:S(2)}) collective-permute-start(bf16[3,32,3840]{2,1,0:T(8,128)(2,1)S(1)} %get-tuple-element.236), channel_id=1, source_target_pairs={{0,16},{4,20},{8,24},{12,28},{16,0},{20,4},{24,8},{28,12},{1,17},{... | collective-permute-start | bytes 2211848 | tf_op jit(solution)/shard_map/ppermute | solution.py:739
  144.4 30.8 %collective-permute-start.7 = (bf16[3,2,32,1600]{3,2,0,1:T(8,128)(2,1)S(1)}, bf16[3,2,32,1600]{3,2,0,1:T(8,128)(2,1)S(1)}, u32[]{:S(2)}, u32[]{:S(2)}) collective-permute-start(bf16[3,2,32,1600]{3,2,0,1:T(8,128)(2,1)S(1)} %pad_maximum_fusion.36), channel_id=1, source_target_pairs={{0,16},{4,20},{8,24},{12,28},{16,0},{20,4},{24,8},{28,12},{1,17},{... | collective-permute-start | bytes 1843208 | tf_op jit(solution)/shard_map/ppermute | solution.py:739
  146.0 33.3 %collective-permute-start.29 = (bf16[3,2,2,88,512]{4,3,0,1,2:T(8,128)(2,1)S(1)}, bf16[3,2,2,88,512]{4,3,0,1,2:T(8,128)(2,1)S(1)}, u32[]{:S(2)}, u32[]{:S(2)}) collective-permute-start(bf16[3,2,2,88,512]{4,3,0,1,2:T(8,128)(2,1)S(1)} %pad_maximum_fusion.27), channel_id=1, source_target_pairs={{0,4},{4,0},{8,12},{12,8},{16,20},{20,16},{24,28},{28,24},{1,5},{5... | collective-permute-start | bytes 3244040 | tf_op jit(solution)/shard_map/ppermute | solution.py:739
  175.3 19.3 %collective-permute-start.11 = (bf16[3,2,2,32,1600]{4,3,0,1,2:T(8,128)(2,1)S(1)}, bf16[3,2,2,32,1600]{4,3,0,1,2:T(8,128)(2,1)S(1)}, u32[]{:S(2)}, u32[]{:S(2)}) collective-permute-start(bf16[3,2,2,32,1600]{4,3,0,1,2:T(8,128)(2,1)S(1)} %pad_maximum_fusion.25), channel_id=1, source_target_pairs={{0,4},{4,0},{8,12},{12,8},{16,20},{20,16},{24,28},{28,24},{1,5},{5... | collective-permute-start | bytes 3686408 | tf_op jit(solution)/shard_map/ppermute | solution.py:739
  175.6 18.9 %collective-permute-start.8 = (bf16[3,2,2,32,1600]{4,3,0,1,2:T(8,128)(2,1)S(1)}, bf16[3,2,2,32,1600]{4,3,0,1,2:T(8,128)(2,1)S(1)}, u32[]{:S(2)}, u32[]{:S(2)}) collective-permute-start(bf16[3,2,2,32,1600]{4,3,0,1,2:T(8,128)(2,1)S(1)} %pad_maximum_fusion.24), channel_id=1, source_target_pairs={{0,4},{4,0},{8,12},{12,8},{16,20},{20,16},{24,28},{28,24},{1,5},{5... | collective-permute-start | bytes 3686408 | tf_op jit(solution)/shard_map/ppermute | solution.py:739
  177.8 63.0 %collective-permute-start.19 = (bf16[3,2,32,3840]{3,2,0,1:T(8,128)(2,1)}, bf16[3,2,32,3840]{3,2,0,1:T(8,128)(2,1)}, u32[]{:S(2)}, u32[]{:S(2)}) collective-permute-start(bf16[3,2,32,3840]{3,2,0,1:T(8,128)(2,1)} %pad_maximum_fusion.21), channel_id=1, source_target_pairs={{0,8},{4,12},{8,0},{12,4},{16,24},{20,28},{24,16},{28,20},{1,9},{5... | collective-permute-start | bytes 4423688 | tf_op jit(solution)/shard_map/ppermute | solution.py:739
  179.4 66.6 %collective-permute-start.16 = (bf16[3,2,32,3840]{3,2,0,1:T(8,128)(2,1)}, bf16[3,2,32,3840]{3,2,0,1:T(8,128)(2,1)}, u32[]{:S(2)}, u32[]{:S(2)}) collective-permute-start(bf16[3,2,32,3840]{3,2,0,1:T(8,128)(2,1)} %pad_maximum_fusion.20), channel_id=1, source_target_pairs={{0,16},{4,20},{8,24},{12,28},{16,0},{20,4},{24,8},{28,12},{1,17},{... | collective-permute-start | bytes 4423688 | tf_op jit(solution)/shard_map/ppermute | solution.py:739
  246.0 42.1 %collective-permute-start.20 = (bf16[3,2,2,32,3840]{4,3,0,1,2:T(8,128)(2,1)}, bf16[3,2,2,32,3840]{4,3,0,1,2:T(8,128)(2,1)}, u32[]{:S(2)}, u32[]{:S(2)}) collective-permute-start(bf16[3,2,2,32,3840]{4,3,0,1,2:T(8,128)(2,1)} %pad_maximum_fusion.12), channel_id=1, source_target_pairs={{0,4},{4,0},{8,12},{12,8},{16,20},{20,16},{24,28},{28,24},{1,5},{5... | collective-permute-start | bytes 8847368 | tf_op jit(solution)/shard_map/ppermute | solution.py:739
  250.2 44.3 %collective-permute-start.17 = (bf16[3,2,2,32,3840]{4,3,0,1,2:T(8,128)(2,1)}, bf16[3,2,2,32,3840]{4,3,0,1,2:T(8,128)(2,1)}, u32[]{:S(2)}, u32[]{:S(2)}) collective-permute-start(bf16[3,2,2,32,3840]{4,3,0,1,2:T(8,128)(2,1)} %pad_maximum_fusion.11), channel_id=1, source_target_pairs={{0,4},{4,0},{8,12},{12,8},{16,20},{20,16},{24,28},{28,24},{1,5},{5... | collective-permute-start | bytes 8847368 | tf_op jit(solution)/shard_map/ppermute | solution.py:739
  529.7 92.5 %collective-permute-start.31 = (bf16[512,1024]{1,0:T(8,128)(2,1)}, bf16[512,1024]{1,0:T(8,128)(2,1)S(1)}, u32[]{:S(2)}, u32[]{:S(2)}) collective-permute-start(bf16[512,1024]{1,0:T(8,128)(2,1)} %get-tuple-element.226), channel_id=1, source_target_pairs={{8,0},{12,4},{16,8},{20,12},{24,16},{28,20},{9,1},{13,5},{17,9},{2... | collective-permute-start | bytes 3145736 | tf_op jit(solution)/shard_map/ppermute | solution.py:645
  531.0 92.9 %collective-permute-start.30 = (bf16[512,1024]{1,0:T(8,128)(2,1)}, bf16[512,1024]{1,0:T(8,128)(2,1)}, u32[]{:S(2)}, u32[]{:S(2)}) collective-permute-start(bf16[512,1024]{1,0:T(8,128)(2,1)} %get-tuple-element.225), channel_id=1, source_target_pairs={{4,0},{8,4},{12,8},{16,12},{20,16},{24,20},{28,24},{5,1},{9,5},{13... | collective-permute-start | bytes 3145736 | tf_op jit(solution)/shard_map/ppermute | solution.py:645
  570.7 27.0 %collective-permute-start.47 = (bf16[4,2,2,32,2048]{4,3,2,1,0:T(8,128)(2,1)}, bf16[4,2,2,32,2048]{4,3,2,1,0:T(8,128)(2,1)}, u32[]{:S(2)}, u32[]{:S(2)}) collective-permute-start(bf16[4,2,2,32,2048]{4,3,2,1,0:T(8,128)(2,1)} %dynamic-slice_bitcast_fusion.5), channel_id=1, source_target_pairs={{0,4},{4,0},{8,12},{12,8},{16,20},{20,16},{24,28},{28,24},{1,5},{5... | collective-permute-start | bytes 6291464 | tf_op jit(solution)/shard_map/ppermute | solution.py:739
  578.7 53.9 %collective-permute-start.75 = (bf16[4,2,2,88,1024]{4,3,2,1,0:T(8,128)(2,1)}, bf16[4,2,2,88,1024]{4,3,2,1,0:T(8,128)(2,1)}, u32[]{:S(2)}, u32[]{:S(2)}) collective-permute-start(bf16[4,2,2,88,1024]{4,3,2,1,0:T(8,128)(2,1)} %dynamic-slice_bitcast_fusion.4), channel_id=1, source_target_pairs={{0,4},{4,0},{8,12},{12,8},{16,20},{20,16},{24,28},{28,24},{1,5},{5... | collective-permute-start | bytes 8650760 | tf_op jit(solution)/shard_map/ppermute | solution.py:739
  618.3 51.9 %collective-permute-start.33 = (bf16[4,2,2,32,3200]{4,3,0,2,1:T(8,128)(2,1)S(1)}, bf16[4,2,2,32,3200]{4,3,0,2,1:T(8,128)(2,1)S(1)}, u32[]{:S(2)}, u32[]{:S(2)}) collective-permute-start(bf16[4,2,2,32,3200]{4,3,0,2,1:T(8,128)(2,1)S(1)} %bitcast.520), channel_id=1, source_target_pairs={{0,4},{4,0},{8,12},{12,8},{16,20},{20,16},{24,28},{28,24},{1,5},{5... | collective-permute-start | bytes 9830408 | tf_op jit(solution)/shard_map/ppermute | solution.py:739
  621.0 152.8 %collective-permute-start.61 = (bf16[4,2,2,32,5632]{4,3,2,1,0:T(8,128)(2,1)S(1)}, bf16[4,2,2,32,5632]{4,3,2,1,0:T(8,128)(2,1)}, u32[]{:S(2)}, u32[]{:S(2)}) collective-permute-start(bf16[4,2,2,32,5632]{4,3,2,1,0:T(8,128)(2,1)S(1)} %bitcast.513), channel_id=1, source_target_pairs={{0,4},{4,0},{8,12},{12,8},{16,20},{20,16},{24,28},{28,24},{1,5},{5... | collective-permute-start | bytes 17301512 | tf_op jit(solution)/shard_map/ppermute | solution.py:739
  646.1 30.5 %collective-permute-start.76 = (bf16[4,2,88,512]{3,2,0,1:T(8,128)(2,1)S(1)}, bf16[4,2,88,512]{3,2,0,1:T(8,128)(2,1)S(1)}, u32[]{:S(2)}, u32[]{:S(2)}) collective-permute-start(bf16[4,2,88,512]{3,2,0,1:T(8,128)(2,1)S(1)} %bitcast.530), channel_id=1, source_target_pairs={{0,8},{4,12},{8,0},{12,4},{16,24},{20,28},{24,16},{28,20},{1,9},{5... | collective-permute-start | bytes 2162696 | tf_op jit(solution)/shard_map/ppermute | solution.py:739
  650.5 27.3 %collective-permute-start.78 = (bf16[4,2,88,512]{3,2,1,0:T(8,128)(2,1)S(1)}, bf16[4,2,88,512]{3,2,1,0:T(8,128)(2,1)S(1)}, u32[]{:S(2)}, u32[]{:S(2)}) collective-permute-start(bf16[4,2,88,512]{3,2,1,0:T(8,128)(2,1)S(1)} %dynamic-slice_bitcast_fusion.17), channel_id=1, source_target_pairs={{0,16},{4,20},{8,24},{12,28},{16,0},{20,4},{24,8},{28,12},{1,17},{... | collective-permute-start | bytes 2162696 | tf_op jit(solution)/shard_map/ppermute | solution.py:739
  673.1 34.0 %collective-permute-start.34 = (bf16[4,2,32,1600]{3,2,0,1:T(8,128)(2,1)S(1)}, bf16[4,2,32,1600]{3,2,0,1:T(8,128)(2,1)S(1)}, u32[]{:S(2)}, u32[]{:S(2)}) collective-permute-start(bf16[4,2,32,1600]{3,2,0,1:T(8,128)(2,1)S(1)} %dynamic-slice_bitcast_fusion.16), channel_id=1, source_target_pairs={{0,8},{4,12},{8,0},{12,4},{16,24},{20,28},{24,16},{28,20},{1,9},{5... | collective-permute-start | bytes 2457608 | tf_op jit(solution)/shard_map/ppermute | solution.py:739
  674.9 49.4 %collective-permute-start.36 = (bf16[4,2,32,1600]{3,2,0,1:T(8,128)(2,1)S(1)}, bf16[4,2,32,1600]{3,2,0,1:T(8,128)(2,1)S(1)}, u32[]{:S(2)}, u32[]{:S(2)}) collective-permute-start(bf16[4,2,32,1600]{3,2,0,1:T(8,128)(2,1)S(1)} %dynamic-slice_bitcast_fusion.15), channel_id=1, source_target_pairs={{0,16},{4,20},{8,24},{12,28},{16,0},{20,4},{24,8},{28,12},{1,17},{... | collective-permute-start | bytes 2457608 | tf_op jit(solution)/shard_map/ppermute | solution.py:739
  676.9 26.4 %collective-permute-start.77 = (bf16[4,88,512]{2,1,0:T(8,128)(2,1)S(1)}, bf16[4,88,512]{2,1,0:T(8,128)(2,1)S(1)}, u32[]{:S(2)}, u32[]{:S(2)}) collective-permute-start(bf16[4,88,512]{2,1,0:T(8,128)(2,1)S(1)} %dynamic-slice_bitcast_fusion.24), channel_id=1, source_target_pairs={{0,16},{4,20},{8,24},{12,28},{16,0},{20,4},{24,8},{28,12},{1,17},{... | collective-permute-start | bytes 1081352 | tf_op jit(solution)/shard_map/ppermute | solution.py:739
  678.0 25.4 %collective-permute-start.79 = (bf16[4,88,512]{2,1,0:T(8,128)(2,1)S(1)}, bf16[4,88,512]{2,1,0:T(8,128)(2,1)S(1)}, u32[]{:S(2)}, u32[]{:S(2)}) collective-permute-start(bf16[4,88,512]{2,1,0:T(8,128)(2,1)S(1)} %dynamic-slice_bitcast_fusion.23), channel_id=1, source_target_pairs={{0,8},{4,12},{8,0},{12,4},{16,24},{20,28},{24,16},{28,20},{1,9},{5... | collective-permute-start | bytes 1081352 | tf_op jit(solution)/shard_map/ppermute | solution.py:739
  705.1 17.1 %collective-permute-start.81 = (bf16[88,1024]{1,0:T(8,128)(2,1)S(1)}, bf16[88,1024]{1,0:T(8,128)(2,1)S(1)}, u32[]{:S(2)}, u32[]{:S(2)}) collective-permute-start(bf16[88,1024]{1,0:T(8,128)(2,1)S(1)} %get-tuple-element.276), channel_id=1, source_target_pairs={{0,2},{1,3},{2,0},{3,1},{4,6},{5,7},{6,4},{7,5},{8,10},{9,11},{10,... | collective-permute-start | bytes 540680 | tf_op jit(solution)/shard_map/ppermute | solution.py:744
  710.1 25.9 %collective-permute-start.35 = (bf16[4,32,1600]{2,1,0:T(8,128)(2,1)S(1)}, bf16[4,32,1600]{2,1,0:T(8,128)(2,1)S(1)}, u32[]{:S(2)}, u32[]{:S(2)}) collective-permute-start(bf16[4,32,1600]{2,1,0:T(8,128)(2,1)S(1)} %dynamic-slice_bitcast_fusion.22), channel_id=1, source_target_pairs={{0,16},{4,20},{8,24},{12,28},{16,0},{20,4},{24,8},{28,12},{1,17},{... | collective-permute-start | bytes 1228808 | tf_op jit(solution)/shard_map/ppermute | solution.py:739
  735.9 28.3 %collective-permute-start.88 = (bf16[2,2,88,512]{3,2,0,1:T(8,128)(2,1)S(1)}, bf16[2,2,88,512]{3,2,0,1:T(8,128)(2,1)S(1)}, u32[]{:S(2)}, u32[]{:S(2)}) collective-permute-start(bf16[2,2,88,512]{3,2,0,1:T(8,128)(2,1)S(1)} %pad_maximum_fusion.49), channel_id=1, source_target_pairs={{0,4},{4,0},{8,12},{12,8},{16,20},{20,16},{24,28},{28,24},{1,5},{5... | collective-permute-start | bytes 1081352 | tf_op jit(solution)/shard_map/ppermute | solution.py:739
  741.1 20.7 %collective-permute-start.39 = (bf16[32,3200]{1,0:T(8,128)(2,1)S(1)}, bf16[32,3200]{1,0:T(8,128)(2,1)S(1)}, u32[]{:S(2)}, u32[]{:S(2)}) collective-permute-start(bf16[32,3200]{1,0:T(8,128)(2,1)S(1)} %get-tuple-element.265), channel_id=1, source_target_pairs={{0,2},{1,3},{2,0},{3,1},{4,6},{5,7},{6,4},{7,5},{8,10},{9,11},{10,... | collective-permute-start | bytes 614408 | tf_op jit(solution)/shard_map/ppermute | solution.py:744
  769.7 18.1 %collective-permute-start.42 = (bf16[2,32,1600]{2,1,0:T(8,128)(2,1)S(1)}, bf16[2,32,1600]{2,1,0:T(8,128)(2,1)S(1)}, u32[]{:S(2)}, u32[]{:S(2)}) collective-permute-start(bf16[2,32,1600]{2,1,0:T(8,128)(2,1)S(1)} %pad_maximum_fusion.52), channel_id=1, source_target_pairs={{0,16},{4,20},{8,24},{12,28},{16,0},{20,4},{24,8},{28,12},{1,17},{... | collective-permute-start | bytes 614408 | tf_op jit(solution)/shard_map/ppermute | solution.py:739
  785.7 34.3 %collective-permute-start.62 = (bf16[4,2,32,2816]{3,2,0,1:T(8,128)(2,1)S(1)}, bf16[4,2,32,2816]{3,2,0,1:T(8,128)(2,1)S(1)}, u32[]{:S(2)}, u32[]{:S(2)}) collective-permute-start(bf16[4,2,32,2816]{3,2,0,1:T(8,128)(2,1)S(1)} %bitcast.526), channel_id=1, source_target_pairs={{0,8},{4,12},{8,0},{12,4},{16,24},{20,28},{24,16},{28,20},{1,9},{5... | collective-permute-start | bytes 4325384 | tf_op jit(solution)/shard_map/ppermute | solution.py:739
  788.0 35.5 %collective-permute-start.43 = (bf16[2,2,32,1600]{3,2,1,0:T(8,128)(2,1)S(1)}, bf16[2,2,32,1600]{3,2,1,0:T(8,128)(2,1)S(1)}, u32[]{:S(2)}, u32[]{:S(2)}) collective-permute-start(bf16[2,2,32,1600]{3,2,1,0:T(8,128)(2,1)S(1)} %pad_maximum_fusion.44), channel_id=1, source_target_pairs={{0,4},{4,0},{8,12},{12,8},{16,20},{20,16},{24,28},{28,24},{1,5},{5... | collective-permute-start | bytes 1228808 | tf_op jit(solution)/shard_map/ppermute | solution.py:739
  788.3 34.3 %collective-permute-start.64 = (bf16[4,2,32,2816]{3,2,1,0:T(8,128)(2,1)S(1)}, bf16[4,2,32,2816]{3,2,1,0:T(8,128)(2,1)S(1)}, u32[]{:S(2)}, u32[]{:S(2)}) collective-permute-start(bf16[4,2,32,2816]{3,2,1,0:T(8,128)(2,1)S(1)} %dynamic-slice_bitcast_fusion.10), channel_id=1, source_target_pairs={{0,16},{4,20},{8,24},{12,28},{16,0},{20,4},{24,8},{28,12},{1,17},{... | collective-permute-start | bytes 4325384 | tf_op jit(solution)/shard_map/ppermute | solution.py:739
  820.5 18.1 %collective-permute-start.63 = (bf16[4,32,2816]{2,1,0:T(8,128)(2,1)S(1)}, bf16[4,32,2816]{2,1,0:T(8,128)(2,1)S(1)}, u32[]{:S(2)}, u32[]{:S(2)}) collective-permute-start(bf16[4,32,2816]{2,1,0:T(8,128)(2,1)S(1)} %dynamic-slice_bitcast_fusion.19), channel_id=1, source_target_pairs={{0,16},{4,20},{8,24},{12,28},{16,0},{20,4},{24,8},{28,12},{1,17},{... | collective-permute-start | bytes 2162696 | tf_op jit(solution)/shard_map/ppermute | solution.py:739
  823.1 17.5 %collective-permute-start.65 = (bf16[4,32,2816]{2,1,0:T(8,128)(2,1)S(1)}, bf16[4,32,2816]{2,1,0:T(8,128)(2,1)S(1)}, u32[]{:S(2)}, u32[]{:S(2)}) collective-permute-start(bf16[4,32,2816]{2,1,0:T(8,128)(2,1)S(1)} %dynamic-slice_bitcast_fusion.18), channel_id=1, source_target_pairs={{0,8},{4,12},{8,0},{12,4},{16,24},{20,28},{24,16},{28,20},{1,9},{5... | collective-permute-start | bytes 2162696 | tf_op jit(solution)/shard_map/ppermute | solution.py:739
  841.0 30.0 %collective-permute-start.67 = (bf16[32,5632]{1,0:T(8,128)(2,1)S(1)}, bf16[32,5632]{1,0:T(8,128)(2,1)S(1)}, u32[]{:S(2)}, u32[]{:S(2)}) collective-permute-start(bf16[32,5632]{1,0:T(8,128)(2,1)S(1)} %get-tuple-element.244), channel_id=1, source_target_pairs={{0,2},{1,3},{2,0},{3,1},{4,6},{5,7},{6,4},{7,5},{8,10},{9,11},{10,... | collective-permute-start | bytes 1081352 | tf_op jit(solution)/shard_map/ppermute | solution.py:744
  841.0 29.9 %collective-permute-start.66 = (bf16[32,5632]{1,0:T(8,128)(2,1)S(1)}, bf16[32,5632]{1,0:T(8,128)(2,1)S(1)}, u32[]{:S(2)}, u32[]{:S(2)}) collective-permute-start(bf16[32,5632]{1,0:T(8,128)(2,1)S(1)} %get-tuple-element.243), channel_id=1, source_target_pairs={{0,1},{1,2},{2,3},{3,0},{4,5},{5,6},{6,7},{7,4},{8,9},{9,10},{10,1... | collective-permute-start | bytes 1081352 | tf_op jit(solution)/shard_map/ppermute | solution.py:744
  (131 other events, 1412.2 us)

commit v3 on v2

--- a/solution.py
+++ b/solution.py
@@ -13,6 +13,8 @@
 WINDOW = 1024
 PRE = 16
 SMALL = 128
+EXTRA = 512
+MESH = pl.DeviceIdType.MESH
 f32 = jnp.float32
 bf16 = jnp.bfloat16
 QB = 256
@@ -730,116 +732,365 @@
     return section_out
 
 
-def bit_of(rank, bit):
-    return lax.rem(lax.div(rank, 1 << bit), 2)
-
-
-def swap_bit(value, bit):
+class Here:
+    def __init__(self):
+        rank = lax.axis_index("seq")
+        self.place = lax.axis_index("wshard")
+        self.shards = lax.axis_size("wshard")
+        self.core = rank % 2
+        self.x = (rank // 2) % 2
+        self.y = (rank // 4) % 2
+        self.core_next = rank + 1 - 2 * self.core
+        self.x_next = rank + 2 - 4 * self.x
+        self.y_next = rank + 4 - 8 * self.y
+
+    def other(self, step):
+        return (self.place + step) % self.shards
+
+    def meet(self):
+        barrier = pltpu.get_barrier_semaphore()
+        for near in (self.core_next, self.x_next, self.y_next):
+            pl.semaphore_signal(barrier, inc=1, device_id={"seq": near}, device_id_type=MESH)
+        for step in range(1, self.shards):
+            pl.semaphore_signal(
+                barrier, inc=1, device_id={"wshard": self.other(step)}, device_id_type=MESH
+            )
+        pl.semaphore_wait(barrier, 3 + self.shards - 1)
+
+
+class Sends:
+    def __init__(self, send_sems, recv_sems):
+        self.send_sems = send_sems
+        self.recv_sems = recv_sems
+
+    def make(self, index, source, target, **device):
+        return pltpu.make_async_remote_copy(
+            src_ref=source,
+            dst_ref=target,
+            send_sem=self.send_sems.at[index],
+            recv_sem=self.recv_sems.at[index],
+            device_id=device,
+            device_id_type=MESH,
+        )
+
+
+def span(start, size):
+    return pl.ds(pl.multiple_of(start, 128), size)
+
+
+GATHER_COPIES = 18
+
+
+def gather_copies(here, sends, source, target, phase):
+    half = source.shape[-1] // 2
+    quarter = half // 2
+    mine = span(here.core * half, half)
+    one = span(here.core * half, quarter)
+    two = span(here.core * half + quarter, quarter)
+    y, x = here.y, here.x
+    others = range(1, here.shards)
+    if phase == 0:
+        return [
+            sends.make(
+                step - 1,
+                source.at[y, x, :, mine],
+                target.at[here.place, y, x, :, mine],
+                wshard=here.other(step),
+            )
+            for step in others
+        ]
+    found = []
+    for step in others:
+        at = target.at[here.other(step)]
+        if phase == 1:
+            found.append((at.at[y, x, :, one], here.x_next))
+            found.append((at.at[y, x, :, two], here.y_next))
+        elif phase == 2:
+            found.append((at.at[y, :, :, one], here.y_next))
+            found.append((at.at[:, x, :, two], here.x_next))
+        else:
+            found.append((at.at[:, :, :, mine], here.core_next))
+    first = {1: 3, 2: 9, 3: 15}[phase]
+    return [
+        sends.make(first + index, ref, ref, seq=near) for index, (ref, near) in enumerate(found)
+    ]
+
+
+def gather_kernel(count, *refs):
+    sources = refs[:count]
+    targets = refs[count : 2 * count]
+    send_sems, recv_sems, own_sems = refs[2 * count :]
+    here = Here()
+    here.meet()
+    every = []
+    local = []
+    for index in range(count):
+        sends = Sends(send_sems.at[index], recv_sems.at[index])
+        every.append(
+            [
+                gather_copies(here, sends, sources[index], targets[index], phase)
+                for phase in range(4)
+            ]
+        )
+        local.append(
+            pltpu.make_async_copy(
+                sources[index], targets[index].at[here.place], own_sems.at[index]
+            )
+        )
+    for slot in range(count + 4):
+        for index in range(count):
+            phase = slot - index
+            if 1 <= phase <= 4:
+                for copy in every[index][phase - 1]:
+                    copy.wait_recv()
+            if 0 <= phase <= 3:
+                for copy in every[index][phase]:
+                    copy.start()
+                if phase == 0:
+                    local[index].start()
+    for index in range(count):
+        for phase in range(4):
+            for copy in every[index][phase]:
+                copy.wait_send()
+        local[index].wait()
+
+
+def gather(shards, collective_id):
+    places = lax.axis_size("wshard")
+    split = [shard.reshape(2, 2, shard.shape[0] // 4, shard.shape[1]) for shard in shards]
+    count = len(shards)
+    anywhere = pl.BlockSpec(memory_space=pl.ANY)
+    whole = pl.pallas_call(
+        functools.partial(gather_kernel, count),
+        in_specs=[anywhere] * count,
+        out_specs=[anywhere] * count,
+        out_shape=[jax.ShapeDtypeStruct((places,) + part.shape, part.dtype) for part in split],
+        scratch_shapes=[
+            pltpu.SemaphoreType.DMA((count, GATHER_COPIES)),
+            pltpu.SemaphoreType.DMA((count, GATHER_COPIES)),
+            pltpu.SemaphoreType.DMA((count,)),
+        ],
+        compiler_params=pltpu.CompilerParams(
+            collective_id=collective_id, has_side_effects=True, vmem_limit_bytes=50 << 20
+        ),
+        name="gather",
+    )(*split)
+    return [
+        part.reshape(places * shard.shape[0], shard.shape[1]) for part, shard in zip(whole, shards)
+    ]
+
+
+SUM_COPIES = 13
+
+
+class SumPart:
+    def __init__(self, here, sends, local, grad, out, held, core_in, far_a, far_b, next_a, next_b, last, total):
+        self.here, self.sends, self.local = here, sends, local
+        self.grad, self.out, self.held = grad, out, held
+        self.core_in, self.far_a, self.far_b = core_in, far_a, far_b
+        self.next_a, self.next_b, self.last, self.total = next_a, next_b, last, total
+        self.half = held.shape[-1]
+        self.quarter = self.half // 2
+        self.waiting = []
+        self.sent = []
+
+    def launch(self, copies):
+        for copy in copies:
+            copy.start()
+        self.waiting = copies
+        self.sent += copies
+
+    def arrive(self):
+        for copy in self.waiting:
+            copy.wait_recv()
+
+    def local_copy(self, index, source, target):
+        return pltpu.make_async_copy(source, target, self.local.at[index])
+
+    def step(self, phase):
+        here, make, half, quarter = self.here, self.sends.make, self.half, self.quarter
+        y, x, held, out = here.y, here.x, self.held, self.out
+        places = here.shards
+        one, two = pl.ds(0, quarter), pl.ds(quarter, quarter)
+        mine = span(here.core * half, half)
+        yours = span((1 - here.core) * half, half)
+        out_one = span(here.core * half, quarter)
+        out_two = span(here.core * half + quarter, quarter)
+        self.arrive()
+        if phase == 0:
+            self.own = self.local_copy(0, self.grad.at[:, :, :, :, mine], held)
+            self.own.start()
+            self.launch(
+                [make(0, self.grad.at[:, :, :, :, yours], self.core_in, seq=here.core_next)]
+            )
+        elif phase == 1:
+            self.own.wait()
+
+            def add(index, carry):
+                at = (index // 4, (index // 2) % 2, index % 2)
+                held[at] = (held[at].astype(f32) + self.core_in[at].astype(f32)).astype(bf16)
+                return carry
+
+            lax.fori_loop(0, 4 * places, add, 0)
+            self.launch(
+                [
+                    make(1, held.at[:, :, 1 - x, :, one], self.far_a, seq=here.x_next),
+                    make(2, held.at[:, 1 - y, :, :, two], self.far_b, seq=here.y_next),
+                ]
+            )
+        elif phase == 2:
+
+            def add(index, carry):
+                place, side = index // 2, index % 2
+                at = (place, side, x, slice(None), slice(0, quarter))
+                held[at] = (
+                    held[at].astype(f32) + self.far_a[place, side].astype(f32)
+                ).astype(bf16)
+                at = (place, y, side, slice(None), slice(quarter, half))
+                held[at] = (
+                    held[at].astype(f32) + self.far_b[place, side].astype(f32)
+                ).astype(bf16)
+                return carry
+
+            lax.fori_loop(0, 2 * places, add, 0)
+            self.launch(
+                [
+                    make(3, held.at[:, 1 - y, x, :, one], self.next_a, seq=here.y_next),
+                    make(4, held.at[:, y, 1 - x, :, two], self.next_b, seq=here.x_next),
+                ]
+            )
+        elif phase == 3:
+
+            def add(place, carry):
+                at = (place, y, x, slice(None), slice(0, quarter))
+                held[at] = (held[at].astype(f32) + self.next_a[place].astype(f32)).astype(bf16)
+                at = (place, y, x, slice(None), slice(quarter, half))
+                held[at] = (held[at].astype(f32) + self.next_b[place].astype(f32)).astype(bf16)
+                return carry
+
+            lax.fori_loop(0, places, add, 0)
+            self.launch(
+                [
+                    make(
+                        4 + step,
+                        held.at[here.other(step), y, x],
+                        self.last.at[step - 1],
+                        wshard=here.other(step),
+                    )
+                    for step in range(1, places)
+                ]
+            )
+        elif phase == 4:
+            total = held[here.place, y, x].astype(f32)
+            for step in range(places - 1):
+                total = total + self.last[step].astype(f32)
+            self.total[...] = total.astype(bf16)
+            self.own = self.local_copy(1, self.total, out.at[y, x, :, mine])
+            self.own.start()
+            self.launch(
+                [
+                    make(8, self.total.at[:, one], out.at[y, x, :, out_one], seq=here.y_next),
+                    make(9, self.total.at[:, two], out.at[y, x, :, out_two], seq=here.x_next),
+                ]
+            )
+        elif phase == 5:
+            self.own.wait()
+            both_one, both_two = out.at[:, x, :, out_one], out.at[y, :, :, out_two]
+            self.launch(
+                [
+                    make(10, both_one, both_one, seq=here.x_next),
+                    make(11, both_two, both_two, seq=here.y_next),
+                ]
+            )
+        elif phase == 6:
+            ref = out.at[:, :, :, mine]
+            self.launch([make(12, ref, ref, seq=here.core_next)])
+
+    def finish(self):
+        for copy in self.sent:
+            copy.wait_send()
+
+
+def sum_kernel(parts, *refs):
+    count = max(part[0] for part in parts) + 1
+    grads = refs[:count]
+    outs = refs[count : 2 * count]
+    send_sems, recv_sems, local_sems = refs[2 * count : 2 * count + 3]
+    scratch = refs[2 * count + 3 :]
+    here = Here()
+    here.meet()
+    moving = []
+    for index, (which, start, size) in enumerate(parts):
+        rows = pl.ds(start, size)
+        moving.append(
+            SumPart(
+                here,
+                Sends(send_sems.at[index], recv_sems.at[index]),
+                local_sems.at[index],
+                grads[which].at[:, :, :, rows],
+                outs[which].at[:, :, rows],
+                *scratch[8 * index : 8 * index + 8],
+            )
+        )
+    phases = 7
+    for slot in range(len(parts) + phases):
+        for index, part in enumerate(moving):
+            phase = slot - index
+            if 0 <= phase < phases:
+                part.step(phase)
+            elif phase == phases:
+                part.arrive()
+    for part in moving:
+        part.finish()
+
+
+def sum_over_devices(grads, parts, collective_id):
+    places = lax.axis_size("wshard")
+    split = [grad.reshape(places, 2, 2, grad.shape[0] // places // 4, grad.shape[1]) for grad in grads]
+    anywhere = pl.BlockSpec(memory_space=pl.ANY)
+    scratch = []
+    for which, start, size in parts:
+        half = grads[which].shape[1] // 2
+        quarter = half // 2
+        scratch += [
+            pltpu.VMEM((places, 2, 2, size, half), bf16),
+            pltpu.VMEM((places, 2, 2, size, half), bf16),
+            pltpu.VMEM((places, 2, size, quarter), bf16),
+            pltpu.VMEM((places, 2, size, quarter), bf16),
+            pltpu.VMEM((places, size, quarter), bf16),
+            pltpu.VMEM((places, size, quarter), bf16),
+            pltpu.VMEM((places - 1, size, half), bf16),
+            pltpu.VMEM((size, half), bf16),
+        ]
+    outs = pl.pallas_call(
+        functools.partial(sum_kernel, parts),
+        in_specs=[anywhere] * len(grads),
+        out_specs=[anywhere] * len(grads),
+        out_shape=[jax.ShapeDtypeStruct(part.shape[1:], bf16) for part in split],
+        scratch_shapes=[
+            pltpu.SemaphoreType.DMA((len(parts), SUM_COPIES)),
+            pltpu.SemaphoreType.DMA((len(parts), SUM_COPIES)),
+            pltpu.SemaphoreType.DMA((len(parts), 2)),
+        ]
+        + scratch,
+        compiler_params=pltpu.CompilerParams(
+            collective_id=collective_id, has_side_effects=True, vmem_limit_bytes=60 << 20
+        ),
+        name="sum_over_devices",
+    )(*split)
     count = lax.axis_size("seq")
-    return lax.ppermute(value, "seq", [(source, source ^ (1 << bit)) for source in range(count)])
-
-
-def rotate(value, steps):
-    count = lax.axis_size("wshard")
-    return lax.ppermute(
-        value, "wshard", [(source, (source + steps) % count) for source in range(count)]
-    )
-
-
-def seq_orders():
-    bits = lax.axis_size("seq").bit_length() - 1
-    far = list(range(1, bits))
-    return far, far[::-1]
-
-
-def gather_seq(value, order, lead):
-    rank = lax.axis_index("seq")
-    done = []
-    for bit in order:
-        other = swap_bit(value, bit)
-        place = lead + sum(1 for earlier in done if earlier > bit)
-        upper = bit_of(rank, bit) == 1
-        low_half = jnp.where(upper, other, value)
-        high_half = jnp.where(upper, value, other)
-        value = jnp.stack([low_half, high_half], axis=place)
-        done.append(bit)
-    shape = value.shape
-    return value.reshape(shape[:lead] + (1 << len(order),) + shape[lead + len(order) :])
-
-
-def gather_seq_both(value, lead):
-    half = value.shape[-1] // 2
-    one, two = seq_orders()
-    return jnp.concatenate(
-        [
-            gather_seq(value[..., :half], one + [0], lead),
-            gather_seq(value[..., half:], two + [0], lead),
-        ],
-        axis=-1,
-    )
-
-
-def gather_weight(shard):
-    rank = lax.axis_index("seq")
-    place = lax.axis_index("wshard")
-    parts = lax.axis_size("seq")
-    shards = lax.axis_size("wshard")
-    rows, columns = shard.shape
-    piece = lax.dynamic_slice_in_dim(shard, rank * (rows // parts), rows // parts, 0)
-    foreign = jnp.stack([rotate(piece, step) for step in range(1, shards)])
-    foreign = gather_seq_both(foreign, 1).reshape(shards - 1, rows, columns)
-    pieces = jnp.concatenate([shard[None], foreign])
-    return jnp.concatenate(
-        [
-            lax.dynamic_index_in_dim(pieces, lax.rem(place - index + shards, shards), 0, False)
-            for index in range(shards)
+    bit = 8
+    while bit < count:
+        pairs = [(source, source ^ bit) for source in range(count)]
+        outs = [
+            (part.astype(f32) + lax.ppermute(part, "seq", pairs).astype(f32)).astype(bf16)
+            for part in outs
         ]
-    )
-
-
-def add_low(left, right):
-    return (left.astype(jnp.float32) + right.astype(jnp.float32)).astype(jnp.bfloat16)
-
-
-def halve_seq(value, order, remaining):
-    rank = lax.axis_index("seq")
-    remaining = list(remaining)
-    for bit in order:
-        axis = 1 + sum(1 for other in remaining if other > bit)
-        mine = bit_of(rank, bit)
-        keep = lax.dynamic_index_in_dim(value, mine, axis, False)
-        send = lax.dynamic_index_in_dim(value, 1 - mine, axis, False)
-        value = add_low(keep, swap_bit(send, bit))
-        remaining.remove(bit)
-    return value
-
-
-def sum_weight(grad):
-    place = lax.axis_index("wshard")
-    parts = lax.axis_size("seq")
-    shards = lax.axis_size("wshard")
-    rows, columns = grad.shape
-    bits = parts.bit_length() - 1
-    everything = list(range(bits))
-    piece_rows = rows // shards // parts
-    value = grad.astype(jnp.bfloat16).reshape((shards,) + (2,) * bits + (piece_rows, columns))
-    value = halve_seq(value, [0], everything)
-    half = columns // 2
-    one, two = seq_orders()
-    value = jnp.concatenate(
-        [
-            halve_seq(value[..., :half], one, everything[1:]),
-            halve_seq(value[..., half:], two, everything[1:]),
-        ],
-        axis=-1,
-    )
-    total = lax.dynamic_index_in_dim(value, place, 0, False).astype(jnp.float32)
-    for step in range(1, shards):
-        target = lax.rem(place + step, shards)
-        arrived = rotate(lax.dynamic_index_in_dim(value, target, 0, False), step)
-        total = total + arrived.astype(jnp.float32)
-    whole = gather_seq_both(total.astype(jnp.bfloat16), 0)
-    return whole.reshape(rows // shards, columns).astype(jnp.float32)
+        bit *= 2
+    return [
+        part.reshape(grad.shape[0] // places, grad.shape[1]).astype(f32)
+        for part, grad in zip(outs, grads)
+    ]
 
 
 def on_device(
@@ -887,18 +1138,24 @@
         ],
         axis=1,
     )
-    small = jnp.pad(small, ((0, 0), (0, SMALL - small.shape[1])))
-    w_front = gather_weight(jnp.concatenate([w_qkv, small], axis=1))
-    middle = gather_weight(jnp.concatenate([w_outgate, w_out, w_gate, w_up], axis=1))
-    all_down = gather_weight(w_down)
+    small = jnp.pad(small, ((0, 0), (0, EXTRA - small.shape[1])))
+    (w_front,) = gather([jnp.concatenate([w_qkv, small], axis=1)], 0)
+    mats, ffn_in, all_down = gather(
+        [
+            jnp.concatenate([w_outgate, w_out], axis=1),
+            jnp.concatenate([w_gate, w_up], axis=1),
+            w_down,
+        ],
+        1,
+    )
     small = w_front[:, 3 * D :].astype(f32)
     gain_in, all_ridge, gain_head, gain_ffn = (small[:, HEADS + index] for index in range(4))
     taps = small[:, HEADS + 4 : HEADS + 4 + tap_columns]
     taps = taps.reshape(shards, TAPS, -1).transpose(1, 0, 2).reshape(TAPS, 3 * D)
-    all_og = middle[:, :D]
-    all_out = middle[:, D : 2 * D].astype(f32)
-    all_gate = middle[:, 2 * D : 2 * D + ffn].astype(f32)
-    all_up = middle[:, 2 * D + ffn :].astype(f32)
+    all_og = mats[:, :D]
+    all_out = mats[:, D:].astype(f32)
+    all_gate = ffn_in[:, :ffn].astype(f32)
+    all_up = ffn_in[:, ffn:].astype(f32)
     all_down = all_down.astype(f32)
 
     rank = lax.axis_index("seq")
@@ -940,9 +1197,6 @@
     grad_out = cotangent[0].astype(f32)
     d_xout, d_mixed, d_gate, d_ghead, d_wout, d_gffn, d_wgate, d_wup, d_wdown = pull_back(grad_out)
     d_gate = d_gate.astype(bf16)
-
-    total_down = sum_weight(d_wdown)
-    total_ffn = sum_weight(jnp.concatenate([d_wgate, d_wup], axis=1).astype(bf16))
 
     d_query, d_key, d_value, d_beta, d_ridge = attn_bwd(
         queries, keys, values, beta, mask, ridge_column, image0, image1, d_mixed.astype(bf16)
@@ -997,9 +1251,21 @@
         ],
         axis=1,
     ).astype(bf16)
-    d_small = jnp.pad(d_small, ((0, 0), (0, SMALL - d_small.shape[1])))
-    total_middle = sum_weight(jnp.concatenate([d_wog, d_wout.astype(bf16)], axis=1))
-    total_front = sum_weight(jnp.concatenate([d_wq, d_wkv, d_small], axis=1))
+    d_small = jnp.pad(d_small, ((0, 0), (0, EXTRA - d_small.shape[1])))
+    all_grads = [
+        d_wdown.astype(bf16),
+        jnp.concatenate([d_wgate, d_wup], axis=1).astype(bf16),
+        jnp.concatenate([d_wog, d_wout.astype(bf16)], axis=1),
+        jnp.concatenate([d_wq, d_wkv, d_small], axis=1),
+    ]
+    parts = [
+        (0, 0, w_down.shape[0] // 4),
+        (1, 0, shard_rows // 8),
+        (1, shard_rows // 8, shard_rows // 8),
+        (2, 0, shard_rows // 4),
+        (3, 0, shard_rows // 4),
+    ]
+    total_down, total_ffn, total_middle, total_front = sum_over_devices(all_grads, parts, 2)
     t_small = total_front[:, 3 * D :]
     return (
         output.astype(bf16)[None],

time: 906 us -> 761 us (0.84)
  Pallas kernels: 173 us -> 517 us
  waiting for transfers between devices: 296 us -> 27.3 us
  starting transfers between devices: 109 us -> 15.2 us
  other arithmetic: 123 us -> 48.8 us
  local copies, waits for them, and re-layouts: 92.5 us -> 50.1 us
  matrix products: 100 us -> 89 us
    pallas_call x0 -> x3, Pallas kernels: none -> 343 us  [the longest x1 187 us: sum_over_devices(): pl.pallas_call(functools.partial(sum_kernel, parts), in_specs=[anywhere]...]
    ppermute x83 -> x0, waiting for transfers between devices: 294 us -> none  [the longest x62 213 us: swap_bit(): lax.ppermute(value, 'seq', [(source, source ^ 1 << bit) for source in ran...]
    ppermute x83 -> x0, starting transfers between devices: 96.9 us -> none  [the longest x62 57.4 us: swap_bit(): lax.ppermute(value, 'seq', [(source, source ^ 1 << bit) for source in ran...]
    ppermute x6, waiting for transfers between devices: 2.4 us -> 27.3 us  [passed_along(): lax.ppermute(value, axis, [(source, source + steps) for source in range(i...]
    another operation x82 -> x3, other arithmetic: 25.3 us -> 0.87 us  [the longest x76 22.6 us: gather_seq(): value = jnp.stack([low_half, high_half], axis=place)]
    concatenate x6 -> x5, other arithmetic: 38.6 us -> 16.4 us  [the longest x1 7.32 us: on_device(): jnp.concatenate([d_wgate, d_wup], axis=1).astype(bf16)]
    convert_element_type x28 -> x4, other arithmetic: 21.6 us -> 5.34 us  [sum_over_devices(): part.reshape(grad.shape[0] // places, grad.shape[1]).astype(f32)]
    squeeze x18 -> x0, local copies, waits for them, and re-layouts: 12.9 us -> none  [the longest x3 6.77 us: gather_weight(): lax.dynamic_index_in_dim(pieces, lax.rem(place - index + shards, shards),...]
  transfers between devices with their start and end apart: 89 -> 6, of which waited for: 40 -> 2; matrix products, arithmetic and copies ran while one was open for 20% -> 5% of each run, Pallas kernels for 6% -> 21%
where the time goes in v3:
time: 761 us; the launch traced here: 749 us
  Pallas kernels  517 us (68%)
  matrix products  89 us (12%)
  local copies, waits for them, and re-layouts  50.1 us (7%)
  other arithmetic  48.8 us (6%)
  waiting for transfers between devices  27.3 us (4%)
  starting transfers between devices  15.2 us (2%)
    pallas_call x1, Pallas kernels, sum_over_devices(): pl.pallas_call(functools.partial(sum_kernel, parts), in_specs=[anywhere]...  187 us
    pallas_call x2, Pallas kernels, gather(): pl.pallas_call(functools.partial(gather_kernel, count), in_specs=[anywher...  157 us
    pallas_call x1, Pallas kernels, attn_bwd(): pl.pallas_call(attn_bwd_kernel, grid=(HEADS,), in_specs=[head(rows), head...  66.2 us
    pallas_call x1, Pallas kernels, back(): pl.pallas_call(functools.partial(back_kernel, blocks, first_own), grid=(b...  51.2 us
    pallas_call x1, Pallas kernels, attn_fwd(): pl.pallas_call(attn_fwd_kernel, grid=(HEADS,), in_specs=[head(rows), head...  31.2 us
    ppermute x6, waiting for transfers between devices, passed_along(): lax.ppermute(value, axis, [(source, source + steps) for source in range(i...  27.3 us
    pallas_call x1, Pallas kernels, front(): pl.pallas_call(functools.partial(front_kernel, first_own), grid=(blocks +...  25.1 us
    dot_general x4, matrix products, weight_grad(): lax.dot_general(left, right, (((0,), (0,)), ((), ())), preferred_element_...  21.9 us
  transfers between devices with their start and end apart: 6, of which 2 were waited for; matrix products, arithmetic and copies ran while one was open for 5% of the time, Pallas kernels for 21%

profile of v3, /device:TPU:0, one launch (start us, length us, event | category | flops | bytes accessed | tf_op | source)
XLA Modules:
  0.0 749.5 jit_solution(412525431828979750)
XLA Ops:
  0.6 5.8 collective-permute-start
  6.5 2.5 collective-permute-start.1
  9.7 3.0 collective-permute-start.2
  21.9 50.1 %gather.2 = bf16[4,2,2,64,3584]{4,3,2,1,0:T(8,128)(2,1)} custom-call(bf16[2,2,64,3584]{3,2,1,0:T(8,128)(2,1)S(1)} %bitcast.97), custom_call_target="tpu_custom_call" | custom-call | tf_op jit(solution)/shard_map/gather/pallas_call | solution.py:863
  76.2 2.5 fusion.20.mask_ref
  78.8 106.6 %gather.3 = (bf16[4,2,2,64,2048]{4,3,2,1,0:T(8,128)(2,1)}, bf16[4,2,2,64,5632]{4,3,2,1,0:T(8,128)(2,1)}, bf16[4,2,2,176,1024]{4,3,2,1,0:T(8,128)(2,1)}) custom-call(bf16[2,2,64,2048]{3,2,1,0:T(8,128)(2,1)S(1)} %bitcast.98, bf16[2,2,64,5632]{3,2,1,0:T(8,128)(2,1)} %bitcast.106, bf16[2,2,176,1024]{3,2,1,0:T(8,128)(2,1)S(1)} %bitcast.99), custom_call_target="tpu_custom_call" | custom-call | tf_op jit(solution)/shard_map/gather/pallas_call | solution.py:863
  185.4 7.6 %fusion.57 = f32[512,2816]{1,0:T(8,128)} fusion(bf16[512,1024]{1,0:T(8,128)(2,1)S(1)} %fusion.26, bf16[2816,1024]{1,0:T(8,128)(2,1)} %bitcast.138), kind=kOutput, calls=%fused_computation.124 | convolution fusion | flops 2952790016 | bytes 12582912 | tf_op jit(solution)/shard_map/transpose(jvp())/dot_general | solution.py:730
  195.1 3.3 slice.179.wog_ref
  198.4 3.1 pad_maximum_fusion.2.x_ref
  201.5 25.1 %front.1 = (bf16[1552,1024]{1,0:T(8,128)(2,1)}, bf16[1552,2048]{1,0:T(8,128)(2,1)}, bf16[512,1024]{1,0:T(8,128)(2,1)S(1)}, bf16[16,1024]{1,0:T(8,128)(2,1)S(1)},...) custom-call(bf16[1552,1024]{1,0:T(8,128)(2,1)} %pad_maximum_fusion.2, ...), custom_call_target="tpu_custom_call" | custom-call | flops 15032385536 | bytes 31457280 | tf_op jit(solution)/shard_map/front/pallas_call | solution.py:155
  226.7 31.2 %attn_fwd.1 = (f32[512,1024]{1,0:T(8,128)S(1)}, f32[1024,512]{1,0:T(8,128)}, f32[1024,512]{1,0:T(8,128)}) custom-call(bf16[512,1024]{1,0:T(8,128)(2,1)S(1)} %get-tuple-element.45.q_ref, bf16[1536,1024]{1,0:T(8,128)(2,1)} %get-tuple-element.46.k_ref, bf16[1536,1024]{1,0:T(8,128)(2,1)} %get-tuple-element.47.v_ref, f32[1536,128]{1,0:T(8,128)S(1)} %get-tuple-element.48.beta_ref, ...), custom_call_target="tpu_custom_call" | custom-call | flops 16106127360 | bytes 20971520 | tf_op jit(solution)/shard_map/attn_fwd/pallas_call | solution.py:520
  258.1 1.8 copy.105
  259.9 2.2 reduce_sum.84
  263.0 4.4 multiply_convert_fusion.4
  269.2 2.0 slice-done.5
  272.3 5.0 fusion.8
  277.3 10.5 %fusion.4 = (bf16[512,2816]{1,0:T(8,128)(2,1)S(1)}, bf16[512,2816]{1,0:T(8,128)(2,1)}, bf16[512,2816]{1,0:T(8,128)(2,1)}) fusion(f32[512,2816]{1,0:T(8,128)S(1)} %bitcast.143, f32[512,2816]{1,0:T(8,128)} %fusion.8, bf16[512,1024]{1,0:T(8,128)(2,1)S(1)} %multiply_convert_fusion.3, bf16[1024,5632]{1,0:T(8,128)(2,1)} %bitcast.132), kind=kOutput, calls=%fused_computation.7 | convolution fusion | flops 2975858688 | bytes 27000832 | tf_op jit(solution)/shard_map/jvp()/dot_general | solution.py:698
  287.8 6.1 fusion.6
  293.9 5.9 multiply_reduce_fusion
  299.8 2.0 fusion.53
  303.1 2.7 convolution_convert_fusion.5
  305.8 5.0 convolution_convert_fusion.1
  310.8 5.0 convolution_convert_fusion
  316.6 1.8 copy.107
  318.4 2.2 reduce_sum.90
  322.5 4.0 fusion.24
  326.5 2.6 convolution_convert_fusion.6
  329.1 66.2 %attn_bwd.1 = (f32[512,1024]{1,0:T(8,128)}, f32[1536,1024]{1,0:T(8,128)}, f32[1536,1024]{1,0:T(8,128)}, f32[1536,128]{1,0:T(8,128)S(1)}, f32[1024,1]{1,0:T(8,128)S(1)}) custom-call(bf16[512,1024]{1,0:T(8,128)(2,1)S(1)} %copy-done.10, bf16[1536,1024]{1,0:T(8,128)(2,1)} %get-tuple-element.46.k_ref, bf16[1536,1024]{1,0:T(8,128)(2,1)} %get-tuple-element.47.v_ref, ...), custom_call_target="tpu_custom_call" | custom-call | flops 40265318400 | bytes 31457280 | tf_op jit(solution)/shard_map/attn_bwd/pallas_call | solution.py:632
  396.3 51.2 %back.1 = (bf16[1552,2048]{1,0:T(8,128)(2,1)}, bf16[512,1024]{1,0:T(8,128)(2,1)}, bf16[16,1024]{1,0:T(8,128)(2,1)}, bf16[1536,128]{1,0:T(8,128)(2,1)}, bf16[1040...) custom-call(bf16[1552,1024]{1,0:T(8,128)(2,1)} %pad_maximum_fusion.2.x_ref, ...), custom_call_target="tpu_custom_call" | custom-call | flops 22548578304 | bytes 41943040 | tf_op jit(solution)/shard_map/back/pallas_call | solution.py:388
  447.5 3.2 fusion.55
  451.4 3.2 convolution_convert_fusion.4
  454.6 2.9 copy.100
  457.5 3.6 fusion.15
  463.9 12.5 %convolution_convert_fusion.3 = bf16[1024,2048]{1,0:T(8,128)(2,1)} fusion(bf16[1552,1024]{1,0:T(8,128)(2,1)} %get-tuple-element.50, bf16[1552,2048]{1,0:T(8,128)(2,1)} %get-tuple-element.67), kind=kOutput, calls=%fused_computation.26 | convolution fusion | flops 6511656960 | bytes 13729792 | tf_op jit(solution)/shard_map/dot_general | solution.py:1224
  476.4 2.4 pad_maximum_fusion.1
  478.8 6.5 copy.94
  485.3 7.9 %convolution_convert_fusion.2 = bf16[2816,1024]{1,0:T(8,128)(2,1)} fusion(bf16[512,2816]{1,0:T(8,128)(2,1)} %get-tuple-element.91, bf16[512,1024]{1,0:T(8,128)(2,1)} %copy-done.31), kind=kOutput, calls=%fused_computation.14 | convolution fusion | flops 2955673600 | bytes 9699328 | tf_op jit(solution)/shard_map/transpose(jvp())/dot_general | solution.py:730
  493.3 7.3 pad_maximum_fusion.refs_1_
  502.2 5.7 fusion.1
  507.9 186.6 %sum_over_devices.1 = (bf16[2,2,176,1024]{3,2,1,0:T(8,128)(2,1)}, bf16[2,2,64,5632]{3,2,1,0:T(8,128)(2,1)}, bf16[2,2,64,2048]{3,2,1,0:T(8,128)(2,1)}, bf16[2,2,64,3584]{3,2,1,0:T(8,128)(2,1)}) custom-call(bf16[4,2,2,176,1024]{4,3,2,1,0:T(8,128)(2,1)} %bitcast.115, bf16[4,2,2,64,5632]{4,3,2,1,0:T(8,128)(2,1)} %pad_maximum_fusion.refs_1_, ...), custom_call_target="tpu_custom_call" | custom-call | tf_op jit(solution)/shard_map/sum_over_devices/pallas_call | solution.py:1065
  694.5 2.5 bitcast_convert_fusion
  697.0 3.3 fusion.54
  704.4 2.0 bitcast_convert_fusion.2
  710.3 4.2 fusion.38
  715.5 1.9 slice.186
  719.0 17.8 %collective-permute-done.5 = bf16[16,1024]{1,0:T(8,128)(2,1)S(1)} collective-permute-done((bf16[16,1024]{1,0:T(8,128)(2,1)S(1)}, bf16[16,1024]{1,0:T(8,128)(2,1)S(1)}, u32[]{:S(2)}, u32[]{:S(2)}) %collective-permute-start.5) | collective-permute-done | bytes 32800 | tf_op jit(solution)/shard_map/ppermute | solution.py:647
  736.7 9.6 %collective-permute-done.4 = bf16[512,1024]{1,0:T(8,128)(2,1)} collective-permute-done((bf16[512,1024]{1,0:T(8,128)(2,1)}, bf16[512,1024]{1,0:T(8,128)(2,1)}, u32[]{:S(2)}, u32[]{:S(2)}) %collective-permute-start.4) | collective-permute-done | bytes 1048608 | tf_op jit(solution)/shard_map/ppermute | solution.py:647
  746.3 2.7 fusion.43
  (191 shorter events, 40.1 us)
Async XLA Ops:
  0.6 197.7 %collective-permute-start = (bf16[512,1024]{1,0:T(8,128)(2,1)}, bf16[512,1024]{1,0:T(8,128)(2,1)}, u32[]{:S(2)}, u32[]{:S(2)}) collective-permute-start(bf16[512,1024]{1,0:T(8,128)(2,1)} %bitcast.122), channel_id=1, source_target_pairs={{0,8},{4,12},{8,16},{12,20},{16,24},{20,28},{1,9},{5,13},{9,17},{1... | collective-permute-start | bytes 3145736 | tf_op jit(solution)/shard_map/ppermute | solution.py:647
  6.5 191.9 %collective-permute-start.1 = (bf16[512,1024]{1,0:T(8,128)(2,1)}, bf16[512,1024]{1,0:T(8,128)(2,1)}, u32[]{:S(2)}, u32[]{:S(2)}) collective-permute-start(bf16[512,1024]{1,0:T(8,128)(2,1)} %bitcast.123), channel_id=1, source_target_pairs={{0,4},{4,8},{8,12},{12,16},{16,20},{20,24},{24,28},{1,5},{5,9},{9,... | collective-permute-start | bytes 3145736 | tf_op jit(solution)/shard_map/ppermute | solution.py:647
  9.7 188.6 %collective-permute-start.2 = (bf16[16,1024]{1,0:T(8,128)(2,1)S(1)}, bf16[16,1024]{1,0:T(8,128)(2,1)S(1)}, u32[]{:S(2)}, u32[]{:S(2)}) collective-permute-start(bf16[16,1024]{1,0:T(8,128)(2,1)S(1)} %slice_bitcast_fusion), channel_id=1, source_target_pairs={{0,12},{4,16},{8,20},{12,24},{16,28},{1,13},{5,17},{9,21},{13,25},... | collective-permute-start | bytes 98312 | tf_op jit(solution)/shard_map/ppermute | solution.py:647
  75.8 3.0 copy-start.1
  76.1 109.3 %copy-start.31 = (bf16[512,1024]{1,0:T(8,128)(2,1)}, bf16[512,1024]{1,0:T(8,128)(2,1)S(1)}, u32[]{:S(2)}) copy-start(bf16[512,1024]{1,0:T(8,128)(2,1)S(1)} %fusion.26) | copy-start | bytes 3145732
  194.1 7.4 copy-start.4
  194.7 3.7 copy-start.27
  194.8 6.7 copy-start.2
  195.1 6.4 copy-start.3
  201.5 25.2 %copy-start = (bf16[1536,512]{1,0:T(8,128)(2,1)S(1)}, bf16[1536,512]{1,0:T(8,128)(2,1)}, u32[]{:S(2)}) copy-start(bf16[1536,512]{1,0:T(8,128)(2,1)} %fusion.20.mask_ref) | copy-start | bytes 4718596
  226.6 31.2 %copy-start.5 = (bf16[512,1024]{1,0:T(8,128)(2,1)}, bf16[512,1024]{1,0:T(8,128)(2,1)S(1)}, u32[]{:S(2)}) copy-start(bf16[512,1024]{1,0:T(8,128)(2,1)S(1)} %get-tuple-element.55.qin_ref.qprev_ref) | copy-start | bytes 3145732
  226.6 31.2 %copy-start.6 = (f32[1536,128]{1,0:T(8,128)}, f32[1536,128]{1,0:T(8,128)S(1)}, u32[]{:S(2)}) copy-start(f32[1536,128]{1,0:T(8,128)S(1)} %get-tuple-element.48.beta_ref) | copy-start | bytes 2359300
  226.6 31.2 %copy-start.9 = (bf16[512,1024]{1,0:T(8,128)(2,1)}, bf16[512,1024]{1,0:T(8,128)(2,1)S(1)}, u32[]{:S(2)}) copy-start(bf16[512,1024]{1,0:T(8,128)(2,1)S(1)} %get-tuple-element.45.q_ref) | copy-start | bytes 3145732
  226.7 31.2 %copy-start.11 = (bf16[16,1024]{1,0:T(8,128)(2,1)}, bf16[16,1024]{1,0:T(8,128)(2,1)S(1)}, u32[]{:S(2)}) copy-start(bf16[16,1024]{1,0:T(8,128)(2,1)S(1)} %get-tuple-element.56.qpre_ref) | copy-start | bytes 98308
  263.0 4.5 copy-start.12
  263.0 4.5 copy-start.28
  263.0 4.5 copy-start.33
  263.0 6.2 slice-start.4
  263.0 8.1 %slice-start.5 = ((s8[11534336]{0:T(1024)(128)(4,1)}), s8[4194304]{0:T(1024)(128)(4,1)S(1)}, s32[]{:S(2)}) async-start(s8[11534336]{0:T(1024)(128)(4,1)} %bitcast.135), calls=%async_computation.5 | async-start | bytes 8388608
  267.5 48.3 %copy-start.14 = (f32[512,1024]{1,0:T(8,128)}, f32[512,1024]{1,0:T(8,128)S(1)}, u32[]{:S(2)}) copy-start(f32[512,1024]{1,0:T(8,128)S(1)} %get-tuple-element.106) | copy-start | bytes 6291460
  267.5 4.7 slice-start.6
  268.9 30.9 %copy-start.16 = (f32[512,1024]{1,0:T(8,128)}, f32[512,1024]{1,0:T(8,128)S(1)}, u32[]{:S(2)}) copy-start(f32[512,1024]{1,0:T(8,128)S(1)} %get-tuple-element.108) | copy-start | bytes 6291460
  268.9 8.3 %slice-start.9 = ((s8[5767168]{0:T(1024)(128)(4,1)}), s8[4194304]{0:T(1024)(128)(4,1)S(1)}, s32[]{:S(2)}) async-start(s8[5767168]{0:T(1024)(128)(4,1)} %bitcast.142), calls=%async_computation.9 | async-start | bytes 8388608
  272.3 5.0 slice-start.10
  293.9 6.0 copy-start.19
  303.1 12.7 %copy-start.15 = (f32[512,1024]{1,0:T(8,128)}, f32[512,1024]{1,0:T(8,128)S(1)}, u32[]{:S(2)}) copy-start(f32[512,1024]{1,0:T(8,128)S(1)} %fusion.28) | copy-start | bytes 6291460
  305.8 5.0 copy-start.41
  322.5 4.0 copy-start.38
  447.5 3.9 copy-start.42
  447.5 3.9 copy-start.43
  457.5 3.7 copy-start.36
  457.5 4.3 copy-start.37
  463.9 12.5 %copy-start.21 = (bf16[1024,1024]{0,1:T(8,128)(2,1)S(1)}, bf16[1024,1024]{0,1:T(8,128)(2,1)}, u32[]{:S(2)}) copy-start(bf16[1024,1024]{0,1:T(8,128)(2,1)} %convolution_convert_fusion.5) | copy-start | bytes 6291460
  463.9 12.5 %copy-start.22 = (bf16[1024,1024]{0,1:T(8,128)(2,1)S(1)}, bf16[1024,1024]{0,1:T(8,128)(2,1)}, u32[]{:S(2)}) copy-start(bf16[1024,1024]{0,1:T(8,128)(2,1)} %convolution_convert_fusion.6) | copy-start | bytes 6291460
  485.3 8.0 %slice-start = ((s8[5767168]{0:T(1024)(128)(4,1)}), s8[4194304]{0:T(1024)(128)(4,1)S(1)}, s32[]{:S(2)}) async-start(s8[5767168]{0:T(1024)(128)(4,1)} %bitcast.116), calls=%async_computation | async-start | bytes 8388608
  485.3 8.0 %slice-start.2 = ((s8[5767168]{0:T(1024)(128)(4,1)}), s8[4194304]{0:T(1024)(128)(4,1)S(1)}, s32[]{:S(2)}) async-start(s8[5767168]{0:T(1024)(128)(4,1)} %bitcast.119), calls=%async_computation.2 | async-start | bytes 8388608
  485.3 8.0 %slice-start.1 = ((s8[5767168]{0:T(1024)(128)(4,1)}), s8[1572864]{0:T(1024)(128)(4,1)S(1)}, s32[]{:S(2)}) async-start(s8[5767168]{0:T(1024)(128)(4,1)} %bitcast.116), calls=%async_computation.1 | async-start | bytes 3145728
  485.3 8.0 %slice-start.3 = ((s8[5767168]{0:T(1024)(128)(4,1)}), s8[1572864]{0:T(1024)(128)(4,1)S(1)}, s32[]{:S(2)}) async-start(s8[5767168]{0:T(1024)(128)(4,1)} %bitcast.119), calls=%async_computation.3 | async-start | bytes 3145728
  493.3 7.3 copy-start.32
  697.0 3.4 copy-start.23
  697.0 13.3 %slice-start.7 = ((s8[5767168]{0:T(1024)(128)(4,1)}), s8[4194304]{0:T(1024)(128)(4,1)S(1)}, s32[]{:S(2)}) async-start(s8[5767168]{0:T(1024)(128)(4,1)} %bitcast.139), calls=%async_computation.7 | async-start | bytes 8388608
  700.3 10.0 %slice-start.8 = ((s8[5767168]{0:T(1024)(128)(4,1)}), s8[1572864]{0:T(1024)(128)(4,1)S(1)}, s32[]{:S(2)}) async-start(s8[5767168]{0:T(1024)(128)(4,1)} %bitcast.139), calls=%async_computation.8 | async-start | bytes 3145728
  702.4 8.0 %copy-start.40 = (bf16[512,2816]{1,0:T(8,128)(2,1)S(1)}, bf16[512,2816]{1,0:T(8,128)(2,1)}, u32[]{:S(2)}) copy-start(bf16[512,2816]{1,0:T(8,128)(2,1)} %get-tuple-element.91) | copy-start | bytes 8650756
  703.8 6.5 copy-start.17
  706.4 30.3 %collective-permute-start.3 = (bf16[512,1024]{1,0:T(8,128)(2,1)}, bf16[512,1024]{1,0:T(8,128)(2,1)S(1)}, u32[]{:S(2)}, u32[]{:S(2)}) collective-permute-start(bf16[512,1024]{1,0:T(8,128)(2,1)} %get-tuple-element.97), channel_id=1, source_target_pairs={{4,0},{8,4},{12,8},{16,12},{20,16},{24,20},{28,24},{5,1},{9,5},{13... | collective-permute-start | bytes 3145736 | tf_op jit(solution)/shard_map/ppermute | solution.py:647
  707.7 38.6 %collective-permute-start.4 = (bf16[512,1024]{1,0:T(8,128)(2,1)}, bf16[512,1024]{1,0:T(8,128)(2,1)}, u32[]{:S(2)}, u32[]{:S(2)}) collective-permute-start(bf16[512,1024]{1,0:T(8,128)(2,1)} %get-tuple-element.98), channel_id=1, source_target_pairs={{8,0},{12,4},{16,8},{20,12},{24,16},{28,20},{9,1},{13,5},{17,9},{2... | collective-permute-start | bytes 3145736 | tf_op jit(solution)/shard_map/ppermute | solution.py:647
  709.0 27.7 %collective-permute-start.5 = (bf16[16,1024]{1,0:T(8,128)(2,1)S(1)}, bf16[16,1024]{1,0:T(8,128)(2,1)S(1)}, u32[]{:S(2)}, u32[]{:S(2)}) collective-permute-start(bf16[16,1024]{1,0:T(8,128)(2,1)S(1)} %slice.150), channel_id=1, source_target_pairs={{12,0},{16,4},{20,8},{24,12},{28,16},{13,1},{17,5},{21,9},{25,13},... | collective-permute-start | bytes 98312 | tf_op jit(solution)/shard_map/ppermute | solution.py:647
  715.5 30.8 %copy-start.20 = (f32[512,1024]{1,0:T(8,128)S(1)}, f32[512,1024]{1,0:T(8,128)}, u32[]{:S(2)}) copy-start(f32[512,1024]{1,0:T(8,128)} %get-tuple-element.63) | copy-start | bytes 6291460
  (13 other events, 28.4 us)

commit v4 on v2

--- a/solution.py
+++ b/solution.py
@@ -13,6 +13,8 @@
 WINDOW = 1024
 PRE = 16
 SMALL = 128
+EXTRA = 512
+MESH = pl.DeviceIdType.MESH
 f32 = jnp.float32
 bf16 = jnp.bfloat16
 QB = 256
@@ -74,21 +76,25 @@
 ):
     step = pl.program_id(0)
     gain = gain_ref[...]
+    main_rows = k_ref.shape[0]
+    before_at = pl.ds(main_rows, PRE)
+    rows_at = pl.ds(pl.multiple_of(jnp.maximum(step - 1, 0) * ROWS, ROWS), ROWS)
+    own_at = pl.ds(pl.multiple_of(jnp.maximum(step - 1 - first_own, 0) * ROWS, ROWS), ROWS)
     kv_slots = 2 * D // CH
 
     @pl.when(step == 0)
     def before():
-        hidden = row_norm(x_ref[0:PRE].astype(f32), gain)
-        hid_ref[0:PRE] = hidden
+        hidden = row_norm(x_ref[before_at].astype(f32), gain)
+        hid_ref[before_at] = hidden
         for slot in range(kv_slots):
             rows = mm(hidden, w_ref[:, D + CH * slot : D + CH * (slot + 1)]).astype(bf16)
-            kvin_ref[0:PRE, CH * slot : CH * (slot + 1)] = rows
+            kvin_ref[before_at, CH * slot : CH * (slot + 1)] = rows
             ext_ref[slot, ROWS : ROWS + 8, :] = rows.astype(f32)[PRE - 8 :]
 
-    def through(slot, hidden, same, column, in_ref, at):
+    def through(slot, hidden, same, column, in_ref, in_rows, at):
         ext_ref[slot, 0:8, :] = ext_ref[slot, ROWS : ROWS + 8, :]
         rows = mm(hidden, w_ref[:, column : column + CH]).astype(bf16)
-        in_ref[:, at : at + CH] = rows
+        in_ref[in_rows, at : at + CH] = rows
         ext_ref[slot, 8 : 8 + ROWS, :] = rows.astype(f32)
         total = conv_total(ext_ref, slot, same, taps_ref[:, column : column + CH])
         return total * jax.nn.sigmoid(total)
@@ -98,19 +104,19 @@
 
     @pl.when(step > 0)
     def main():
-        same = [same_ref[:, tap : tap + 1] for tap in range(TAPS)]
-        hidden = row_norm(x_ref[...].astype(f32), gain)
-        hid_ref[...] = hidden
+        same = [same_ref[rows_at, tap : tap + 1] for tap in range(TAPS)]
+        hidden = row_norm(x_ref[rows_at].astype(f32), gain)
+        hid_ref[rows_at] = hidden
         for slot in range(kv_slots):
             at = CH * slot
-            active = through(slot, hidden, same, D + at, kvin_ref, at)
+            active = through(slot, hidden, same, D + at, kvin_ref, rows_at, at)
             if at < D:
-                k_ref[:, at : at + CH] = unit(active)
+                k_ref[rows_at, at : at + CH] = unit(active)
             else:
-                v_ref[:, at - D : at - D + CH] = active.astype(bf16)
+                v_ref[rows_at, at - D : at - D + CH] = active.astype(bf16)
         gates = jax.nn.sigmoid(mm(hidden, w_ref[:, 3 * D : 3 * D + SMALL])).astype(bf16)
         lane = lax.broadcasted_iota(jnp.int32, (ROWS, SMALL), 1)
-        beta_ref[...] = jnp.where(lane < HEADS, gates.astype(f32), 0.0)
+        beta_ref[rows_at] = jnp.where(lane < HEADS, gates.astype(f32), 0.0)
 
         @pl.when(step == first_own + 1)
         def own_history():
@@ -125,73 +131,49 @@
         def own():
             for slot in range(D // CH):
                 at = CH * slot
-                active = through(kv_slots + slot, hidden, same, at, qin_ref, at)
-                q_ref[:, at : at + CH] = unit(active)
+                active = through(kv_slots + slot, hidden, same, at, qin_ref, own_at, at)
+                q_ref[own_at, at : at + CH] = unit(active)
 
         tail_ref[...] = hidden[ROWS - PRE :]
 
 
-def front(ext_tokens, same, gain, w_front, taps, own_rows):
+def front(ext_tokens, same, gain, w_front, taps, own_rows, **riding):
     ext_rows = ext_tokens.shape[0]
     main_rows = ext_rows - PRE
     blocks = main_rows // ROWS
     first_own = (main_rows - own_rows) // ROWS
 
-    def ext_block(step):
-        return (jnp.where(step == 0, blocks, step - 1), 0)
-
-    def main_block(step):
-        return (jnp.maximum(step - 1, 0), 0)
-
-    def own_block(step):
-        return (jnp.maximum(step - 1 - first_own, 0), 0)
-
     def fixed(array):
-        return pl.BlockSpec(array.shape, lambda step: (0, 0))
+        return pl.BlockSpec(array.shape, lambda step: (0, 0), pipeline_mode=pl.Buffered(1))
 
     shape = jax.ShapeDtypeStruct
-    return pl.pallas_call(
+    outs = [
+        shape((ext_rows, D), bf16),
+        shape((ext_rows, 2 * D), bf16),
+        shape((own_rows, D), bf16),
+        shape((PRE, D), bf16),
+        shape((own_rows, D), bf16),
+        shape((main_rows, D), bf16),
+        shape((main_rows, D), bf16),
+        shape((main_rows, SMALL), f32),
+    ]
+    return call(
         functools.partial(front_kernel, first_own),
-        grid=(blocks + 1,),
-        in_specs=[
-            pl.BlockSpec((ROWS, D), ext_block),
-            pl.BlockSpec((ROWS, TAPS), main_block),
-            fixed(gain),
-            fixed(w_front),
-            fixed(taps),
-        ],
-        out_specs=[
-            pl.BlockSpec((ROWS, D), ext_block),
-            pl.BlockSpec((ROWS, 2 * D), ext_block),
-            pl.BlockSpec((ROWS, D), own_block),
-            pl.BlockSpec((PRE, D), lambda step: (0, 0)),
-            pl.BlockSpec((ROWS, D), own_block),
-            pl.BlockSpec((ROWS, D), main_block),
-            pl.BlockSpec((ROWS, D), main_block),
-            pl.BlockSpec((ROWS, SMALL), main_block),
-        ],
-        out_shape=[
-            shape((ext_rows, D), bf16),
-            shape((ext_rows, 2 * D), bf16),
-            shape((own_rows, D), bf16),
-            shape((PRE, D), bf16),
-            shape((own_rows, D), bf16),
-            shape((main_rows, D), bf16),
-            shape((main_rows, D), bf16),
-            shape((main_rows, SMALL), f32),
-        ],
-        scratch_shapes=[
+        blocks + 1,
+        (ext_tokens, same, gain, w_front, taps),
+        [fixed(array) for array in (ext_tokens, same, gain, w_front, taps)],
+        [fixed(array) for array in outs],
+        outs,
+        [
             pltpu.VMEM((3 * D // CH, 8 + ROWS, CH), f32),
             pltpu.VMEM((PRE, D), bf16),
         ],
-        compiler_params=pltpu.CompilerParams(
-            dimension_semantics=("arbitrary",), vmem_limit_bytes=50 << 20
-        ),
-        cost_estimate=pl.CostEstimate(
-            flops=4 * (main_rows * 2 + own_rows) * D * D, bytes_accessed=30 << 20, transcendentals=0
-        ),
+        vmem=50,
+        flops=4 * (main_rows * 2 + own_rows) * D * D,
+        traffic=30 << 20,
         name="front",
-    )(ext_tokens, same, gain, w_front, taps)
+        **riding,
+    )
 
 
 def back_kernel(
@@ -246,9 +228,9 @@
         return scale * (scaled - normal * jnp.mean(scaled * normal, axis=-1, keepdims=True))
 
     def shifted(slot, start, count):
-        total = buf_ref[slot, 1, start + 1 : start + 1 + count, :]
+        total = buf_ref[slot, 0, start + 1 : start + 1 + count, :]
         for tap in range(2, TAPS):
-            total = total + buf_ref[slot, tap, start + tap : start + tap + count, :]
+            total = total + buf_ref[slot, tap - 1, start + tap : start + tap + count, :]
         return total
 
     def through(slot, column, history, rows, grad, unit, same):
@@ -278,15 +260,15 @@
             dtaps_ref[tap : tap + 1, column : column + CH] += jnp.sum(
                 held * ext_ref[slot, 8 - tap : 8 - tap + ROWS, :], axis=0, keepdims=True
             )
-            buf_ref[slot, tap, 0:ROWS, :] = held * taps[tap : tap + 1]
+            buf_ref[slot, tap - 1, 0:ROWS, :] = held * taps[tap : tap + 1]
         result = (result + shifted(slot, 0, ROWS)).astype(bf16)
         for tap in range(1, TAPS):
-            buf_ref[slot, tap, ROWS : ROWS + 8, :] = buf_ref[slot, tap, 0:8, :]
+            buf_ref[slot, tap - 1, ROWS : ROWS + 8, :] = buf_ref[slot, tap - 1, 0:8, :]
         return result
 
     def before_rows(slot):
         for tap in range(1, TAPS):
-            buf_ref[slot, tap, ROWS - PRE : ROWS, :] = jnp.zeros((PRE, CH), f32)
+            buf_ref[slot, tap - 1, ROWS - PRE : ROWS, :] = jnp.zeros((PRE, CH), f32)
         return shifted(slot, ROWS - PRE, PRE).astype(bf16)
 
     @pl.when(step < blocks)
@@ -350,7 +332,7 @@
 
 
 def back(
-    ext_tokens, kvin, same, qin, qpre, dk, dv, dq, beta, dbeta, dgate, dres, gain, w_front, w_og, taps
+    ext_tokens, kvin, same, qin, qpre, dk, dv, dq, beta, dbeta, dgate, dres, gain, w_front, w_og, taps, **riding
 ):
     ext_rows = ext_tokens.shape[0]
     main_rows = ext_rows - PRE
@@ -380,13 +362,33 @@
         return (jnp.where(step == blocks, first_own, block), 0)
 
     def fixed(array):
-        return pl.BlockSpec(array.shape, lambda step: (0, 0))
+        return pl.BlockSpec(array.shape, lambda step: (0, 0), pipeline_mode=pl.Buffered(1))
 
     shape = jax.ShapeDtypeStruct
-    return pl.pallas_call(
+    return call(
         functools.partial(back_kernel, blocks, first_own),
-        grid=(blocks + 1,),
-        in_specs=[
+        blocks + 1,
+        (
+            ext_tokens,
+            kvin,
+            kvin,
+            same,
+            qin,
+            qin,
+            qpre,
+            dk,
+            dv,
+            dq,
+            beta,
+            dbeta,
+            dgate,
+            dres,
+            gain,
+            w_front,
+            w_og,
+            taps,
+        ),
+        [
             pl.BlockSpec((ROWS, D), ext_block),
             pl.BlockSpec((ROWS, 2 * D), ext_block),
             pl.BlockSpec((PRE, 2 * D), prev_block),
@@ -406,7 +408,7 @@
             fixed(w_og),
             fixed(taps),
         ],
-        out_specs=[
+        [
             pl.BlockSpec((ROWS, 2 * D), ext_block),
             pl.BlockSpec((ROWS, D), own_block),
             pl.BlockSpec((PRE, D), lambda step: (0, 0)),
@@ -416,7 +418,7 @@
             pl.BlockSpec((1, D), lambda step: (0, 0)),
             pl.BlockSpec((TAPS, 3 * D), lambda step: (0, 0)),
         ],
-        out_shape=[
+        [
             shape((ext_rows, 2 * D), bf16),
             shape((own_rows, D), bf16),
             shape((PRE, D), bf16),
@@ -426,37 +428,16 @@
             shape((1, D), f32),
             shape((TAPS, 3 * D), f32),
         ],
-        scratch_shapes=[
+        [
             pltpu.VMEM((3 * D // CH, 8 + ROWS, CH), f32),
-            pltpu.VMEM((3 * D // CH, TAPS, ROWS + 8, CH), f32),
+            pltpu.VMEM((3 * D // CH, TAPS - 1, ROWS + 8, CH), f32),
             pltpu.VMEM((ROWS, D), f32),
         ],
-        compiler_params=pltpu.CompilerParams(
-            dimension_semantics=("arbitrary",), vmem_limit_bytes=56 << 20
-        ),
-        cost_estimate=pl.CostEstimate(
-            flops=6 * (main_rows * 2 + own_rows) * D * D, bytes_accessed=40 << 20, transcendentals=0
-        ),
+        vmem=62,
+        flops=6 * (main_rows * 2 + own_rows) * D * D,
+        traffic=40 << 20,
         name="back",
-    )(
-        ext_tokens,
-        kvin,
-        kvin,
-        same,
-        qin,
-        qin,
-        qpre,
-        dk,
-        dv,
-        dq,
-        beta,
-        dbeta,
-        dgate,
-        dres,
-        gain,
-        w_front,
-        w_og,
-        taps,
+        **riding,
     )
 
 
@@ -509,22 +490,26 @@
     for b in blocks:
         o_ref[QB*b:QB*(b+1),:]=apply(b,x2[b],vt_ref).T
 
-def attn_fwd(q,k,v,beta,mask_t,ridge):
+def attn_fwd(q,k,v,beta,mask_t,ridge,**riding):
     rows=q.shape[0]; keys=k.shape[0]
     head=lambda n: pl.BlockSpec((n,HEAD_DIM),lambda h:(0,h))
     heads_t=pl.BlockSpec((HEAD_DIM,rows),lambda h:(h,0))
     fixed=lambda a: pl.BlockSpec(a.shape,lambda h:(0,0))
     flops=6*2*rows*(WINDOW+QB)*D
-    return pl.pallas_call(
-        attn_fwd_kernel, grid=(HEADS,),
-        in_specs=[head(rows),head(keys),head(keys),fixed(beta),fixed(mask_t),pl.BlockSpec((HEAD_DIM,1),lambda h:(h,0))],
-        out_specs=[head(rows),heads_t,heads_t],
-        out_shape=[jax.ShapeDtypeStruct((rows,D),f32)]+[jax.ShapeDtypeStruct((D,rows),f32)]*2,
-        scratch_shapes=[pltpu.VMEM((HEAD_DIM,keys),bf16)]*2+[pltpu.VMEM((rows//QB,WINDOW+QB,QB),f32)],
-        compiler_params=pltpu.CompilerParams(dimension_semantics=("arbitrary",),vmem_limit_bytes=48<<20),
-        cost_estimate=pl.CostEstimate(flops=2*flops,bytes_accessed=20<<20,transcendentals=0),
+    return call(
+        attn_fwd_kernel,
+        HEADS,
+        (q, k, v, beta, mask_t, ridge),
+        [head(rows), head(keys), head(keys), fixed(beta), fixed(mask_t), pl.BlockSpec((HEAD_DIM, 1), lambda h: (h, 0))],
+        [head(rows), heads_t, heads_t],
+        [jax.ShapeDtypeStruct((rows, D), f32)] + [jax.ShapeDtypeStruct((D, rows), f32)] * 2,
+        [pltpu.VMEM((HEAD_DIM, keys), bf16)] * 2 + [pltpu.VMEM((rows // QB, WINDOW + QB, QB), f32)],
+        flops=2 * flops,
+        traffic=20 << 20,
         name="attn_fwd",
-    )(q,k,v,beta,mask_t,ridge)
+        **riding,
+    )
+
 
 def attn_bwd_kernel(q_ref,k_ref,v_ref,beta_ref,mask_ref,ridge_ref,a0_ref,a1_ref,do_ref,dq_ref,dk_ref,dv_ref,dbeta_ref,dridge_ref,kt_ref,w_ref,acc_ref):
     h=pl.program_id(0)
@@ -620,29 +605,36 @@
         dbeta_ref[...]=jnp.zeros_like(dbeta_ref)
     dbeta_ref[...]=jnp.where(lane==h,found,dbeta_ref[...])
 
-def attn_bwd(q,k,v,beta,mask_t,ridge,a0,a1,do):
+def attn_bwd(q,k,v,beta,mask_t,ridge,a0,a1,do,**riding):
     rows=q.shape[0]; keys=k.shape[0]
     head=lambda n: pl.BlockSpec((n,HEAD_DIM),lambda h:(0,h))
     heads_t=pl.BlockSpec((HEAD_DIM,rows),lambda h:(h,0))
     fixed=lambda a: pl.BlockSpec(a.shape,lambda h:(0,0))
     rd=pl.BlockSpec((HEAD_DIM,1),lambda h:(h,0))
     flops=15*2*rows*(WINDOW+QB)*D
-    return pl.pallas_call(
-        attn_bwd_kernel, grid=(HEADS,),
-        in_specs=[head(rows),head(keys),head(keys),fixed(beta),fixed(mask_t),rd,heads_t,heads_t,head(rows)],
-        out_specs=[head(rows),head(keys),head(keys),fixed(beta),rd],
-        out_shape=[jax.ShapeDtypeStruct((rows,D),f32),jax.ShapeDtypeStruct((keys,D),f32),jax.ShapeDtypeStruct((keys,D),f32),jax.ShapeDtypeStruct(beta.shape,f32),jax.ShapeDtypeStruct((D,1),f32)],
-        scratch_shapes=[pltpu.VMEM((HEAD_DIM,keys),bf16),pltpu.VMEM((rows//QB,WINDOW+QB,QB),f32),pltpu.VMEM((keys,128),f32)],
-        compiler_params=pltpu.CompilerParams(dimension_semantics=("arbitrary",),vmem_limit_bytes=48<<20),
-        cost_estimate=pl.CostEstimate(flops=2*flops,bytes_accessed=30<<20,transcendentals=0),
+    return call(
+        attn_bwd_kernel,
+        HEADS,
+        (q, k, v, beta, mask_t, ridge, a0, a1, do),
+        [head(rows), head(keys), head(keys), fixed(beta), fixed(mask_t), rd, heads_t, heads_t, head(rows)],
+        [head(rows), head(keys), head(keys), fixed(beta), rd],
+        [
+            jax.ShapeDtypeStruct((rows, D), f32),
+            jax.ShapeDtypeStruct((keys, D), f32),
+            jax.ShapeDtypeStruct((keys, D), f32),
+            jax.ShapeDtypeStruct(beta.shape, f32),
+            jax.ShapeDtypeStruct((D, 1), f32),
+        ],
+        [
+            pltpu.VMEM((HEAD_DIM, keys), bf16),
+            pltpu.VMEM((rows // QB, WINDOW + QB, QB), f32),
+            pltpu.VMEM((keys, 128), f32),
+        ],
+        flops=2 * flops,
+        traffic=30 << 20,
         name="attn_bwd",
-    )(q,k,v,beta,mask_t,ridge,a0,a1,do)
-
-
-def passed_along(value, axis, steps):
-    count = lax.axis_size(axis)
-    initial, last = (max(0, -steps), min(count, count - steps))
-    return lax.ppermute(value, axis, [(source, source + steps) for source in range(initial, last)])
+        **riding,
+    )
 
 
 def token_layout(slot_row, live_row, positions):
@@ -730,116 +722,521 @@
     return section_out
 
 
-def bit_of(rank, bit):
-    return lax.rem(lax.div(rank, 1 << bit), 2)
-
-
-def swap_bit(value, bit):
+class Here:
+    def __init__(self):
+        self.rank = lax.axis_index("seq")
+        self.ranks = lax.axis_size("seq")
+        self.place = lax.axis_index("wshard")
+        self.shards = lax.axis_size("wshard")
+        self.core = self.rank % 2
+        self.x = (self.rank // 2) % 2
+        self.y = (self.rank // 4) % 2
+        self.core_next = self.rank + 1 - 2 * self.core
+        self.x_next = self.rank + 2 - 4 * self.x
+        self.y_next = self.rank + 4 - 8 * self.y
+
+    def other(self, step):
+        return (self.place + step) % self.shards
+
+    def along(self, step):
+        return (self.rank + step + self.ranks) % self.ranks
+
+    def meet(self, reach):
+        barrier = pltpu.get_barrier_semaphore()
+        near = [self.core_next, self.x_next, self.y_next]
+        for step in range(1, reach + 1):
+            near += [self.along(step), self.along(-step)]
+        for device in near:
+            pl.semaphore_signal(barrier, inc=1, device_id={"seq": device}, device_id_type=MESH)
+        for step in range(1, self.shards):
+            pl.semaphore_signal(
+                barrier, inc=1, device_id={"wshard": self.other(step)}, device_id_type=MESH
+            )
+        pl.semaphore_wait(barrier, len(near) + self.shards - 1)
+
+
+def span(start, size):
+    return pl.ds(pl.multiple_of(start, 128), size)
+
+
+class Rider:
+    reach = 0
+    first, last = 0, 0
+    inputs, outputs, scratch, aliases = (), (), (), ()
+
+    def bind(self, here, inputs, outputs, scratch):
+        self.here = here
+        self.inputs_, self.outputs_ = inputs, outputs
+        self.send_sems, self.recv_sems, self.local_sems = scratch[:3]
+        self.held = scratch[3:]
+
+    def semaphores(self):
+        return [
+            pltpu.SemaphoreType.DMA((self.remote_count,)),
+            pltpu.SemaphoreType.DMA((self.remote_count,)),
+            pltpu.SemaphoreType.DMA((self.local_count,)),
+        ]
+
+    def send(self, index, source, target, **device):
+        return pltpu.make_async_remote_copy(
+            src_ref=source,
+            dst_ref=target,
+            send_sem=self.send_sems.at[index],
+            recv_sem=self.recv_sems.at[index],
+            device_id=device,
+            device_id_type=MESH,
+        )
+
+    def keep(self, index, source, target):
+        return pltpu.make_async_copy(source, target, self.local_sems.at[index])
+
+    def remote(self, phase):
+        return []
+
+    def local(self, phase):
+        return []
+
+    def work(self, phase):
+        pass
+
+    def run(self, phase):
+        if phase > self.first:
+            for copy in self.remote(phase - 1):
+                copy.wait_recv()
+            for copy in self.local(phase - 1):
+                copy.wait()
+        if phase <= self.last:
+            self.work(phase)
+            for copy in self.remote(phase) + self.local(phase):
+                copy.start()
+
+    def finish(self):
+        for phase in range(self.first, self.last + 1):
+            for copy in self.remote(phase):
+                copy.wait_send()
+
+
+class Gather(Rider):
+    remote_count, local_count = 18, 2
+
+    def __init__(self, shard, first=0, last=3, begun=None):
+        self.first, self.last = first, last
+        if begun is None:
+            split = shard.reshape(2, 2, shard.shape[0] // 4, shard.shape[1])
+            places = lax.axis_size("wshard")
+            self.inputs = (split,)
+            self.outputs = (jax.ShapeDtypeStruct((places,) + split.shape, shard.dtype),)
+            self.scratch = (pltpu.VMEM(split.shape, shard.dtype),)
+        else:
+            self.inputs = (begun,)
+            self.outputs = (jax.ShapeDtypeStruct(begun.shape, begun.dtype),)
+            self.aliases = ((0, 0),)
+
+    def work(self, phase):
+        if phase == 0:
+            copy = self.keep(1, self.inputs_[0], self.held[0])
+            copy.start()
+            copy.wait()
+
+    def local(self, phase):
+        if phase:
+            return []
+        return [self.keep(0, self.held[0], self.outputs_[0].at[self.here.place])]
+
+    def remote(self, phase):
+        here, (target,) = self.here, self.outputs_
+        half = target.shape[-1] // 2
+        quarter = half // 2
+        mine = span(here.core * half, half)
+        one = span(here.core * half, quarter)
+        two = span(here.core * half + quarter, quarter)
+        y, x = here.y, here.x
+        if phase == 0:
+            return [
+                self.send(
+                    step - 1,
+                    self.inputs_[0].at[y, x, :, mine],
+                    target.at[here.place, y, x, :, mine],
+                    wshard=here.other(step),
+                )
+                for step in range(1, here.shards)
+            ]
+        found = []
+        for step in range(1, here.shards):
+            at = target.at[here.other(step)]
+            if phase == 1:
+                found.append((at.at[y, x, :, one], here.x_next))
+                found.append((at.at[y, x, :, two], here.y_next))
+            elif phase == 2:
+                found.append((at.at[y, :, :, one], here.y_next))
+                found.append((at.at[:, x, :, two], here.x_next))
+            else:
+                found.append((at.at[:, :, :, mine], here.core_next))
+        start = {1: 3, 2: 9, 3: 15}[phase]
+        return [
+            self.send(start + index, ref, ref, seq=near) for index, (ref, near) in enumerate(found)
+        ]
+
+
+class WindowTokens(Rider):
+    last = 1
+    remote_count, local_count = 0, 2
+
+    def __init__(self, tokens, depth):
+        self.depth = depth
+        self.reach = depth + 1
+        self.remote_count = depth + 1
+        self.rows = tokens.shape[0]
+        self.inputs = (tokens,)
+        rows = self.rows * (depth + 1) + PRE
+        self.outputs = (jax.ShapeDtypeStruct((rows, tokens.shape[1]), tokens.dtype),)
+        self.scratch = (pltpu.VMEM(tokens.shape, tokens.dtype),)
+
+    def work(self, phase):
+        if phase == 0:
+            copy = self.keep(1, self.inputs_[0], self.held[0])
+            copy.start()
+            copy.wait()
+
+    def local(self, phase):
+        rows = pl.ds(self.depth * self.rows, self.rows)
+        return [self.keep(0, self.held[0], self.outputs_[0].at[rows])] if phase == 0 else []
+
+    def remote(self, phase):
+        here, rows, depth = self.here, self.rows, self.depth
+        (own,), (ext,) = self.inputs_, self.outputs_
+        if phase == 1:
+            start = pl.multiple_of((1 - here.core) * depth * rows + here.core * (depth - 2) * rows, 16)
+            ref = ext.at[pl.ds((depth - 1) * rows, rows)]
+            return [self.send(0, ext.at[pl.ds(start, rows)], ref, seq=here.core_next)]
+        found = [
+            self.send(
+                hop - 1, own, ext.at[pl.ds((depth - hop) * rows, rows)], seq=here.along(hop)
+            )
+            for hop in range(2, depth + 1)
+        ]
+        found.append(
+            self.send(
+                depth,
+                own.at[pl.ds(rows - PRE, PRE)],
+                ext.at[pl.ds((depth + 1) * rows, PRE)],
+                seq=here.along(depth + 1),
+            )
+        )
+        return found
+
+
+class WindowGrads(Rider):
+    local_count = 1
+
+    def __init__(self, grads, rows, depth):
+        self.rows, self.depth = rows, depth
+        self.reach = depth + 1
+        self.remote_count = depth + 1
+        self.inputs = (grads,)
+        columns = grads.shape[1]
+        self.outputs = (
+            jax.ShapeDtypeStruct((depth, rows, columns), grads.dtype),
+            jax.ShapeDtypeStruct((PRE, columns), grads.dtype),
+        )
+
+    def remote(self, phase):
+        here, rows, depth = self.here, self.rows, self.depth
+        (grads,), (near, far) = self.inputs_, self.outputs_
+        found = [
+            self.send(
+                hop - 1,
+                grads.at[pl.ds((depth - hop) * rows, rows)],
+                near.at[hop - 1],
+                seq=here.along(-hop),
+            )
+            for hop in range(1, depth + 1)
+        ]
+        found.append(
+            self.send(
+                depth, grads.at[pl.ds(depth * rows, PRE)], far, seq=here.along(-depth - 1)
+            )
+        )
+        return found
+
+
+def add_into(target, at, value):
+    target[at] = (target[at].astype(f32) + value.astype(f32)).astype(bf16)
+
+
+class SumFar(Rider):
+    last = 3
+    remote_count, local_count = 5, 2
+
+    def __init__(self, grad, start=0, size=None):
+        places = lax.axis_size("wshard")
+        if grad.ndim == 2:
+            grad = grad.reshape(places, 2, 2, grad.shape[0] // places // 4, grad.shape[1])
+        size = grad.shape[3] if size is None else size
+        self.rows = pl.ds(start, size)
+        half = grad.shape[-1] // 2
+        quarter = half // 2
+        self.inputs = (grad,)
+        self.outputs = (jax.ShapeDtypeStruct((places, size, half), bf16),)
+        self.scratch = (
+            pltpu.VMEM((places, 2, 2, size, half), bf16),
+            pltpu.VMEM((places, 2, 2, size, half), bf16),
+            pltpu.VMEM((places, 2, size, quarter), bf16),
+            pltpu.VMEM((places, 2, size, quarter), bf16),
+            pltpu.VMEM((places, size, quarter), bf16),
+            pltpu.VMEM((places, size, quarter), bf16),
+        )
+        self.half = half
+
+    def local(self, phase):
+        here, held = self.here, self.held[0]
+        if phase == 0:
+            mine = span(here.core * self.half, self.half)
+            return [self.keep(0, self.inputs_[0].at[:, :, :, self.rows, mine], held)]
+        if phase == 3:
+            return [self.keep(1, held.at[:, here.y, here.x], self.outputs_[0])]
+        return []
+
+    def remote(self, phase):
+        here = self.here
+        y, x = here.y, here.x
+        held, core_in, far_a, far_b, next_a, next_b = self.held
+        one, two = pl.ds(0, self.half // 2), pl.ds(self.half // 2, self.half // 2)
+        if phase == 0:
+            yours = span((1 - here.core) * self.half, self.half)
+            ref = self.inputs_[0].at[:, :, :, self.rows, yours]
+            return [self.send(0, ref, core_in, seq=here.core_next)]
+        if phase == 1:
+            return [
+                self.send(1, held.at[:, :, 1 - x, :, one], far_a, seq=here.x_next),
+                self.send(2, held.at[:, 1 - y, :, :, two], far_b, seq=here.y_next),
+            ]
+        if phase == 2:
+            return [
+                self.send(3, held.at[:, 1 - y, x, :, one], next_a, seq=here.y_next),
+                self.send(4, held.at[:, y, 1 - x, :, two], next_b, seq=here.x_next),
+            ]
+        return []
+
+    def work(self, phase):
+        y, x = self.here.y, self.here.x
+        held, core_in, far_a, far_b, next_a, next_b = self.held
+        places = held.shape[0]
+        one, two = slice(0, self.half // 2), slice(self.half // 2, self.half)
+        every = slice(None)
+        if phase == 1:
+
+            def add(index, carry):
+                at = (index // 4, (index // 2) % 2, index % 2)
+                add_into(held, at, core_in[at])
+                return carry
+
+            lax.fori_loop(0, 4 * places, add, 0)
+        elif phase == 2:
+
+            def add(index, carry):
+                place, side = index // 2, index % 2
+                add_into(held, (place, side, x, every, one), far_a[place, side])
+                add_into(held, (place, y, side, every, two), far_b[place, side])
+                return carry
+
+            lax.fori_loop(0, 2 * places, add, 0)
+        elif phase == 3:
+
+            def add(place, carry):
+                add_into(held, (place, y, x, every, one), next_a[place])
+                add_into(held, (place, y, x, every, two), next_b[place])
+                return carry
+
+            lax.fori_loop(0, places, add, 0)
+
+
+class SumNear(Rider):
+    last = 3
+    local_count = 2
+
+    def __init__(self, sums=None, after=None):
+        self.after = after
+        places, size, half = (sums if after is None else after.outputs[0]).shape
+        self.remote_count = places - 1 + 5
+        self.half = half
+        self.inputs = (sums,) if after is None else ()
+        self.outputs = (jax.ShapeDtypeStruct((2, 2, size, 2 * half), bf16),)
+        self.scratch = (pltpu.VMEM((places, size, half), bf16), pltpu.VMEM((size, half), bf16))
+
+    def bind(self, here, inputs, outputs, scratch):
+        super().bind(here, inputs, outputs, scratch)
+        if self.after is not None:
+            self.inputs_ = self.after.outputs_
+
+    def local(self, phase):
+        here = self.here
+        arrived, total = self.held
+        if phase == 0:
+            return [self.keep(0, self.inputs_[0].at[here.place], arrived.at[0])]
+        if phase == 1:
+            mine = span(here.core * self.half, self.half)
+            return [self.keep(1, total, self.outputs_[0].at[here.y, here.x, :, mine])]
+        return []
+
+    def remote(self, phase):
+        here = self.here
+        y, x = here.y, here.x
+        arrived, total = self.held
+        (out,) = self.outputs_
+        quarter = self.half // 2
+        others = here.shards - 1
+        if phase == 0:
+            return [
+                self.send(
+                    step - 1,
+                    self.inputs_[0].at[here.other(step)],
+                    arrived.at[step],
+                    wshard=here.other(step),
+                )
+                for step in range(1, here.shards)
+            ]
+        one = span(here.core * self.half, quarter)
+        two = span(here.core * self.half + quarter, quarter)
+        if phase == 1:
+            held_one, held_two = total.at[:, pl.ds(0, quarter)], total.at[:, pl.ds(quarter, quarter)]
+            return [
+                self.send(others, held_one, out.at[y, x, :, one], seq=here.y_next),
+                self.send(others + 1, held_two, out.at[y, x, :, two], seq=here.x_next),
+            ]
+        if phase == 2:
+            both_one, both_two = out.at[:, x, :, one], out.at[y, :, :, two]
+            return [
+                self.send(others + 2, both_one, both_one, seq=here.x_next),
+                self.send(others + 3, both_two, both_two, seq=here.y_next),
+            ]
+        ref = out.at[:, :, :, span(here.core * self.half, self.half)]
+        return [self.send(others + 4, ref, ref, seq=here.core_next)]
+
+    def work(self, phase):
+        if phase == 1:
+            arrived, total = self.held
+            value = arrived[0].astype(f32)
+            for step in range(1, arrived.shape[0]):
+                value = value + arrived[step].astype(f32)
+            total[...] = value.astype(bf16)
+
+
+def call(
+    kernel,
+    grid,
+    args,
+    in_specs,
+    out_specs,
+    out_shape,
+    scratch_shapes=(),
+    riders=(),
+    table=None,
+    collective_id=None,
+    vmem=48,
+    flops=0,
+    traffic=0,
+    name=None,
+):
+    anywhere = pl.BlockSpec(memory_space=pl.ANY)
+    sizes = [len(args), len(out_shape), len(scratch_shapes)]
+    rider_in = [array for rider in riders for array in rider.inputs]
+    rider_out = [shape for rider in riders for shape in rider.outputs]
+    rider_scratch = [entry for rider in riders for entry in rider.semaphores() + list(rider.scratch)]
+    aliases = {}
+    at_in, at_out = sizes[0], sizes[1]
+    for rider in riders:
+        for source, target in rider.aliases:
+            aliases[at_in + source] = at_out + target
+        at_in += len(rider.inputs)
+        at_out += len(rider.outputs)
+
+    def body(*refs):
+        refs = list(refs)
+
+        def take(count):
+            found = refs[:count]
+            del refs[:count]
+            return found
+
+        own_in, their_in = take(sizes[0]), take(len(rider_in))
+        own_out, their_out = take(sizes[1]), take(len(rider_out))
+        own_scratch, their_scratch = take(sizes[2]), refs
+        if not riders:
+            return kernel(*own_in, *own_out, *own_scratch)
+        here = Here()
+        step = pl.program_id(0)
+        reach = max(rider.reach for rider in riders)
+
+        @pl.when(step == 0)
+        def start():
+            here.meet(reach)
+
+        for rider in riders:
+            counts = (len(rider.inputs), len(rider.outputs), 3 + len(rider.scratch))
+            parts = []
+            for pool, count in zip((their_in, their_out, their_scratch), counts):
+                parts.append(pool[:count])
+                del pool[:count]
+            rider.bind(here, *parts)
+
+        def run(events):
+            for which, phase in events:
+                riders[which].run(phase)
+
+        for at in sorted(table):
+            if at < grid:
+
+                @pl.when(step == at)
+                def early():
+                    run(table[at])
+
+        kernel(*own_in, *own_out, *own_scratch)
+
+        @pl.when(step == grid - 1)
+        def late():
+            for at in sorted(table):
+                if at >= grid:
+                    run(table[at])
+            for rider in riders:
+                rider.finish()
+
+    found = pl.pallas_call(
+        body,
+        grid=(grid,),
+        in_specs=list(in_specs) + [anywhere] * len(rider_in),
+        out_specs=list(out_specs) + [anywhere] * len(rider_out),
+        out_shape=list(out_shape) + rider_out,
+        scratch_shapes=list(scratch_shapes) + rider_scratch,
+        input_output_aliases=aliases,
+        compiler_params=pltpu.CompilerParams(
+            dimension_semantics=("arbitrary",),
+            vmem_limit_bytes=vmem << 20,
+            **({"collective_id": collective_id, "has_side_effects": True} if riders else {}),
+        ),
+        cost_estimate=pl.CostEstimate(flops=flops, bytes_accessed=traffic, transcendentals=0),
+        name=name,
+    )(*args, *rider_in)
+    own, found = found[: sizes[1]], found[sizes[1] :]
+    carried = []
+    for rider in riders:
+        carried.append(found[: len(rider.outputs)])
+        found = found[len(rider.outputs) :]
+    return own, carried
+
+
+def whole_rows(gathered):
+    return gathered.reshape(-1, gathered.shape[-1])
+
+
+def finish_sum(part):
     count = lax.axis_size("seq")
-    return lax.ppermute(value, "seq", [(source, source ^ (1 << bit)) for source in range(count)])
-
-
-def rotate(value, steps):
-    count = lax.axis_size("wshard")
-    return lax.ppermute(
-        value, "wshard", [(source, (source + steps) % count) for source in range(count)]
-    )
-
-
-def seq_orders():
-    bits = lax.axis_size("seq").bit_length() - 1
-    far = list(range(1, bits))
-    return far, far[::-1]
-
-
-def gather_seq(value, order, lead):
-    rank = lax.axis_index("seq")
-    done = []
-    for bit in order:
-        other = swap_bit(value, bit)
-        place = lead + sum(1 for earlier in done if earlier > bit)
-        upper = bit_of(rank, bit) == 1
-        low_half = jnp.where(upper, other, value)
-        high_half = jnp.where(upper, value, other)
-        value = jnp.stack([low_half, high_half], axis=place)
-        done.append(bit)
-    shape = value.shape
-    return value.reshape(shape[:lead] + (1 << len(order),) + shape[lead + len(order) :])
-
-
-def gather_seq_both(value, lead):
-    half = value.shape[-1] // 2
-    one, two = seq_orders()
-    return jnp.concatenate(
-        [
-            gather_seq(value[..., :half], one + [0], lead),
-            gather_seq(value[..., half:], two + [0], lead),
-        ],
-        axis=-1,
-    )
-
-
-def gather_weight(shard):
-    rank = lax.axis_index("seq")
-    place = lax.axis_index("wshard")
-    parts = lax.axis_size("seq")
-    shards = lax.axis_size("wshard")
-    rows, columns = shard.shape
-    piece = lax.dynamic_slice_in_dim(shard, rank * (rows // parts), rows // parts, 0)
-    foreign = jnp.stack([rotate(piece, step) for step in range(1, shards)])
-    foreign = gather_seq_both(foreign, 1).reshape(shards - 1, rows, columns)
-    pieces = jnp.concatenate([shard[None], foreign])
-    return jnp.concatenate(
-        [
-            lax.dynamic_index_in_dim(pieces, lax.rem(place - index + shards, shards), 0, False)
-            for index in range(shards)
-        ]
-    )
-
-
-def add_low(left, right):
-    return (left.astype(jnp.float32) + right.astype(jnp.float32)).astype(jnp.bfloat16)
-
-
-def halve_seq(value, order, remaining):
-    rank = lax.axis_index("seq")
-    remaining = list(remaining)
-    for bit in order:
-        axis = 1 + sum(1 for other in remaining if other > bit)
-        mine = bit_of(rank, bit)
-        keep = lax.dynamic_index_in_dim(value, mine, axis, False)
-        send = lax.dynamic_index_in_dim(value, 1 - mine, axis, False)
-        value = add_low(keep, swap_bit(send, bit))
-        remaining.remove(bit)
-    return value
-
-
-def sum_weight(grad):
-    place = lax.axis_index("wshard")
-    parts = lax.axis_size("seq")
-    shards = lax.axis_size("wshard")
-    rows, columns = grad.shape
-    bits = parts.bit_length() - 1
-    everything = list(range(bits))
-    piece_rows = rows // shards // parts
-    value = grad.astype(jnp.bfloat16).reshape((shards,) + (2,) * bits + (piece_rows, columns))
-    value = halve_seq(value, [0], everything)
-    half = columns // 2
-    one, two = seq_orders()
-    value = jnp.concatenate(
-        [
-            halve_seq(value[..., :half], one, everything[1:]),
-            halve_seq(value[..., half:], two, everything[1:]),
-        ],
-        axis=-1,
-    )
-    total = lax.dynamic_index_in_dim(value, place, 0, False).astype(jnp.float32)
-    for step in range(1, shards):
-        target = lax.rem(place + step, shards)
-        arrived = rotate(lax.dynamic_index_in_dim(value, target, 0, False), step)
-        total = total + arrived.astype(jnp.float32)
-    whole = gather_seq_both(total.astype(jnp.bfloat16), 0)
-    return whole.reshape(rows // shards, columns).astype(jnp.float32)
+    bit = 8
+    while bit < count:
+        pairs = [(source, source ^ bit) for source in range(count)]
+        part = (part.astype(f32) + lax.ppermute(part, "seq", pairs).astype(f32)).astype(bf16)
+        bit *= 2
+    return part
 
 
 def on_device(
@@ -871,11 +1268,6 @@
     ffn = w_gate.shape[1]
 
     own_tokens = tokens[0]
-    pieces = [passed_along(own_tokens, "seq", hop) for hop in range(depth, 0, -1)]
-    pieces.append(own_tokens)
-    pieces.append(passed_along(own_tokens[row_count - PRE :], "seq", depth + 1))
-    ext_tokens = jnp.concatenate(pieces)
-
     small = jnp.concatenate(
         [
             w_beta,
@@ -887,19 +1279,24 @@
         ],
         axis=1,
     )
-    small = jnp.pad(small, ((0, 0), (0, SMALL - small.shape[1])))
-    w_front = gather_weight(jnp.concatenate([w_qkv, small], axis=1))
-    middle = gather_weight(jnp.concatenate([w_outgate, w_out, w_gate, w_up], axis=1))
-    all_down = gather_weight(w_down)
+    small = jnp.pad(small, ((0, 0), (0, EXTRA - small.shape[1])))
+    out_mats = jnp.concatenate([w_outgate, w_out], axis=1)
+    ffn_mats = jnp.concatenate([w_gate, w_up], axis=1)
+
+    riders = [
+        Gather(jnp.concatenate([w_qkv, small], axis=1)),
+        WindowTokens(own_tokens, depth),
+        Gather(ffn_mats, 0, 0),
+    ]
+    events = [(1, 0), (0, 0), (0, 1), (2, 0), (1, 1), (0, 2), (0, 3), (0, 4), (1, 2), (2, 1)]
+    _, ((w_front,), (ext_tokens,), (ffn_in,)) = call(
+        lambda: None, 1, (), [], [], [], riders=riders, table={0: events}, collective_id=0, name="begin"
+    )
+    w_front = whole_rows(w_front)
     small = w_front[:, 3 * D :].astype(f32)
     gain_in, all_ridge, gain_head, gain_ffn = (small[:, HEADS + index] for index in range(4))
     taps = small[:, HEADS + 4 : HEADS + 4 + tap_columns]
     taps = taps.reshape(shards, TAPS, -1).transpose(1, 0, 2).reshape(TAPS, 3 * D)
-    all_og = middle[:, :D]
-    all_out = middle[:, D : 2 * D].astype(f32)
-    all_gate = middle[:, 2 * D : 2 * D + ffn].astype(f32)
-    all_up = middle[:, 2 * D + ffn :].astype(f32)
-    all_down = all_down.astype(f32)
 
     rank = lax.axis_index("seq")
     first = rank * row_count - halo_rows - PRE
@@ -922,12 +1319,42 @@
     ridge_column = all_ridge[:, None]
     x_own = own_tokens.astype(f32)
 
-    hidden, kv_in, q_in, q_pre, queries, keys, values, beta = front(
-        ext_tokens, same, gain_row, w_front, taps, row_count
+    (hidden, kv_in, q_in, q_pre, queries, keys, values, beta), ((ffn_in,), (mats,), (all_down,)) = front(
+        ext_tokens,
+        same,
+        gain_row,
+        w_front,
+        taps,
+        row_count,
+        riders=[Gather(None, 1, 2, ffn_in), Gather(out_mats, 0, 0), Gather(w_down, 0, 0)],
+        table={0: [(0, 1), (1, 0), (2, 0)], 4: [(0, 2)], 99: [(1, 1), (2, 1), (0, 3)]},
+        collective_id=1,
     )
+    (mixed, image0, image1), ((ffn_in,), (mats,), (all_down,)) = attn_fwd(
+        queries,
+        keys,
+        values,
+        beta,
+        mask,
+        ridge_column,
+        riders=[Gather(None, 3, 3, ffn_in), Gather(None, 1, 3, mats), Gather(None, 1, 3, all_down)],
+        table={
+            0: [(1, 1), (2, 1), (0, 3)],
+            2: [(1, 2)],
+            3: [(2, 2)],
+            5: [(1, 3)],
+            99: [(2, 3), (0, 4), (1, 4), (2, 4)],
+        },
+        collective_id=2,
+    )
+    mats, ffn_in, all_down = (whole_rows(part) for part in (mats, ffn_in, all_down))
+    all_og = mats[:, :D]
+    all_out = mats[:, D:].astype(f32)
+    all_gate = ffn_in[:, :ffn].astype(f32)
+    all_up = ffn_in[:, ffn:].astype(f32)
+    all_down = all_down.astype(f32)
     hidden_own = hidden[halo_rows:main_rows]
     gate_pre = jnp.dot(hidden_own, all_og, preferred_element_type=f32)
-    mixed, image0, image1 = attn_fwd(queries, keys, values, beta, mask, ridge_column)
 
     def back_half(xrow, mixed, gate_pre, gain_head, mat_out, gain_ffn, mat_gate, mat_up, mat_down):
         return section_out(
@@ -941,13 +1368,40 @@
     d_xout, d_mixed, d_gate, d_ghead, d_wout, d_gffn, d_wgate, d_wup, d_wdown = pull_back(grad_out)
     d_gate = d_gate.astype(bf16)
 
-    total_down = sum_weight(d_wdown)
-    total_ffn = sum_weight(jnp.concatenate([d_wgate, d_wup], axis=1).astype(bf16))
-
-    d_query, d_key, d_value, d_beta, d_ridge = attn_bwd(
-        queries, keys, values, beta, mask, ridge_column, image0, image1, d_mixed.astype(bf16)
+    def weight_grad(left, right):
+        return lax.dot_general(
+            left, right, (((0,), (0,)), ((), ())), preferred_element_type=f32
+        ).astype(bf16)
+
+    part_rows = shard_rows // 8
+    grad_down = d_wdown.astype(bf16)
+    grad_ffn = jnp.concatenate([d_wgate.astype(bf16), d_wup.astype(bf16)], axis=1)
+    grad_mats = jnp.concatenate([weight_grad(hidden_own, d_gate), d_wout.astype(bf16)], axis=1)
+    (d_query, d_key, d_value, d_beta, d_ridge), ((sum_down,), (sum_ffn0,)) = attn_bwd(
+        queries,
+        keys,
+        values,
+        beta,
+        mask,
+        ridge_column,
+        image0,
+        image1,
+        d_mixed.astype(bf16),
+        riders=[SumFar(grad_down), SumFar(grad_ffn, 0, part_rows)],
+        table={
+            0: [(0, 0), (1, 0)],
+            1: [(0, 1), (1, 1)],
+            4: [(0, 2)],
+            5: [(1, 2), (0, 3)],
+            7: [(1, 3)],
+            99: [(0, 4), (1, 4)],
+        },
+        collective_id=3,
     )
-    d_kv_in, d_q_in, d_q_pre, d_beta_pre, d_halo, d_own, d_gain, d_taps = back(
+    (
+        (d_kv_in, d_q_in, d_q_pre, d_beta_pre, d_halo, d_own, d_gain, d_taps),
+        ((total_down,), (total_ffn0,), (sum_ffn1,), (sum_mats,)),
+    ) = back(
         ext_tokens,
         kv_in,
         same,
@@ -964,27 +1418,27 @@
         w_front,
         all_og,
         taps,
+        riders=[
+            SumNear(sum_down),
+            SumNear(sum_ffn0),
+            SumFar(grad_ffn, part_rows, part_rows),
+            SumFar(grad_mats),
+        ],
+        table={
+            0: [(2, 0), (3, 0), (0, 0), (1, 0)],
+            1: [(2, 1)],
+            2: [(3, 1)],
+            3: [(2, 2)],
+            4: [(0, 1), (1, 1), (3, 2)],
+            5: [(2, 3), (0, 2), (1, 2)],
+            6: [(3, 3), (0, 3), (1, 3)],
+            99: [(0, 4), (1, 4), (2, 4), (3, 4)],
+        },
+        collective_id=4,
     )
-
-    def weight_grad(left, right):
-        return lax.dot_general(
-            left, right, (((0,), (0,)), ((), ())), preferred_element_type=f32
-        ).astype(bf16)
-
-    d_wog = weight_grad(hidden_own, d_gate)
-    d_wq = weight_grad(
-        hidden[halo_rows - PRE : main_rows], jnp.concatenate([d_q_pre, d_q_in])
-    )
+    d_wq = weight_grad(hidden[halo_rows - PRE : main_rows], jnp.concatenate([d_q_pre, d_q_in]))
     d_wkv = weight_grad(hidden, d_kv_in)
     d_wbeta = weight_grad(hidden[:main_rows], d_beta_pre)[:, :HEADS]
-
-    d_tokens = d_own
-    for hop in range(1, depth + 1):
-        start = halo_rows - hop * row_count
-        part = passed_along(d_halo[start : start + row_count], "seq", -hop)
-        d_tokens = d_tokens + part.astype(f32)
-    part = passed_along(d_halo[halo_rows:], "seq", -(depth + 1)).astype(f32)
-    d_tokens = d_tokens + jnp.pad(part, ((row_count - PRE, 0), (0, 0)))
 
     d_small = jnp.concatenate(
         [
@@ -997,9 +1451,43 @@
         ],
         axis=1,
     ).astype(bf16)
-    d_small = jnp.pad(d_small, ((0, 0), (0, SMALL - d_small.shape[1])))
-    total_middle = sum_weight(jnp.concatenate([d_wog, d_wout.astype(bf16)], axis=1))
-    total_front = sum_weight(jnp.concatenate([d_wq, d_wkv, d_small], axis=1))
+    d_small = jnp.pad(d_small, ((0, 0), (0, EXTRA - d_small.shape[1])))
+    grad_front = jnp.concatenate([d_wq, d_wkv, d_small], axis=1)
+    far0, far1 = SumFar(grad_front, 0, part_rows), SumFar(grad_front, part_rows, part_rows)
+    riders = [
+        WindowGrads(d_halo, row_count, depth),
+        SumNear(sum_ffn1),
+        SumNear(sum_mats),
+        far0,
+        far1,
+        SumNear(after=far0),
+        SumNear(after=far1),
+    ]
+    events = [
+        (3, 0), (4, 0), (0, 0), (1, 0), (2, 0),
+        (3, 1), (4, 1), (3, 2), (4, 2), (1, 1), (2, 1),
+        (3, 3), (3, 4), (5, 0), (4, 3), (4, 4), (6, 0),
+        (1, 2), (2, 2), (1, 3), (2, 3), (0, 1),
+        (5, 1), (6, 1), (5, 2), (6, 2), (5, 3), (6, 3),
+        (1, 4), (2, 4), (5, 4), (6, 4),
+    ]
+    _, (back_grads, (total_ffn1,), (total_mats,), _, _, (total0,), (total1,)) = call(
+        lambda: None, 1, (), [], [], [], riders=riders, table={0: events}, collective_id=5, vmem=60, name="end"
+    )
+    near, far = back_grads
+    d_tokens = d_own
+    for hop in range(depth):
+        d_tokens = d_tokens + near[hop].astype(f32)
+    d_tokens = d_tokens + jnp.pad(far.astype(f32), ((row_count - PRE, 0), (0, 0)))
+
+    def final(*sums):
+        whole = jnp.concatenate([finish_sum(part) for part in sums], axis=2)
+        return whole.reshape(-1, whole.shape[-1]).astype(f32)
+
+    total_down = final(total_down)
+    total_ffn = final(total_ffn0, total_ffn1)
+    total_middle = final(total_mats)
+    total_front = final(total0, total1)
     t_small = total_front[:, 3 * D :]
     return (
         output.astype(bf16)[None],

time: 906 us -> 583 us (0.64)
  waiting for transfers between devices: 296 us -> 0 us
  Pallas kernels: 173 us -> 402 us
  starting transfers between devices: 109 us -> 0 us
  other arithmetic: 123 us -> 40.8 us
  local copies, waits for them, and re-layouts: 92.5 us -> 44.2 us
  matrix products: 100 us -> 84.3 us
    ppermute x89 -> x0, waiting for transfers between devices: 296 us -> none  [the longest x62 213 us: swap_bit(): lax.ppermute(value, 'seq', [(source, source ^ 1 << bit) for source in ran...]
    pallas_call x4 -> x6, Pallas kernels: 173 us -> 402 us  [call(): pl.pallas_call(body, grid=(grid,), in_specs=list(in_specs) + [anywhere] *...]
    ppermute x89 -> x0, starting transfers between devices: 109 us -> none  [the longest x62 57.4 us: swap_bit(): lax.ppermute(value, 'seq', [(source, source ^ 1 << bit) for source in ran...]
    concatenate x8, other arithmetic: 45.6 us -> 18.4 us  [the longest x1 7.09 us: on_device(): jnp.concatenate([d_wgate.astype(bf16), d_wup.astype(bf16)], axis=1)]
    another operation x82 -> x3, other arithmetic: 25.3 us -> 0.22 us  [the longest x76 22.6 us: gather_seq(): value = jnp.stack([low_half, high_half], axis=place)]
    convert_element_type x28 -> x4, other arithmetic: 21.6 us -> 3.72 us  [final(): return whole.reshape(-1, whole.shape[-1]).astype(f32)]
    squeeze x18 -> x0, local copies, waits for them, and re-layouts: 12.9 us -> none  [the longest x3 6.77 us: gather_weight(): lax.dynamic_index_in_dim(pieces, lax.rem(place - index + shards, shards),...]
    unnamed x190 -> x118, local copies, waits for them, and re-layouts: 22.3 us -> 11.7 us
  transfers between devices with their start and end apart: 89 -> 0, of which waited for: 40 -> 0; matrix products, arithmetic and copies ran while one was open for 20% -> 0% of each run, Pallas kernels for 6% -> 0%
where the time goes in v4:
time: 583 us; the launch traced here: 573 us
  Pallas kernels  402 us (69%)
  matrix products  84.3 us (14%)
  local copies, waits for them, and re-layouts  44.2 us (8%)
  other arithmetic  40.8 us (7%)
    pallas_call x6, Pallas kernels, call(): pl.pallas_call(body, grid=(grid,), in_specs=list(in_specs) + [anywhere] *...  402 us
    dot_general x4, matrix products, matmul_keep(): jnp.dot(left_low, right_low, preferred_element_type=jnp.float32)  27.5 us
    dot_general x4, matrix products, weight_grad(): lax.dot_general(left, right, (((0,), (0,)), ((), ())), preferred_element_...  21.1 us
    unnamed x118, local copies, waits for them, and re-layouts  11.7 us

profile of v4, /device:TPU:0, one launch (start us, length us, event | category | flops | bytes accessed | tf_op | source)
XLA Modules:
  0.0 573.2 jit_solution(1338437802370384377)
XLA Ops:
  5.3 1.6 fusion.34
  8.4 60.5 %begin.1 = (bf16[4,2,2,64,3584]{4,3,2,1,0:T(8,128)(2,1)}, bf16[1552,1024]{1,0:T(8,128)(2,1)}, bf16[4,2,2,64,5632]{4,3,2,1,0:T(8,128)(2,1)}) custom-call(bf16[2,2,64,3584]{3,2,1,0:T(8,128)(2,1)S(1)} %bitcast.101, bf16[512,1024]{1,0:T(8,128)(2,1)S(1)} %bitcast.102, bf16[2,2,64,5632]{3,2,1,0:T(8,128)(2,1)S(1)} %bitcast.100), custom_call_target="tpu_custom_call" | custom-call | tf_op jit(solution)/shard_map/begin/pallas_call | solution.py:1204
  68.9 1.5 slice_convert_fusion
  70.5 1.3 copy-done.17
  71.8 1.4 slice_reduce_fusion
  74.2 1.5 slice.160
  77.1 51.8 %front.1 = (bf16[1552,1024]{1,0:T(8,128)(2,1)}, bf16[1552,2048]{1,0:T(8,128)(2,1)}, bf16[512,1024]{1,0:T(8,128)(2,1)S(1)}, bf16[16,1024]{1,0:T(8,128)(2,1)S(1)},...) custom-call(bf16[1552,1024]{1,0:T(8,128)(2,1)} %get-tuple-element.59, ...), custom_call_target="tpu_custom_call", output_to_operand_aliasing={{8}: (5, {})} | custom-call | flops 15032385536 | bytes 31457280 | tf_op jit(solution)/shard_map/front/pallas_call | solution.py:1204
  130.1 1.6 fusion.20.refs_4_
  131.7 42.4 %attn_fwd.1 = (f32[512,1024]{1,0:T(8,128)S(1)}, f32[1024,512]{1,0:T(8,128)}, f32[1024,512]{1,0:T(8,128)}, bf16[4,2,2,64,5632]{4,3,2,1,0:T(8,128)(2,1)}, bf16[4,2...) custom-call(bf16[512,1024]{1,0:T(8,128)(2,1)S(1)} %get-tuple-element, ...), custom_call_target="tpu_custom_call", output_to_operand_aliasing={{3}: (6, {}), {4}: (7, {}), {5}: (8, {})} | custom-call | flops 16106127360 | bytes 20971520 | tf_op jit(solution)/shard_map/attn_fwd/pallas_call | solution.py:1204
  174.4 1.8 copy.109
  176.2 2.2 reduce_sum.84
  179.3 5.0 multiply_convert_fusion.4
  184.3 1.4 multiply_reduce_fusion.3
  186.6 5.2 fusion.58
  192.0 7.9 %fusion.8 = f32[512,2816]{1,0:T(8,128)} fusion(bf16[512,1024]{1,0:T(8,128)(2,1)S(1)} %multiply_convert_fusion.3, bf16[1024,5632]{1,0:T(8,128)(2,1)} %bitcast.128), kind=kOutput, calls=%fused_computation.17 | convolution fusion | flops 2952790016 | bytes 12582912 | tf_op jit(solution)/shard_map/jvp()/dot_general | solution.py:688
  199.9 11.1 %fusion.4 = (bf16[512,2816]{1,0:T(8,128)(2,1)S(1)}, bf16[512,2816]{1,0:T(8,128)(2,1)}, bf16[512,2816]{1,0:T(8,128)(2,1)}) fusion(f32[512,2816]{1,0:T(8,128)} %fusion.58, f32[512,2816]{1,0:T(8,128)} %fusion.8, bf16[512,1024]{1,0:T(8,128)(2,1)S(1)} %multiply_convert_fusion.3, bf16[1024,5632]{1,0:T(8,128)(2,1)} %bitcast.129), kind=kOutput, calls=%fused_computation.7 | convolution fusion | flops 2975858688 | bytes 27000832 | tf_op jit(solution)/shard_map/jvp()/dot_general | solution.py:688
  211.0 7.1 %fusion.40 = bf16[1,512,1024]{2,1,0:T(8,128)(2,1)} fusion(f32[512,1024]{1,0:T(8,128)S(1)} %get-tuple-element.134, bf16[512,2816]{1,0:T(8,128)(2,1)} %get-tuple-element.119, bf16[2816,1024]{1,0:T(8,128)(2,1)S(1)} %bitcast.136, f32[512]{0:T(512)S(1)} %slice_convert_fusion.2), kind=kOutput, calls=%fused_computation.79 | convolution fusion | flops 2954362880 | bytes 11798528 | tf_op jit(solution)/shard_map/jvp()/dot_general | solution.py:688
  218.1 5.4 fusion.6
  223.5 5.7 multiply_reduce_fusion
  229.2 2.0 fusion.55
  231.2 1.3 fusion.30
  233.9 1.8 copy.111
  235.6 2.2 reduce_sum.90
  239.7 3.6 fusion.24
  243.4 5.1 convolution_convert_fusion.2
  248.5 3.5 convolution_convert_fusion
  252.0 3.4 convolution_convert_fusion.1
  255.5 7.1 %pad_maximum_fusion = bf16[1024,5632]{1,0:T(8,128)(2,1)} fusion(bf16[1024,2816]{1,0:T(8,128)(2,1)S(1)} %convolution_convert_fusion, bf16[1024,2816]{1,0:T(8,128)(2,1)S(1)} %convolution_convert_fusion.1), kind=kLoop, calls=%fused_computation.2 | loop fusion | flops 23068672 | bytes 23068672 | tf_op jit(solution)/shard_map/concatenate | solution.py:1378
  262.6 79.7 %attn_bwd.1 = (f32[512,1024]{1,0:T(8,128)}, f32[1536,1024]{1,0:T(8,128)}, f32[1536,1024]{1,0:T(8,128)}, f32[1536,128]{1,0:T(8,128)S(1)}, f32[1024,1]{1,0:T(8,128...) custom-call(bf16[512,1024]{1,0:T(8,128)(2,1)S(1)} %copy-done.14, ...), custom_call_target="tpu_custom_call" | custom-call | flops 40265318400 | bytes 31457280 | tf_op jit(solution)/shard_map/attn_bwd/pallas_call | solution.py:1204
  342.4 1.6 slice.167.refs_16_
  345.4 1.3 convolution_convert_fusion.5
  347.3 1.3 convolution_convert_fusion.6
  348.6 2.4 pad_maximum_fusion.1
  351.1 6.5 %copy.98 = bf16[1024,2048]{1,0:T(8,128)(2,1)} copy(bf16[1024,2048]{0,1:T(8,128)(2,1)} %pad_maximum_fusion.1) | data formatting | bytes 8388608 | tf_op jit(solution)/shard_map/concatenate | solution.py:1379
  357.6 74.9 %back.1 = (bf16[1552,2048]{1,0:T(8,128)(2,1)}, bf16[512,1024]{1,0:T(8,128)(2,1)}, bf16[16,1024]{1,0:T(8,128)(2,1)}, bf16[1536,128]{1,0:T(8,128)(2,1)}, bf16[1040...) custom-call(bf16[1552,1024]{1,0:T(8,128)(2,1)} %get-tuple-element.59, ...), custom_call_target="tpu_custom_call" | custom-call | flops 22548578304 | bytes 41943040 | tf_op jit(solution)/shard_map/back/pallas_call | solution.py:1204
  432.5 3.0 fusion.15
  437.6 12.4 %convolution_convert_fusion.3 = bf16[1024,2048]{1,0:T(8,128)(2,1)} fusion(bf16[1552,1024]{1,0:T(8,128)(2,1)} %get-tuple-element.70, bf16[1552,2048]{1,0:T(8,128)(2,1)} %get-tuple-element.91), kind=kOutput, calls=%fused_computation.26 | convolution fusion | flops 6511656960 | bytes 13729792 | tf_op jit(solution)/shard_map/dot_general | solution.py:1372
  450.0 4.4 convolution_convert_fusion.4
  454.4 2.9 copy.104
  457.2 5.7 fusion.1
  462.9 92.6 %end.1 = (bf16[2,512,1024]{2,1,0:T(8,128)(2,1)}, bf16[16,1024]{1,0:T(8,128)(2,1)}, bf16[2,2,32,5632]{3,2,1,0:T(8,128)(2,1)}, bf16[2,2,64,2048]{3,2,1,0:T(8,128)(...) custom-call(bf16[1040,1024]{1,0:T(8,128)(2,1)} %get-tuple-element.86, ...), custom_call_target="tpu_custom_call" | custom-call | tf_op jit(solution)/shard_map/end/pallas_call | solution.py:1204
  555.6 3.2 fusion.45
  559.5 1.2 slice_reduce_fusion.3
  560.7 1.9 slice.174
  563.6 1.5 fusion.57
  565.0 1.1 slice.177
  568.0 2.9 fusion.56
  571.0 2.0 bitcast_convert_fusion.2
  (176 shorter events, 22.5 us)
Async XLA Ops:
  0.6 6.3 %copy-start.25 = (bf16[256,2816]{1,0:T(8,128)(2,1)S(1)}, bf16[256,2816]{1,0:T(8,128)(2,1)}, u32[]{:S(2)}) copy-start(bf16[256,2816]{1,0:T(8,128)(2,1)} %param.29) | copy-start | bytes 4325380
  68.9 4.3 copy-start.44
  71.8 4.3 copy-start.39
  71.8 4.3 copy-start.40
  73.2 55.8 %copy-start.6 = (f32[1024]{0:T(1024)}, f32[1024]{0:T(1024)S(1)}, u32[]{:S(2)}) copy-start(f32[1024]{0:T(1024)S(1)} %get-tuple-element.112) | copy-start | bytes 12292
  74.2 54.8 %copy-start.2 = (f32[1536,4]{1,0:T(8,128)}, f32[1536,4]{1,0:T(8,128)S(1)}, u32[]{:S(2)}) copy-start(f32[1536,4]{1,0:T(8,128)S(1)} %convert_element_type.152.refs_1_.refs_3_) | copy-start | bytes 73732
  76.0 53.0 %copy-start.5 = (f32[4,4,768]{2,1,0:T(4,128)}, f32[4,4,768]{2,1,0:T(4,128)S(1)}, u32[]{:S(2)}) copy-start(f32[4,4,768]{2,1,0:T(4,128)S(1)} %reshape.182) | copy-start | bytes 147460
  77.1 52.8 %copy-start.43 = (s32[1,3]{1,0:T(1,128)S(1)}, s32[1,3]{1,0:T(1,128)}, u32[]{:S(2)}) copy-start(s32[1,3]{1,0:T(1,128)} %param.18) | copy-start | bytes 40
  77.1 54.6 %copy-start.3 = (f32[1024,1]{1,0:T(8,128)S(1)}, f32[1024,1]{1,0:T(8,128)}, u32[]{:S(2)}) copy-start(f32[1024,1]{1,0:T(8,128)} %get-tuple-element.127.refs_5_) | copy-start | bytes 12292
  129.6 2.1 copy-start.7
  129.6 44.5 %copy-start.8 = (f32[1536,128]{1,0:T(8,128)}, f32[1536,128]{1,0:T(8,128)S(1)}, u32[]{:S(2)}) copy-start(f32[1536,128]{1,0:T(8,128)S(1)} %get-tuple-element.65.refs_3_.refs_10_) | copy-start | bytes 2359300
  129.6 44.5 %copy-start.13 = (bf16[512,1024]{1,0:T(8,128)(2,1)}, bf16[512,1024]{1,0:T(8,128)(2,1)S(1)}, u32[]{:S(2)}) copy-start(bf16[512,1024]{1,0:T(8,128)(2,1)S(1)} %get-tuple-element.62.refs_0_) | copy-start | bytes 3145732
  131.7 42.4 %copy-start = (bf16[1536,512]{1,0:T(8,128)(2,1)}, bf16[1536,512]{1,0:T(8,128)(2,1)S(1)}, u32[]{:S(2)}) copy-start(bf16[1536,512]{1,0:T(8,128)(2,1)S(1)} %fusion.20.refs_4_) | copy-start | bytes 4718596
  178.6 7.9 %slice-start = ((s8[5767168]{0:T(1024)(128)(4,1)}), s8[4194304]{0:T(1024)(128)(4,1)S(1)}, s32[]{:S(2)}) async-start(s8[5767168]{0:T(1024)(128)(4,1)} %bitcast.133), calls=%async_computation | async-start | bytes 8388608
  179.3 5.0 copy-start.18
  179.3 5.0 copy-start.31
  179.3 7.3 %slice-start.1 = ((s8[5767168]{0:T(1024)(128)(4,1)}), s8[1572864]{0:T(1024)(128)(4,1)S(1)}, s32[]{:S(2)}) async-start(s8[5767168]{0:T(1024)(128)(4,1)} %bitcast.133), calls=%async_computation.1 | async-start | bytes 3145728
  184.3 48.2 %copy-start.20 = (f32[512,1024]{1,0:T(8,128)}, f32[512,1024]{1,0:T(8,128)S(1)}, u32[]{:S(2)}) copy-start(f32[512,1024]{1,0:T(8,128)S(1)} %get-tuple-element.132) | copy-start | bytes 6291460
  184.3 2.0 copy-start.22
  192.0 7.9 %copy-start.33 = (bf16[512,1024]{1,0:T(8,128)(2,1)}, bf16[512,1024]{1,0:T(8,128)(2,1)S(1)}, u32[]{:S(2)}) copy-start(bf16[512,1024]{1,0:T(8,128)(2,1)S(1)} %multiply_convert_fusion.3) | copy-start | bytes 3145732
  211.0 12.5 %copy-start.48 = (bf16[512,2816]{1,0:T(8,128)(2,1)}, bf16[512,2816]{1,0:T(8,128)(2,1)S(1)}, u32[]{:S(2)}) copy-start(bf16[512,2816]{1,0:T(8,128)(2,1)S(1)} %get-tuple-element.117) | copy-start | bytes 8650756
  211.0 7.1 %copy-start.51 = (bf16[512,2816]{1,0:T(8,128)(2,1)S(1)}, bf16[512,2816]{1,0:T(8,128)(2,1)}, u32[]{:S(2)}) copy-start(bf16[512,2816]{1,0:T(8,128)(2,1)} %get-tuple-element.118) | copy-start | bytes 8650756
  239.7 3.6 copy-start.50
  243.3 103.4 %copy-start.29 = (bf16[512,1024]{1,0:T(8,128)(2,1)}, bf16[512,1024]{1,0:T(8,128)(2,1)S(1)}, u32[]{:S(2)}) copy-start(bf16[512,1024]{1,0:T(8,128)(2,1)S(1)} %get-tuple-element.120.refs_12_) | copy-start | bytes 3145732
  243.3 5.1 copy-start.34
  243.3 5.1 copy-start.52
  248.5 3.5 copy-start.49
  255.4 7.1 %copy-start.4 = (f32[1024,1]{1,0:T(8,128)S(1)}, f32[1024,1]{1,0:T(8,128)}, u32[]{:S(2)}) copy-start(f32[1024,1]{1,0:T(8,128)} %get-tuple-element.127.refs_5_) | copy-start | bytes 12292
  255.4 7.1 %copy-start.9 = (f32[1536,128]{1,0:T(8,128)S(1)}, f32[1536,128]{1,0:T(8,128)}, u32[]{:S(2)}) copy-start(f32[1536,128]{1,0:T(8,128)} %copy-done.8) | copy-start | bytes 2359300
  255.4 7.1 %copy-start.14 = (bf16[512,1024]{1,0:T(8,128)(2,1)S(1)}, bf16[512,1024]{1,0:T(8,128)(2,1)}, u32[]{:S(2)}) copy-start(bf16[512,1024]{1,0:T(8,128)(2,1)} %copy-done.13) | copy-start | bytes 3145732
  262.6 79.8 %copy-start.32 = (bf16[4,2,2,64,2048]{4,3,2,1,0:T(8,128)(2,1)S(1)}, bf16[4,2,2,64,2048]{4,3,2,1,0:T(8,128)(2,1)}, u32[]{:S(2)}) copy-start(bf16[4,2,2,64,2048]{4,3,2,1,0:T(8,128)(2,1)} %get-tuple-element.71) | copy-start | bytes 12582916
  342.3 4.4 copy-start.10
  342.3 4.4 copy-start.11
  342.3 4.4 copy-start.12
  342.3 2.0 copy-start.36
  342.3 3.1 copy-start.47
  432.5 3.0 copy-start.42
  432.5 3.7 copy-start.41
  437.6 12.4 %copy-start.53 = (bf16[512,1024]{1,0:T(8,128)(2,1)S(1)}, bf16[512,1024]{1,0:T(8,128)(2,1)}, u32[]{:S(2)}) copy-start(bf16[512,1024]{1,0:T(8,128)(2,1)} %get-tuple-element.90) | copy-start | bytes 3145732
  437.6 12.4 %copy-start.54 = (bf16[16,1024]{1,0:T(8,128)(2,1)S(1)}, bf16[16,1024]{1,0:T(8,128)(2,1)}, u32[]{:S(2)}) copy-start(bf16[16,1024]{1,0:T(8,128)(2,1)} %get-tuple-element.89) | copy-start | bytes 98308
  462.9 92.6 %copy-start.23 = (f32[512,1024]{1,0:T(8,128)S(1)}, f32[512,1024]{1,0:T(8,128)}, u32[]{:S(2)}) copy-start(f32[512,1024]{1,0:T(8,128)} %get-tuple-element.85) | copy-start | bytes 6291460
  555.5 3.2 copy-start.37
  555.5 3.2 copy-start.38
  559.4 3.1 copy-start.16
  560.7 2.6 copy-start.30
  563.6 3.4 copy-start.27
  563.6 3.4 copy-start.28
  568.0 3.0 copy-start.24
  (9 other events, 12.6 us)

commit v5 on v4

--- a/solution.py
+++ b/solution.py
@@ -19,6 +19,7 @@
 bf16 = jnp.bfloat16
 QB = 256
 CH = 256
+KEYS = 640
 ROWS = 256
 
 
@@ -168,7 +169,7 @@
             pltpu.VMEM((3 * D // CH, 8 + ROWS, CH), f32),
             pltpu.VMEM((PRE, D), bf16),
         ],
-        vmem=50,
+        vmem=62,
         flops=4 * (main_rows * 2 + own_rows) * D * D,
         traffic=30 << 20,
         name="front",
@@ -201,13 +202,13 @@
     dqin_ref,
     dqpre_ref,
     dbp_ref,
-    dxhalo_ref,
-    dxown_ref,
     dgain_ref,
     dtaps_ref,
     ext_ref,
     buf_ref,
     dh_ref,
+    dxhalo_ref,
+    dxown_ref,
 ):
     step = pl.program_id(0)
     block = blocks - 1 - step
@@ -304,7 +305,8 @@
                 )
                 dqin_ref[:, at : at + CH] = rows
                 dh = dh + mm_t(rows, w_ref[:, at : at + CH])
-            dxown_ref[...] = dres_ref[...] + norm_back(x_ref[...].astype(f32), dh_ref[...] + dh)
+            at = pl.ds(pl.multiple_of((block - first_own) * ROWS, ROWS), ROWS)
+            dxown_ref[at] = dres_ref[...] + norm_back(x_ref[...].astype(f32), dh_ref[...] + dh)
 
         @pl.when(block == first_own - 1)
         def own_history():
@@ -318,7 +320,8 @@
 
         @pl.when(block < first_own)
         def halo():
-            dxhalo_ref[...] = norm_back(x_ref[...].astype(f32), dh_ref[...]).astype(bf16)
+            at = pl.ds(pl.multiple_of(block * ROWS, ROWS), ROWS)
+            dxhalo_ref[at] = norm_back(x_ref[...].astype(f32), dh_ref[...]).astype(bf16)
 
     @pl.when(step == blocks)
     def before():
@@ -328,11 +331,11 @@
             rows = before_rows(slot)
             dkvin_ref[0:PRE, at : at + CH] = rows
             dh = dh + mm_t(rows, w_ref[:, D + at : D + at + CH])
-        dxhalo_ref[0:PRE, :] = norm_back(x_ref[0:PRE].astype(f32), dh).astype(bf16)
+        dxhalo_ref[first_own * ROWS : first_own * ROWS + PRE, :] = norm_back(x_ref[0:PRE].astype(f32), dh).astype(bf16)
 
 
 def back(
-    ext_tokens, kvin, same, qin, qpre, dk, dv, dq, beta, dbeta, dgate, dres, gain, w_front, w_og, taps, **riding
+    ext_tokens, kvin, same, qin, qpre, dk, dv, dq, beta, dbeta, dgate, dres, gain, w_front, mats, taps, **riding
 ):
     ext_rows = ext_tokens.shape[0]
     main_rows = ext_rows - PRE
@@ -356,10 +359,6 @@
 
     def own_prev_block(step):
         return (jnp.maximum(small_blocks * (blocks - 1 - step - first_own) - 1, 0), 0)
-
-    def halo_block(step):
-        block = jnp.minimum(blocks - 1 - step, first_own - 1)
-        return (jnp.where(step == blocks, first_own, block), 0)
 
     def fixed(array):
         return pl.BlockSpec(array.shape, lambda step: (0, 0), pipeline_mode=pl.Buffered(1))
@@ -385,7 +384,7 @@
             dres,
             gain,
             w_front,
-            w_og,
+            mats,
             taps,
         ),
         [
@@ -405,7 +404,7 @@
             pl.BlockSpec((ROWS, D), own_block),
             fixed(gain),
             fixed(w_front),
-            fixed(w_og),
+            pl.BlockSpec((D, D), lambda step: (0, 0), pipeline_mode=pl.Buffered(1)),
             fixed(taps),
         ],
         [
@@ -413,8 +412,6 @@
             pl.BlockSpec((ROWS, D), own_block),
             pl.BlockSpec((PRE, D), lambda step: (0, 0)),
             pl.BlockSpec((ROWS, SMALL), main_block),
-            pl.BlockSpec((ROWS, D), halo_block),
-            pl.BlockSpec((ROWS, D), own_block),
             pl.BlockSpec((1, D), lambda step: (0, 0)),
             pl.BlockSpec((TAPS, 3 * D), lambda step: (0, 0)),
         ],
@@ -423,8 +420,6 @@
             shape((own_rows, D), bf16),
             shape((PRE, D), bf16),
             shape((main_rows, SMALL), bf16),
-            shape((main_rows - own_rows + PRE, D), bf16),
-            shape((own_rows, D), f32),
             shape((1, D), f32),
             shape((TAPS, 3 * D), f32),
         ],
@@ -432,6 +427,8 @@
             pltpu.VMEM((3 * D // CH, 8 + ROWS, CH), f32),
             pltpu.VMEM((3 * D // CH, TAPS - 1, ROWS + 8, CH), f32),
             pltpu.VMEM((ROWS, D), f32),
+            pltpu.VMEM((main_rows - own_rows + PRE, D), bf16),
+            pltpu.VMEM((own_rows, D), f32),
         ],
         vmem=62,
         flops=6 * (main_rows * 2 + own_rows) * D * D,
@@ -458,18 +455,18 @@
     column=head_column(beta_ref,h)
     ridge=ridge_ref[...]
     blocks=range(rows//QB)
-    chunks=range(span//CH)
+    chunks=range(span//KEYS)
     for b in blocks:
         for c in chunks:
-            at=slice(QB*b+CH*c,QB*b+CH*(c+1))
-            w_ref[b,CH*c:CH*(c+1),:]=mask_ref[at,QB*b:QB*(b+1)].astype(f32)*column[at]
+            at=slice(QB*b+KEYS*c,QB*b+KEYS*(c+1))
+            w_ref[b,KEYS*c:KEYS*(c+1),:]=mask_ref[at,QB*b:QB*(b+1)].astype(f32)*column[at]
     def apply(b,vector,right):
         low=vector.astype(bf16)
         out=jnp.zeros((HEAD_DIM,QB),f32)
         for c in chunks:
-            at=slice(QB*b+CH*c,QB*b+CH*(c+1))
+            at=slice(QB*b+KEYS*c,QB*b+KEYS*(c+1))
             s=mm(k_ref[at,:],low)
-            s=(w_ref[b,CH*c:CH*(c+1),:]*s).astype(bf16)
+            s=(w_ref[b,KEYS*c:KEYS*(c+1),:]*s).astype(bf16)
             out=out+mm(right[:,at],s)
         return out
     q=[q_ref[QB*b:QB*(b+1),:].astype(f32).T for b in blocks]
@@ -504,6 +501,7 @@
         [head(rows), heads_t, heads_t],
         [jax.ShapeDtypeStruct((rows, D), f32)] + [jax.ShapeDtypeStruct((D, rows), f32)] * 2,
         [pltpu.VMEM((HEAD_DIM, keys), bf16)] * 2 + [pltpu.VMEM((rows // QB, WINDOW + QB, QB), f32)],
+        vmem=62,
         flops=2 * flops,
         traffic=20 << 20,
         name="attn_fwd",
@@ -519,21 +517,21 @@
     column=head_column(beta_ref,h)
     ridge=ridge_ref[...]
     blocks=range(rows//QB)
-    chunks=range(span//CH)
+    chunks=range(span//KEYS)
     dk_ref[...]=jnp.zeros_like(dk_ref)
     dv_ref[...]=jnp.zeros_like(dv_ref)
     acc_ref[...]=jnp.zeros_like(acc_ref)
     for b in blocks:
         for c in chunks:
-            at=slice(QB*b+CH*c,QB*b+CH*(c+1))
-            w_ref[b,CH*c:CH*(c+1),:]=mask_ref[at,QB*b:QB*(b+1)].astype(f32)*column[at]
+            at=slice(QB*b+KEYS*c,QB*b+KEYS*(c+1))
+            w_ref[b,KEYS*c:KEYS*(c+1),:]=mask_ref[at,QB*b:QB*(b+1)].astype(f32)*column[at]
     def apply_back(b,vector,grad,grad_rows,right_ref,dright_ref):
         low=vector.astype(bf16)
         low_rows=vector.T.astype(bf16)
         out=jnp.zeros((HEAD_DIM,QB),f32)
         for c in chunks:
-            at=slice(QB*b+CH*c,QB*b+CH*(c+1))
-            w=w_ref[b,CH*c:CH*(c+1),:]
+            at=slice(QB*b+KEYS*c,QB*b+KEYS*(c+1))
+            w=w_ref[b,KEYS*c:KEYS*(c+1),:]
             s=mm(k_ref[at,:],low)
             dw=mm(right_ref[at,:],grad)
             masked=dw*mask_ref[at,QB*b:QB*(b+1)].astype(f32)
@@ -630,6 +628,7 @@
             pltpu.VMEM((rows // QB, WINDOW + QB, QB), f32),
             pltpu.VMEM((keys, 128), f32),
         ],
+        vmem=62,
         flops=2 * flops,
         traffic=30 << 20,
         name="attn_bwd",
@@ -637,89 +636,22 @@
     )
 
 
-def token_layout(slot_row, live_row, positions):
-    starts = (jnp.cumsum(slot_row) - slot_row).astype(jnp.int32)
-    after = positions[:, None] >= starts[None, :]
-    segment = (jnp.sum(after.astype(jnp.int32), axis=1) - 1).astype(jnp.int32)
-    chosen = segment[:, None] == jnp.arange(slot_row.shape[0], dtype=jnp.int32)[None, :]
-    begin = jnp.sum(jnp.where(chosen, starts[None, :], 0), axis=1).astype(jnp.int32)
-    limit = jnp.sum(jnp.where(chosen, live_row[None, :], 0), axis=1).astype(jnp.int32)
-    valid = (segment >= 0) & (positions - begin < limit)
-    return (segment, valid)
-
-
-def make_kit():
-
-    @jax.custom_vjp
-    def low(v):
-        return lax.optimization_barrier(v.astype(jnp.bfloat16)).astype(jnp.float32)
-
-    @jax.custom_vjp
-    def low_back(v):
-        return v
-
-    def low_keep(v):
-        return (low(v), None)
-
-    def low_pass(kept, grad):
-        return (grad,)
-
-    def back_keep(v):
-        return (v, None)
-
-    def back_low(kept, grad):
-        return (low(grad),)
-
-    low.defvjp(low_keep, low_pass)
-    low_back.defvjp(back_keep, back_low)
-
-    @jax.custom_vjp
-    def matmul(left, right):
-        return jnp.dot(
-            left.astype(jnp.bfloat16),
-            right.astype(jnp.bfloat16),
-            preferred_element_type=jnp.float32,
-        )
-
-    def matmul_keep(left, right):
-        left_low = left.astype(jnp.bfloat16)
-        right_low = right.astype(jnp.bfloat16)
-        return (
-            jnp.dot(left_low, right_low, preferred_element_type=jnp.float32),
-            (left_low, right_low),
-        )
-
-    def matmul_grads(kept, grad):
-        left_low, right_low = kept
-        grad_low = grad.astype(jnp.bfloat16)
-        grad_left = lax.dot_general(
-            grad_low, right_low, (((1,), (1,)), ((), ())), preferred_element_type=jnp.float32
-        )
-        grad_right = lax.dot_general(
-            left_low, grad_low, (((0,), (0,)), ((), ())), preferred_element_type=jnp.float32
-        )
-        return (grad_left, grad_right)
-
-    matmul.defvjp(matmul_keep, matmul_grads)
-
-    def section_out(
-        xrow, mixed, gate_pre, gain_head, mat_out, gain_ffn, mat_gate, mat_up, mat_down, valid
-    ):
-        row_count = xrow.shape[0]
-        shaped = mixed.reshape(row_count, HEADS, HEAD_DIM)
-        shaped = shaped * lax.rsqrt(jnp.mean(shaped * shaped, axis=-1, keepdims=True) + 1e-05)
-        normed = shaped.reshape(row_count, D) * gain_head
-        gated = low(normed * jax.nn.silu(gate_pre))
-        middle = xrow + low_back(matmul(gated, mat_out))
-        hidden = low(
-            middle * lax.rsqrt(jnp.mean(middle * middle, axis=-1, keepdims=True) + 1e-06) * gain_ffn
-        )
-        inner = low(
-            jax.nn.silu(low_back(matmul(hidden, mat_gate))) * low_back(matmul(hidden, mat_up))
-        )
-        return valid[:, None] * (middle + low_back(matmul(inner, mat_down)))
-
-    return section_out
+def slot_of(positions, lengths):
+    slot = (positions >= 0).astype(jnp.int32) - 1
+    start = 0
+    for index in range(lengths.shape[0] - 1):
+        start = start + lengths[index]
+        slot = slot + (positions >= start).astype(jnp.int32)
+    return slot
+
+
+def is_live(positions, lengths, live):
+    found = positions < 0
+    start = 0
+    for index in range(lengths.shape[0]):
+        found = found | ((positions >= start) & (positions < start + live[index]))
+        start = start + lengths[index]
+    return found & (positions >= 0)
 
 
 class Here:
@@ -762,6 +694,7 @@
 class Rider:
     reach = 0
     first, last = 0, 0
+    inside = 0
     inputs, outputs, scratch, aliases = (), (), (), ()
 
     def bind(self, here, inputs, outputs, scratch):
@@ -927,37 +860,71 @@
 
 
 class WindowGrads(Rider):
-    local_count = 1
-
-    def __init__(self, grads, rows, depth):
-        self.rows, self.depth = rows, depth
+    inside = 2
+    last = 4
+    remote_count, local_count = 4, 1
+
+    def __init__(self, rows, columns, depth):
+        assert depth == 2
+        self.rows = rows
         self.reach = depth + 1
-        self.remote_count = depth + 1
-        self.inputs = (grads,)
-        columns = grads.shape[1]
-        self.outputs = (
-            jax.ShapeDtypeStruct((depth, rows, columns), grads.dtype),
-            jax.ShapeDtypeStruct((PRE, columns), grads.dtype),
+        self.outputs = (jax.ShapeDtypeStruct((rows, columns), bf16),)
+        self.scratch = (
+            pltpu.VMEM((rows, columns), bf16),
+            pltpu.VMEM((rows, columns), bf16),
+            pltpu.VMEM((PRE, columns), bf16),
         )
 
     def remote(self, phase):
-        here, rows, depth = self.here, self.rows, self.depth
-        (grads,), (near, far) = self.inputs_, self.outputs_
-        found = [
-            self.send(
-                hop - 1,
-                grads.at[pl.ds((depth - hop) * rows, rows)],
-                near.at[hop - 1],
-                seq=here.along(-hop),
-            )
-            for hop in range(1, depth + 1)
-        ]
-        found.append(
-            self.send(
-                depth, grads.at[pl.ds(depth * rows, PRE)], far, seq=here.along(-depth - 1)
-            )
-        )
-        return found
+        here, rows = self.here, self.rows
+        grads, _ = self.inputs_
+        given, near, far = self.held
+        if phase == 0:
+            return [self.send(0, grads.at[pl.ds(rows, rows)], given, seq=here.core_next)]
+        if phase == 1 or phase == 2:
+            half = pl.ds((2 - phase) * (rows // 2), rows // 2)
+            return [self.send(phase, grads.at[half], near.at[half], seq=here.along(-2))]
+        if phase == 3:
+            return [self.send(3, grads.at[pl.ds(2 * rows, PRE)], far, seq=here.along(-3))]
+        return []
+
+    def run(self, phase):
+        grads, own = self.inputs_
+        given, near, far = self.held
+        half = self.rows // 2
+        chunk = 2 * PRE
+        if phase == 1:
+            self.remote(0)[0].wait_recv()
+        if phase == 1 or phase == 2:
+
+            @pl.when(self.here.core == 1)
+            def join():
+                def add(index, carry):
+                    start = (2 - phase) * half + index * chunk
+                    at = pl.ds(pl.multiple_of(start, chunk), chunk)
+                    add_into(grads, at, given[at])
+                    return carry
+
+                lax.fori_loop(0, half // chunk, add, 0)
+
+        if phase == 4:
+            for earlier in (1, 2, 3):
+                self.remote(earlier)[0].wait_recv()
+            own[self.rows - PRE :, :] += far[...].astype(f32)
+            first_core = (self.here.core == 0).astype(f32)
+
+            def add_up(index, carry):
+                at = pl.ds(pl.multiple_of(index * chunk, chunk), chunk)
+                value = own[at] + near[at].astype(f32) + first_core * given[at].astype(f32)
+                given[at] = value.astype(bf16)
+                return carry
+
+            lax.fori_loop(0, self.rows // chunk, add_up, 0)
+            self.keep(0, given, self.outputs_[0]).start()
+        elif phase == 5:
+            self.keep(0, given, self.outputs_[0]).wait()
+        else:
+            self.remote(phase)[0].start()
 
 
 def add_into(target, at, value):
@@ -968,15 +935,18 @@
     last = 3
     remote_count, local_count = 5, 2
 
-    def __init__(self, grad, start=0, size=None):
+    def __init__(self, grad=None, start=0, size=None, columns=None, offset=0):
         places = lax.axis_size("wshard")
-        if grad.ndim == 2:
-            grad = grad.reshape(places, 2, 2, grad.shape[0] // places // 4, grad.shape[1])
-        size = grad.shape[3] if size is None else size
+        self.inside = int(grad is None)
+        self.offset = offset
+        if not self.inside:
+            columns = grad.shape[-1]
+            grad = grad.reshape(places, 2, 2, grad.shape[0] // places // 4, columns)
+            size = grad.shape[3] if size is None else size
+            self.inputs = (grad,)
         self.rows = pl.ds(start, size)
-        half = grad.shape[-1] // 2
+        half = columns // 2
         quarter = half // 2
-        self.inputs = (grad,)
         self.outputs = (jax.ShapeDtypeStruct((places, size, half), bf16),)
         self.scratch = (
             pltpu.VMEM((places, 2, 2, size, half), bf16),
@@ -991,7 +961,7 @@
     def local(self, phase):
         here, held = self.here, self.held[0]
         if phase == 0:
-            mine = span(here.core * self.half, self.half)
+            mine = span(self.offset + here.core * self.half, self.half)
             return [self.keep(0, self.inputs_[0].at[:, :, :, self.rows, mine], held)]
         if phase == 3:
             return [self.keep(1, held.at[:, here.y, here.x], self.outputs_[0])]
@@ -1003,7 +973,7 @@
         held, core_in, far_a, far_b, next_a, next_b = self.held
         one, two = pl.ds(0, self.half // 2), pl.ds(self.half // 2, self.half // 2)
         if phase == 0:
-            yours = span((1 - here.core) * self.half, self.half)
+            yours = span(self.offset + (1 - here.core) * self.half, self.half)
             ref = self.inputs_[0].at[:, :, :, self.rows, yours]
             return [self.send(0, ref, core_in, seq=here.core_next)]
         if phase == 1:
@@ -1055,14 +1025,22 @@
     last = 3
     local_count = 2
 
-    def __init__(self, sums=None, after=None):
-        self.after = after
-        places, size, half = (sums if after is None else after.outputs[0]).shape
+    def __init__(self, sums=None, after=None, stop=False, total=None):
+        self.after, self.stop, self.resume = after, stop, total is not None
+        if self.resume:
+            (size, half), places = total.shape, lax.axis_size("wshard")
+            self.inputs = (total,)
+        else:
+            places, size, half = (sums if after is None else after.outputs[0]).shape
+            self.inputs = (sums,) if after is None else ()
         self.remote_count = places - 1 + 5
         self.half = half
-        self.inputs = (sums,) if after is None else ()
         self.outputs = (jax.ShapeDtypeStruct((2, 2, size, 2 * half), bf16),)
-        self.scratch = (pltpu.VMEM((places, size, half), bf16), pltpu.VMEM((size, half), bf16))
+        if stop:
+            self.last = 1
+            self.outputs = (jax.ShapeDtypeStruct((size, half), bf16),)
+        arrived = (1, 16, 128) if self.resume else (places, size, half)
+        self.scratch = (pltpu.VMEM(arrived, bf16), pltpu.VMEM((size, half), bf16))
 
     def bind(self, here, inputs, outputs, scratch):
         super().bind(here, inputs, outputs, scratch)
@@ -1072,8 +1050,12 @@
     def local(self, phase):
         here = self.here
         arrived, total = self.held
+        if phase == 0 and self.resume:
+            return [self.keep(0, self.inputs_[0], total)]
         if phase == 0:
             return [self.keep(0, self.inputs_[0].at[here.place], arrived.at[0])]
+        if phase == 1 and self.stop:
+            return [self.keep(1, total, self.outputs_[0])]
         if phase == 1:
             mine = span(here.core * self.half, self.half)
             return [self.keep(1, total, self.outputs_[0].at[here.y, here.x, :, mine])]
@@ -1086,6 +1068,8 @@
         (out,) = self.outputs_
         quarter = self.half // 2
         others = here.shards - 1
+        if (phase == 0 and self.resume) or (phase == 1 and self.stop):
+            return []
         if phase == 0:
             return [
                 self.send(
@@ -1114,12 +1098,154 @@
         return [self.send(others + 4, ref, ref, seq=here.core_next)]
 
     def work(self, phase):
-        if phase == 1:
+        if phase == 1 and not self.resume:
             arrived, total = self.held
             value = arrived[0].astype(f32)
             for step in range(1, arrived.shape[0]):
                 value = value + arrived[step].astype(f32)
             total[...] = value.astype(bf16)
+
+
+class SumPlace(Rider):
+    last = 2
+    local_count = 2
+
+    def __init__(self, grad):
+        places = lax.axis_size("wshard")
+        size, columns = grad.shape[0] // places // 4, grad.shape[1]
+        self.half = columns // 2
+        self.remote_count = places
+        self.inputs = (grad.reshape(places, 2, 2, size, columns),)
+        part = (2, 2, size, self.half)
+        self.outputs = (jax.ShapeDtypeStruct(part, bf16),)
+        self.scratch = (
+            pltpu.VMEM((places,) + part, bf16),
+            pltpu.VMEM((places,) + part, bf16),
+            pltpu.VMEM((places - 1,) + part, bf16),
+        )
+
+    def local(self, phase):
+        held, core_in, _ = self.held
+        if phase == 0:
+            mine = span(self.here.core * self.half, self.half)
+            return [self.keep(0, self.inputs_[0].at[:, :, :, :, mine], held)]
+        if phase == 2:
+            return [self.keep(1, core_in.at[0], self.outputs_[0])]
+        return []
+
+    def remote(self, phase):
+        here = self.here
+        held, core_in, arrived = self.held
+        if phase == 0:
+            yours = span((1 - here.core) * self.half, self.half)
+            return [self.send(0, self.inputs_[0].at[:, :, :, :, yours], core_in, seq=here.core_next)]
+        if phase == 1:
+            return [
+                self.send(
+                    step,
+                    held.at[here.other(step)],
+                    arrived.at[step - 1],
+                    wshard=here.other(step),
+                )
+                for step in range(1, here.shards)
+            ]
+        return []
+
+    def work(self, phase):
+        held, core_in, arrived = self.held
+        if phase == 1:
+
+            def add(index, carry):
+                at = (index // 4, (index // 2) % 2, index % 2)
+                add_into(held, at, core_in[at])
+                return carry
+
+            lax.fori_loop(0, 4 * held.shape[0], add, 0)
+        elif phase == 2:
+
+            def gather_up(index, carry):
+                at = (index // 2, index % 2)
+                value = held[(self.here.place,) + at].astype(f32)
+                for step in range(arrived.shape[0]):
+                    value = value + arrived[(step,) + at].astype(f32)
+                core_in[(0,) + at] = value.astype(bf16)
+                return carry
+
+            lax.fori_loop(0, 4, gather_up, 0)
+
+
+class SumSpread(Rider):
+    last = 5
+    remote_count, local_count = 9, 2
+
+    def __init__(self, sums):
+        _, _, size, half = sums.shape
+        self.half = half
+        quarter = half // 2
+        self.inputs = (sums,)
+        self.outputs = (jax.ShapeDtypeStruct((2, 2, size, 2 * half), bf16),)
+        self.scratch = (
+            pltpu.VMEM((2, 2, size, half), bf16),
+            pltpu.VMEM((2, size, quarter), bf16),
+            pltpu.VMEM((2, size, quarter), bf16),
+            pltpu.VMEM((size, quarter), bf16),
+            pltpu.VMEM((size, quarter), bf16),
+        )
+
+    def local(self, phase):
+        here, held = self.here, self.held[0]
+        if phase == 0:
+            return [self.keep(0, self.inputs_[0], held)]
+        if phase == 3:
+            mine = span(here.core * self.half, self.half)
+            return [self.keep(1, held.at[here.y, here.x], self.outputs_[0].at[here.y, here.x, :, mine])]
+        return []
+
+    def remote(self, phase):
+        here, (out,) = self.here, self.outputs_
+        y, x, quarter = here.y, here.x, self.half // 2
+        held, far_a, far_b, next_a, next_b = self.held
+        one, two = pl.ds(0, quarter), pl.ds(quarter, quarter)
+        out_one = span(here.core * self.half, quarter)
+        out_two = span(here.core * self.half + quarter, quarter)
+        if phase == 1:
+            return [
+                self.send(0, held.at[:, 1 - x, :, one], far_a, seq=here.x_next),
+                self.send(1, held.at[1 - y, :, :, two], far_b, seq=here.y_next),
+            ]
+        if phase == 2:
+            return [
+                self.send(2, held.at[1 - y, x, :, one], next_a, seq=here.y_next),
+                self.send(3, held.at[y, 1 - x, :, two], next_b, seq=here.x_next),
+            ]
+        if phase == 3:
+            return [
+                self.send(4, held.at[y, x, :, one], out.at[y, x, :, out_one], seq=here.y_next),
+                self.send(5, held.at[y, x, :, two], out.at[y, x, :, out_two], seq=here.x_next),
+            ]
+        if phase == 4:
+            both_one, both_two = out.at[:, x, :, out_one], out.at[y, :, :, out_two]
+            return [
+                self.send(6, both_one, both_one, seq=here.x_next),
+                self.send(7, both_two, both_two, seq=here.y_next),
+            ]
+        if phase == 5:
+            ref = out.at[:, :, :, span(here.core * self.half, self.half)]
+            return [self.send(8, ref, ref, seq=here.core_next)]
+        return []
+
+    def work(self, phase):
+        y, x = self.here.y, self.here.x
+        held, far_a, far_b, next_a, next_b = self.held
+        every = slice(None)
+        one, two = slice(0, self.half // 2), slice(self.half // 2, self.half)
+        if phase == 2:
+            for side in range(2):
+                add_into(held, (side, x, every, one), far_a[side])
+                add_into(held, (y, side, every, two), far_b[side])
+        elif phase == 3:
+            add_into(held, (y, x, every, one), next_a[...])
+            add_into(held, (y, x, every, two), next_b[...])
 
 
 def call(
@@ -1178,6 +1304,8 @@
             for pool, count in zip((their_in, their_out, their_scratch), counts):
                 parts.append(pool[:count])
                 del pool[:count]
+            if rider.inside:
+                parts[0] = own_scratch[-rider.inside :]
             rider.bind(here, *parts)
 
         def run(events):
@@ -1239,6 +1367,324 @@
     return part
 
 
+def mid_kernel(
+    x_ref,
+    o_ref,
+    hid_ref,
+    cot_ref,
+    live_ref,
+    hgain_ref,
+    fgain_ref,
+    mats_in,
+    ffn_in,
+    down_in,
+    out_ref,
+    y_ref,
+    h2_ref,
+    u_ref,
+    dab_ref,
+    dd_ref,
+    dyw_ref,
+    dgate_ref,
+    do_ref,
+    dres_ref,
+    dhg_ref,
+    dfg_ref,
+    mats_ref,
+    ffn_ref,
+    down_ref,
+    sems,
+):
+    step = pl.program_id(0)
+    inner = down_ref.shape[0]
+    copies = [
+        pltpu.make_async_copy(source, target, sems.at[index])
+        for index, (source, target) in enumerate(
+            ((mats_in, mats_ref), (ffn_in, ffn_ref), (down_in, down_ref))
+        )
+    ]
+
+    @pl.when(step == 0)
+    def begin():
+        for copy in copies:
+            copy.start()
+        dhg_ref[...] = jnp.zeros_like(dhg_ref)
+        dfg_ref[...] = jnp.zeros_like(dfg_ref)
+        copies[0].wait()
+
+    hgain, fgain = hgain_ref[...], fgain_ref[...]
+    gate_pre = mm(hid_ref[...], mats_ref[:, :D])
+    gate = jax.nn.sigmoid(gate_pre)
+    gate_silu = gate_pre * gate
+
+    def head_scale(part):
+        return lax.rsqrt(jnp.mean(part * part, axis=-1, keepdims=True) + 1e-05)
+
+    mixed = o_ref[...]
+    normal = in_heads(lambda part: part * head_scale(part), mixed)
+    scaled = normal * hgain
+    y = (scaled * gate_silu).astype(bf16)
+    y_ref[...] = y
+    x1 = x_ref[...].astype(f32) + mm(y, mats_ref[:, D:])
+    x1_scale = lax.rsqrt(jnp.mean(x1 * x1, axis=-1, keepdims=True) + 1e-06)
+    h2 = (x1 * x1_scale * fgain).astype(bf16)
+    h2_ref[...] = h2
+    live = live_ref[...]
+    grad_out = live * cot_ref[...].astype(f32)
+    dd = grad_out.astype(bf16)
+    dd_ref[...] = dd
+
+    @pl.when(step == 0)
+    def rest():
+        copies[1].wait()
+        copies[2].wait()
+
+    forward = jnp.zeros_like(x1)
+    dh2 = jnp.zeros_like(x1)
+    for at in range(0, inner, CH):
+        one, two = slice(at, at + CH), slice(inner + at, inner + at + CH)
+        a = mm(h2, ffn_ref[:, one])
+        b = mm(h2, ffn_ref[:, two])
+        sig = jax.nn.sigmoid(a)
+        silu = a * sig
+        u = (silu * b).astype(bf16)
+        u_ref[:, one] = u
+        forward = forward + mm(u, down_ref[one, :])
+        du = mm_t(dd, down_ref[one, :])
+        da = (du * b * (sig + silu * (1.0 - sig))).astype(bf16)
+        db = (du * silu).astype(bf16)
+        dab_ref[:, one] = da
+        dab_ref[:, two] = db
+        dh2 = dh2 + mm_t(da, ffn_ref[:, one]) + mm_t(db, ffn_ref[:, two])
+    out_ref[...] = (live * (x1 + forward)).astype(bf16)
+    x1_normal = x1 * x1_scale
+    dfg_ref[...] += jnp.sum(dh2 * x1_normal, axis=0, keepdims=True)
+    dh2 = dh2 * fgain
+    dx1 = grad_out + x1_scale * (
+        dh2 - x1_normal * jnp.mean(dh2 * x1_normal, axis=-1, keepdims=True)
+    )
+    dres_ref[...] = dx1
+    dyw = dx1.astype(bf16)
+    dyw_ref[...] = dyw
+    dy = mm_t(dyw, mats_ref[:, D:])
+    dgate_ref[...] = (dy * scaled * (gate + gate_silu * (1.0 - gate))).astype(bf16)
+    dscaled = dy * gate_silu
+    dhg_ref[...] += jnp.sum(dscaled * normal, axis=0, keepdims=True)
+
+    def head_back(part, part_normal, grad):
+        return head_scale(part) * (
+            grad - part_normal * jnp.mean(grad * part_normal, axis=-1, keepdims=True)
+        )
+
+    do_ref[...] = in_heads(head_back, mixed, normal, dscaled * hgain).astype(bf16)
+
+
+def mid(x, mixed, hidden, first_own, cotangent, live, hgain, fgain, mats, ffn, down):
+    rows = x.shape[0]
+    inner = down.shape[0]
+    shape = jax.ShapeDtypeStruct
+
+    def block(columns):
+        return pl.BlockSpec((ROWS, columns), lambda step: (step, 0))
+
+    row = pl.BlockSpec((1, D), lambda step: (0, 0))
+    anywhere = pl.BlockSpec(memory_space=pl.ANY)
+    outs = [
+        shape((rows, D), bf16),
+        shape((rows, D), bf16),
+        shape((rows, D), bf16),
+        shape((rows, inner), bf16),
+        shape((rows, 2 * inner), bf16),
+        shape((rows, D), bf16),
+        shape((rows, D), bf16),
+        shape((rows, D), bf16),
+        shape((rows, D), bf16),
+        shape((rows, D), f32),
+    ]
+    found, _ = call(
+        mid_kernel,
+        rows // ROWS,
+        (x, mixed, hidden, cotangent, live, hgain, fgain, mats, ffn, down),
+        [
+            block(D),
+            block(D),
+            pl.BlockSpec((ROWS, D), lambda step: (step + first_own, 0)),
+            block(D),
+            block(1),
+            row,
+            row,
+            anywhere,
+            anywhere,
+            anywhere,
+        ],
+        [block(out.shape[1]) for out in outs] + [row, row],
+        outs + [shape((1, D), f32)] * 2,
+        [
+            pltpu.VMEM(mats.shape, bf16),
+            pltpu.VMEM(ffn.shape, bf16),
+            pltpu.VMEM(down.shape, bf16),
+            pltpu.SemaphoreType.DMA((3,)),
+        ],
+        vmem=62,
+        flops=8 * rows * D * (D + 3 * inner // 2),
+        traffic=50 << 20,
+        name="mid",
+    )
+    return found
+
+
+def mid_grads_kernel(
+    hid_ref, y_ref, h2_ref, u_ref, dab_ref, dd_ref, dyw_ref, dgate_ref,
+    down_ref, ffn_ref, mats_ref, hid_t, y_t, h2_t,
+):
+    step = pl.program_id(0)
+    width = ffn_ref.shape[1]
+
+    @pl.when(step == 0)
+    def begin():
+        hid_t[...] = hid_ref[...].T
+        y_t[...] = y_ref[...].T
+        h2_t[...] = h2_ref[...].T
+
+    ffn_ref[...] = mm(h2_t[...], dab_ref[...]).astype(bf16)
+    down_ref[...] = mm(u_ref[...].T, dd_ref[...]).astype(bf16)
+    for index in range(2 * D // width):
+        at = width * index
+
+        @pl.when(step == index)
+        def mats():
+            if at < D:
+                mats_ref[...] = mm(hid_t[...], dgate_ref[:, at : at + width]).astype(bf16)
+            else:
+                mats_ref[...] = mm(y_t[...], dyw_ref[:, at - D : at - D + width]).astype(bf16)
+
+
+def mid_grads(hidden, first_own, y, h2, u, dab, dd, dyw, dgate):
+    rows, inner = u.shape
+    width = 2 * CH
+    steps = 2 * inner // width
+    shape = jax.ShapeDtypeStruct
+
+    def fixed(array):
+        return pl.BlockSpec(array.shape, lambda step: (0, 0))
+
+    found, _ = call(
+        mid_grads_kernel,
+        steps,
+        (hidden, y, h2, u, dab, dd, dyw, dgate),
+        [
+            pl.BlockSpec((rows, D), lambda step: (first_own, 0)),
+            fixed(y),
+            fixed(h2),
+            pl.BlockSpec((rows, inner // steps), lambda step: (0, step)),
+            pl.BlockSpec((rows, width), lambda step: (0, step)),
+            fixed(dd),
+            fixed(dyw),
+            fixed(dgate),
+        ],
+        [
+            pl.BlockSpec((inner // steps, D), lambda step: (step, 0)),
+            pl.BlockSpec((D, width), lambda step: (0, step)),
+            pl.BlockSpec((D, width), lambda step: (0, jnp.minimum(step, 2 * D // width - 1))),
+        ],
+        [shape((inner, D), bf16), shape((D, 2 * inner), bf16), shape((D, 2 * D), bf16)],
+        [pltpu.VMEM((D, rows), bf16)] * 3,
+        vmem=62,
+        flops=2 * rows * D * (2 * D + 3 * inner),
+        traffic=40 << 20,
+        name="mid_grads",
+    )
+    return found
+
+
+def front_grads_kernel(
+    hid_ref, pre_ref, qpre_ref, dkv_ref, dkvpre_ref, dq_ref, dqpre_ref, dbp_ref, small_ref,
+    hid_t, pre_t, qpre_t, out_ref,
+):
+    step = pl.program_id(0)
+    width = EXTRA
+    split = out_ref.shape[:-1]
+    first_query = 2 * D // width
+    column = jnp.where(
+        step < first_query,
+        D + step * width,
+        jnp.where(step < 3 * D // width, (step - first_query) * width, 3 * D),
+    )
+    at_step = pl.ds(pl.multiple_of(column, width), width)
+
+    def put(value):
+        out_ref[:, :, :, :, at_step] = value.astype(bf16).reshape(split + (width,))
+    own = dq_ref.shape[0]
+    main = hid_t.shape[1]
+
+    @pl.when(step == 0)
+    def begin():
+        hid_t[...] = hid_ref[...].T
+        pre_t[...] = pre_ref[...].T
+        qpre_t[...] = qpre_ref[...].T
+
+    @pl.when((step >= first_query) & (step < 3 * D // width))
+    def queries():
+        at = pl.ds(pl.multiple_of((step - first_query) * width, width), width)
+        put(mm(hid_t[:, main - own :], dq_ref[:, at]) + mm(qpre_t[...], dqpre_ref[:, at]))
+
+    @pl.when(step < first_query)
+    def others():
+        put(mm(hid_t[...], dkv_ref[...]) + mm(pre_t[...], dkvpre_ref[...]))
+
+    @pl.when(step == 3 * D // width)
+    def rest():
+        lane = lax.broadcasted_iota(jnp.int32, (D, SMALL), 1)
+        gates = mm(hid_t[...], dbp_ref[...]).astype(bf16)
+        first = jnp.where(lane < HEADS, gates, small_ref[...])
+        put(jnp.concatenate([first, jnp.zeros((D, width - SMALL), bf16)], axis=1))
+
+
+def front_grads(hidden, dkv, dq, dqpre, dbp, small, **riding):
+    own = dq.shape[0]
+    main = dbp.shape[0]
+    width = EXTRA
+    blocks = 3 * D // width
+
+    def fixed(array):
+        return pl.BlockSpec(array.shape, lambda step: (0, 0))
+
+    def kv_block(step):
+        return jnp.minimum(step, 2 * D // width - 1)
+
+    places = lax.axis_size("wshard")
+    _, carried = call(
+        front_grads_kernel,
+        blocks + 1,
+        (hidden, hidden, hidden, dkv, dkv, dq, dqpre, dbp, small),
+        [
+            pl.BlockSpec((main, D), lambda step: (0, 0)),
+            pl.BlockSpec((PRE, D), lambda step: (main // PRE, 0)),
+            pl.BlockSpec((PRE, D), lambda step: ((main - own) // PRE - 1, 0)),
+            pl.BlockSpec((main, width), lambda step: (0, kv_block(step))),
+            pl.BlockSpec((PRE, width), lambda step: (main // PRE, kv_block(step))),
+            fixed(dq),
+            fixed(dqpre),
+            fixed(dbp),
+            fixed(small),
+        ],
+        [],
+        [],
+        [
+            pltpu.VMEM((D, main), bf16),
+            pltpu.VMEM((D, PRE), bf16),
+            pltpu.VMEM((D, PRE), bf16),
+            pltpu.VMEM((places, 2, 2, D // places // 4, 3 * D + EXTRA), bf16),
+        ],
+        vmem=62,
+        flops=2 * D * D * (2 * main + own),
+        traffic=25 << 20,
+        name="end",
+        **riding,
+    )
+    return carried
+
+
 def on_device(
     tokens,
     slot_lengths,
@@ -1257,7 +1703,6 @@
     w_down,
     cotangent,
 ):
-    section_out = make_kit()
     row_count = tokens.shape[1]
     depth = (WINDOW + row_count - 1) // row_count
     halo_rows = depth * row_count
@@ -1271,10 +1716,7 @@
     small = jnp.concatenate(
         [
             w_beta,
-            norm_gain[:, None],
-            ridge[:, None],
-            head_gain[:, None],
-            ffn_gain[:, None],
+            jnp.stack([norm_gain, ridge, head_gain, ffn_gain]).T,
             conv_weight.reshape(shard_rows, tap_columns),
         ],
         axis=1,
@@ -1299,25 +1741,28 @@
     taps = taps.reshape(shards, TAPS, -1).transpose(1, 0, 2).reshape(TAPS, 3 * D)
 
     rank = lax.axis_index("seq")
-    first = rank * row_count - halo_rows - PRE
-    positions = first + jnp.arange(PRE + main_rows, dtype=jnp.int32)
-    segment, valid = token_layout(slot_lengths[0], live_lengths[0], positions)
-    main_seg = segment[PRE:]
-    own_seg = main_seg[halo_rows:]
-    valid_own = valid[PRE + halo_rows :].astype(f32)
-    same = jnp.stack(
-        [segment[PRE - tap : PRE - tap + main_rows] == main_seg for tap in range(TAPS)], axis=1
-    ).astype(f32)
-    spacing = positions[None, PRE + halo_rows :] - positions[PRE:, None]
+    first = rank * row_count - halo_rows
+    lengths, live = slot_lengths[0], live_lengths[0]
+
+    def positions(start, shape, dim):
+        return start + lax.broadcasted_iota(jnp.int32, shape, dim)
+
+    conv_at = positions(first, (main_rows, TAPS), 0)
+    tap_at = lax.broadcasted_iota(jnp.int32, (main_rows, TAPS), 1)
+    same = (slot_of(conv_at, lengths) == slot_of(conv_at - tap_at, lengths)).astype(f32)
+    key_at = positions(first, (main_rows, 1), 0)
+    query_at = positions(first + halo_rows, (1, row_count), 1)
+    spacing = query_at - key_at
     mask = (
         (spacing >= 0)
         & (spacing < WINDOW)
-        & (main_seg[:, None] == own_seg[None, :])
-        & valid[PRE:, None]
+        & (slot_of(key_at, lengths) == slot_of(query_at, lengths))
+        & is_live(key_at, lengths, live)
     ).astype(bf16)
+    own_at = positions(first + halo_rows, (row_count, 1), 0)
+    valid_own = is_live(own_at, lengths, live).astype(f32)
     gain_row = gain_in[None, :]
     ridge_column = all_ridge[:, None]
-    x_own = own_tokens.astype(f32)
 
     (hidden, kv_in, q_in, q_pre, queries, keys, values, beta), ((ffn_in,), (mats,), (all_down,)) = front(
         ext_tokens,
@@ -1348,36 +1793,26 @@
         collective_id=2,
     )
     mats, ffn_in, all_down = (whole_rows(part) for part in (mats, ffn_in, all_down))
-    all_og = mats[:, :D]
-    all_out = mats[:, D:].astype(f32)
-    all_gate = ffn_in[:, :ffn].astype(f32)
-    all_up = ffn_in[:, ffn:].astype(f32)
-    all_down = all_down.astype(f32)
-    hidden_own = hidden[halo_rows:main_rows]
-    gate_pre = jnp.dot(hidden_own, all_og, preferred_element_type=f32)
-
-    def back_half(xrow, mixed, gate_pre, gain_head, mat_out, gain_ffn, mat_gate, mat_up, mat_down):
-        return section_out(
-            xrow, mixed, gate_pre, gain_head, mat_out, gain_ffn, mat_gate, mat_up, mat_down, valid_own
-        )
-
-    output, pull_back = jax.vjp(
-        back_half, x_own, mixed, gate_pre, gain_head, all_out, gain_ffn, all_gate, all_up, all_down
-    )
-    grad_out = cotangent[0].astype(f32)
-    d_xout, d_mixed, d_gate, d_ghead, d_wout, d_gffn, d_wgate, d_wup, d_wdown = pull_back(grad_out)
-    d_gate = d_gate.astype(bf16)
-
-    def weight_grad(left, right):
-        return lax.dot_general(
-            left, right, (((0,), (0,)), ((), ())), preferred_element_type=f32
-        ).astype(bf16)
+    first_own = halo_rows // ROWS
+    output, y, h2, u, d_ab, d_down_in, d_out_in, d_gate, d_mixed, d_xout, d_ghead, d_gffn = mid(
+        own_tokens,
+        mixed,
+        hidden,
+        first_own,
+        cotangent[0],
+        valid_own,
+        gain_head[None, :],
+        gain_ffn[None, :],
+        mats,
+        ffn_in,
+        all_down,
+    )
+    grad_down, grad_ffn, grad_mats = mid_grads(
+        hidden, halo_rows // row_count, y, h2, u, d_ab, d_down_in, d_out_in, d_gate
+    )
 
     part_rows = shard_rows // 8
-    grad_down = d_wdown.astype(bf16)
-    grad_ffn = jnp.concatenate([d_wgate.astype(bf16), d_wup.astype(bf16)], axis=1)
-    grad_mats = jnp.concatenate([weight_grad(hidden_own, d_gate), d_wout.astype(bf16)], axis=1)
-    (d_query, d_key, d_value, d_beta, d_ridge), ((sum_down,), (sum_ffn0,)) = attn_bwd(
+    (d_query, d_key, d_value, d_beta, d_ridge), ((sum_down,), (sum_ffn0,), (sum_mats,)) = attn_bwd(
         queries,
         keys,
         values,
@@ -1386,21 +1821,21 @@
         ridge_column,
         image0,
         image1,
-        d_mixed.astype(bf16),
-        riders=[SumFar(grad_down), SumFar(grad_ffn, 0, part_rows)],
+        d_mixed,
+        riders=[SumFar(grad_down), SumFar(grad_ffn, 0, part_rows), SumPlace(grad_mats)],
         table={
-            0: [(0, 0), (1, 0)],
-            1: [(0, 1), (1, 1)],
+            0: [(2, 0), (0, 0), (1, 0)],
+            1: [(2, 1), (0, 1)],
+            2: [(1, 1)],
             4: [(0, 2)],
-            5: [(1, 2), (0, 3)],
-            7: [(1, 3)],
-            99: [(0, 4), (1, 4)],
+            7: [(1, 2)],
+            99: [(0, 3), (1, 3), (2, 2), (2, 3), (0, 4), (1, 4)],
         },
         collective_id=3,
     )
     (
-        (d_kv_in, d_q_in, d_q_pre, d_beta_pre, d_halo, d_own, d_gain, d_taps),
-        ((total_down,), (total_ffn0,), (sum_ffn1,), (sum_mats,)),
+        (d_kv_in, d_q_in, d_q_pre, d_beta_pre, d_gain, d_taps),
+        ((sum_down,), (sum_ffn0,), (sum_ffn1,), (total_mats,), (d_tokens,)),
     ) = back(
         ext_tokens,
         kv_in,
@@ -1416,94 +1851,96 @@
         d_xout,
         gain_row,
         w_front,
-        all_og,
+        mats,
         taps,
         riders=[
-            SumNear(sum_down),
-            SumNear(sum_ffn0),
+            SumNear(sum_down, stop=True),
+            SumNear(sum_ffn0, stop=True),
             SumFar(grad_ffn, part_rows, part_rows),
-            SumFar(grad_mats),
+            SumSpread(sum_mats),
+            WindowGrads(row_count, D, depth),
         ],
         table={
-            0: [(2, 0), (3, 0), (0, 0), (1, 0)],
-            1: [(2, 1)],
-            2: [(3, 1)],
-            3: [(2, 2)],
-            4: [(0, 1), (1, 1), (3, 2)],
-            5: [(2, 3), (0, 2), (1, 2)],
-            6: [(3, 3), (0, 3), (1, 3)],
-            99: [(0, 4), (1, 4), (2, 4), (3, 4)],
+            0: [(2, 0), (3, 0), (3, 1), (0, 0), (1, 0)],
+            1: [(3, 2), (2, 1)],
+            3: [(2, 2), (3, 3)],
+            4: [(4, 0)],
+            5: [(4, 1), (0, 1), (1, 1), (3, 4)],
+            6: [(4, 2), (2, 3), (3, 5)],
+            99: [(4, 3), (2, 4), (0, 2), (1, 2), (3, 6), (4, 4), (4, 5)],
         },
         collective_id=4,
     )
-    d_wq = weight_grad(hidden[halo_rows - PRE : main_rows], jnp.concatenate([d_q_pre, d_q_in]))
-    d_wkv = weight_grad(hidden, d_kv_in)
-    d_wbeta = weight_grad(hidden[:main_rows], d_beta_pre)[:, :HEADS]
-
     d_small = jnp.concatenate(
         [
-            d_wbeta.astype(f32),
+            jnp.zeros((D, HEADS), f32),
             d_gain.reshape(D, 1),
             d_ridge,
-            d_ghead[:, None],
-            d_gffn[:, None],
+            d_ghead.reshape(D, 1),
+            d_gffn.reshape(D, 1),
             d_taps.reshape(TAPS, shards, -1).transpose(1, 0, 2).reshape(D, tap_columns),
         ],
         axis=1,
     ).astype(bf16)
-    d_small = jnp.pad(d_small, ((0, 0), (0, EXTRA - d_small.shape[1])))
-    grad_front = jnp.concatenate([d_wq, d_wkv, d_small], axis=1)
-    far0, far1 = SumFar(grad_front, 0, part_rows), SumFar(grad_front, part_rows, part_rows)
-    riders = [
-        WindowGrads(d_halo, row_count, depth),
-        SumNear(sum_ffn1),
-        SumNear(sum_mats),
-        far0,
-        far1,
-        SumNear(after=far0),
-        SumNear(after=far1),
+    d_small = jnp.pad(d_small, ((0, 0), (0, SMALL - d_small.shape[1])))
+    rows = shard_rows // 4
+    fars = [
+        SumFar(None, 0, rows, D, D),
+        SumFar(None, 0, rows, D, 2 * D),
+        SumFar(None, 0, rows, D, 0),
+        SumFar(None, 0, rows, EXTRA, 3 * D),
     ]
-    events = [
-        (3, 0), (4, 0), (0, 0), (1, 0), (2, 0),
-        (3, 1), (4, 1), (3, 2), (4, 2), (1, 1), (2, 1),
-        (3, 3), (3, 4), (5, 0), (4, 3), (4, 4), (6, 0),
-        (1, 2), (2, 2), (1, 3), (2, 3), (0, 1),
-        (5, 1), (6, 1), (5, 2), (6, 2), (5, 3), (6, 3),
-        (1, 4), (2, 4), (5, 4), (6, 4),
+    riders = [SumNear(sum_ffn1)] + fars + [SumNear(after=far) for far in fars]
+    riders += [SumNear(total=sum_down), SumNear(total=sum_ffn0)]
+    late = [
+        (3, 0), (4, 0), (9, 3), (10, 3), (2, 1), (1, 2), (3, 1), (4, 1), (2, 2), (1, 3), (1, 4), (5, 0),
+        (3, 2), (4, 2), (0, 1), (2, 3), (2, 4), (6, 0), (5, 1), (3, 3), (4, 3), (3, 4), (4, 4),
+        (7, 0), (8, 0), (0, 2), (6, 1), (5, 2), (6, 2), (5, 3), (7, 1), (8, 1), (6, 3), (0, 3),
+        (7, 2), (8, 2), (7, 3), (8, 3), (5, 4), (6, 4), (0, 4), (7, 4), (8, 4),
+        (9, 4), (10, 4),
     ]
-    _, (back_grads, (total_ffn1,), (total_mats,), _, _, (total0,), (total1,)) = call(
-        lambda: None, 1, (), [], [], [], riders=riders, table={0: events}, collective_id=5, vmem=60, name="end"
-    )
-    near, far = back_grads
-    d_tokens = d_own
-    for hop in range(depth):
-        d_tokens = d_tokens + near[hop].astype(f32)
-    d_tokens = d_tokens + jnp.pad(far.astype(f32), ((row_count - PRE, 0), (0, 0)))
-
+    carried = front_grads(
+        hidden,
+        d_kv_in,
+        d_q_in,
+        d_q_pre,
+        d_beta_pre,
+        d_small,
+        riders=riders,
+        table={
+            0: [(0, 0), (9, 0), (10, 0), (9, 1), (10, 1)],
+            2: [(9, 2), (10, 2), (1, 0)],
+            4: [(1, 1), (2, 0)],
+            99: late,
+        },
+        collective_id=5,
+    )
+    (total_ffn1,), _, _, _, _, (total_k,), (total_v,), (total_q,), (total_small,) = carried[:9]
+    (total_down,), (total_ffn0,) = carried[9:]
     def final(*sums):
         whole = jnp.concatenate([finish_sum(part) for part in sums], axis=2)
-        return whole.reshape(-1, whole.shape[-1]).astype(f32)
+        return whole.reshape(-1, whole.shape[-1])
 
     total_down = final(total_down)
     total_ffn = final(total_ffn0, total_ffn1)
     total_middle = final(total_mats)
-    total_front = final(total0, total1)
-    t_small = total_front[:, 3 * D :]
+    total_front = jnp.concatenate([final(total_q), final(total_k), final(total_v)], axis=1)
+    t_small = final(total_small).astype(f32)
     return (
-        output.astype(bf16)[None],
-        d_tokens.astype(bf16)[None],
+        output[None],
+        d_tokens[None],
         t_small[:, HEADS],
-        total_front[:, : 3 * D],
+        total_front.astype(f32),
         t_small[:, :HEADS],
-        total_middle[:, :D],
+        total_middle[:, :D].astype(f32),
         t_small[:, HEADS + 4 : HEADS + 4 + tap_columns].reshape(TAPS, -1),
         t_small[:, HEADS + 1],
         t_small[:, HEADS + 2],
-        total_middle[:, D:],
+        total_middle[:, D:].astype(f32),
         t_small[:, HEADS + 3],
-        total_ffn[:, :ffn],
-        total_ffn[:, ffn:],
-        total_down,
+        total_ffn[:, :ffn].astype(f32),
+        total_ffn[:, ffn:].astype(f32),
+        total_down.astype(f32),
     )
 
 

time: 583 us -> 495 us (0.85)
  matrix products: 84.3 us -> 0 us
  Pallas kernels: 402 us -> 431 us
  local copies, waits for them, and re-layouts: 44.2 us -> 21.1 us
  other arithmetic: 40.8 us -> 28.8 us
    dot_general x17 -> x0, matrix products: 84.3 us -> none  [the longest x4 27.5 us: matmul_keep(): jnp.dot(left_low, right_low, preferred_element_type=jnp.float32)]
    pallas_call x6 -> x8, Pallas kernels: 402 us -> 431 us  [call(): pl.pallas_call(body, grid=(grid,), in_specs=list(in_specs) + [anywhere] *...]
    concatenate x3 -> x1, other arithmetic: 15.2 us -> 0.7 us  [on_device(): jnp.concatenate([w_beta, jnp.stack([norm_gain, ridge, head_gain, ffn_gain...]
    convert_element_type x11 -> x8, other arithmetic: 11.5 us -> 19.4 us  [the longest x1 3.38 us: on_device(): total_front.astype(f32)]
    concatenate x3 -> x1, local copies, waits for them, and re-layouts: 8.1 us -> 0.98 us  [on_device(): jnp.concatenate([jnp.zeros((D, HEADS), f32), d_gain.reshape(D, 1), d_ridg...]
    slice x9 -> x2, local copies, waits for them, and re-layouts: 8.21 us -> 1.17 us  [the longest x1 0.59 us: is_live(): found = found | (positions >= start) & (positions < start + live[index])]
    unnamed x118 -> x34, local copies, waits for them, and re-layouts: 11.7 us -> 7.65 us
where the time goes in v5:
time: 495 us; the launch traced here: 485 us
  Pallas kernels  431 us (87%)
  other arithmetic  28.8 us (6%)
  local copies, waits for them, and re-layouts  21.1 us (4%)
    pallas_call x8, Pallas kernels, call(): pl.pallas_call(body, grid=(grid,), in_specs=list(in_specs) + [anywhere] *...  431 us

profile of v5, /device:TPU:0, one launch (start us, length us, event | category | flops | bytes accessed | tf_op | source)
XLA Modules:
  0.0 485.4 jit_solution(2712620787871810961)
XLA Ops:
  0.7 1.0 reshape.264
  1.7 0.7 stack.18
  2.4 0.7 stack.17
  3.0 0.7 stack.16
  3.7 0.7 stack.15
  4.4 0.7 pad_maximum_fusion.3
  5.2 1.6 fusion.5
  7.2 1.0 copy-done
  8.3 60.5 %begin.1 = (bf16[4,2,2,64,3584]{4,3,2,1,0:T(8,128)(2,1)}, bf16[1552,1024]{1,0:T(8,128)(2,1)}, bf16[4,2,2,64,5632]{4,3,2,1,0:T(8,128)(2,1)}) custom-call(bf16[2,2,64,3584]{3,2,1,0:T(8,128)(2,1)S(1)} %bitcast.52, bf16[512,1024]{1,0:T(8,128)(2,1)S(1)} %bitcast.54, bf16[2,2,64,5632]{3,2,1,0:T(8,128)(2,1)S(1)} %bitcast.51), custom_call_target="tpu_custom_call" | custom-call | tf_op jit(solution)/shard_map/begin/pallas_call | solution.py:1332
  68.8 0.6 fusion.44
  70.7 0.7 convert_add_fusion
  71.4 2.4 fusion.9.refs_1_.refs_3_
  73.8 1.5 slice_convert_fusion.2
  75.3 2.0 slice_reduce_fusion
  77.5 0.9 reshape.268
  78.5 1.1 pad_maximum_fusion.2
  79.5 53.1 %front.1 = (bf16[1552,1024]{1,0:T(8,128)(2,1)}, bf16[1552,2048]{1,0:T(8,128)(2,1)}, bf16[512,1024]{1,0:T(8,128)(2,1)}, bf16[16,1024]{1,0:T(8,128)(2,1)}, bf16[51...) custom-call(bf16[1552,1024]{1,0:T(8,128)(2,1)} %get-tuple-element.75, ...), custom_call_target="tpu_custom_call", output_to_operand_aliasing={{8}: (5, {})} | custom-call | flops 15032385536 | bytes 31457280 | tf_op jit(solution)/shard_map/front/pallas_call | solution.py:1332
  132.6 0.7 convert_add_fusion.1
  133.3 0.6 fusion.43
  135.8 1.3 fusion.32
  137.1 2.5 fusion.4.refs_4_
  139.7 41.3 %attn_fwd.1 = (f32[512,1024]{1,0:T(8,128)}, f32[1024,512]{1,0:T(8,128)}, f32[1024,512]{1,0:T(8,128)}, bf16[4,2,2,64,5632]{4,3,2,1,0:T(8,128)(2,1)}, bf16[4,2,2,6...) custom-call(bf16[512,1024]{1,0:T(8,128)(2,1)} %get-tuple-element.78., ...), custom_call_target="tpu_custom_call", output_to_operand_aliasing={{3}: (6, {}), {4}: (7, {}), {5}: (8, {})} | custom-call | flops 16106127360 | bytes 20971520 | tf_op jit(solution)/shard_map/attn_fwd/pallas_call | solution.py:1332
  181.0 2.2 fusion.22.refs_4_
  183.2 36.5 %mid.1 = (bf16[512,1024]{1,0:T(8,128)(2,1)}, bf16[512,1024]{1,0:T(8,128)(2,1)}, bf16[512,1024]{1,0:T(8,128)(2,1)}, bf16[512,2816]{1,0:T(8,128)(2,1)}, bf16[512,5...) custom-call(bf16[512,1024]{1,0:T(8,128)(2,1)} %bitcast.53, ...), custom_call_target="tpu_custom_call" | custom-call | flops 22011707392 | bytes 52428800 | tf_op jit(solution)/shard_map/mid/pallas_call | solution.py:1332
  219.7 21.8 %mid_grads.1 = (bf16[2816,1024]{1,0:T(8,128)(2,1)}, bf16[1024,5632]{1,0:T(8,128)(2,1)}, bf16[1024,2048]{1,0:T(8,128)(2,1)}) custom-call(bf16[1552,1024]{1,0:T(8,128)(2,1)} %get-tuple-element.86.refs_2_.refs_0_.refs_1_, bf16[512,1024]{1,0:T(8,128)(2,1)} %get-tuple-element.97.refs_1_, bf16[512,1024]{1,0:T(8,128)(2,1)} %get-tuple-element.98.refs_2_, ...), custom_call_target="tpu_custom_call" | custom-call | flops 11005853696 | bytes 41943040 | tf_op jit(solution)/shard_map/mid_grads/pallas_call | solution.py:1332
  241.5 65.0 %attn_bwd.1 = (f32[512,1024]{1,0:T(8,128)}, f32[1536,1024]{1,0:T(8,128)}, f32[1536,1024]{1,0:T(8,128)}, f32[1536,128]{1,0:T(8,128)}, f32[1024,1]{1,0:T(8,128)}, ...) custom-call(bf16[512,1024]{1,0:T(8,128)(2,1)} %get-tuple-element.78.refs_0_, ...), custom_call_target="tpu_custom_call" | custom-call | flops 40265318400 | bytes 31457280 | tf_op jit(solution)/shard_map/attn_bwd/pallas_call | solution.py:1332
  306.6 80.9 %back.1 = (bf16[1552,2048]{1,0:T(8,128)(2,1)}, bf16[512,1024]{1,0:T(8,128)(2,1)}, bf16[16,1024]{1,0:T(8,128)(2,1)}, bf16[1536,128]{1,0:T(8,128)(2,1)}, f32[1,102...) custom-call(bf16[1552,1024]{1,0:T(8,128)(2,1)} %get-tuple-element.75, ...), custom_call_target="tpu_custom_call" | custom-call | flops 22548578304 | bytes 41943040 | tf_op jit(solution)/shard_map/back/pallas_call | solution.py:1332
  387.4 0.7 convert_bitcast_fusion.2
  388.1 0.2 copy.73
  388.4 0.2 copy.74
  388.8 0.8 convert.29
  389.6 0.6 reshape.282
  390.3 1.0 concatenate.26
  391.3 0.8 pad.9.refs_8_
  392.0 71.7 %end.1 = (bf16[2,2,32,5632]{3,2,1,0:T(8,128)(2,1)}, bf16[4,64,512]{2,1,0:T(8,128)(2,1)}, bf16[4,64,512]{2,1,0:T(8,128)(2,1)}, bf16[4,64,512]{2,1,0:T(8,128)(2,1)...) custom-call(bf16[1552,1024]{1,0:T(8,128)(2,1)} %get-tuple-element.86, ...), custom_call_target="tpu_custom_call" | custom-call | flops 7516192768 | bytes 26214400 | tf_op jit(solution)/shard_map/end/pallas_call | solution.py:1332
  463.7 1.0 bitcast_convert_fusion.1
  464.7 1.6 fusion.42
  466.3 3.4 maximum_convert_fusion
  469.7 0.7 copy.80
  470.4 2.9 slice_convert_fusion.3
  473.4 0.7 reshape.287
  474.1 1.5 copy.81
  475.7 1.5 copy.82
  477.2 1.5 copy.83
  478.8 0.2 pad_maximum_fusion.1
  479.0 2.9 slice_convert_fusion
  481.9 2.0 bitcast_convert_fusion
  484.0 1.0 copy.91
  (39 shorter events, 1.2 us)
Async XLA Ops:
  0.6 6.2 %copy-start.2 = (bf16[256,2816]{1,0:T(8,128)(2,1)S(1)}, bf16[256,2816]{1,0:T(8,128)(2,1)}, u32[]{:S(2)}) copy-start(bf16[256,2816]{1,0:T(8,128)(2,1)} %param.29) | copy-start | bytes 4325380
  5.2 1.8 copy-start.3
  7.0 1.2 copy-start
  8.3 60.5 %copy-start.13 = (s32[1,3]{1,0:T(1,128)S(1)}, s32[1,3]{1,0:T(1,128)}, u32[]{:S(2)}) copy-start(s32[1,3]{1,0:T(1,128)} %param.17) | copy-start | bytes 40
  75.3 3.2 copy-start.8
  75.3 3.2 copy-start.9
  79.5 53.7 %copy-start.10 = (s32[1,3]{1,0:T(1,128)S(1)}, s32[1,3]{1,0:T(1,128)}, u32[]{:S(2)}) copy-start(s32[1,3]{1,0:T(1,128)} %param.18) | copy-start | bytes 40
  306.5 81.8 %copy-start.7 = (f32[1024,1]{1,0:T(8,128)S(1)}, f32[1024,1]{1,0:T(8,128)}, u32[]{:S(2)}) copy-start(f32[1024,1]{1,0:T(8,128)} %get-tuple-element.121) | copy-start | bytes 12292
  306.5 81.8 %copy-start.12 = (f32[1,1024]{1,0:T(1,128)S(1)}, f32[1,1024]{1,0:T(1,128)}, u32[]{:S(2)}) copy-start(f32[1,1024]{1,0:T(1,128)} %get-tuple-element.122) | copy-start | bytes 12292
  306.5 82.0 %copy-start.11 = (f32[1,1024]{1,0:T(1,128)S(1)}, f32[1,1024]{1,0:T(1,128)}, u32[]{:S(2)}) copy-start(f32[1,1024]{1,0:T(1,128)} %get-tuple-element.123) | copy-start | bytes 12292
  469.7 9.1 %copy-start.4 = (bf16[2,2,32,5632]{3,2,1,0:T(8,128)(2,1)S(1)}, bf16[2,2,32,5632]{3,2,1,0:T(8,128)(2,1)}, u32[]{:S(2)}) copy-start(bf16[2,2,32,5632]{3,2,1,0:T(8,128)(2,1)} %get-tuple-element.134) | copy-start | bytes 4325380
  469.7 9.1 %copy-start.5 = (bf16[2,2,32,5632]{3,2,1,0:T(8,128)(2,1)S(1)}, bf16[2,2,32,5632]{3,2,1,0:T(8,128)(2,1)}, u32[]{:S(2)}) copy-start(bf16[2,2,32,5632]{3,2,1,0:T(8,128)(2,1)} %get-tuple-element.133) | copy-start | bytes 4325380
  479.0 2.9 copy-start.1
  481.9 2.0 copy-start.6

commit v6 on v5

--- a/solution.py
+++ b/solution.py
@@ -23,6 +23,66 @@
 ROWS = 256
 
 
+def slot_info(lengths, live, first):
+    table = jnp.array(
+        [
+            [1, 0, 0, 0, 0, 0],
+            [1, 1, 0, 0, 0, 0],
+            [0, 0, 0, 1, 0, 0],
+            [1, 0, 0, 0, 1, 0],
+            [1, 1, 0, 0, 0, 1],
+            [0, 0, 0, 0, 0, 0],
+            [0, 0, 0, 0, 0, 0],
+            [0, 0, 0, 0, 0, 0],
+        ],
+        jnp.int32,
+    )
+    found = jnp.sum(table * jnp.concatenate([lengths, live])[None, :], axis=1, keepdims=True)
+    row = lax.broadcasted_iota(jnp.int32, (8, 128), 0)
+    return found + jnp.where(row == 5, first, 0)
+
+
+def slot_of(info, positions):
+    found = (positions >= 0).astype(jnp.int32)
+    for index in range(2):
+        found = found + (positions >= info[index : index + 1, 0:1]).astype(jnp.int32)
+    return found
+
+
+def is_live(info, positions):
+    found = (positions >= 0) & (positions < info[2:3, 0:1])
+    for index in range(2):
+        found = found | (
+            (positions >= info[index : index + 1, 0:1])
+            & (positions < info[index + 3 : index + 4, 0:1])
+        )
+    return found
+
+
+def rows_from(info, start, count):
+    return info[5:6, 0:1] + start + lax.broadcasted_iota(jnp.int32, (count, 1), 0)
+
+
+def same_slots(info, start):
+    at = rows_from(info, start, ROWS)
+    own = slot_of(info, at)
+    return [(own == slot_of(info, at - tap)).astype(f32) for tap in range(TAPS)]
+
+
+def window_mask(info, mask_ref):
+    keys, queries = mask_ref.shape
+    at_query = (
+        info[5:6, 0:1] + (keys - queries) + lax.broadcasted_iota(jnp.int32, (1, queries), 1)
+    )
+    query_slot = slot_of(info, at_query)
+    for start in range(0, keys, ROWS):
+        at = rows_from(info, start, ROWS)
+        key_slot = jnp.where(is_live(info, at), slot_of(info, at), -1)
+        spacing = at_query - at
+        inside = (spacing >= 0) & (spacing < WINDOW) & (key_slot == query_slot)
+        mask_ref[start : start + ROWS, :] = inside.astype(f32).astype(bf16)
+
+
 def mm(left, right):
     return jnp.dot(left, right, preferred_element_type=f32)
 
@@ -60,10 +120,8 @@
 def front_kernel(
     first_own,
     x_ref,
-    same_ref,
-    gain_ref,
+    info_ref,
     w_ref,
-    taps_ref,
     hid_ref,
     kvin_ref,
     qin_ref,
@@ -72,11 +130,28 @@
     k_ref,
     v_ref,
     beta_ref,
+    params_ref,
+    taps_ref,
     ext_ref,
     tail_ref,
 ):
     step = pl.program_id(0)
-    gain = gain_ref[...]
+    shards = lax.axis_size("wshard")
+
+    @pl.when(step == 0)
+    def unpack():
+        small = w_ref[:, 3 * D : 3 * D + SMALL].astype(f32).T
+        params_ref[...] = small[HEADS : HEADS + 8]
+        wide = D // shards
+        for place in range(shards):
+            for third in range(3):
+                row = HEADS + 4 + TAPS * third
+                at = 3 * wide * place + wide * third
+                taps_ref[:, at : at + wide] = small[
+                    row : row + TAPS, wide * place : wide * (place + 1)
+                ]
+
+    gain = params_ref[0:1, :]
     main_rows = k_ref.shape[0]
     before_at = pl.ds(main_rows, PRE)
     rows_at = pl.ds(pl.multiple_of(jnp.maximum(step - 1, 0) * ROWS, ROWS), ROWS)
@@ -105,7 +180,7 @@
 
     @pl.when(step > 0)
     def main():
-        same = [same_ref[rows_at, tap : tap + 1] for tap in range(TAPS)]
+        same = same_slots(info_ref[...], (step - 1) * ROWS)
         hidden = row_norm(x_ref[rows_at].astype(f32), gain)
         hid_ref[rows_at] = hidden
         for slot in range(kv_slots):
@@ -138,7 +213,7 @@
         tail_ref[...] = hidden[ROWS - PRE :]
 
 
-def front(ext_tokens, same, gain, w_front, taps, own_rows, **riding):
+def front(ext_tokens, info, w_front, own_rows, **riding):
     ext_rows = ext_tokens.shape[0]
     main_rows = ext_rows - PRE
     blocks = main_rows // ROWS
@@ -157,12 +232,14 @@
         shape((main_rows, D), bf16),
         shape((main_rows, D), bf16),
         shape((main_rows, SMALL), f32),
+        shape((8, D), f32),
+        shape((TAPS, 3 * D), f32),
     ]
     return call(
         functools.partial(front_kernel, first_own),
         blocks + 1,
-        (ext_tokens, same, gain, w_front, taps),
-        [fixed(array) for array in (ext_tokens, same, gain, w_front, taps)],
+        (ext_tokens, info, w_front),
+        [fixed(array) for array in (ext_tokens, info, w_front)],
         [fixed(array) for array in outs],
         outs,
         [
@@ -183,7 +260,7 @@
     x_ref,
     kvin_ref,
     kvprev_ref,
-    same_ref,
+    info_ref,
     qin_ref,
     qprev_ref,
     qpre_ref,
@@ -194,7 +271,7 @@
     dbeta_ref,
     dgate_ref,
     dres_ref,
-    gain_ref,
+    params_ref,
     w_ref,
     wog_ref,
     taps_ref,
@@ -213,7 +290,7 @@
     step = pl.program_id(0)
     block = blocks - 1 - step
     kv_slots = 2 * D // CH
-    gain = gain_ref[...]
+    gain = params_ref[0:1, :]
 
     @pl.when(step == 0)
     def clear():
@@ -274,7 +351,7 @@
 
     @pl.when(step < blocks)
     def main():
-        same = [same_ref[:, tap : tap + 1] for tap in range(TAPS)]
+        same = same_slots(info_ref[...], block * ROWS)
         beta = beta_ref[...]
         gates = (dbeta_ref[...] * beta * (1.0 - beta)).astype(bf16)
         dbp_ref[...] = gates
@@ -335,7 +412,7 @@
 
 
 def back(
-    ext_tokens, kvin, same, qin, qpre, dk, dv, dq, beta, dbeta, dgate, dres, gain, w_front, mats, taps, **riding
+    ext_tokens, kvin, info, qin, qpre, dk, dv, dq, beta, dbeta, dgate, dres, params, w_front, mats, taps, **riding
 ):
     ext_rows = ext_tokens.shape[0]
     main_rows = ext_rows - PRE
@@ -371,7 +448,7 @@
             ext_tokens,
             kvin,
             kvin,
-            same,
+            info,
             qin,
             qin,
             qpre,
@@ -382,7 +459,7 @@
             dbeta,
             dgate,
             dres,
-            gain,
+            params,
             w_front,
             mats,
             taps,
@@ -391,7 +468,7 @@
             pl.BlockSpec((ROWS, D), ext_block),
             pl.BlockSpec((ROWS, 2 * D), ext_block),
             pl.BlockSpec((PRE, 2 * D), prev_block),
-            pl.BlockSpec((ROWS, TAPS), main_block),
+            fixed(info),
             pl.BlockSpec((ROWS, D), own_block),
             pl.BlockSpec((PRE, D), own_prev_block),
             fixed(qpre),
@@ -402,7 +479,7 @@
             pl.BlockSpec((ROWS, SMALL), main_block),
             pl.BlockSpec((ROWS, D), own_block),
             pl.BlockSpec((ROWS, D), own_block),
-            fixed(gain),
+            fixed(params),
             fixed(w_front),
             pl.BlockSpec((D, D), lambda step: (0, 0), pipeline_mode=pl.Buffered(1)),
             fixed(taps),
@@ -446,14 +523,19 @@
     lane=lax.broadcasted_iota(jnp.int32,beta.shape,1)
     return jnp.sum(jnp.where(lane==h,beta,0.0),axis=1,keepdims=True)
 
-def attn_fwd_kernel(q_ref,k_ref,v_ref,beta_ref,mask_ref,ridge_ref,o_ref,a0_ref,a1_ref,kt_ref,vt_ref,w_ref):
+def attn_fwd_kernel(q_ref,k_ref,v_ref,beta_ref,info_ref,small_ref,o_ref,a0_ref,a1_ref,kt_ref,vt_ref,w_ref,mask_ref):
     h=pl.program_id(0)
     rows=q_ref.shape[0]
     span=WINDOW+QB
     kt_ref[...]=k_ref[...].T
     vt_ref[...]=v_ref[...].T
     column=head_column(beta_ref,h)
-    ridge=ridge_ref[...]
+    ridge=small_ref[:,HEADS+1:HEADS+2].astype(f32)
+
+    @pl.when(h==0)
+    def fill():
+        window_mask(info_ref[...],mask_ref)
+
     blocks=range(rows//QB)
     chunks=range(span//KEYS)
     for b in blocks:
@@ -487,20 +569,21 @@
     for b in blocks:
         o_ref[QB*b:QB*(b+1),:]=apply(b,x2[b],vt_ref).T
 
-def attn_fwd(q,k,v,beta,mask_t,ridge,**riding):
+def attn_fwd(q,k,v,beta,info,w_front,**riding):
     rows=q.shape[0]; keys=k.shape[0]
     head=lambda n: pl.BlockSpec((n,HEAD_DIM),lambda h:(0,h))
     heads_t=pl.BlockSpec((HEAD_DIM,rows),lambda h:(h,0))
     fixed=lambda a: pl.BlockSpec(a.shape,lambda h:(0,0))
+    small=pl.BlockSpec((HEAD_DIM,SMALL),lambda h:(h,3*D//SMALL))
     flops=6*2*rows*(WINDOW+QB)*D
     return call(
         attn_fwd_kernel,
         HEADS,
-        (q, k, v, beta, mask_t, ridge),
-        [head(rows), head(keys), head(keys), fixed(beta), fixed(mask_t), pl.BlockSpec((HEAD_DIM, 1), lambda h: (h, 0))],
+        (q, k, v, beta, info, w_front),
+        [head(rows), head(keys), head(keys), fixed(beta), fixed(info), small],
         [head(rows), heads_t, heads_t],
         [jax.ShapeDtypeStruct((rows, D), f32)] + [jax.ShapeDtypeStruct((D, rows), f32)] * 2,
-        [pltpu.VMEM((HEAD_DIM, keys), bf16)] * 2 + [pltpu.VMEM((rows // QB, WINDOW + QB, QB), f32)],
+        [pltpu.VMEM((HEAD_DIM, keys), bf16)] * 2 + [pltpu.VMEM((rows // QB, WINDOW + QB, QB), f32), pltpu.VMEM((keys, rows), bf16)],
         vmem=62,
         flops=2 * flops,
         traffic=20 << 20,
@@ -509,13 +592,18 @@
     )
 
 
-def attn_bwd_kernel(q_ref,k_ref,v_ref,beta_ref,mask_ref,ridge_ref,a0_ref,a1_ref,do_ref,dq_ref,dk_ref,dv_ref,dbeta_ref,dridge_ref,kt_ref,w_ref,acc_ref):
+def attn_bwd_kernel(q_ref,k_ref,v_ref,beta_ref,info_ref,small_ref,a0_ref,a1_ref,do_ref,dq_ref,dk_ref,dv_ref,dbeta_ref,dridge_ref,kt_ref,w_ref,acc_ref,mask_ref):
     h=pl.program_id(0)
     rows=q_ref.shape[0]
     span=WINDOW+QB
     kt_ref[...]=k_ref[...].T
     column=head_column(beta_ref,h)
-    ridge=ridge_ref[...]
+    ridge=small_ref[:,HEADS+1:HEADS+2].astype(f32)
+
+    @pl.when(h==0)
+    def fill():
+        window_mask(info_ref[...],mask_ref)
+
     blocks=range(rows//QB)
     chunks=range(span//KEYS)
     dk_ref[...]=jnp.zeros_like(dk_ref)
@@ -603,18 +691,19 @@
         dbeta_ref[...]=jnp.zeros_like(dbeta_ref)
     dbeta_ref[...]=jnp.where(lane==h,found,dbeta_ref[...])
 
-def attn_bwd(q,k,v,beta,mask_t,ridge,a0,a1,do,**riding):
+def attn_bwd(q,k,v,beta,info,w_front,a0,a1,do,**riding):
     rows=q.shape[0]; keys=k.shape[0]
     head=lambda n: pl.BlockSpec((n,HEAD_DIM),lambda h:(0,h))
     heads_t=pl.BlockSpec((HEAD_DIM,rows),lambda h:(h,0))
     fixed=lambda a: pl.BlockSpec(a.shape,lambda h:(0,0))
     rd=pl.BlockSpec((HEAD_DIM,1),lambda h:(h,0))
+    small=pl.BlockSpec((HEAD_DIM,SMALL),lambda h:(h,3*D//SMALL))
     flops=15*2*rows*(WINDOW+QB)*D
     return call(
         attn_bwd_kernel,
         HEADS,
-        (q, k, v, beta, mask_t, ridge, a0, a1, do),
-        [head(rows), head(keys), head(keys), fixed(beta), fixed(mask_t), rd, heads_t, heads_t, head(rows)],
+        (q, k, v, beta, info, w_front, a0, a1, do),
+        [head(rows), head(keys), head(keys), fixed(beta), fixed(info), small, heads_t, heads_t, head(rows)],
         [head(rows), head(keys), head(keys), fixed(beta), rd],
         [
             jax.ShapeDtypeStruct((rows, D), f32),
@@ -627,6 +716,7 @@
             pltpu.VMEM((HEAD_DIM, keys), bf16),
             pltpu.VMEM((rows // QB, WINDOW + QB, QB), f32),
             pltpu.VMEM((keys, 128), f32),
+            pltpu.VMEM((keys, rows), bf16),
         ],
         vmem=62,
         flops=2 * flops,
@@ -634,24 +724,6 @@
         name="attn_bwd",
         **riding,
     )
-
-
-def slot_of(positions, lengths):
-    slot = (positions >= 0).astype(jnp.int32) - 1
-    start = 0
-    for index in range(lengths.shape[0] - 1):
-        start = start + lengths[index]
-        slot = slot + (positions >= start).astype(jnp.int32)
-    return slot
-
-
-def is_live(positions, lengths, live):
-    found = positions < 0
-    start = 0
-    for index in range(lengths.shape[0]):
-        found = found | ((positions >= start) & (positions < start + live[index]))
-        start = start + lengths[index]
-    return found & (positions >= 0)
 
 
 class Here:
@@ -1368,13 +1440,13 @@
 
 
 def mid_kernel(
+    before,
     x_ref,
     o_ref,
     hid_ref,
     cot_ref,
-    live_ref,
-    hgain_ref,
-    fgain_ref,
+    info_ref,
+    params_ref,
     mats_in,
     ffn_in,
     down_in,
@@ -1412,7 +1484,7 @@
         dfg_ref[...] = jnp.zeros_like(dfg_ref)
         copies[0].wait()
 
-    hgain, fgain = hgain_ref[...], fgain_ref[...]
+    hgain, fgain = params_ref[2:3, :], params_ref[3:4, :]
     gate_pre = mm(hid_ref[...], mats_ref[:, :D])
     gate = jax.nn.sigmoid(gate_pre)
     gate_silu = gate_pre * gate
@@ -1429,7 +1501,8 @@
     x1_scale = lax.rsqrt(jnp.mean(x1 * x1, axis=-1, keepdims=True) + 1e-06)
     h2 = (x1 * x1_scale * fgain).astype(bf16)
     h2_ref[...] = h2
-    live = live_ref[...]
+    info = info_ref[...]
+    live = is_live(info, rows_from(info, before + step * ROWS, ROWS)).astype(f32)
     grad_out = live * cot_ref[...].astype(f32)
     dd = grad_out.astype(bf16)
     dd_ref[...] = dd
@@ -1479,7 +1552,7 @@
     do_ref[...] = in_heads(head_back, mixed, normal, dscaled * hgain).astype(bf16)
 
 
-def mid(x, mixed, hidden, first_own, cotangent, live, hgain, fgain, mats, ffn, down):
+def mid(x, mixed, hidden, first_own, cotangent, info, params, mats, ffn, down):
     rows = x.shape[0]
     inner = down.shape[0]
     shape = jax.ShapeDtypeStruct
@@ -1502,17 +1575,16 @@
         shape((rows, D), f32),
     ]
     found, _ = call(
-        mid_kernel,
+        functools.partial(mid_kernel, first_own * ROWS),
         rows // ROWS,
-        (x, mixed, hidden, cotangent, live, hgain, fgain, mats, ffn, down),
+        (x, mixed, hidden, cotangent, info, params, mats, ffn, down),
         [
             block(D),
             block(D),
             pl.BlockSpec((ROWS, D), lambda step: (step + first_own, 0)),
             block(D),
-            block(1),
-            row,
-            row,
+            pl.BlockSpec(info.shape, lambda step: (0, 0)),
+            pl.BlockSpec(params.shape, lambda step: (0, 0)),
             anywhere,
             anywhere,
             anywhere,
@@ -1685,6 +1757,40 @@
     return carried
 
 
+def widen_kernel(down_in, ffn0_in, ffn1_in, mats_in, k_in, v_in, q_in, down, gate, up, og, out, qkv):
+    down[...] = down_in[0, 0].astype(f32)
+    for source, start in ((ffn0_in, 0), (ffn1_in, ffn0_in.shape[2])):
+        rows = slice(start, start + source.shape[2])
+        inner = gate.shape[1]
+        gate[rows, :] = source[0, 0, :, :inner].astype(f32)
+        up[rows, :] = source[0, 0, :, inner:].astype(f32)
+    og[...] = mats_in[0, 0, :, :D].astype(f32)
+    out[...] = mats_in[0, 0, :, D:].astype(f32)
+    for index, source in enumerate((q_in, k_in, v_in)):
+        qkv[:, D * index : D * (index + 1)] = source[0, 0].astype(f32)
+
+
+def widen(down, ffn0, ffn1, mats, keys, values, queries):
+    ins = (down, ffn0, ffn1, mats, keys, values, queries)
+    rows, inner = mats.shape[2], ffn0.shape[3] // 2
+    widths = [(down.shape[2], D), (rows, inner), (rows, inner), (rows, D), (rows, D), (rows, 3 * D)]
+    found, _ = call(
+        widen_kernel,
+        4,
+        ins,
+        [
+            pl.BlockSpec((1, 1) + part.shape[2:], lambda step: (step // 2, step % 2, 0, 0))
+            for part in ins
+        ],
+        [pl.BlockSpec(width, lambda step: (step, 0)) for width in widths],
+        [jax.ShapeDtypeStruct((4 * height, width), f32) for height, width in widths],
+        vmem=62,
+        traffic=25 << 20,
+        name="widen",
+    )
+    return found
+
+
 def on_device(
     tokens,
     slot_lengths,
@@ -1710,14 +1816,13 @@
     shards = lax.axis_size("wshard")
     shard_rows = norm_gain.shape[0]
     tap_columns = TAPS * conv_weight.shape[1] // shard_rows
-    ffn = w_gate.shape[1]
 
     own_tokens = tokens[0]
     small = jnp.concatenate(
         [
             w_beta,
             jnp.stack([norm_gain, ridge, head_gain, ffn_gain]).T,
-            conv_weight.reshape(shard_rows, tap_columns),
+            conv_weight.reshape(TAPS, 3, shard_rows).transpose(2, 1, 0).reshape(shard_rows, -1),
         ],
         axis=1,
     )
@@ -1735,41 +1840,13 @@
         lambda: None, 1, (), [], [], [], riders=riders, table={0: events}, collective_id=0, name="begin"
     )
     w_front = whole_rows(w_front)
-    small = w_front[:, 3 * D :].astype(f32)
-    gain_in, all_ridge, gain_head, gain_ffn = (small[:, HEADS + index] for index in range(4))
-    taps = small[:, HEADS + 4 : HEADS + 4 + tap_columns]
-    taps = taps.reshape(shards, TAPS, -1).transpose(1, 0, 2).reshape(TAPS, 3 * D)
-
     rank = lax.axis_index("seq")
-    first = rank * row_count - halo_rows
-    lengths, live = slot_lengths[0], live_lengths[0]
-
-    def positions(start, shape, dim):
-        return start + lax.broadcasted_iota(jnp.int32, shape, dim)
-
-    conv_at = positions(first, (main_rows, TAPS), 0)
-    tap_at = lax.broadcasted_iota(jnp.int32, (main_rows, TAPS), 1)
-    same = (slot_of(conv_at, lengths) == slot_of(conv_at - tap_at, lengths)).astype(f32)
-    key_at = positions(first, (main_rows, 1), 0)
-    query_at = positions(first + halo_rows, (1, row_count), 1)
-    spacing = query_at - key_at
-    mask = (
-        (spacing >= 0)
-        & (spacing < WINDOW)
-        & (slot_of(key_at, lengths) == slot_of(query_at, lengths))
-        & is_live(key_at, lengths, live)
-    ).astype(bf16)
-    own_at = positions(first + halo_rows, (row_count, 1), 0)
-    valid_own = is_live(own_at, lengths, live).astype(f32)
-    gain_row = gain_in[None, :]
-    ridge_column = all_ridge[:, None]
-
-    (hidden, kv_in, q_in, q_pre, queries, keys, values, beta), ((ffn_in,), (mats,), (all_down,)) = front(
+    info = slot_info(slot_lengths[0], live_lengths[0], rank * row_count - halo_rows)
+
+    (hidden, kv_in, q_in, q_pre, queries, keys, values, beta, params, taps), ((ffn_in,), (mats,), (all_down,)) = front(
         ext_tokens,
-        same,
-        gain_row,
+        info,
         w_front,
-        taps,
         row_count,
         riders=[Gather(None, 1, 2, ffn_in), Gather(out_mats, 0, 0), Gather(w_down, 0, 0)],
         table={0: [(0, 1), (1, 0), (2, 0)], 4: [(0, 2)], 99: [(1, 1), (2, 1), (0, 3)]},
@@ -1780,8 +1857,8 @@
         keys,
         values,
         beta,
-        mask,
-        ridge_column,
+        info,
+        w_front,
         riders=[Gather(None, 3, 3, ffn_in), Gather(None, 1, 3, mats), Gather(None, 1, 3, all_down)],
         table={
             0: [(1, 1), (2, 1), (0, 3)],
@@ -1800,9 +1877,8 @@
         hidden,
         first_own,
         cotangent[0],
-        valid_own,
-        gain_head[None, :],
-        gain_ffn[None, :],
+        info,
+        params,
         mats,
         ffn_in,
         all_down,
@@ -1817,8 +1893,8 @@
         keys,
         values,
         beta,
-        mask,
-        ridge_column,
+        info,
+        w_front,
         image0,
         image1,
         d_mixed,
@@ -1839,7 +1915,7 @@
     ) = back(
         ext_tokens,
         kv_in,
-        same,
+        info,
         q_in,
         q_pre,
         d_key,
@@ -1849,7 +1925,7 @@
         d_beta,
         d_gate,
         d_xout,
-        gain_row,
+        params,
         w_front,
         mats,
         taps,
@@ -1878,7 +1954,7 @@
             d_ridge,
             d_ghead.reshape(D, 1),
             d_gffn.reshape(D, 1),
-            d_taps.reshape(TAPS, shards, -1).transpose(1, 0, 2).reshape(D, tap_columns),
+            d_taps.reshape(TAPS, shards, 3, -1).transpose(1, 3, 2, 0).reshape(D, tap_columns),
         ],
         axis=1,
     ).astype(bf16)
@@ -1917,30 +1993,25 @@
     )
     (total_ffn1,), _, _, _, _, (total_k,), (total_v,), (total_q,), (total_small,) = carried[:9]
     (total_down,), (total_ffn0,) = carried[9:]
-    def final(*sums):
-        whole = jnp.concatenate([finish_sum(part) for part in sums], axis=2)
-        return whole.reshape(-1, whole.shape[-1])
-
-    total_down = final(total_down)
-    total_ffn = final(total_ffn0, total_ffn1)
-    total_middle = final(total_mats)
-    total_front = jnp.concatenate([final(total_q), final(total_k), final(total_v)], axis=1)
-    t_small = final(total_small).astype(f32)
+    sums = (total_down, total_ffn0, total_ffn1, total_mats, total_k, total_v, total_q)
+    t_down, t_gate, t_up, t_og, t_out, t_qkv = widen(*(finish_sum(part) for part in sums))
+    t_small = finish_sum(total_small)[..., :SMALL].reshape(shard_rows, SMALL).astype(f32)
+    t_taps = t_small[:, HEADS + 4 : HEADS + 4 + tap_columns]
     return (
         output[None],
         d_tokens[None],
         t_small[:, HEADS],
-        total_front.astype(f32),
+        t_qkv,
         t_small[:, :HEADS],
-        total_middle[:, :D].astype(f32),
-        t_small[:, HEADS + 4 : HEADS + 4 + tap_columns].reshape(TAPS, -1),
+        t_og,
+        t_taps.reshape(shard_rows, 3, TAPS).transpose(2, 1, 0).reshape(TAPS, -1),
         t_small[:, HEADS + 1],
         t_small[:, HEADS + 2],
-        total_middle[:, D:].astype(f32),
+        t_out,
         t_small[:, HEADS + 3],
-        total_ffn[:, :ffn].astype(f32),
-        total_ffn[:, ffn:].astype(f32),
-        total_down.astype(f32),
+        t_gate,
+        t_up,
+        t_down,
     )
 
 

time: 495 us -> 472 us (0.954)
  other arithmetic: 28.8 us -> 5.36 us
  Pallas kernels: 431 us -> 442 us
  local copies, waits for them, and re-layouts: 21.1 us -> 14.2 us
    convert_element_type x9 -> x1, other arithmetic: 20.9 us -> 0.02 us  [on_device(): finish_sum(total_small)[..., :SMALL].reshape(shard_rows, SMALL).astype(f32)]
    pallas_call x8 -> x9, Pallas kernels: 431 us -> 442 us  [call(): pl.pallas_call(body, grid=(grid,), in_specs=list(in_specs) + [anywhere] *...]
where the time goes in v6:
time: 472 us; the launch traced here: 463 us
  Pallas kernels  442 us (94%)
  local copies, waits for them, and re-layouts  14.2 us (3%)
  other arithmetic  5.36 us (1%)
    pallas_call x9, Pallas kernels, call(): pl.pallas_call(body, grid=(grid,), in_specs=list(in_specs) + [anywhere] *...  442 us

profile of v6, /device:TPU:0, one launch (start us, length us, event | category | flops | bytes accessed | tf_op | source)
XLA Modules:
  0.0 463.0 jit_solution(8659748488430515771)
XLA Ops:
  0.6 0.0 copy-start.1
  0.7 0.8 reshape.100
  1.5 0.7 stack.18
  2.1 0.7 stack.17
  2.8 0.7 stack.16
  3.4 0.7 stack.15
  4.1 0.7 pad_maximum_fusion.2
  4.8 0.1 copy.80
  4.9 1.6 fusion.1
  6.6 0.2 copy-done.2
  6.8 0.2 pad_maximum_fusion
  7.0 1.0 copy-done
  8.0 0.0 copy-start.6
  8.0 60.7 %begin.1 = (bf16[4,2,2,64,3584]{4,3,2,1,0:T(8,128)(2,1)}, bf16[1552,1024]{1,0:T(8,128)(2,1)}, bf16[4,2,2,64,5632]{4,3,2,1,0:T(8,128)(2,1)}) custom-call(bf16[2,2,64,3584]{3,2,1,0:T(8,128)(2,1)S(1)} %bitcast.51, bf16[512,1024]{1,0:T(8,128)(2,1)S(1)} %bitcast.53, bf16[2,2,64,5632]{3,2,1,0:T(8,128)(2,1)S(1)} %bitcast.50), custom_call_target="tpu_custom_call" | custom-call | tf_op jit(solution)/shard_map/begin/pallas_call | solution.py:1404
  68.7 0.1 pad_add_fusion
  68.8 0.1 multiply_reduce_fusion
  68.9 0.7 add.14.refs_1_.refs_4_.refs_3_
  69.6 0.0 copy-done.5
  69.6 1.1 pad_maximum_fusion.1
  70.7 52.6 %front.1 = (bf16[1552,1024]{1,0:T(8,128)(2,1)}, bf16[1552,2048]{1,0:T(8,128)(2,1)}, bf16[512,1024]{1,0:T(8,128)(2,1)}, bf16[16,1024]{1,0:T(8,128)(2,1)}, bf16[51...) custom-call(bf16[1552,1024]{1,0:T(8,128)(2,1)} %get-tuple-element.83, ...), custom_call_target="tpu_custom_call", output_to_operand_aliasing={{10}: (3, {})} | custom-call | flops 15032385536 | bytes 31457280 | tf_op jit(solution)/shard_map/front/pallas_call | solution.py:1404
  123.3 41.5 %attn_fwd.1 = (f32[512,1024]{1,0:T(8,128)}, f32[1024,512]{1,0:T(8,128)}, f32[1024,512]{1,0:T(8,128)}, bf16[4,2,2,64,5632]{4,3,2,1,0:T(8,128)(2,1)}, bf16[4,2,2,6...) custom-call(bf16[512,1024]{1,0:T(8,128)(2,1)} %get-tuple-element.86., ...), custom_call_target="tpu_custom_call", output_to_operand_aliasing={{3}: (6, {}), {4}: (7, {}), {5}: (8, {})} | custom-call | flops 16106127360 | bytes 20971520 | tf_op jit(solution)/shard_map/attn_fwd/pallas_call | solution.py:1404
  164.8 36.7 %mid.1 = (bf16[512,1024]{1,0:T(8,128)(2,1)}, bf16[512,1024]{1,0:T(8,128)(2,1)}, bf16[512,1024]{1,0:T(8,128)(2,1)}, bf16[512,2816]{1,0:T(8,128)(2,1)}, bf16[512,5...) custom-call(bf16[512,1024]{1,0:T(8,128)(2,1)} %bitcast.52, ...), custom_call_target="tpu_custom_call" | custom-call | flops 22011707392 | bytes 52428800 | tf_op jit(solution)/shard_map/mid/pallas_call | solution.py:1404
  201.5 21.8 %mid_grads.1 = (bf16[2816,1024]{1,0:T(8,128)(2,1)}, bf16[1024,5632]{1,0:T(8,128)(2,1)}, bf16[1024,2048]{1,0:T(8,128)(2,1)}) custom-call(bf16[1552,1024]{1,0:T(8,128)(2,1)} %get-tuple-element.94.refs_2_.refs_0_.refs_1_, bf16[512,1024]{1,0:T(8,128)(2,1)} %get-tuple-element.106.refs_1_, bf16[512,1024]{1,0:T(8,128)(2,1)} %get-tuple-element.107.refs_2_, ...), custom_call_target="tpu_custom_call" | custom-call | flops 11005853696 | bytes 41943040 | tf_op jit(solution)/shard_map/mid_grads/pallas_call | solution.py:1404
  223.3 67.5 %attn_bwd.1 = (f32[512,1024]{1,0:T(8,128)}, f32[1536,1024]{1,0:T(8,128)}, f32[1536,1024]{1,0:T(8,128)}, f32[1536,128]{1,0:T(8,128)}, f32[1024,1]{1,0:T(8,128)}, ...) custom-call(bf16[512,1024]{1,0:T(8,128)(2,1)} %get-tuple-element.86.refs_0_, ...), custom_call_target="tpu_custom_call" | custom-call | flops 40265318400 | bytes 31457280 | tf_op jit(solution)/shard_map/attn_bwd/pallas_call | solution.py:1404
  290.8 0.0 copy-start.8
  290.8 81.1 %back.1 = (bf16[1552,2048]{1,0:T(8,128)(2,1)}, bf16[512,1024]{1,0:T(8,128)(2,1)}, bf16[16,1024]{1,0:T(8,128)(2,1)}, bf16[1536,128]{1,0:T(8,128)(2,1)}, f32[1,102...) custom-call(bf16[1552,1024]{1,0:T(8,128)(2,1)} %get-tuple-element.83, ...), custom_call_target="tpu_custom_call" | custom-call | flops 22548578304 | bytes 41943040 | tf_op jit(solution)/shard_map/back/pallas_call | solution.py:1404
  372.0 0.7 convert_bitcast_fusion.2
  372.7 0.2 copy.64
  373.0 0.2 copy.65
  373.2 0.2 copy.66
  373.4 0.8 convert.28
  374.3 0.2 copy.67
  374.5 1.0 concatenate.24
  375.5 0.8 pad.9.refs_8_
  376.3 72.0 %end.1 = (bf16[2,2,32,5632]{3,2,1,0:T(8,128)(2,1)}, bf16[4,64,512]{2,1,0:T(8,128)(2,1)}, bf16[4,64,512]{2,1,0:T(8,128)(2,1)}, bf16[4,64,512]{2,1,0:T(8,128)(2,1)...) custom-call(bf16[1552,1024]{1,0:T(8,128)(2,1)} %get-tuple-element.94, ...), custom_call_target="tpu_custom_call" | custom-call | flops 7516192768 | bytes 26214400 | tf_op jit(solution)/shard_map/end/pallas_call | solution.py:1404
  448.3 0.8 slice.21
  449.1 0.2 fusion.3
  449.3 0.6 copy.74
  450.0 8.2 %widen.1 = (f32[704,1024]{1,0:T(8,128)}, f32[256,2816]{1,0:T(8,128)}, f32[256,2816]{1,0:T(8,128)}, f32[256,1024]{1,0:T(8,128)}, f32[256,1024]{1,0:T(8,128)}, /*index=5*/f32[256,3072]{1,0:T(8,128)}) custom-call(bf16[2,2,176,1024]{3,2,1,0:T(8,128)(2,1)} %get-tuple-element.139.refs_0_, bf16[2,2,32,5632]{3,2,1,0:T(8,128)(2,1)} %get-tuple-element.140.refs_1_, ...), custom_call_target="tpu_custom_call" | custom-call | bytes 26214400 | tf_op jit(solution)/shard_map/widen/pallas_call | solution.py:1404
  458.2 0.7 copy.75
  458.8 0.1 slice.30
  458.9 0.1 copy.76
  459.0 0.6 reshape.117
  459.6 0.6 copy.77
  460.3 0.6 copy.78
  460.9 0.6 copy.79
  461.6 0.0 copy-done.3
  461.6 1.0 copy.87
  (27 shorter events, 0.2 us)
Async XLA Ops:
  0.6 6.0 %copy-start.1 = (bf16[256,2816]{1,0:T(8,128)(2,1)S(1)}, bf16[256,2816]{1,0:T(8,128)(2,1)}, u32[]{:S(2)}) copy-start(bf16[256,2816]{1,0:T(8,128)(2,1)} %param.30) | copy-start | bytes 4325380
  4.9 1.8 copy-start.2
  6.8 1.2 copy-start
  8.0 60.7 %copy-start.10 = (s32[1,3]{1,0:T(1,128)S(1)}, s32[1,3]{1,0:T(1,128)}, u32[]{:S(2)}) copy-start(s32[1,3]{1,0:T(1,128)} %param.19) | copy-start | bytes 40
  8.0 60.7 %copy-start.11 = (s32[1,3]{1,0:T(1,128)S(1)}, s32[1,3]{1,0:T(1,128)}, u32[]{:S(2)}) copy-start(s32[1,3]{1,0:T(1,128)} %param.18) | copy-start | bytes 40
  8.0 60.8 %copy-start.7 = (s32[8,6]{1,0:T(8,128)S(1)}, s32[8,6]{1,0:T(8,128)}, u32[]{:S(2)}) copy-start(s32[8,6]{1,0:T(8,128)} %constant.21.clone) | copy-start | bytes 580
  8.0 61.6 %copy-start.5 = (bf16[256,1024]{1,0:T(8,128)(2,1)S(1)}, bf16[256,1024]{1,0:T(8,128)(2,1)}, u32[]{:S(2)}) copy-start(bf16[256,1024]{1,0:T(8,128)(2,1)} %param.27) | copy-start | bytes 1572868
  8.0 61.6 %copy-start.6 = (bf16[256,1024]{1,0:T(8,128)(2,1)S(1)}, bf16[256,1024]{1,0:T(8,128)(2,1)}, u32[]{:S(2)}) copy-start(bf16[256,1024]{1,0:T(8,128)(2,1)} %param.23) | copy-start | bytes 1572868
  290.8 82.1 %copy-start.4 = (f32[1024,1]{1,0:T(8,128)S(1)}, f32[1024,1]{1,0:T(8,128)}, u32[]{:S(2)}) copy-start(f32[1024,1]{1,0:T(8,128)} %get-tuple-element.131) | copy-start | bytes 12292
  290.8 82.1 %copy-start.8 = (f32[1,1024]{1,0:T(1,128)S(1)}, f32[1,1024]{1,0:T(1,128)}, u32[]{:S(2)}) copy-start(f32[1,1024]{1,0:T(1,128)} %get-tuple-element.132) | copy-start | bytes 12292
  290.8 82.1 %copy-start.9 = (f32[1,1024]{1,0:T(1,128)S(1)}, f32[1,1024]{1,0:T(1,128)}, u32[]{:S(2)}) copy-start(f32[1,1024]{1,0:T(1,128)} %get-tuple-element.133) | copy-start | bytes 12292
  450.0 11.6 %copy-start.3 = (bf16[512,1024]{1,0:T(8,128)(2,1)S(1)}, bf16[512,1024]{1,0:T(8,128)(2,1)}, u32[]{:S(2)}) copy-start(bf16[512,1024]{1,0:T(8,128)(2,1)} %get-tuple-element.125) | copy-start | bytes 3145732
